TPU v7x, 512 devices: a whole 4x8x8 slice. The times are simulated.
512 devices in a mesh: bulk: 32 (over z, y_hi), blk: 16 (over y_lo, x, core).
Axes of the slice: x: 4, y: 8 (y_hi: 4, y_lo: 2; y = y_hi * 2 + y_lo), z: 8, core: 2. Of those that a mesh axis runs over, the one named last changes fastest.
Arguments:
- aux_factors: bfloat16 [64, 1024, 4096], P('bulk', None, 'blk')
- tile_cols: int32 [16, 9], P('blk'), may hold values from -1 to 15, as said below
Outputs:
- exchange_tiles: float32 [144, 256, 256], P('blk', 'bulk')
Inputs may be any that keep to these rules, and one draw needn't show every extreme that they name: `tile_cols`: row a lists distinct blocks, a itself first; every unordered pair of blocks stands in exactly one of its two rows; -1 marks empty slots, which come last; some row has no empty slot.
All inputs are finite; a program needn't handle non-finite values.
Results may differ from a plain program's by a relative error of at most 0.0003.
Values may be sent and summed in bfloat16 or wider, within the bound.
No kernel may reach another device: no remote copies, remote signals or barrier semaphores. Data moves between devices by JAX's collectives and lax.ppermute only.
A program may use at most 64 MiB of HBM per device.

v0:
```python
import jax
import jax.numpy as jnp
from jax import lax
from jax.sharding import PartitionSpec as P


def shifted(value, axis, by):
    size = lax.axis_size(axis)
    return lax.ppermute(value, axis, [(i, (i + by) % size) for i in range(size)])


def local(aux_factors, tile_cols):
    mine = aux_factors.reshape(-1, aux_factors.shape[2])
    targets = tile_cols[0]
    blocks = lax.axis_size("blk")
    me = lax.axis_index("blk")
    width = mine.shape[1]

    def product(held):
        return lax.dot_general(
            mine, held, (((0,), (0,)), ((), ())), preferred_element_type=jnp.float32
        )

    def nothing(held):
        return jnp.zeros((width, width), jnp.float32)

    def settle(stack, held, which):
        wanted = targets == which
        tile = lax.cond(jnp.any(wanted), product, nothing, held)
        return stack + jnp.where(wanted[:, None, None], tile[None], 0.0)

    stack = jnp.zeros((targets.shape[0], width, width), jnp.float32)
    stack = settle(stack, mine, me)

    def forward_turn(turn, carry):
        totals, held = carry
        held = shifted(held, "blk", 1)
        return (settle(totals, held, (me - turn) % blocks), held)

    stack, held = lax.fori_loop(1, blocks, forward_turn, (stack, mine))
    stack = lax.psum_scatter(stack, "bulk", scatter_dimension=1, tiled=True)
    return stack


def solution(mesh):
    in_specs = (P("bulk", None, "blk"), P("blk", None))
    out_specs = P("blk", "bulk", None)
    return jax.shard_map(local, mesh=mesh, in_specs=in_specs, out_specs=out_specs, check_vma=False)
```

profile of v0, /device:TPU:1, one launch (start us, length us, event | category | flops | bytes accessed | tf_op | source)
XLA Modules:
  0.0 587.1 jit_solution(7574917306655654227)
XLA Ops:
  13.1 330.7 %while.17 = (s32[]{:T(128)}, f32[9,256,256]{2,1,0:T(8,128)S(1)}, bf16[2048,256]{1,0:T(8,128)(2,1)}, s32[]{:T(128)}, s32[9]{0:T(128)S(1)}, /*index=5*/bf16[2048,2...) while((s32[]{:T(128)}, f32[9,256,256]{2,1,0:T(8,128)S(1)}, bf16[2048,256]{1,0:T(8,128)(2,1)}, ...), condition=%wide.region_7.8_spmd, body=%wide.region_3.7_spmd.sunk | while | flops 269615136 | bytes 13631838 | solution.py:40
  13.1 4.5 collective-permute-start
  18.9 10.7 %collective-permute-done = bf16[2048,256]{1,0:T(8,128)(2,1)S(1)} collective-permute-done((bf16[2048,256]{1,0:T(8,128)(2,1)}, bf16[2048,256]{1,0:T(8,128)(2,1)S(1)}, u32[]{:S(2)}, u32[]{:S(2)}) %collective-permute-start) | collective-permute-done | bytes 1048608 | tf_op jit(solution)/shard_map/while/body/eval_jaxpr/ppermute | solution.py:9
  32.8 4.3 collective-permute-start
  38.4 10.7 %collective-permute-done = bf16[2048,256]{1,0:T(8,128)(2,1)S(1)} collective-permute-done((bf16[2048,256]{1,0:T(8,128)(2,1)}, bf16[2048,256]{1,0:T(8,128)(2,1)S(1)}, u32[]{:S(2)}, u32[]{:S(2)}) %collective-permute-start) | collective-permute-done | bytes 1048608 | tf_op jit(solution)/shard_map/while/body/eval_jaxpr/ppermute | solution.py:9
  54.0 2.6 collective-permute-start
  58.0 11.2 %collective-permute-done = bf16[2048,256]{1,0:T(8,128)(2,1)S(1)} collective-permute-done((bf16[2048,256]{1,0:T(8,128)(2,1)}, bf16[2048,256]{1,0:T(8,128)(2,1)S(1)}, u32[]{:S(2)}, u32[]{:S(2)}) %collective-permute-start) | collective-permute-done | bytes 1048608 | tf_op jit(solution)/shard_map/while/body/eval_jaxpr/ppermute | solution.py:9
  69.1 2.4 conditional.4
  74.0 3.8 collective-permute-start
  79.2 13.3 %collective-permute-done = bf16[2048,256]{1,0:T(8,128)(2,1)S(1)} collective-permute-done((bf16[2048,256]{1,0:T(8,128)(2,1)}, bf16[2048,256]{1,0:T(8,128)(2,1)S(1)}, u32[]{:S(2)}, u32[]{:S(2)}) %collective-permute-start) | collective-permute-done | bytes 1048608 | tf_op jit(solution)/shard_map/while/body/eval_jaxpr/ppermute | solution.py:9
  100.6 15.2 %collective-permute-done = bf16[2048,256]{1,0:T(8,128)(2,1)S(1)} collective-permute-done((bf16[2048,256]{1,0:T(8,128)(2,1)}, bf16[2048,256]{1,0:T(8,128)(2,1)S(1)}, u32[]{:S(2)}, u32[]{:S(2)}) %collective-permute-start) | collective-permute-done | bytes 1048608 | tf_op jit(solution)/shard_map/while/body/eval_jaxpr/ppermute | solution.py:9
  123.9 15.2 %collective-permute-done = bf16[2048,256]{1,0:T(8,128)(2,1)S(1)} collective-permute-done((bf16[2048,256]{1,0:T(8,128)(2,1)}, bf16[2048,256]{1,0:T(8,128)(2,1)S(1)}, u32[]{:S(2)}, u32[]{:S(2)}) %collective-permute-start) | collective-permute-done | bytes 1048608 | tf_op jit(solution)/shard_map/while/body/eval_jaxpr/ppermute | solution.py:9
  145.6 15.2 %collective-permute-done = bf16[2048,256]{1,0:T(8,128)(2,1)S(1)} collective-permute-done((bf16[2048,256]{1,0:T(8,128)(2,1)}, bf16[2048,256]{1,0:T(8,128)(2,1)S(1)}, u32[]{:S(2)}, u32[]{:S(2)}) %collective-permute-start) | collective-permute-done | bytes 1048608 | tf_op jit(solution)/shard_map/while/body/eval_jaxpr/ppermute | solution.py:9
  167.2 15.2 %collective-permute-done = bf16[2048,256]{1,0:T(8,128)(2,1)S(1)} collective-permute-done((bf16[2048,256]{1,0:T(8,128)(2,1)}, bf16[2048,256]{1,0:T(8,128)(2,1)S(1)}, u32[]{:S(2)}, u32[]{:S(2)}) %collective-permute-start) | collective-permute-done | bytes 1048608 | tf_op jit(solution)/shard_map/while/body/eval_jaxpr/ppermute | solution.py:9
  188.8 15.2 %collective-permute-done = bf16[2048,256]{1,0:T(8,128)(2,1)S(1)} collective-permute-done((bf16[2048,256]{1,0:T(8,128)(2,1)}, bf16[2048,256]{1,0:T(8,128)(2,1)S(1)}, u32[]{:S(2)}, u32[]{:S(2)}) %collective-permute-start) | collective-permute-done | bytes 1048608 | tf_op jit(solution)/shard_map/while/body/eval_jaxpr/ppermute | solution.py:9
  210.5 16.8 %collective-permute-done = bf16[2048,256]{1,0:T(8,128)(2,1)S(1)} collective-permute-done((bf16[2048,256]{1,0:T(8,128)(2,1)}, bf16[2048,256]{1,0:T(8,128)(2,1)S(1)}, u32[]{:S(2)}, u32[]{:S(2)}) %collective-permute-start) | collective-permute-done | bytes 1048608 | tf_op jit(solution)/shard_map/while/body/eval_jaxpr/ppermute | solution.py:9
  235.4 13.5 %collective-permute-done = bf16[2048,256]{1,0:T(8,128)(2,1)S(1)} collective-permute-done((bf16[2048,256]{1,0:T(8,128)(2,1)}, bf16[2048,256]{1,0:T(8,128)(2,1)S(1)}, u32[]{:S(2)}, u32[]{:S(2)}) %collective-permute-start) | collective-permute-done | bytes 1048608 | tf_op jit(solution)/shard_map/while/body/eval_jaxpr/ppermute | solution.py:9
  252.1 3.2 collective-permute-start
  256.7 13.9 %collective-permute-done = bf16[2048,256]{1,0:T(8,128)(2,1)S(1)} collective-permute-done((bf16[2048,256]{1,0:T(8,128)(2,1)}, bf16[2048,256]{1,0:T(8,128)(2,1)S(1)}, u32[]{:S(2)}, u32[]{:S(2)}) %collective-permute-start) | collective-permute-done | bytes 1048608 | tf_op jit(solution)/shard_map/while/body/eval_jaxpr/ppermute | solution.py:9
  273.8 2.7 collective-permute-start
  277.9 14.3 %collective-permute-done = bf16[2048,256]{1,0:T(8,128)(2,1)S(1)} collective-permute-done((bf16[2048,256]{1,0:T(8,128)(2,1)}, bf16[2048,256]{1,0:T(8,128)(2,1)S(1)}, u32[]{:S(2)}, u32[]{:S(2)}) %collective-permute-start) | collective-permute-done | bytes 1048608 | tf_op jit(solution)/shard_map/while/body/eval_jaxpr/ppermute | solution.py:9
  300.4 15.2 %collective-permute-done = bf16[2048,256]{1,0:T(8,128)(2,1)S(1)} collective-permute-done((bf16[2048,256]{1,0:T(8,128)(2,1)}, bf16[2048,256]{1,0:T(8,128)(2,1)S(1)}, u32[]{:S(2)}, u32[]{:S(2)}) %collective-permute-start) | collective-permute-done | bytes 1048608 | tf_op jit(solution)/shard_map/while/body/eval_jaxpr/ppermute | solution.py:9
  323.7 15.2 %collective-permute-done = bf16[2048,256]{1,0:T(8,128)(2,1)S(1)} collective-permute-done((bf16[2048,256]{1,0:T(8,128)(2,1)}, bf16[2048,256]{1,0:T(8,128)(2,1)S(1)}, u32[]{:S(2)}, u32[]{:S(2)}) %collective-permute-start) | collective-permute-done | bytes 1048608 | tf_op jit(solution)/shard_map/while/body/eval_jaxpr/ppermute | solution.py:9
  345.2 235.1 %reduce-scatter.2.cloned.1.call-done = f32[9,8,256]{2,1,0:T(8,128)} async-done(((f32[9,256,256]{2,1,0:T(8,128)}), f32[9,8,256]{2,1,0:T(8,128)}) %reduce-scatter.2.cloned.1.call-update) | async-done | bytes 73744 | tf_op jit(solution)/shard_map/reduce_scatter | solution.py:41
  (94 shorter events, 120.0 us)
Async XLA Ops:
  6.5 573.7 %reduce-scatter.2.cloned.1.call-start = ((), (), s32[]{:S(2)}) async-start(), calls=%async_computation.1 | async-start | bytes 2433024 | tf_op jit(solution)/shard_map/reduce_scatter | solution.py:41
  10.7 2.3 copy-start.1
  13.1 16.6 %collective-permute-start = (bf16[2048,256]{1,0:T(8,128)(2,1)}, bf16[2048,256]{1,0:T(8,128)(2,1)S(1)}, u32[]{:S(2)}, u32[]{:S(2)}) collective-permute-start(bf16[2048,256]{1,0:T(8,128)(2,1)} %get-tuple-element.250), channel_id=1, source_target_pairs={{0,1},{1,2},{2,3},{3,4},{4,5},{5,6},{6,7},{7,8},{8,9},{9,10},{10,1... | collective-permute-start | bytes 3145736 | tf_op jit(solution)/shard_map/while/body/eval_jaxpr/ppermute | solution.py:9
  32.8 16.3 %collective-permute-start = (bf16[2048,256]{1,0:T(8,128)(2,1)}, bf16[2048,256]{1,0:T(8,128)(2,1)S(1)}, u32[]{:S(2)}, u32[]{:S(2)}) collective-permute-start(bf16[2048,256]{1,0:T(8,128)(2,1)} %get-tuple-element.250), channel_id=1, source_target_pairs={{0,1},{1,2},{2,3},{3,4},{4,5},{5,6},{6,7},{7,8},{8,9},{9,10},{10,1... | collective-permute-start | bytes 3145736 | tf_op jit(solution)/shard_map/while/body/eval_jaxpr/ppermute | solution.py:9
  54.0 15.1 %collective-permute-start = (bf16[2048,256]{1,0:T(8,128)(2,1)}, bf16[2048,256]{1,0:T(8,128)(2,1)S(1)}, u32[]{:S(2)}, u32[]{:S(2)}) collective-permute-start(bf16[2048,256]{1,0:T(8,128)(2,1)} %get-tuple-element.250), channel_id=1, source_target_pairs={{0,1},{1,2},{2,3},{3,4},{4,5},{5,6},{6,7},{7,8},{8,9},{9,10},{10,1... | collective-permute-start | bytes 3145736 | tf_op jit(solution)/shard_map/while/body/eval_jaxpr/ppermute | solution.py:9
  74.0 18.4 %collective-permute-start = (bf16[2048,256]{1,0:T(8,128)(2,1)}, bf16[2048,256]{1,0:T(8,128)(2,1)S(1)}, u32[]{:S(2)}, u32[]{:S(2)}) collective-permute-start(bf16[2048,256]{1,0:T(8,128)(2,1)} %get-tuple-element.250), channel_id=1, source_target_pairs={{0,1},{1,2},{2,3},{3,4},{4,5},{5,6},{6,7},{7,8},{8,9},{9,10},{10,1... | collective-permute-start | bytes 3145736 | tf_op jit(solution)/shard_map/while/body/eval_jaxpr/ppermute | solution.py:9
  97.3 18.4 %collective-permute-start = (bf16[2048,256]{1,0:T(8,128)(2,1)}, bf16[2048,256]{1,0:T(8,128)(2,1)S(1)}, u32[]{:S(2)}, u32[]{:S(2)}) collective-permute-start(bf16[2048,256]{1,0:T(8,128)(2,1)} %get-tuple-element.250), channel_id=1, source_target_pairs={{0,1},{1,2},{2,3},{3,4},{4,5},{5,6},{6,7},{7,8},{8,9},{9,10},{10,1... | collective-permute-start | bytes 3145736 | tf_op jit(solution)/shard_map/while/body/eval_jaxpr/ppermute | solution.py:9
  120.7 18.4 %collective-permute-start = (bf16[2048,256]{1,0:T(8,128)(2,1)}, bf16[2048,256]{1,0:T(8,128)(2,1)S(1)}, u32[]{:S(2)}, u32[]{:S(2)}) collective-permute-start(bf16[2048,256]{1,0:T(8,128)(2,1)} %get-tuple-element.250), channel_id=1, source_target_pairs={{0,1},{1,2},{2,3},{3,4},{4,5},{5,6},{6,7},{7,8},{8,9},{9,10},{10,1... | collective-permute-start | bytes 3145736 | tf_op jit(solution)/shard_map/while/body/eval_jaxpr/ppermute | solution.py:9
  142.3 18.4 %collective-permute-start = (bf16[2048,256]{1,0:T(8,128)(2,1)}, bf16[2048,256]{1,0:T(8,128)(2,1)S(1)}, u32[]{:S(2)}, u32[]{:S(2)}) collective-permute-start(bf16[2048,256]{1,0:T(8,128)(2,1)} %get-tuple-element.250), channel_id=1, source_target_pairs={{0,1},{1,2},{2,3},{3,4},{4,5},{5,6},{6,7},{7,8},{8,9},{9,10},{10,1... | collective-permute-start | bytes 3145736 | tf_op jit(solution)/shard_map/while/body/eval_jaxpr/ppermute | solution.py:9
  163.9 18.4 %collective-permute-start = (bf16[2048,256]{1,0:T(8,128)(2,1)}, bf16[2048,256]{1,0:T(8,128)(2,1)S(1)}, u32[]{:S(2)}, u32[]{:S(2)}) collective-permute-start(bf16[2048,256]{1,0:T(8,128)(2,1)} %get-tuple-element.250), channel_id=1, source_target_pairs={{0,1},{1,2},{2,3},{3,4},{4,5},{5,6},{6,7},{7,8},{8,9},{9,10},{10,1... | collective-permute-start | bytes 3145736 | tf_op jit(solution)/shard_map/while/body/eval_jaxpr/ppermute | solution.py:9
  185.6 18.4 %collective-permute-start = (bf16[2048,256]{1,0:T(8,128)(2,1)}, bf16[2048,256]{1,0:T(8,128)(2,1)S(1)}, u32[]{:S(2)}, u32[]{:S(2)}) collective-permute-start(bf16[2048,256]{1,0:T(8,128)(2,1)} %get-tuple-element.250), channel_id=1, source_target_pairs={{0,1},{1,2},{2,3},{3,4},{4,5},{5,6},{6,7},{7,8},{8,9},{9,10},{10,1... | collective-permute-start | bytes 3145736 | tf_op jit(solution)/shard_map/while/body/eval_jaxpr/ppermute | solution.py:9
  207.2 20.1 %collective-permute-start = (bf16[2048,256]{1,0:T(8,128)(2,1)}, bf16[2048,256]{1,0:T(8,128)(2,1)S(1)}, u32[]{:S(2)}, u32[]{:S(2)}) collective-permute-start(bf16[2048,256]{1,0:T(8,128)(2,1)} %get-tuple-element.250), channel_id=1, source_target_pairs={{0,1},{1,2},{2,3},{3,4},{4,5},{5,6},{6,7},{7,8},{8,9},{9,10},{10,1... | collective-permute-start | bytes 3145736 | tf_op jit(solution)/shard_map/while/body/eval_jaxpr/ppermute | solution.py:9
  232.2 16.7 %collective-permute-start = (bf16[2048,256]{1,0:T(8,128)(2,1)}, bf16[2048,256]{1,0:T(8,128)(2,1)S(1)}, u32[]{:S(2)}, u32[]{:S(2)}) collective-permute-start(bf16[2048,256]{1,0:T(8,128)(2,1)} %get-tuple-element.250), channel_id=1, source_target_pairs={{0,1},{1,2},{2,3},{3,4},{4,5},{5,6},{6,7},{7,8},{8,9},{9,10},{10,1... | collective-permute-start | bytes 3145736 | tf_op jit(solution)/shard_map/while/body/eval_jaxpr/ppermute | solution.py:9
  252.1 18.4 %collective-permute-start = (bf16[2048,256]{1,0:T(8,128)(2,1)}, bf16[2048,256]{1,0:T(8,128)(2,1)S(1)}, u32[]{:S(2)}, u32[]{:S(2)}) collective-permute-start(bf16[2048,256]{1,0:T(8,128)(2,1)} %get-tuple-element.250), channel_id=1, source_target_pairs={{0,1},{1,2},{2,3},{3,4},{4,5},{5,6},{6,7},{7,8},{8,9},{9,10},{10,1... | collective-permute-start | bytes 3145736 | tf_op jit(solution)/shard_map/while/body/eval_jaxpr/ppermute | solution.py:9
  273.8 18.4 %collective-permute-start = (bf16[2048,256]{1,0:T(8,128)(2,1)}, bf16[2048,256]{1,0:T(8,128)(2,1)S(1)}, u32[]{:S(2)}, u32[]{:S(2)}) collective-permute-start(bf16[2048,256]{1,0:T(8,128)(2,1)} %get-tuple-element.250), channel_id=1, source_target_pairs={{0,1},{1,2},{2,3},{3,4},{4,5},{5,6},{6,7},{7,8},{8,9},{9,10},{10,1... | collective-permute-start | bytes 3145736 | tf_op jit(solution)/shard_map/while/body/eval_jaxpr/ppermute | solution.py:9
  297.1 18.4 %collective-permute-start = (bf16[2048,256]{1,0:T(8,128)(2,1)}, bf16[2048,256]{1,0:T(8,128)(2,1)S(1)}, u32[]{:S(2)}, u32[]{:S(2)}) collective-permute-start(bf16[2048,256]{1,0:T(8,128)(2,1)} %get-tuple-element.250), channel_id=1, source_target_pairs={{0,1},{1,2},{2,3},{3,4},{4,5},{5,6},{6,7},{7,8},{8,9},{9,10},{10,1... | collective-permute-start | bytes 3145736 | tf_op jit(solution)/shard_map/while/body/eval_jaxpr/ppermute | solution.py:9
  320.4 18.4 %collective-permute-start = (bf16[2048,256]{1,0:T(8,128)(2,1)}, bf16[2048,256]{1,0:T(8,128)(2,1)S(1)}, u32[]{:S(2)}, u32[]{:S(2)}) collective-permute-start(bf16[2048,256]{1,0:T(8,128)(2,1)} %get-tuple-element.250), channel_id=1, source_target_pairs={{0,1},{1,2},{2,3},{3,4},{4,5},{5,6},{6,7},{7,8},{8,9},{9,10},{10,1... | collective-permute-start | bytes 3145736 | tf_op jit(solution)/shard_map/while/body/eval_jaxpr/ppermute | solution.py:9
  343.7 1.4 copy-start
Sparse Core Ops, SparseCore 0:
  345.3 234.8 reduce-scatter.1
where the time goes:
time: 592 us; the launch traced here: 587 us
  waiting for transfers between devices  446 us (75%)
  starting transfers between devices  38.2 us (6%)
  other arithmetic  34.9 us (6%)
  local copies, waits for them, and re-layouts  23.2 us (4%)
  matrix products  21.1 us (4%)
  between operations  14 us (2%)
  loops' own time  9.97 us (2%)
    reduce_scatter x1, waiting for transfers between devices, local(): stack = lax.psum_scatter(stack, 'bulk', scatter_dimension=1, tiled=True)  235 us
    ppermute x15, waiting for transfers between devices, shifted(): lax.ppermute(value, axis, [(i, (i + by) % size) for i in range(size)])  211 us
    ppermute x15, starting transfers between devices, shifted(): lax.ppermute(value, axis, [(i, (i + by) % size) for i in range(size)])  38.2 us
    add x15, other arithmetic, settle(): return stack + jnp.where(wanted[:, None, None], tile[None], 0.0)  22.8 us
    dot_general x9, matrix products, product(): lax.dot_general(mine, held, (((0,), (0,)), ((), ())), preferred_element_t...  21.1 us
    while x15, local copies, waits for them, and re-layouts  14.5 us
  transfers between devices with their start and end apart: 16, of which 16 were waited for; matrix products, arithmetic and copies ran while one was open for 2% of the time, Pallas kernels for 0%

commit v1 on v0

v1 whole, which is shorter than its diff:
```python
import functools

import jax
import jax.numpy as jnp
import numpy as np
from jax import lax
from jax.experimental import pallas as pl
from jax.experimental.pallas import tpu as pltpu
from jax.sharding import Mesh
from jax.sharding import PartitionSpec as P

Z, H, L, X, C = 8, 4, 2, 4, 2
BLK = ("l", "x", "c")
BULK = ("z", "h")
SLOTS = 9
W = 256
ROWS = 1024


def place(l, x, c):
    return ((l % L) * X + x % X) * C + c % C


def far(x):
    return (x % X) // 2


def sib_of(l, x, c):
    return (l, x, 1 - c)


def x_of(l, x, c):
    return (l, (x + 1) % X, c)


def w_of(l, x, c):
    return (l, (x - 1) % X, c ^ l ^ far(x))


def v_of(l, x, c):
    return (1 - l, (x + 1) % X, c ^ l)


def v_via(l, x, c):
    return (1 - l, x, c ^ l)


ALL = [(l, x, c) for l in range(L) for x in range(X) for c in range(C)]


def fetch(value, role):
    return lax.ppermute(value, BLK, [(place(*role(*d)), place(*d)) for d in ALL])


def hand(value, role):
    return lax.ppermute(value, BLK, [(place(*d), place(*role(*d))) for d in ALL])


def table(f):
    return np.array([f(*d) for d in ALL], np.int32)


def candidates(l, x, c):
    me = (l, x, c)
    inverse = {}
    for d in ALL:
        for name, role in (("x", x_of), ("w", w_of), ("v", v_of)):
            if role(*d) == me:
                inverse[name] = d
    out = [place(*me), place(*sib_of(*me)), place(*x_of(*me)), place(*v_of(*me))]
    s = sib_of(*me)
    out += [place(*x_of(*s)), place(*v_of(*s))]
    h = inverse["x"]
    out += [place(*h), place(*sib_of(*h)), place(*w_of(*h)), place(*v_of(*h))]
    h = inverse["v"]
    out += [place(*x_of(*h)), place(*h), place(*sib_of(*h)), place(*w_of(*h))]
    h = inverse["w"]
    out += [place(*x_of(*h)), place(*v_of(*h))]
    assert sorted(out) == list(range(16)), out
    return out


def tiles_kernel(plan, n_in, first, keep_ref, *refs):
    ins, out_ref = refs[:n_in], refs[-1]
    step = pl.program_id(0)

    def dot(a, b):
        return lax.dot_general(
            a, b, (((0,), (0,)), ((), ())), preferred_element_type=jnp.float32
        )

    for i, (lhs, rhs, flag) in enumerate(plan):

        @pl.when(step == i)
        def _(lhs=lhs, rhs=rhs, flag=flag):
            tile = dot(ins[lhs[0]][...], ins[rhs[0]][...])
            tile += dot(ins[lhs[1]][...], ins[rhs[1]][...])
            if flag is None:
                out_ref[...] = tile.reshape(out_ref.shape)
            else:

                @pl.when(keep_ref[flag] != 0)
                def _():
                    out_ref[...] = tile.reshape(out_ref.shape)

                @pl.when(keep_ref[flag] == 0)
                def _():
                    out_ref[...] = tile.T.reshape(out_ref.shape)


def tiles(plan, first, keep, ins, out=None):
    shape = (Z, H, SLOTS, W // (Z * H), W)
    n = len(ins)
    in_specs = [pl.BlockSpec(memory_space=pltpu.SMEM)]
    in_specs += [pl.BlockSpec((ROWS, W), lambda i: (0, 0)) for _ in ins]
    args = [keep, *ins]
    aliases = {}
    if out is not None:
        in_specs.append(pl.BlockSpec(memory_space=pl.ANY))
        aliases = {len(args): 0}
        args.append(out)
    return pl.pallas_call(
        functools.partial(tiles_kernel, plan, n, first),
        grid=(len(plan),),
        out_shape=jax.ShapeDtypeStruct(shape, jnp.float32),
        in_specs=in_specs,
        out_specs=pl.BlockSpec(
            (Z, H, 1, W // (Z * H), W), lambda i: (0, 0, first + i, 0, 0)
        ),
        input_output_aliases=aliases,
        compiler_params=pltpu.CompilerParams(vmem_limit_bytes=40 * 2**20),
        cost_estimate=pl.CostEstimate(
            flops=len(plan) * 4 * W * W * ROWS,
            bytes_accessed=n * ROWS * W * 2 + len(plan) * W * W * 4,
            transcendentals=0,
        ),
    )(*args)


def local(aux_factors, tile_cols):
    row = tile_cols
    a1, a2 = aux_factors[0], aux_factors[1]
    me = lax.axis_index(BLK)

    x1 = fetch(a1, x_of)
    w1 = fetch(a1, w_of)
    b1 = fetch(a1, sib_of)
    x2 = fetch(a2, x_of)
    w2 = fetch(a2, w_of)
    b2 = fetch(a2, sib_of)
    row_x = fetch(row, x_of)[0]
    row_v = fetch(row, v_of)[0]
    v1 = fetch(x1, v_via)
    v2 = fetch(x2, v_via)

    ids = [
        jnp.asarray(table(lambda *d, r=r: place(*r(*d))))[me]
        for r in (sib_of, w_of, v_of)
    ]
    id_b, id_w, id_v = ids
    keep = jnp.stack(
        [
            jnp.any(row_x == me),
            jnp.any(row_x == id_b),
            jnp.any(row_x == id_w),
            jnp.any(row_x == id_v),
            jnp.any(row_v == me),
            jnp.any(row_v == id_b),
            jnp.any(row_v == id_w),
        ]
    ).astype(jnp.int32)

    a, b, x, w, v = (0, 1), (2, 3), (4, 5), (6, 7), (8, 9)
    early = [a1, a2, b1, b2, x1, x2, w1, w2]
    parts = tiles(
        [(a, a, None), (a, b, None), (x, a, 0), (x, b, 1), (x, w, 2)], 0, keep, early
    )
    parts = tiles(
        [(x, v, 3), (v, a, 4), (v, b, 5), (v, w, 6)],
        5,
        keep,
        early + [v1, v2],
        parts,
    )

    part = lax.psum_scatter(
        parts.reshape(Z, H * SLOTS * 8, W), "z", scatter_dimension=0, tiled=True
    )
    part = part.reshape(H, SLOTS, 8, W)
    part = lax.all_to_all(part, "h", 0, 0, tiled=True)
    done = part.sum(0)

    to_sib = hand(jnp.stack([done[3], done[7]]), sib_of)
    to_x = hand(done[2:6], x_of)
    to_v = hand(done[5:9], v_of)
    to_w = hand(jnp.stack([done[4], done[8]]), w_of)
    slabs = [done[0], done[1], done[2], done[6]]
    slabs += [to_sib[0], to_sib[1]]
    slabs += [to_x[i] for i in range(4)]
    slabs += [to_v[i] for i in range(4)]
    slabs += [to_w[0], to_w[1]]
    others = jnp.asarray(table(candidates))[me]
    wanted = row[0][:, None] == others[None, :]
    out = jnp.zeros((SLOTS, 8, W), jnp.float32)
    for k, slab in enumerate(slabs):
        out = out + jnp.where(wanted[:, k][:, None, None], slab[None], 0.0)
    return out


def solution(mesh):
    fine = Mesh(mesh.devices.reshape(Z, H, L, X, C), (*BULK, *BLK))
    in_specs = (P(BULK, None, BLK), P(BLK, None))
    out_specs = P(BLK, BULK, None)
    return jax.shard_map(
        local, mesh=fine, in_specs=in_specs, out_specs=out_specs, check_vma=False
    )
```

time: 592 us -> 166 us (0.28)
  waiting for transfers between devices: 446 us -> 66 us
  other arithmetic: 34.9 us -> 5.57 us
  starting transfers between devices: 38.2 us -> 59.7 us
  matrix products: 21.1 us -> 0 us
  local copies, waits for them, and re-layouts: 23.2 us -> 10.2 us
  loops' own time: 9.97 us -> 0 us
  Pallas kernels: 0 us -> 9.79 us
    ppermute x15 -> x14, waiting for transfers between devices: 211 us -> 12.9 us  [the longest x10 11.9 us: fetch(): lax.ppermute(value, BLK, [(place(*role(*d)), place(*d)) for d in ALL])]
    reduce_scatter x1, waiting for transfers between devices: 235 us -> 45.1 us  [local(): lax.psum_scatter(parts.reshape(Z, H * SLOTS * 8, W), 'z', scatter_dimensi...]
    add x15 -> x1, other arithmetic: 22.8 us -> 0.9 us  [local(): out = out + jnp.where(wanted[:, k][:, None, None], slab[None], 0.0)]
    dot_general x9 -> x0, matrix products: 21.1 us -> none  [product(): lax.dot_general(mine, held, (((0,), (0,)), ((), ())), preferred_element_t...]
    ppermute x15 -> x14, starting transfers between devices: 38.2 us -> 53.4 us  [the longest x10 34.7 us: fetch(): lax.ppermute(value, BLK, [(place(*role(*d)), place(*d)) for d in ALL])]
    while x15 -> x0, local copies, waits for them, and re-layouts: 14.5 us -> none
    another operation x17 -> x0, loops' own time: 9.97 us -> none  [the longest x1 9.95 us: local(): stack, held = lax.fori_loop(1, blocks, forward_turn, (stack, mine))]
    pallas_call x0 -> x2, Pallas kernels: none -> 9.79 us  [tiles(): pl.pallas_call(functools.partial(tiles_kernel, plan, n, first), grid=(len...]
  transfers between devices with their start and end apart: 16 -> 16, of which waited for: 16 -> 5; matrix products, arithmetic and copies ran while one was open for 2% -> 8% of each run, Pallas kernels for 0% -> 3%
where the time goes in v1:
time: 166 us; the launch traced here: 165 us
  waiting for transfers between devices  66 us (40%)
  starting transfers between devices  59.7 us (36%)
  between operations  13.6 us (8%)
  local copies, waits for them, and re-layouts  10.2 us (6%)
  Pallas kernels  9.79 us (6%)
  other arithmetic  5.57 us (3%)
    reduce_scatter x1, waiting for transfers between devices, local(): lax.psum_scatter(parts.reshape(Z, H * SLOTS * 8, W), 'z', scatter_dimensi...  45.1 us
    ppermute x10, starting transfers between devices, fetch(): lax.ppermute(value, BLK, [(place(*role(*d)), place(*d)) for d in ALL])  34.7 us
    ppermute x4, starting transfers between devices, hand(): lax.ppermute(value, BLK, [(place(*d), place(*role(*d))) for d in ALL])  18.6 us
    ppermute x10, waiting for transfers between devices, fetch(): lax.ppermute(value, BLK, [(place(*role(*d)), place(*d)) for d in ALL])  11.9 us
    pallas_call x2, Pallas kernels, tiles(): pl.pallas_call(functools.partial(tiles_kernel, plan, n, first), grid=(len...  9.79 us
    all_to_all x1, waiting for transfers between devices, local(): part = lax.all_to_all(part, 'h', 0, 0, tiled=True)  8.01 us
    all_to_all x1, starting transfers between devices, local(): part = lax.all_to_all(part, 'h', 0, 0, tiled=True)  6.39 us
    another operation x1, local copies, waits for them, and re-layouts, local(): jnp.stack([jnp.any(row_x == me), jnp.any(row_x == id_b), jnp.any(row_x ==...  4.46 us
  transfers between devices with their start and end apart: 16, of which 5 were waited for; matrix products, arithmetic and copies ran while one was open for 8% of the time, Pallas kernels for 3%

profile of v1, /device:TPU:1, one launch (start us, length us, event | category | flops | bytes accessed | tf_op | source)
XLA Modules:
  0.0 165.0 jit_solution(6001970744905769560)
XLA Ops:
  7.8 5.2 %collective-permute-start.4 = (bf16[1024,256]{1,0:T(8,128)(2,1)S(1)}, bf16[1024,256]{1,0:T(8,128)(2,1)S(1)}, u32[]{:S(2)}, u32[]{:S(2)}) collective-permute-start(bf16[1024,256]{1,0:T(8,128)(2,1)S(1)} %get-tuple-element.13.refs_0_), channel_id=1, source_target_pairs={{2,0},{3,1},{4,2},{5,3},{6,4},{7,5},{0,6},{1,7},{10,8},{11,9},{12,... | collective-permute-start | bytes 1572872 | tf_op jit(solution)/shard_map/ppermute | solution.py:52
  13.0 2.5 %collective-permute-start.5 = (bf16[1024,256]{1,0:T(8,128)(2,1)S(1)}, bf16[1024,256]{1,0:T(8,128)(2,1)S(1)}, u32[]{:S(2)}, u32[]{:S(2)}) collective-permute-start(bf16[1024,256]{1,0:T(8,128)(2,1)S(1)} %get-tuple-element.12.refs_1_), channel_id=1, source_target_pairs={{2,0},{3,1},{4,2},{5,3},{6,4},{7,5},{0,6},{1,7},{10,8},{11,9},{12,... | collective-permute-start | bytes 1572872 | tf_op jit(solution)/shard_map/ppermute | solution.py:52
  15.5 5.0 %collective-permute-start.2 = (bf16[1024,256]{1,0:T(8,128)(2,1)S(1)}, bf16[1024,256]{1,0:T(8,128)(2,1)S(1)}, u32[]{:S(2)}, u32[]{:S(2)}) collective-permute-start(bf16[1024,256]{1,0:T(8,128)(2,1)S(1)} %get-tuple-element.13.refs_0_), channel_id=1, source_target_pairs={{1,0},{0,1},{3,2},{2,3},{5,4},{4,5},{7,6},{6,7},{9,8},{8,9},{11,10... | collective-permute-start | bytes 1572872 | tf_op jit(solution)/shard_map/ppermute | solution.py:52
  20.5 1.9 %collective-permute-start = (s32[1,9]{1,0:T(1,128)}, s32[1,9]{1,0:T(1,128)S(1)}, u32[]{:S(2)}, u32[]{:S(2)}) collective-permute-start(s32[1,9]{1,0:T(1,128)} %param.7), channel_id=1, source_target_pairs={{2,0},{3,1},{4,2},{5,3},{6,4},{7,5},{0,6},{1,7},{10,8},{11,9},{12,... | collective-permute-start | bytes 116 | tf_op jit(solution)/shard_map/ppermute | solution.py:52
  22.4 1.9 %collective-permute-start.1 = (s32[1,9]{1,0:T(1,128)}, s32[1,9]{1,0:T(1,128)S(1)}, u32[]{:S(2)}, u32[]{:S(2)}) collective-permute-start(s32[1,9]{1,0:T(1,128)} %param.7), channel_id=1, source_target_pairs={{10,0},{11,1},{12,2},{13,3},{14,4},{15,5},{8,6},{9,7},{3,8},{2,9},... | collective-permute-start | bytes 116 | tf_op jit(solution)/shard_map/ppermute | solution.py:52
  24.3 7.9 %collective-permute-done = s32[1,9]{1,0:T(1,128)S(1)} collective-permute-done((s32[1,9]{1,0:T(1,128)}, s32[1,9]{1,0:T(1,128)S(1)}, u32[]{:S(2)}, u32[]{:S(2)}) %collective-permute-start) | collective-permute-done | bytes 68 | tf_op jit(solution)/shard_map/ppermute | solution.py:52
  32.2 6.1 %collective-permute-start.3 = (bf16[1024,256]{1,0:T(8,128)(2,1)S(1)}, bf16[1024,256]{1,0:T(8,128)(2,1)S(1)}, u32[]{:S(2)}, u32[]{:S(2)}) collective-permute-start(bf16[1024,256]{1,0:T(8,128)(2,1)S(1)} %get-tuple-element.12.refs_1_), channel_id=1, source_target_pairs={{1,0},{0,1},{3,2},{2,3},{5,4},{4,5},{7,6},{6,7},{9,8},{8,9},{11,10... | collective-permute-start | bytes 1572872 | tf_op jit(solution)/shard_map/ppermute | solution.py:52
  38.4 2.9 %collective-permute-start.6 = (bf16[1024,256]{1,0:T(8,128)(2,1)S(1)}, bf16[1024,256]{1,0:T(8,128)(2,1)}, u32[]{:S(2)}, u32[]{:S(2)}) collective-permute-start(bf16[1024,256]{1,0:T(8,128)(2,1)S(1)} %get-tuple-element.13.refs_0_), channel_id=1, source_target_pairs={{6,0},{7,1},{0,2},{1,3},{3,4},{2,5},{5,6},{4,7},{15,8},{14,9},{9,1... | collective-permute-start | bytes 1572872 | tf_op jit(solution)/shard_map/ppermute | solution.py:52
  41.2 3.0 %collective-permute-start.7 = (bf16[1024,256]{1,0:T(8,128)(2,1)S(1)}, bf16[1024,256]{1,0:T(8,128)(2,1)}, u32[]{:S(2)}, u32[]{:S(2)}) collective-permute-start(bf16[1024,256]{1,0:T(8,128)(2,1)S(1)} %get-tuple-element.12.refs_1_), channel_id=1, source_target_pairs={{6,0},{7,1},{0,2},{1,3},{3,4},{2,5},{5,6},{4,7},{15,8},{14,9},{9,1... | collective-permute-start | bytes 1572872 | tf_op jit(solution)/shard_map/ppermute | solution.py:52
  44.3 3.6 %collective-permute-start.8 = (bf16[1024,256]{1,0:T(8,128)(2,1)S(1)}, bf16[1024,256]{1,0:T(8,128)(2,1)}, u32[]{:S(2)}, u32[]{:S(2)}) collective-permute-start(bf16[1024,256]{1,0:T(8,128)(2,1)S(1)} %collective-permute-done.4.refs_4_), channel_id=1, source_target_pairs={{8,0},{9,1},{10,2},{11,3},{12,4},{13,5},{14,6},{15,7},{1,8},{0,9},... | collective-permute-start | bytes 1572872 | tf_op jit(solution)/shard_map/ppermute | solution.py:52
  47.9 2.6 %collective-permute-start.9 = (bf16[1024,256]{1,0:T(8,128)(2,1)S(1)}, bf16[1024,256]{1,0:T(8,128)(2,1)}, u32[]{:S(2)}, u32[]{:S(2)}) collective-permute-start(bf16[1024,256]{1,0:T(8,128)(2,1)S(1)} %collective-permute-done.5.refs_5_), channel_id=1, source_target_pairs={{8,0},{9,1},{10,2},{11,3},{12,4},{13,5},{14,6},{15,7},{1,8},{0,9},... | collective-permute-start | bytes 1572872 | tf_op jit(solution)/shard_map/ppermute | solution.py:52
  54.3 2.0 %compare_reduce_fusion = (pred[]{:T(512)}, pred[]{:T(512)}, pred[]{:T(512)}) fusion(s32[1,9]{1,0:T(1,128)S(1)} %collective-permute-done.1, s32[]{:T(128)} %bitcast.6, s32[]{:T(128)} %bitcast.4, s32[]{:T(128)S(6)} %add.60), kind=kLoop, calls=%fused_computation.38 | loop fusion | flops 51 | bytes 51 | tf_op jit(solution)/shard_map/reduce_or | solution.py:169
  56.3 2.6 %compare_reduce_fusion.3 = (pred[]{:T(512)}, pred[]{:T(512)}, pred[]{:T(512)}, pred[]{:T(512)}) fusion(s32[1,9]{1,0:T(1,128)S(1)} %collective-permute-done, s32[]{:T(128)} %bitcast.8, s32[]{:T(128)} %bitcast.6, s32[]{:T(128)} %bitcast.4, s32[]{:T(128)S(6)} %add.60), kind=kLoop, calls=%fused_computation.41 | loop fusion | flops 68 | bytes 56 | tf_op jit(solution)/shard_map/reduce_or | solution.py:166
  58.9 4.5 %stack.37 = pred[7]{0:T(512)(128)(4,1)S(1)} concatenate(pred[1]{0:T(512)(128)(4,1)} %bitcast.3, pred[1]{0:T(512)(128)(4,1)} %bitcast.5, pred[1]{0:T(512)(128)(4,1)} %bitcast.7, pred[1]{0:T(512)(128)(4,1)} %bitcast.9, pred[1]{0:T(512)(128)(4,1)} %bitcast.10, pred[1]{0:T(512)(128)(4,1)} %bitcast.11, pred[1]{0:T(512)(128)(4,1)} %bitcast.12), dimensions={0} | concatenate | bytes 14 | tf_op jit(solution)/shard_map/stack | solution.py:161
  63.3 4.0 %collective-permute-done.7.refs_7_ = bf16[1024,256]{1,0:T(8,128)(2,1)} collective-permute-done((bf16[1024,256]{1,0:T(8,128)(2,1)S(1)}, bf16[1024,256]{1,0:T(8,128)(2,1)}, u32[]{:S(2)}, u32[]{:S(2)}) %collective-permute-start.7) | collective-permute-done | bytes 524320 | tf_op jit(solution)/shard_map/ppermute | solution.py:52
  67.3 5.0 %shard_map.64.refs_10_ = f32[8,4,9,8,256]{4,3,2,1,0:T(8,128)} custom-call(s32[7]{0:T(128)S(1)} %convert_element_type.3.keep_ref, bf16[1024,256]{1,0:T(8,128)(2,1)S(1)} %get-tuple-element.13.refs_0_, bf16[1024,256]{1,0:T(8,128)(2,1)S(1)} %get-tuple-element.12.refs_1_, bf16[1024,256]{1,0:T(8,128)(2,1)S(1)} %collective-permute-done.2.refs_2_, ...), custom_call_target="tpu_custom_call" | custom-call | flops 1342177280 | bytes 5505024 | tf_op jit(solution)/shard_map/pallas_call | solution.py:122
  72.3 4.8 %shard_map.65 = f32[8,4,9,8,256]{4,3,2,1,0:T(8,128)} custom-call(s32[7]{0:T(128)S(1)} %convert_element_type.3.keep_ref, bf16[1024,256]{1,0:T(8,128)(2,1)S(1)} %get-tuple-element.13.refs_0_, bf16[1024,256]{1,0:T(8,128)(2,1)S(1)} %get-tuple-element.12.refs_1_, bf16[1024,256]{1,0:T(8,128)(2,1)S(1)} %collective-permute-done.2.refs_2_, ...), custom_call_target="tpu_custom_call", output_to_operand_aliasing={{}: (11, {})} | custom-call | flops 1073741824 | bytes 6291456 | tf_op jit(solution)/shard_map/pallas_call | solution.py:122
  77.8 45.1 %reduce-scatter.2.cloned.1.call-done = f32[1,288,256]{2,1,0:T(8,128)} async-done(((f32[8,288,256]{2,1,0:T(8,128)}), f32[1,288,256]{2,1,0:T(8,128)}) %reduce-scatter.2.cloned.1.call-update) | async-done | bytes 294928 | tf_op jit(solution)/shard_map/reduce_scatter | solution.py:186
  123.0 6.4 %all-to-all-start = ((f32[4,9,8,256]{3,2,1,0:T(8,128)}), f32[4,9,8,256]{3,2,1,0:T(8,128)S(1)}, u32[]{:S(2)}, u32[]{:S(2)}) async-start(f32[4,9,8,256]{3,2,1,0:T(8,128)} %bitcast.83), calls=%async_computation.1 | async-start | bytes 589824 | tf_op jit(solution)/shard_map/all_to_all | solution.py:190
  129.4 8.0 %all-to-all-done = f32[4,9,8,256]{3,2,1,0:T(8,128)S(1)} async-done(((f32[4,9,8,256]{3,2,1,0:T(8,128)}), f32[4,9,8,256]{3,2,1,0:T(8,128)S(1)}, u32[]{:S(2)}, u32[]{:S(2)}) %all-to-all-start) | async-done | bytes 294944 | tf_op jit(solution)/shard_map/all_to_all | solution.py:190
  137.5 8.3 %collective-permute-start.10 = (f32[2,8,256]{2,1,0:T(8,128)S(1)}, f32[2,8,256]{2,1,0:T(8,128)S(1)}, u32[]{:S(2)}, u32[]{:S(2)}) collective-permute-start(f32[2,8,256]{2,1,0:T(8,128)S(1)} %pad_maximum_fusion), channel_id=1, source_target_pairs={{0,1},{1,0},{2,3},{3,2},{4,5},{5,4},{6,7},{7,6},{8,9},{9,8},{10,11... | collective-permute-start | bytes 49160 | tf_op jit(solution)/shard_map/ppermute | solution.py:56
  145.8 3.1 %collective-permute-start.11 = (f32[4,8,256]{2,1,0:T(8,128)S(1)}, f32[4,8,256]{2,1,0:T(8,128)S(1)}, u32[]{:S(2)}, u32[]{:S(2)}) collective-permute-start(f32[4,8,256]{2,1,0:T(8,128)S(1)} %get-tuple-element.22), channel_id=1, source_target_pairs={{0,2},{1,3},{2,4},{3,5},{4,6},{5,7},{6,0},{7,1},{8,10},{9,11},{10,... | collective-permute-start | bytes 98312 | tf_op jit(solution)/shard_map/ppermute | solution.py:56
  148.9 3.8 %collective-permute-start.12 = (f32[4,8,256]{2,1,0:T(8,128)S(1)}, f32[4,8,256]{2,1,0:T(8,128)S(1)}, u32[]{:S(2)}, u32[]{:S(2)}) collective-permute-start(f32[4,8,256]{2,1,0:T(8,128)S(1)} %get-tuple-element.23), channel_id=1, source_target_pairs={{0,10},{1,11},{2,12},{3,13},{4,14},{5,15},{6,8},{7,9},{8,3},{9,2},... | collective-permute-start | bytes 98312 | tf_op jit(solution)/shard_map/ppermute | solution.py:56
  152.7 3.5 %collective-permute-start.13 = (f32[2,8,256]{2,1,0:T(8,128)S(1)}, f32[2,8,256]{2,1,0:T(8,128)S(1)}, u32[]{:S(2)}, u32[]{:S(2)}) collective-permute-start(f32[2,8,256]{2,1,0:T(8,128)S(1)} %pad_maximum_fusion.1), channel_id=1, source_target_pairs={{0,6},{1,7},{2,0},{3,1},{4,3},{5,2},{6,5},{7,4},{8,15},{9,14},{10,... | collective-permute-start | bytes 49160 | tf_op jit(solution)/shard_map/ppermute | solution.py:56
  (34 shorter events, 7.8 us)
Async XLA Ops:
  6.5 116.4 %reduce-scatter.2.cloned.1.call-start = ((), (), s32[]{:S(2)}) async-start(), calls=%async_computation.2 | async-start | bytes 2654208 | tf_op jit(solution)/shard_map/reduce_scatter | solution.py:186
  7.8 33.4 %collective-permute-start.4 = (bf16[1024,256]{1,0:T(8,128)(2,1)S(1)}, bf16[1024,256]{1,0:T(8,128)(2,1)S(1)}, u32[]{:S(2)}, u32[]{:S(2)}) collective-permute-start(bf16[1024,256]{1,0:T(8,128)(2,1)S(1)} %get-tuple-element.13.refs_0_), channel_id=1, source_target_pairs={{2,0},{3,1},{4,2},{5,3},{6,4},{7,5},{0,6},{1,7},{10,8},{11,9},{12,... | collective-permute-start | bytes 1572872 | tf_op jit(solution)/shard_map/ppermute | solution.py:52
  13.0 31.2 %collective-permute-start.5 = (bf16[1024,256]{1,0:T(8,128)(2,1)S(1)}, bf16[1024,256]{1,0:T(8,128)(2,1)S(1)}, u32[]{:S(2)}, u32[]{:S(2)}) collective-permute-start(bf16[1024,256]{1,0:T(8,128)(2,1)S(1)} %get-tuple-element.12.refs_1_), channel_id=1, source_target_pairs={{2,0},{3,1},{4,2},{5,3},{6,4},{7,5},{0,6},{1,7},{10,8},{11,9},{12,... | collective-permute-start | bytes 1572872 | tf_op jit(solution)/shard_map/ppermute | solution.py:52
  15.5 32.4 %collective-permute-start.2 = (bf16[1024,256]{1,0:T(8,128)(2,1)S(1)}, bf16[1024,256]{1,0:T(8,128)(2,1)S(1)}, u32[]{:S(2)}, u32[]{:S(2)}) collective-permute-start(bf16[1024,256]{1,0:T(8,128)(2,1)S(1)} %get-tuple-element.13.refs_0_), channel_id=1, source_target_pairs={{1,0},{0,1},{3,2},{2,3},{5,4},{4,5},{7,6},{6,7},{9,8},{8,9},{11,10... | collective-permute-start | bytes 1572872 | tf_op jit(solution)/shard_map/ppermute | solution.py:52
  20.5 11.8 %collective-permute-start = (s32[1,9]{1,0:T(1,128)}, s32[1,9]{1,0:T(1,128)S(1)}, u32[]{:S(2)}, u32[]{:S(2)}) collective-permute-start(s32[1,9]{1,0:T(1,128)} %param.7), channel_id=1, source_target_pairs={{2,0},{3,1},{4,2},{5,3},{6,4},{7,5},{0,6},{1,7},{10,8},{11,9},{12,... | collective-permute-start | bytes 116 | tf_op jit(solution)/shard_map/ppermute | solution.py:52
  22.4 16.0 %collective-permute-start.1 = (s32[1,9]{1,0:T(1,128)}, s32[1,9]{1,0:T(1,128)S(1)}, u32[]{:S(2)}, u32[]{:S(2)}) collective-permute-start(s32[1,9]{1,0:T(1,128)} %param.7), channel_id=1, source_target_pairs={{10,0},{11,1},{12,2},{13,3},{14,4},{15,5},{8,6},{9,7},{3,8},{2,9},... | collective-permute-start | bytes 116 | tf_op jit(solution)/shard_map/ppermute | solution.py:52
  32.2 31.1 %collective-permute-start.3 = (bf16[1024,256]{1,0:T(8,128)(2,1)S(1)}, bf16[1024,256]{1,0:T(8,128)(2,1)S(1)}, u32[]{:S(2)}, u32[]{:S(2)}) collective-permute-start(bf16[1024,256]{1,0:T(8,128)(2,1)S(1)} %get-tuple-element.12.refs_1_), channel_id=1, source_target_pairs={{1,0},{0,1},{3,2},{2,3},{5,4},{4,5},{7,6},{6,7},{9,8},{8,9},{11,10... | collective-permute-start | bytes 1572872 | tf_op jit(solution)/shard_map/ppermute | solution.py:52
  38.4 25.0 %collective-permute-start.6 = (bf16[1024,256]{1,0:T(8,128)(2,1)S(1)}, bf16[1024,256]{1,0:T(8,128)(2,1)}, u32[]{:S(2)}, u32[]{:S(2)}) collective-permute-start(bf16[1024,256]{1,0:T(8,128)(2,1)S(1)} %get-tuple-element.13.refs_0_), channel_id=1, source_target_pairs={{6,0},{7,1},{0,2},{1,3},{3,4},{2,5},{5,6},{4,7},{15,8},{14,9},{9,1... | collective-permute-start | bytes 1572872 | tf_op jit(solution)/shard_map/ppermute | solution.py:52
  41.2 26.1 %collective-permute-start.7 = (bf16[1024,256]{1,0:T(8,128)(2,1)S(1)}, bf16[1024,256]{1,0:T(8,128)(2,1)}, u32[]{:S(2)}, u32[]{:S(2)}) collective-permute-start(bf16[1024,256]{1,0:T(8,128)(2,1)S(1)} %get-tuple-element.12.refs_1_), channel_id=1, source_target_pairs={{6,0},{7,1},{0,2},{1,3},{3,4},{2,5},{5,6},{4,7},{15,8},{14,9},{9,1... | collective-permute-start | bytes 1572872 | tf_op jit(solution)/shard_map/ppermute | solution.py:52
  44.3 28.1 %collective-permute-start.8 = (bf16[1024,256]{1,0:T(8,128)(2,1)S(1)}, bf16[1024,256]{1,0:T(8,128)(2,1)}, u32[]{:S(2)}, u32[]{:S(2)}) collective-permute-start(bf16[1024,256]{1,0:T(8,128)(2,1)S(1)} %collective-permute-done.4.refs_4_), channel_id=1, source_target_pairs={{8,0},{9,1},{10,2},{11,3},{12,4},{13,5},{14,6},{15,7},{1,8},{0,9},... | collective-permute-start | bytes 1572872 | tf_op jit(solution)/shard_map/ppermute | solution.py:52
  47.9 24.5 %collective-permute-start.9 = (bf16[1024,256]{1,0:T(8,128)(2,1)S(1)}, bf16[1024,256]{1,0:T(8,128)(2,1)}, u32[]{:S(2)}, u32[]{:S(2)}) collective-permute-start(bf16[1024,256]{1,0:T(8,128)(2,1)S(1)} %collective-permute-done.5.refs_5_), channel_id=1, source_target_pairs={{8,0},{9,1},{10,2},{11,3},{12,4},{13,5},{14,6},{15,7},{1,8},{0,9},... | collective-permute-start | bytes 1572872 | tf_op jit(solution)/shard_map/ppermute | solution.py:52
  77.1 52.2 %copy-start = (s32[1,9]{1,0:T(1,128)S(1)}, s32[1,9]{1,0:T(1,128)}, u32[]{:S(2)}) copy-start(s32[1,9]{1,0:T(1,128)} %param.7) | copy-start | bytes 112
  123.0 14.5 %all-to-all-start = ((f32[4,9,8,256]{3,2,1,0:T(8,128)}), f32[4,9,8,256]{3,2,1,0:T(8,128)S(1)}, u32[]{:S(2)}, u32[]{:S(2)}) async-start(f32[4,9,8,256]{3,2,1,0:T(8,128)} %bitcast.83), calls=%async_computation.1 | async-start | bytes 589824 | tf_op jit(solution)/shard_map/all_to_all | solution.py:190
  137.5 18.7 %collective-permute-start.10 = (f32[2,8,256]{2,1,0:T(8,128)S(1)}, f32[2,8,256]{2,1,0:T(8,128)S(1)}, u32[]{:S(2)}, u32[]{:S(2)}) collective-permute-start(f32[2,8,256]{2,1,0:T(8,128)S(1)} %pad_maximum_fusion), channel_id=1, source_target_pairs={{0,1},{1,0},{2,3},{3,2},{4,5},{5,4},{6,7},{7,6},{8,9},{9,8},{10,11... | collective-permute-start | bytes 49160 | tf_op jit(solution)/shard_map/ppermute | solution.py:56
  145.8 11.4 %collective-permute-start.11 = (f32[4,8,256]{2,1,0:T(8,128)S(1)}, f32[4,8,256]{2,1,0:T(8,128)S(1)}, u32[]{:S(2)}, u32[]{:S(2)}) collective-permute-start(f32[4,8,256]{2,1,0:T(8,128)S(1)} %get-tuple-element.22), channel_id=1, source_target_pairs={{0,2},{1,3},{2,4},{3,5},{4,6},{5,7},{6,0},{7,1},{8,10},{9,11},{10,... | collective-permute-start | bytes 98312 | tf_op jit(solution)/shard_map/ppermute | solution.py:56
  148.9 8.3 %collective-permute-start.12 = (f32[4,8,256]{2,1,0:T(8,128)S(1)}, f32[4,8,256]{2,1,0:T(8,128)S(1)}, u32[]{:S(2)}, u32[]{:S(2)}) collective-permute-start(f32[4,8,256]{2,1,0:T(8,128)S(1)} %get-tuple-element.23), channel_id=1, source_target_pairs={{0,10},{1,11},{2,12},{3,13},{4,14},{5,15},{6,8},{7,9},{8,3},{9,2},... | collective-permute-start | bytes 98312 | tf_op jit(solution)/shard_map/ppermute | solution.py:56
  152.7 4.5 %collective-permute-start.13 = (f32[2,8,256]{2,1,0:T(8,128)S(1)}, f32[2,8,256]{2,1,0:T(8,128)S(1)}, u32[]{:S(2)}, u32[]{:S(2)}) collective-permute-start(f32[2,8,256]{2,1,0:T(8,128)S(1)} %pad_maximum_fusion.1), channel_id=1, source_target_pairs={{0,6},{1,7},{2,0},{3,1},{4,3},{5,2},{6,5},{7,4},{8,15},{9,14},{10,... | collective-permute-start | bytes 49160 | tf_op jit(solution)/shard_map/ppermute | solution.py:56
Sparse Core Ops, SparseCore 0:
  77.3 45.6 reduce-scatter.1

commit v2 on v0

v2 whole, which is shorter than its diff:
```python
import functools

import jax
import jax.numpy as jnp
import numpy as np
from jax import lax
from jax.experimental import pallas as pl
from jax.experimental.pallas import tpu as pltpu
from jax.sharding import Mesh
from jax.sharding import PartitionSpec as P

Z, H, L, X, C = 8, 4, 2, 4, 2
BLK = ("l", "x", "c")
BULK = ("z", "h")
SLOTS = 9
W = 256
ROWS = 1024
EARLY, LATE = 5, 4
SLAB = W // (Z * H)


def place(l, x, c):
    return (l * X + x) * C + c


def far(x):
    return x // 2


def sib_of(l, x, c):
    return (l, x, 1 - c)


def x_of(l, x, c):
    return (l, (x + 1) % X, c)


def w_of(l, x, c):
    return (l, (x + X - 1) % X, c ^ l ^ far(x))


def v_of(l, x, c):
    return (1 - l, (x + 1) % X, c ^ l)


def v_via(l, x, c):
    return (1 - l, x, c ^ l)


ALL = [(l, x, c) for l in range(L) for x in range(X) for c in range(C)]


def fetch(value, role):
    return lax.ppermute(value, BLK, [(place(*role(*d)), place(*d)) for d in ALL])


def hand(value, role):
    return lax.ppermute(value, BLK, [(place(*d), place(*role(*d))) for d in ALL])


def candidates(l, x, c):
    me = (l, x, c)
    inverse = {}
    for d in ALL:
        for name, role in (("x", x_of), ("w", w_of), ("v", v_of)):
            if role(*d) == me:
                inverse[name] = d
    out = [place(*me), place(*sib_of(*me)), place(*x_of(*me)), place(*v_of(*me))]
    s = sib_of(*me)
    out += [place(*x_of(*s)), place(*v_of(*s))]
    h = inverse["x"]
    out += [place(*h), place(*sib_of(*h)), place(*w_of(*h)), place(*v_of(*h))]
    h = inverse["v"]
    out += [place(*x_of(*h)), place(*h), place(*sib_of(*h)), place(*w_of(*h))]
    h = inverse["w"]
    out += [place(*x_of(*h)), place(*v_of(*h))]
    assert sorted(out) == list(range(16)), out
    return out


def position():
    return tuple(lax.axis_index(name) for name in BLK)


def dot(a, b):
    return lax.dot_general(
        a, b, (((0,), (0,)), ((), ())), preferred_element_type=jnp.float32
    )


def product(lhs, rhs):
    return dot(lhs[0], rhs[0]) + dot(lhs[1], rhs[1])


def owns(carrier, block):
    row = carrier[ROWS:].astype(jnp.float32)
    return jnp.max(jnp.where(row == block.astype(jnp.float32), 1.0, 0.0)) > 0.5


def early_kernel(a, b, x1, x2, w, out):
    me = position()
    x = (x1[:ROWS], x2[...])

    def put(slot, tile):
        out[:, :, slot] = tile.reshape(Z, H, SLAB, W)

    def settle(slot, rhs, block):
        tile = product(x, rhs)
        kept = owns(x1, place(*block))

        @pl.when(kept)
        def _():
            put(slot, tile)

        @pl.when(jnp.logical_not(kept))
        def _():
            put(slot, tile.T)

    put(0, product(a, a))
    put(1, product(a, b))
    settle(2, a, me)
    settle(3, b, sib_of(*me))
    settle(4, w, w_of(*me))


def late_kernel(a, b, x1, x2, w, v1, v2, out):
    me = position()
    x, v = (x1[:ROWS], x2[...]), (v1[:ROWS], v2[...])

    def put(slot, tile):
        tile = tile.reshape(Z, H, SLAB, W)
        for h in range(H):
            out[h, :, slot] = tile[:, h]

    def settle(slot, rhs, block):
        tile = product(v, rhs)
        kept = owns(v1, place(*block))

        @pl.when(kept)
        def _():
            put(slot, tile)

        @pl.when(jnp.logical_not(kept))
        def _():
            put(slot, tile.T)

    settle(0, x, x_of(*me))
    settle(1, a, me)
    settle(2, b, sib_of(*me))
    settle(3, w, w_of(*me))


def call(kernel, shape, n_tiles, *ins):
    vmem = pl.BlockSpec(memory_space=pltpu.VMEM)
    return pl.pallas_call(
        kernel,
        out_shape=jax.ShapeDtypeStruct(shape, jnp.float32),
        in_specs=[vmem] * len(ins),
        out_specs=vmem,
        compiler_params=pltpu.CompilerParams(vmem_limit_bytes=40 * 2**20),
        cost_estimate=pl.CostEstimate(
            flops=n_tiles * 4 * W * W * ROWS,
            bytes_accessed=sum(v.size * 2 for v in ins) + n_tiles * W * W * 4,
            transcendentals=0,
        ),
    )(*ins)


def local(aux_factors, tile_cols):
    a = aux_factors
    row = jnp.pad(tile_cols.astype(jnp.bfloat16), ((0, 15), (0, W - SLOTS)), constant_values=-2)

    x1 = fetch(jnp.concatenate([a[0], row]), x_of)
    w = fetch(a, w_of)
    x2 = fetch(a[1], x_of)
    b = fetch(a, sib_of)
    v1 = fetch(x1, v_via)
    v2 = fetch(x2, v_via)

    early = call(early_kernel, (Z, H, EARLY, SLAB, W), EARLY, a, b, x1, x2, w)
    late = call(late_kernel, (H, Z, LATE, SLAB, W), LATE, a, b, x1, x2, w, v1, v2)

    early = lax.psum_scatter(
        early.reshape(Z, H * EARLY * SLAB, W), "z", scatter_dimension=0, tiled=True
    )
    late = late.reshape(H, Z * LATE * SLAB, W)
    late = lax.all_to_all(late, "h", 0, 0, tiled=True).sum(0)
    late = late.reshape(Z, LATE * SLAB, W)
    late = lax.all_to_all(late, "z", 0, 0, tiled=True).sum(0)
    early = early.reshape(H, EARLY * SLAB, W)
    early = lax.all_to_all(early, "h", 0, 0, tiled=True).sum(0)
    e = early.reshape(EARLY, SLAB, W)
    v = late.reshape(LATE, SLAB, W)

    to_sib = hand(jnp.stack([e[3], v[2]]), sib_of)
    to_x = hand(jnp.concatenate([e[2:5], v[0:1]]), x_of)
    to_v = hand(v, v_of)
    to_w = hand(jnp.stack([e[4], v[3]]), w_of)
    slabs = [e[0], e[1], e[2], v[1]]
    slabs += [to_sib[i] for i in range(2)]
    slabs += [to_x[i] for i in range(4)]
    slabs += [to_v[i] for i in range(4)]
    slabs += [to_w[i] for i in range(2)]
    me = lax.axis_index(BLK)
    others = jnp.asarray(np.array([candidates(*d) for d in ALL], np.int32))[me]
    wanted = tile_cols[0][:, None] == others[None, :]
    out = jnp.zeros((SLOTS, SLAB, W), jnp.float32)
    for k, slab in enumerate(slabs):
        out = out + jnp.where(wanted[:, k][:, None, None], slab[None], 0.0)
    return out


def solution(mesh):
    fine = Mesh(mesh.devices.reshape(Z, H, L, X, C), (*BULK, *BLK))
    in_specs = (P(BULK, None, BLK), P(BLK, None))
    out_specs = P(BLK, BULK, None)
    return jax.shard_map(
        local, mesh=fine, in_specs=in_specs, out_specs=out_specs, check_vma=False
    )
```

time: 592 us -> 156 us (0.26)
  waiting for transfers between devices: 446 us -> 61.4 us
  other arithmetic: 34.9 us -> 2.49 us
  starting transfers between devices: 38.2 us -> 65.2 us
  matrix products: 21.1 us -> 0 us
  local copies, waits for them, and re-layouts: 23.2 us -> 2.1 us
  Pallas kernels: 0 us -> 10.4 us
  loops' own time: 9.97 us -> 0 us
    reduce_scatter x1, waiting for transfers between devices: 235 us -> 0.02 us  [local(): lax.psum_scatter(early.reshape(Z, H * EARLY * SLAB, W), 'z', scatter_dime...]
    ppermute x15 -> x10, waiting for transfers between devices: 211 us -> 29.7 us  [the longest x6 26.6 us: fetch(): lax.ppermute(value, BLK, [(place(*role(*d)), place(*d)) for d in ALL])]
    all_to_all x0 -> x3, waiting for transfers between devices: none -> 31.6 us  [the longest x1 18 us: local(): late = lax.all_to_all(late, 'h', 0, 0, tiled=True).sum(0)]
    add x15 -> x1, other arithmetic: 22.8 us -> 0.9 us  [local(): out = out + jnp.where(wanted[:, k][:, None, None], slab[None], 0.0)]
    dot_general x9 -> x0, matrix products: 21.1 us -> none  [product(): lax.dot_general(mine, held, (((0,), (0,)), ((), ())), preferred_element_t...]
    all_to_all x0 -> x3, starting transfers between devices: none -> 18.1 us  [the longest x1 11.2 us: local(): late = lax.all_to_all(late, 'z', 0, 0, tiled=True).sum(0)]
    while x15 -> x0, local copies, waits for them, and re-layouts: 14.5 us -> none
    reduce_or x16 -> x0, other arithmetic: 11.8 us -> none  [settle(): tile = lax.cond(jnp.any(wanted), product, nothing, held)]
  transfers between devices with their start and end apart: 16 -> 14, of which waited for: 16 -> 8; matrix products, arithmetic and copies ran while one was open for 2% -> 2% of each run, Pallas kernels for 0% -> 7%
where the time goes in v2:
time: 156 us; the launch traced here: 155 us
  starting transfers between devices  65.2 us (42%)
  waiting for transfers between devices  61.4 us (39%)
  between operations  13.6 us (9%)
  Pallas kernels  10.4 us (7%)
  other arithmetic  2.49 us (2%)
  local copies, waits for them, and re-layouts  2.1 us (1%)
    ppermute x6, waiting for transfers between devices, fetch(): lax.ppermute(value, BLK, [(place(*role(*d)), place(*d)) for d in ALL])  26.6 us
    ppermute x4, starting transfers between devices, hand(): lax.ppermute(value, BLK, [(place(*d), place(*role(*d))) for d in ALL])  26.1 us
    ppermute x6, starting transfers between devices, fetch(): lax.ppermute(value, BLK, [(place(*role(*d)), place(*d)) for d in ALL])  21 us
    all_to_all x1, waiting for transfers between devices, local(): late = lax.all_to_all(late, 'h', 0, 0, tiled=True).sum(0)  18 us
    all_to_all x1, starting transfers between devices, local(): late = lax.all_to_all(late, 'z', 0, 0, tiled=True).sum(0)  11.2 us
    pallas_call x2, Pallas kernels, call(): pl.pallas_call(kernel, out_shape=jax.ShapeDtypeStruct(shape, jnp.float32)...  10.4 us
    all_to_all x1, waiting for transfers between devices, local(): late = lax.all_to_all(late, 'z', 0, 0, tiled=True).sum(0)  8.46 us
    all_to_all x1, waiting for transfers between devices, local(): early = lax.all_to_all(early, 'h', 0, 0, tiled=True).sum(0)  5.17 us
  transfers between devices with their start and end apart: 14, of which 8 were waited for; matrix products, arithmetic and copies ran while one was open for 2% of the time, Pallas kernels for 7%

profile of v2, /device:TPU:1, one launch (start us, length us, event | category | flops | bytes accessed | tf_op | source)
XLA Modules:
  0.0 155.2 jit_solution(11488642613925592075)
XLA Ops:
  6.5 8.8 %collective-permute-start = (bf16[2,1024,256]{2,1,0:T(8,128)(2,1)}, bf16[2,1024,256]{2,1,0:T(8,128)(2,1)S(1)}, u32[]{:S(2)}, u32[]{:S(2)}) collective-permute-start(bf16[2,1024,256]{2,1,0:T(8,128)(2,1)} %a.3), channel_id=1, source_target_pairs={{1,0},{0,1},{3,2},{2,3},{5,4},{4,5},{7,6},{6,7},{9,8},{8,9},{11,10... | collective-permute-start | bytes 3145736 | tf_op jit(solution)/shard_map/ppermute | solution.py:54
  15.3 1.9 %collective-permute-start.3 = (bf16[2,1024,256]{2,1,0:T(8,128)(2,1)}, bf16[2,1024,256]{2,1,0:T(8,128)(2,1)S(1)}, u32[]{:S(2)}, u32[]{:S(2)}) collective-permute-start(bf16[2,1024,256]{2,1,0:T(8,128)(2,1)} %a.3), channel_id=1, source_target_pairs={{6,0},{7,1},{0,2},{1,3},{3,4},{2,5},{5,6},{4,7},{15,8},{14,9},{9,1... | collective-permute-start | bytes 3145736 | tf_op jit(solution)/shard_map/ppermute | solution.py:54
  17.9 1.4 slice_bitcast_fusion
  19.3 4.6 %collective-permute-start.1 = (bf16[1040,256]{1,0:T(8,128)(2,1)S(1)}, bf16[1040,256]{1,0:T(8,128)(2,1)}, u32[]{:S(2)}, u32[]{:S(2)}) collective-permute-start(bf16[1040,256]{1,0:T(8,128)(2,1)S(1)} %fusion.1), channel_id=1, source_target_pairs={{2,0},{3,1},{4,2},{5,3},{6,4},{7,5},{0,6},{1,7},{10,8},{11,9},{12,... | collective-permute-start | bytes 1597448 | tf_op jit(solution)/shard_map/ppermute | solution.py:54
  23.9 1.9 %collective-permute-start.2 = (bf16[1024,256]{1,0:T(8,128)(2,1)S(1)}, bf16[1024,256]{1,0:T(8,128)(2,1)}, u32[]{:S(2)}, u32[]{:S(2)}) collective-permute-start(bf16[1024,256]{1,0:T(8,128)(2,1)S(1)} %get-tuple-element.5), channel_id=1, source_target_pairs={{2,0},{3,1},{4,2},{5,3},{6,4},{7,5},{0,6},{1,7},{10,8},{11,9},{12,... | collective-permute-start | bytes 1572872 | tf_op jit(solution)/shard_map/ppermute | solution.py:54
  25.8 9.2 %collective-permute-done.1.x1 = bf16[1040,256]{1,0:T(8,128)(2,1)} collective-permute-done((bf16[1040,256]{1,0:T(8,128)(2,1)S(1)}, bf16[1040,256]{1,0:T(8,128)(2,1)}, u32[]{:S(2)}, u32[]{:S(2)}) %collective-permute-start.1) | collective-permute-done | bytes 532512 | tf_op jit(solution)/shard_map/ppermute | solution.py:54
  35.1 1.9 %collective-permute-start.4 = (bf16[1040,256]{1,0:T(8,128)(2,1)}, bf16[1040,256]{1,0:T(8,128)(2,1)}, u32[]{:S(2)}, u32[]{:S(2)}) collective-permute-start(bf16[1040,256]{1,0:T(8,128)(2,1)} %collective-permute-done.1.x1), channel_id=1, source_target_pairs={{8,0},{9,1},{10,2},{11,3},{12,4},{13,5},{14,6},{15,7},{1,8},{0,9},... | collective-permute-start | bytes 1597448 | tf_op jit(solution)/shard_map/ppermute | solution.py:54
  37.0 9.3 %collective-permute-done.2.x2 = bf16[1024,256]{1,0:T(8,128)(2,1)} collective-permute-done((bf16[1024,256]{1,0:T(8,128)(2,1)S(1)}, bf16[1024,256]{1,0:T(8,128)(2,1)}, u32[]{:S(2)}, u32[]{:S(2)}) %collective-permute-start.2) | collective-permute-done | bytes 524320 | tf_op jit(solution)/shard_map/ppermute | solution.py:54
  46.3 1.9 %collective-permute-start.5 = (bf16[1024,256]{1,0:T(8,128)(2,1)}, bf16[1024,256]{1,0:T(8,128)(2,1)}, u32[]{:S(2)}, u32[]{:S(2)}) collective-permute-start(bf16[1024,256]{1,0:T(8,128)(2,1)} %collective-permute-done.2.x2), channel_id=1, source_target_pairs={{8,0},{9,1},{10,2},{11,3},{12,4},{13,5},{14,6},{15,7},{1,8},{0,9},... | collective-permute-start | bytes 1572872 | tf_op jit(solution)/shard_map/ppermute | solution.py:54
  48.3 4.8 %shard_map.37 = f32[8,4,5,8,256]{4,3,2,1,0:T(8,128)} custom-call(bf16[2,1024,256]{2,1,0:T(8,128)(2,1)S(1)} %copy-done, bf16[2,1024,256]{2,1,0:T(8,128)(2,1)S(1)} %collective-permute-done.b, bf16[1040,256]{1,0:T(8,128)(2,1)} %collective-permute-done.1.x1, bf16[1024,256]{1,0:T(8,128)(2,1)} %collective-permute-done.2.x2, ...), custom_call_target="tpu_custom_call" | custom-call | flops 1342177280 | bytes 5513216 | tf_op jit(solution)/shard_map/pallas_call | solution.py:155
  53.1 8.1 %collective-permute-done.5.v2 = bf16[1024,256]{1,0:T(8,128)(2,1)} collective-permute-done((bf16[1024,256]{1,0:T(8,128)(2,1)}, bf16[1024,256]{1,0:T(8,128)(2,1)}, u32[]{:S(2)}, u32[]{:S(2)}) %collective-permute-start.5) | collective-permute-done | bytes 524320 | tf_op jit(solution)/shard_map/ppermute | solution.py:54
  61.2 5.5 %shard_map.38 = f32[4,8,4,8,256]{4,3,2,1,0:T(8,128)} custom-call(bf16[2,1024,256]{2,1,0:T(8,128)(2,1)S(1)} %copy-done, bf16[2,1024,256]{2,1,0:T(8,128)(2,1)S(1)} %collective-permute-done.b, bf16[1040,256]{1,0:T(8,128)(2,1)} %collective-permute-done.1.x1, bf16[1024,256]{1,0:T(8,128)(2,1)} %collective-permute-done.2.x2, ...), custom_call_target="tpu_custom_call" | custom-call | flops 1073741824 | bytes 6307840 | tf_op jit(solution)/shard_map/pallas_call | solution.py:155
  66.7 3.6 %all-to-all-start.1 = ((f32[4,256,256]{2,1,0:T(8,128)}), f32[4,256,256]{2,1,0:T(8,128)S(1)}, u32[]{:S(2)}, u32[]{:S(2)}) async-start(f32[4,256,256]{2,1,0:T(8,128)} %bitcast.10), calls=%async_computation.2 | async-start | bytes 2097152 | tf_op jit(solution)/shard_map/all_to_all | solution.py:187
  70.3 18.0 %all-to-all-done.1 = f32[4,256,256]{2,1,0:T(8,128)S(1)} async-done(((f32[4,256,256]{2,1,0:T(8,128)}), f32[4,256,256]{2,1,0:T(8,128)S(1)}, u32[]{:S(2)}, u32[]{:S(2)}) %all-to-all-start.1) | async-done | bytes 1048608 | tf_op jit(solution)/shard_map/all_to_all | solution.py:187
  89.0 11.2 %all-to-all-start.2 = ((f32[8,32,256]{2,1,0:T(8,128)}), f32[8,32,256]{2,1,0:T(8,128)S(1)}, u32[]{:S(2)}, u32[]{:S(2)}) async-start(f32[8,32,256]{2,1,0:T(8,128)} %bitcast.11), calls=%async_computation.3 | async-start | bytes 524288 | tf_op jit(solution)/shard_map/all_to_all | solution.py:189
  101.0 8.5 %all-to-all-done.2 = f32[8,32,256]{2,1,0:T(8,128)S(1)} async-done(((f32[8,32,256]{2,1,0:T(8,128)}), f32[8,32,256]{2,1,0:T(8,128)S(1)}, u32[]{:S(2)}, u32[]{:S(2)}) %all-to-all-start.2) | async-done | bytes 262176 | tf_op jit(solution)/shard_map/all_to_all | solution.py:189
  109.5 14.0 %collective-permute-start.8 = (f32[4,8,256]{2,1,0:T(8,128)S(1)}, f32[4,8,256]{2,1,0:T(8,128)S(1)}, u32[]{:S(2)}, u32[]{:S(2)}) collective-permute-start(f32[4,8,256]{2,1,0:T(8,128)S(1)} %bitcast.81), channel_id=1, source_target_pairs={{0,10},{1,11},{2,12},{3,13},{4,14},{5,15},{6,8},{7,9},{8,3},{9,2},... | collective-permute-start | bytes 98312 | tf_op jit(solution)/shard_map/ppermute | solution.py:58
  123.5 3.4 %all-to-all-start = ((f32[4,40,256]{2,1,0:T(8,128)}), f32[4,40,256]{2,1,0:T(8,128)S(1)}, u32[]{:S(2)}, u32[]{:S(2)}) async-start(f32[4,40,256]{2,1,0:T(8,128)} %bitcast.80), calls=%async_computation.1 | async-start | bytes 327680 | tf_op jit(solution)/shard_map/all_to_all | solution.py:191
  126.9 2.3 %collective-permute-done.8 = f32[4,8,256]{2,1,0:T(8,128)S(1)} collective-permute-done((f32[4,8,256]{2,1,0:T(8,128)S(1)}, f32[4,8,256]{2,1,0:T(8,128)S(1)}, u32[]{:S(2)}, u32[]{:S(2)}) %collective-permute-start.8) | collective-permute-done | bytes 32800 | tf_op jit(solution)/shard_map/ppermute | solution.py:58
  129.2 5.2 %all-to-all-done = f32[4,40,256]{2,1,0:T(8,128)S(1)} async-done(((f32[4,40,256]{2,1,0:T(8,128)}), f32[4,40,256]{2,1,0:T(8,128)S(1)}, u32[]{:S(2)}, u32[]{:S(2)}) %all-to-all-start) | async-done | bytes 163872 | tf_op jit(solution)/shard_map/all_to_all | solution.py:191
  134.4 3.6 %collective-permute-start.9 = (f32[2,8,256]{2,1,0:T(8,128)S(1)}, f32[2,8,256]{2,1,0:T(8,128)S(1)}, u32[]{:S(2)}, u32[]{:S(2)}) collective-permute-start(f32[2,8,256]{2,1,0:T(8,128)S(1)} %pad_maximum_fusion.2), channel_id=1, source_target_pairs={{0,6},{1,7},{2,0},{3,1},{4,3},{5,2},{6,5},{7,4},{8,15},{9,14},{10,... | collective-permute-start | bytes 49160 | tf_op jit(solution)/shard_map/ppermute | solution.py:58
  138.0 1.9 %collective-permute-start.7 = (f32[4,8,256]{2,1,0:T(8,128)S(1)}, f32[4,8,256]{2,1,0:T(8,128)S(1)}, u32[]{:S(2)}, u32[]{:S(2)}) collective-permute-start(f32[4,8,256]{2,1,0:T(8,128)S(1)} %pad_maximum_fusion), channel_id=1, source_target_pairs={{0,2},{1,3},{2,4},{3,5},{4,6},{5,7},{6,0},{7,1},{8,10},{9,11},{10,... | collective-permute-start | bytes 98312 | tf_op jit(solution)/shard_map/ppermute | solution.py:58
  139.9 6.7 %collective-permute-start.6 = (f32[2,8,256]{2,1,0:T(8,128)S(1)}, f32[2,8,256]{2,1,0:T(8,128)S(1)}, u32[]{:S(2)}, u32[]{:S(2)}) collective-permute-start(f32[2,8,256]{2,1,0:T(8,128)S(1)} %pad_maximum_fusion.1), channel_id=1, source_target_pairs={{0,1},{1,0},{2,3},{3,2},{4,5},{5,4},{6,7},{7,6},{8,9},{9,8},{10,11... | collective-permute-start | bytes 49160 | tf_op jit(solution)/shard_map/ppermute | solution.py:58
  147.4 0.9 select_add_fusion
  (31 shorter events, 3.2 us)
Async XLA Ops:
  6.5 117.0 %reduce-scatter.2.cloned.1.call-start = ((), (), s32[]{:S(2)}) async-start(), calls=%async_computation.4 | async-start | bytes 1474560 | tf_op jit(solution)/shard_map/reduce_scatter | solution.py:183
  6.5 41.7 %collective-permute-start = (bf16[2,1024,256]{2,1,0:T(8,128)(2,1)}, bf16[2,1024,256]{2,1,0:T(8,128)(2,1)S(1)}, u32[]{:S(2)}, u32[]{:S(2)}) collective-permute-start(bf16[2,1024,256]{2,1,0:T(8,128)(2,1)} %a.3), channel_id=1, source_target_pairs={{1,0},{0,1},{3,2},{2,3},{5,4},{4,5},{7,6},{6,7},{9,8},{8,9},{11,10... | collective-permute-start | bytes 3145736 | tf_op jit(solution)/shard_map/ppermute | solution.py:54
  15.3 32.9 %collective-permute-start.3 = (bf16[2,1024,256]{2,1,0:T(8,128)(2,1)}, bf16[2,1024,256]{2,1,0:T(8,128)(2,1)S(1)}, u32[]{:S(2)}, u32[]{:S(2)}) collective-permute-start(bf16[2,1024,256]{2,1,0:T(8,128)(2,1)} %a.3), channel_id=1, source_target_pairs={{6,0},{7,1},{0,2},{1,3},{3,4},{2,5},{5,6},{4,7},{15,8},{14,9},{9,1... | collective-permute-start | bytes 3145736 | tf_op jit(solution)/shard_map/ppermute | solution.py:54
  17.9 30.3 %copy-start = (bf16[2,1024,256]{2,1,0:T(8,128)(2,1)S(1)}, bf16[2,1024,256]{2,1,0:T(8,128)(2,1)}, u32[]{:S(2)}) copy-start(bf16[2,1024,256]{2,1,0:T(8,128)(2,1)} %a.3) | copy-start | bytes 3145732
  19.3 15.8 %collective-permute-start.1 = (bf16[1040,256]{1,0:T(8,128)(2,1)S(1)}, bf16[1040,256]{1,0:T(8,128)(2,1)}, u32[]{:S(2)}, u32[]{:S(2)}) collective-permute-start(bf16[1040,256]{1,0:T(8,128)(2,1)S(1)} %fusion.1), channel_id=1, source_target_pairs={{2,0},{3,1},{4,2},{5,3},{6,4},{7,5},{0,6},{1,7},{10,8},{11,9},{12,... | collective-permute-start | bytes 1597448 | tf_op jit(solution)/shard_map/ppermute | solution.py:54
  23.9 22.4 %collective-permute-start.2 = (bf16[1024,256]{1,0:T(8,128)(2,1)S(1)}, bf16[1024,256]{1,0:T(8,128)(2,1)}, u32[]{:S(2)}, u32[]{:S(2)}) collective-permute-start(bf16[1024,256]{1,0:T(8,128)(2,1)S(1)} %get-tuple-element.5), channel_id=1, source_target_pairs={{2,0},{3,1},{4,2},{5,3},{6,4},{7,5},{0,6},{1,7},{10,8},{11,9},{12,... | collective-permute-start | bytes 1572872 | tf_op jit(solution)/shard_map/ppermute | solution.py:54
  35.1 26.1 %collective-permute-start.4 = (bf16[1040,256]{1,0:T(8,128)(2,1)}, bf16[1040,256]{1,0:T(8,128)(2,1)}, u32[]{:S(2)}, u32[]{:S(2)}) collective-permute-start(bf16[1040,256]{1,0:T(8,128)(2,1)} %collective-permute-done.1.x1), channel_id=1, source_target_pairs={{8,0},{9,1},{10,2},{11,3},{12,4},{13,5},{14,6},{15,7},{1,8},{0,9},... | collective-permute-start | bytes 1597448 | tf_op jit(solution)/shard_map/ppermute | solution.py:54
  46.3 14.9 %collective-permute-start.5 = (bf16[1024,256]{1,0:T(8,128)(2,1)}, bf16[1024,256]{1,0:T(8,128)(2,1)}, u32[]{:S(2)}, u32[]{:S(2)}) collective-permute-start(bf16[1024,256]{1,0:T(8,128)(2,1)} %collective-permute-done.2.x2), channel_id=1, source_target_pairs={{8,0},{9,1},{10,2},{11,3},{12,4},{13,5},{14,6},{15,7},{1,8},{0,9},... | collective-permute-start | bytes 1572872 | tf_op jit(solution)/shard_map/ppermute | solution.py:54
  66.7 21.5 %all-to-all-start.1 = ((f32[4,256,256]{2,1,0:T(8,128)}), f32[4,256,256]{2,1,0:T(8,128)S(1)}, u32[]{:S(2)}, u32[]{:S(2)}) async-start(f32[4,256,256]{2,1,0:T(8,128)} %bitcast.10), calls=%async_computation.2 | async-start | bytes 2097152 | tf_op jit(solution)/shard_map/all_to_all | solution.py:187
  70.3 30.6 %copy-start.1 = (s32[1,9]{1,0:T(1,128)S(1)}, s32[1,9]{1,0:T(1,128)}, u32[]{:S(2)}) copy-start(s32[1,9]{1,0:T(1,128)} %param.4) | copy-start | bytes 112
  89.0 20.4 %all-to-all-start.2 = ((f32[8,32,256]{2,1,0:T(8,128)}), f32[8,32,256]{2,1,0:T(8,128)S(1)}, u32[]{:S(2)}, u32[]{:S(2)}) async-start(f32[8,32,256]{2,1,0:T(8,128)} %bitcast.11), calls=%async_computation.3 | async-start | bytes 524288 | tf_op jit(solution)/shard_map/all_to_all | solution.py:189
  109.5 19.7 %collective-permute-start.8 = (f32[4,8,256]{2,1,0:T(8,128)S(1)}, f32[4,8,256]{2,1,0:T(8,128)S(1)}, u32[]{:S(2)}, u32[]{:S(2)}) collective-permute-start(f32[4,8,256]{2,1,0:T(8,128)S(1)} %bitcast.81), channel_id=1, source_target_pairs={{0,10},{1,11},{2,12},{3,13},{4,14},{5,15},{6,8},{7,9},{8,3},{9,2},... | collective-permute-start | bytes 98312 | tf_op jit(solution)/shard_map/ppermute | solution.py:58
  123.5 10.8 %all-to-all-start = ((f32[4,40,256]{2,1,0:T(8,128)}), f32[4,40,256]{2,1,0:T(8,128)S(1)}, u32[]{:S(2)}, u32[]{:S(2)}) async-start(f32[4,40,256]{2,1,0:T(8,128)} %bitcast.80), calls=%async_computation.1 | async-start | bytes 327680 | tf_op jit(solution)/shard_map/all_to_all | solution.py:191
  134.4 12.2 %collective-permute-start.9 = (f32[2,8,256]{2,1,0:T(8,128)S(1)}, f32[2,8,256]{2,1,0:T(8,128)S(1)}, u32[]{:S(2)}, u32[]{:S(2)}) collective-permute-start(f32[2,8,256]{2,1,0:T(8,128)S(1)} %pad_maximum_fusion.2), channel_id=1, source_target_pairs={{0,6},{1,7},{2,0},{3,1},{4,3},{5,2},{6,5},{7,4},{8,15},{9,14},{10,... | collective-permute-start | bytes 49160 | tf_op jit(solution)/shard_map/ppermute | solution.py:58
  138.0 9.4 %collective-permute-start.7 = (f32[4,8,256]{2,1,0:T(8,128)S(1)}, f32[4,8,256]{2,1,0:T(8,128)S(1)}, u32[]{:S(2)}, u32[]{:S(2)}) collective-permute-start(f32[4,8,256]{2,1,0:T(8,128)S(1)} %pad_maximum_fusion), channel_id=1, source_target_pairs={{0,2},{1,3},{2,4},{3,5},{4,6},{5,7},{6,0},{7,1},{8,10},{9,11},{10,... | collective-permute-start | bytes 98312 | tf_op jit(solution)/shard_map/ppermute | solution.py:58
  139.9 7.5 %collective-permute-start.6 = (f32[2,8,256]{2,1,0:T(8,128)S(1)}, f32[2,8,256]{2,1,0:T(8,128)S(1)}, u32[]{:S(2)}, u32[]{:S(2)}) collective-permute-start(f32[2,8,256]{2,1,0:T(8,128)S(1)} %pad_maximum_fusion.1), channel_id=1, source_target_pairs={{0,1},{1,0},{2,3},{3,2},{4,5},{5,4},{6,7},{7,6},{8,9},{9,8},{10,11... | collective-permute-start | bytes 49160 | tf_op jit(solution)/shard_map/ppermute | solution.py:58
Sparse Core Ops, SparseCore 0:
  53.2 39.5 reduce-scatter.1

commit v3 on v0

v3 whole, which is shorter than its diff:
```python
import jax
import jax.numpy as jnp
import numpy as np
from jax import lax
from jax.experimental import pallas as pl
from jax.experimental.pallas import tpu as pltpu
from jax.sharding import Mesh
from jax.sharding import PartitionSpec as P

Z, H, L, X, C = 8, 4, 2, 4, 2
BLK = ("l", "x", "c")
BULK = ("z", "h")
N_BLK, N_BULK = L * X * C, Z * H
SLOTS = 9
W = 256
K = 2048
SLAB = W // N_BULK
EARLY = 8
DEPTH = 4


def place(l, x, c):
    return (l * X + x) * C + c


def own(l, x, c):
    return (l, x, c)


def sib(l, x, c):
    return (l, x, 1 - c)


def right(l, x, c):
    return (l, (x + 1) & 3, c)


def left(l, x, c):
    return (l, (x + 3) & 3, c ^ (x >> 1))


def flip(x):
    return (x + 3) >> 2


def over(l, x, c):
    return (1 - l, x, c ^ flip(x))


def diag(l, x, c):
    return (1 - l, (x + 1) & 3, c ^ (x >> 1) ^ l)


def diag_via(l, x, c):
    return (l, (x + 1) & 3, c ^ (x >> 1) ^ l ^ flip((x + 1) & 3))


def mate_bit(l, x):
    return flip(x) ^ l


def mate(l, x, c):
    return (l, x, c ^ mate_bit(l, x))


ALL = [(l, x, c) for l in range(L) for x in range(X) for c in range(C)]
TILES = [
    (own, own),
    (own, sib),
    (right, own),
    (right, sib),
    (right, over),
    (right, left),
    (over, left),
    (over, mate),
    (left, diag),
]


def mailing(l, x, c):
    me = (l, x, c)
    out = {}
    for t, (p, q) in enumerate(TILES):
        p, q = p(*me), q(*me)
        ends = [(p, q)] if t < 2 else [(p, q), (q, p)]
        for owner, other in ends:
            out.setdefault(place(*owner), []).append((t, place(*other)))
    return out


def addresses():
    table = np.full((N_BLK, N_BLK), -1, np.int32)
    for d in ALL:
        for owner, items in mailing(*d).items():
            assert len(items) <= DEPTH
            for slot, (_, other) in enumerate(items):
                assert table[owner, other] < 0
                table[owner, other] = place(*d) * DEPTH + slot
    assert (table >= 0).all()
    return table


def stamps():
    rows = []
    for d in ALL:
        where = {}
        for owner, items in mailing(*d).items():
            for slot, (t, _) in enumerate(items):
                where[(t, owner)] = owner * DEPTH + slot
        row = []
        for t, (p, q) in enumerate(TILES):
            row.append(where[(t, place(*p(*d)))])
            if t >= 2:
                row.append(where[(t, place(*q(*d)))])
        rows.append(row)
    return np.array(rows, np.int32)


def fetch(value, role):
    return lax.ppermute(value, BLK, [(place(*role(*d)), place(*d)) for d in ALL])


def position():
    return tuple(lax.axis_index(name) for name in BLK)


def dot(a, b):
    return lax.dot_general(
        a, b, (((0,), (0,)), ((), ())), preferred_element_type=jnp.float32
    )


def owns(carrier, block):
    row = carrier[K:].astype(jnp.float32)
    return jnp.max(jnp.where(row == block.astype(jnp.float32), 1.0, 0.0)) > 0.5


def settle(carrier, rhs, block, put):
    tile = dot(carrier[:K], rhs)
    kept = owns(carrier, place(*block))

    @pl.when(kept)
    def _():
        put(tile)

    @pl.when(jnp.logical_not(kept))
    def _():
        put(tile.T)


def early_kernel(a, b, xr, xl, yo, out):
    me = position()

    def put(slot):
        def write(tile):
            out[:, pl.ds(slot * SLAB, SLAB)] = tile.reshape(N_BULK, SLAB, W)

        return write

    put(0)(dot(a[:K], a[:K]))
    put(1)(dot(a[:K], b[:K]))
    settle(xr, a[:K], own(*me), put(2))
    settle(xr, b[:K], sib(*me), put(3))
    settle(xr, yo[:K], over(*me), put(4))
    settle(xr, xl[:K], left(*me), put(5))
    settle(yo, xl[:K], left(*me), put(6))
    mine = mate_bit(*me[:2]) == 0

    @pl.when(mine)
    def _():
        settle(yo, a[:K], mate(*me), put(7))

    @pl.when(jnp.logical_not(mine))
    def _():
        settle(yo, b[:K], mate(*me), put(7))


def late_kernel(xl, vd, out):
    def put(tile):
        out[...] = tile.reshape(N_BULK, SLAB, W)

    settle(xl, vd[:K], diag(*position()), put)


def pack_kernel(stamp, e, v, out):
    me = place(*position())
    k = 0
    for t in range(SLOTS):
        tile = e[pl.ds(t * SLAB, SLAB)] if t < EARLY else v[...]
        for _ in range(1 if t < 2 else 2):
            out[stamp[me, k]] = tile
            k += 1


def pick_kernel(table, cols, got, out):
    me = place(*position())
    for j in range(SLOTS):
        b = cols[0, j]

        @pl.when(b >= 0)
        def _():
            out[j] = got[table[me, jnp.maximum(b, 0)]]

        @pl.when(b < 0)
        def _():
            out[j] = jnp.zeros((SLAB, W), jnp.float32)


def call(kernel, shape, n_smem, n_tiles, *ins):
    vmem = pl.BlockSpec(memory_space=pltpu.VMEM)
    smem = pl.BlockSpec(memory_space=pltpu.SMEM)
    return pl.pallas_call(
        kernel,
        out_shape=jax.ShapeDtypeStruct(shape, jnp.float32),
        in_specs=[smem] * n_smem + [vmem] * (len(ins) - n_smem),
        out_specs=vmem,
        compiler_params=pltpu.CompilerParams(vmem_limit_bytes=40 * 2**20),
        cost_estimate=pl.CostEstimate(
            flops=n_tiles * 2 * W * W * K,
            bytes_accessed=sum(v.size * v.dtype.itemsize for v in ins)
            + 4 * int(np.prod(shape)),
            transcendentals=0,
        ),
    )(*ins)


def exchange(parts):
    got = lax.all_to_all(parts, BULK, 0, 0, tiled=True)
    return got.sum(0)


def local(aux_factors, tile_cols):
    row = jnp.pad(
        tile_cols.astype(jnp.bfloat16),
        ((0, 15), (0, W - SLOTS)),
        constant_values=-2,
    )
    a = jnp.concatenate([aux_factors.reshape(K, W), row])
    yo = fetch(a, over)
    xr = fetch(a, right)
    xl = fetch(a, left)
    b = fetch(a, sib)
    vd = fetch(yo, diag_via)

    early = call(early_kernel, (N_BULK, EARLY * SLAB, W), 0, EARLY, a, b, xr, xl, yo)
    late = call(late_kernel, (N_BULK, SLAB, W), 0, 1, xl, vd)
    early, late = exchange(early), exchange(late)

    mail = call(
        pack_kernel, (N_BLK * DEPTH, SLAB, W), 1, 0, jnp.asarray(stamps()), early, late
    )
    mail = lax.all_to_all(mail, BLK, 0, 0, tiled=True)
    return call(
        pick_kernel,
        (SLOTS, SLAB, W),
        2,
        0,
        jnp.asarray(addresses()),
        tile_cols,
        mail,
    )


def solution(mesh):
    fine = Mesh(mesh.devices.reshape(Z, H, L, X, C), (*BULK, *BLK))
    in_specs = (P(BULK, None, BLK), P(BLK, None))
    out_specs = P(BLK, BULK, None)
    return jax.shard_map(
        local, mesh=fine, in_specs=in_specs, out_specs=out_specs, check_vma=False
    )
```

time: 592 us -> 190 us (0.32)
  the two profiles are of different devices: /device:TPU:1 before, /device:TPU:80 now
where the time goes in v3:
time: 190 us
  waiting for transfers between devices  108 us (57%)
  starting transfers between devices  46.6 us (25%)
  blocking collectives  22.2 us (12%)
  Pallas kernels  11.1 us (6%)
  other arithmetic  2.11 us (1%)
    all_to_all x2, waiting for transfers between devices, exchange(): got = lax.all_to_all(parts, BULK, 0, 0, tiled=True)  62.6 us
    ppermute x5, waiting for transfers between devices, fetch(): lax.ppermute(value, BLK, [(place(*role(*d)), place(*d)) for d in ALL])  45.1 us
    all_to_all x2, starting transfers between devices, exchange(): got = lax.all_to_all(parts, BULK, 0, 0, tiled=True)  30.5 us
    all_to_all x1, blocking collectives, local(): mail = lax.all_to_all(mail, BLK, 0, 0, tiled=True)  22.2 us
    ppermute x5, starting transfers between devices, fetch(): lax.ppermute(value, BLK, [(place(*role(*d)), place(*d)) for d in ALL])  16.1 us
    pallas_call x4, Pallas kernels, call(): pl.pallas_call(kernel, out_shape=jax.ShapeDtypeStruct(shape, jnp.float32)...  11.1 us
  transfers between devices with their start and end apart: 7, of which 4 were waited for; matrix products, arithmetic and copies ran while one was open for 0% of the time, Pallas kernels for 5%

profile of v3, /device:TPU:80, one launch (start us, length us, event | category | flops | bytes accessed | tf_op | source)
XLA Modules:
  0.0 189.8 jit_solution(16730495739076000230)
XLA Ops:
  0.0 0.7 convert_element_type.5
  0.7 1.3 fusion.1.a
  2.0 3.5 %collective-permute-start.3 = (bf16[2064,256]{1,0:T(8,128)(2,1)S(1)}, bf16[2064,256]{1,0:T(8,128)(2,1)S(1)}, u32[]{:S(2)}, u32[]{:S(2)}) collective-permute-start(bf16[2064,256]{1,0:T(8,128)(2,1)S(1)} %fusion.1.a), channel_id=1, source_target_pairs={{8,0},{9,1},{11,2},{10,3},{13,4},{12,5},{15,6},{14,7},{0,8},{1,9},... | collective-permute-start | bytes 3170312 | tf_op jit(solution)/shard_map/ppermute | solution.py:120
  5.4 2.8 %collective-permute-start.2 = (bf16[2064,256]{1,0:T(8,128)(2,1)S(1)}, bf16[2064,256]{1,0:T(8,128)(2,1)S(1)}, u32[]{:S(2)}, u32[]{:S(2)}) collective-permute-start(bf16[2064,256]{1,0:T(8,128)(2,1)S(1)} %fusion.1.a), channel_id=1, source_target_pairs={{6,0},{7,1},{0,2},{1,3},{3,4},{2,5},{5,6},{4,7},{14,8},{15,9},{8,1... | collective-permute-start | bytes 3170312 | tf_op jit(solution)/shard_map/ppermute | solution.py:120
  8.3 20.6 %collective-permute-done.3.yo = bf16[2064,256]{1,0:T(8,128)(2,1)S(1)} collective-permute-done((bf16[2064,256]{1,0:T(8,128)(2,1)S(1)}, bf16[2064,256]{1,0:T(8,128)(2,1)S(1)}, u32[]{:S(2)}, u32[]{:S(2)}) %collective-permute-start.3) | collective-permute-done | bytes 1056800 | tf_op jit(solution)/shard_map/ppermute | solution.py:120
  28.9 4.9 %collective-permute-start.4 = (bf16[2064,256]{1,0:T(8,128)(2,1)S(1)}, bf16[2064,256]{1,0:T(8,128)(2,1)S(1)}, u32[]{:S(2)}, u32[]{:S(2)}) collective-permute-start(bf16[2064,256]{1,0:T(8,128)(2,1)S(1)} %collective-permute-done.3.yo), channel_id=1, source_target_pairs={{3,0},{2,1},{5,2},{4,3},{6,4},{7,5},{1,6},{0,7},{10,8},{11,9},{12,... | collective-permute-start | bytes 3170312 | tf_op jit(solution)/shard_map/ppermute | solution.py:120
  33.9 2.2 %collective-permute-start = (bf16[2064,256]{1,0:T(8,128)(2,1)S(1)}, bf16[2064,256]{1,0:T(8,128)(2,1)}, u32[]{:S(2)}, u32[]{:S(2)}) collective-permute-start(bf16[2064,256]{1,0:T(8,128)(2,1)S(1)} %fusion.1.a), channel_id=1, source_target_pairs={{1,0},{0,1},{3,2},{2,3},{5,4},{4,5},{7,6},{6,7},{9,8},{8,9},{11,10... | collective-permute-start | bytes 3170312 | tf_op jit(solution)/shard_map/ppermute | solution.py:120
  36.0 2.6 %collective-permute-start.1 = (bf16[2064,256]{1,0:T(8,128)(2,1)S(1)}, bf16[2064,256]{1,0:T(8,128)(2,1)}, u32[]{:S(2)}, u32[]{:S(2)}) collective-permute-start(bf16[2064,256]{1,0:T(8,128)(2,1)S(1)} %fusion.1.a), channel_id=1, source_target_pairs={{2,0},{3,1},{4,2},{5,3},{6,4},{7,5},{0,6},{1,7},{10,8},{11,9},{12,... | collective-permute-start | bytes 3170312 | tf_op jit(solution)/shard_map/ppermute | solution.py:120
  38.7 18.8 %collective-permute-done.4.vd = bf16[2064,256]{1,0:T(8,128)(2,1)S(1)} collective-permute-done((bf16[2064,256]{1,0:T(8,128)(2,1)S(1)}, bf16[2064,256]{1,0:T(8,128)(2,1)S(1)}, u32[]{:S(2)}, u32[]{:S(2)}) %collective-permute-start.4) | collective-permute-done | bytes 1056800 | tf_op jit(solution)/shard_map/ppermute | solution.py:120
  57.5 1.3 shard_map.47
  58.8 15.2 %all-to-all-start.1 = ((f32[32,8,256]{2,1,0:T(8,128)}), f32[32,8,256]{2,1,0:T(8,128)S(1)}, u32[]{:S(2)}, u32[]{:S(2)}) async-start(f32[32,8,256]{2,1,0:T(8,128)} %shard_map.47), calls=%async_computation.1 | async-start | bytes 524288 | tf_op jit(solution)/shard_map/all_to_all | solution.py:228
  74.1 0.0 collective-permute-done.b
  74.1 5.7 %collective-permute-done.1.xr = bf16[2064,256]{1,0:T(8,128)(2,1)} collective-permute-done((bf16[2064,256]{1,0:T(8,128)(2,1)S(1)}, bf16[2064,256]{1,0:T(8,128)(2,1)}, u32[]{:S(2)}, u32[]{:S(2)}) %collective-permute-start.1) | collective-permute-done | bytes 1056800 | tf_op jit(solution)/shard_map/ppermute | solution.py:120
  79.8 7.6 %shard_map.46 = f32[32,64,256]{2,1,0:T(8,128)} custom-call(bf16[2064,256]{1,0:T(8,128)(2,1)S(1)} %fusion.1.a, bf16[2064,256]{1,0:T(8,128)(2,1)} %collective-permute-done.b, bf16[2064,256]{1,0:T(8,128)(2,1)} %collective-permute-done.1.xr, bf16[2064,256]{1,0:T(8,128)(2,1)S(1)} %collective-permute-done.2.xl, bf16[2064,256]{1,0:T(8,128)(2,1)S(1)} %collective-permute-done.3.yo), custom_call_target="tpu_custom_call" | custom-call | flops 2147483648 | bytes 7380992 | tf_op jit(solution)/shard_map/pallas_call | solution.py:212
  87.3 0.0 all-to-all-done.1
  87.3 15.3 %all-to-all-start = ((f32[32,64,256]{2,1,0:T(8,128)}), f32[32,64,256]{2,1,0:T(8,128)S(1)}, u32[]{:S(2)}, u32[]{:S(2)}) async-start(f32[32,64,256]{2,1,0:T(8,128)} %shard_map.46), calls=%async_computation | async-start | bytes 4194304 | tf_op jit(solution)/shard_map/all_to_all | solution.py:228
  102.7 0.0 copy-start.1
  102.7 62.6 %all-to-all-done = f32[32,64,256]{2,1,0:T(8,128)S(1)} async-done(((f32[32,64,256]{2,1,0:T(8,128)}), f32[32,64,256]{2,1,0:T(8,128)S(1)}, u32[]{:S(2)}, u32[]{:S(2)}) %all-to-all-start) | async-done | bytes 2097184 | tf_op jit(solution)/shard_map/all_to_all | solution.py:228
  165.3 0.1 reduce_sum.18.e
  165.4 0.0 copy-start
  165.4 0.0 copy-start.2
  165.4 0.7 shard_map.48
  166.2 22.2 %all_to_all.15.got = f32[64,8,256]{2,1,0:T(8,128)S(1)} all-to-all(f32[64,8,256]{2,1,0:T(8,128)S(1)} %shard_map.48), channel_id=1, replica_groups=mesh['z'=8,'h'=4,'l'=2,'x'=4,'c'=2] {'l','x','c'}, dimensions={0} | all-to-all | bytes 1048576 | tf_op jit(solution)/shard_map/all_to_all | solution.py:252
  188.3 1.5 shard_map.49
  (5 shorter events, 0.0 us)
Async XLA Ops:
  2.0 27.0 %collective-permute-start.3 = (bf16[2064,256]{1,0:T(8,128)(2,1)S(1)}, bf16[2064,256]{1,0:T(8,128)(2,1)S(1)}, u32[]{:S(2)}, u32[]{:S(2)}) collective-permute-start(bf16[2064,256]{1,0:T(8,128)(2,1)S(1)} %fusion.1.a), channel_id=1, source_target_pairs={{8,0},{9,1},{11,2},{10,3},{13,4},{12,5},{15,6},{14,7},{0,8},{1,9},... | collective-permute-start | bytes 3170312 | tf_op jit(solution)/shard_map/ppermute | solution.py:120
  5.4 33.2 %collective-permute-start.2 = (bf16[2064,256]{1,0:T(8,128)(2,1)S(1)}, bf16[2064,256]{1,0:T(8,128)(2,1)S(1)}, u32[]{:S(2)}, u32[]{:S(2)}) collective-permute-start(bf16[2064,256]{1,0:T(8,128)(2,1)S(1)} %fusion.1.a), channel_id=1, source_target_pairs={{6,0},{7,1},{0,2},{1,3},{3,4},{2,5},{5,6},{4,7},{14,8},{15,9},{8,1... | collective-permute-start | bytes 3170312 | tf_op jit(solution)/shard_map/ppermute | solution.py:120
  28.9 28.6 %collective-permute-start.4 = (bf16[2064,256]{1,0:T(8,128)(2,1)S(1)}, bf16[2064,256]{1,0:T(8,128)(2,1)S(1)}, u32[]{:S(2)}, u32[]{:S(2)}) collective-permute-start(bf16[2064,256]{1,0:T(8,128)(2,1)S(1)} %collective-permute-done.3.yo), channel_id=1, source_target_pairs={{3,0},{2,1},{5,2},{4,3},{6,4},{7,5},{1,6},{0,7},{10,8},{11,9},{12,... | collective-permute-start | bytes 3170312 | tf_op jit(solution)/shard_map/ppermute | solution.py:120
  33.9 40.2 %collective-permute-start = (bf16[2064,256]{1,0:T(8,128)(2,1)S(1)}, bf16[2064,256]{1,0:T(8,128)(2,1)}, u32[]{:S(2)}, u32[]{:S(2)}) collective-permute-start(bf16[2064,256]{1,0:T(8,128)(2,1)S(1)} %fusion.1.a), channel_id=1, source_target_pairs={{1,0},{0,1},{3,2},{2,3},{5,4},{4,5},{7,6},{6,7},{9,8},{8,9},{11,10... | collective-permute-start | bytes 3170312 | tf_op jit(solution)/shard_map/ppermute | solution.py:120
  36.0 43.7 %collective-permute-start.1 = (bf16[2064,256]{1,0:T(8,128)(2,1)S(1)}, bf16[2064,256]{1,0:T(8,128)(2,1)}, u32[]{:S(2)}, u32[]{:S(2)}) collective-permute-start(bf16[2064,256]{1,0:T(8,128)(2,1)S(1)} %fusion.1.a), channel_id=1, source_target_pairs={{2,0},{3,1},{4,2},{5,3},{6,4},{7,5},{0,6},{1,7},{10,8},{11,9},{12,... | collective-permute-start | bytes 3170312 | tf_op jit(solution)/shard_map/ppermute | solution.py:120
  58.8 28.5 %all-to-all-start.1 = ((f32[32,8,256]{2,1,0:T(8,128)}), f32[32,8,256]{2,1,0:T(8,128)S(1)}, u32[]{:S(2)}, u32[]{:S(2)}) async-start(f32[32,8,256]{2,1,0:T(8,128)} %shard_map.47), calls=%async_computation.1 | async-start | bytes 524288 | tf_op jit(solution)/shard_map/all_to_all | solution.py:228
  87.3 77.9 %all-to-all-start = ((f32[32,64,256]{2,1,0:T(8,128)}), f32[32,64,256]{2,1,0:T(8,128)S(1)}, u32[]{:S(2)}, u32[]{:S(2)}) async-start(f32[32,64,256]{2,1,0:T(8,128)} %shard_map.46), calls=%async_computation | async-start | bytes 4194304 | tf_op jit(solution)/shard_map/all_to_all | solution.py:228
  102.7 62.7 %copy-start.1 = (s32[16,16]{1,0:T(8,128)S(1)}, s32[16,16]{1,0:T(8,128)}, u32[]{:S(2)}) copy-start(s32[16,16]{1,0:T(8,128)} %constant.9.clone.stamp) | copy-start | bytes 3076
  165.4 22.9 %copy-start = (s32[16,16]{1,0:T(8,128)S(1)}, s32[16,16]{1,0:T(8,128)}, u32[]{:S(2)}) copy-start(s32[16,16]{1,0:T(8,128)} %constant.10.clone.table) | copy-start | bytes 3076
  165.4 22.9 %copy-start.2 = (s32[1,9]{1,0:T(1,128)S(1)}, s32[1,9]{1,0:T(1,128)}, u32[]{:S(2)}) copy-start(s32[1,9]{1,0:T(1,128)} %cols.1) | copy-start | bytes 112

commit v4 on v3

--- a/solution.py
+++ b/solution.py
@@ -17,6 +17,7 @@
 SLAB = W // N_BULK
 EARLY = 8
 DEPTH = 4
+DATA, MARK, TOP = EARLY * W // Z, 16, 14.0
 
 
 def place(l, x, c):
@@ -136,57 +137,73 @@
 
 
 def settle(carrier, rhs, block, put):
-    tile = dot(carrier[:K], rhs)
     kept = owns(carrier, place(*block))
 
     @pl.when(kept)
     def _():
-        put(tile)
+        put(dot(carrier[:K], rhs[:K]))
 
     @pl.when(jnp.logical_not(kept))
     def _():
-        put(tile.T)
-
-
-def early_kernel(a, b, xr, xl, yo, out):
+        put(dot(rhs[:K], carrier[:K]))
+
+
+def early_kernel(a, b, xr, xl, yo, out, scale):
     me = position()
 
     def put(slot):
         def write(tile):
-            out[:, pl.ds(slot * SLAB, SLAB)] = tile.reshape(N_BULK, SLAB, W)
+            tile = tile.reshape(Z, H, SLAB, W)
+            for h in range(H):
+                row = (h * EARLY + slot) * SLAB
+                out[:, pl.ds(row, SLAB)] = tile[:, h]
 
         return write
 
     put(0)(dot(a[:K], a[:K]))
     put(1)(dot(a[:K], b[:K]))
-    settle(xr, a[:K], own(*me), put(2))
-    settle(xr, b[:K], sib(*me), put(3))
-    settle(xr, yo[:K], over(*me), put(4))
-    settle(xr, xl[:K], left(*me), put(5))
-    settle(yo, xl[:K], left(*me), put(6))
+    settle(xr, a, own(*me), put(2))
+    settle(xr, b, sib(*me), put(3))
+    settle(xr, yo, over(*me), put(4))
+    settle(xr, xl, left(*me), put(5))
+    settle(yo, xl, left(*me), put(6))
     mine = mate_bit(*me[:2]) == 0
 
     @pl.when(mine)
     def _():
-        settle(yo, a[:K], mate(*me), put(7))
+        settle(yo, a, mate(*me), put(7))
 
     @pl.when(jnp.logical_not(mine))
     def _():
-        settle(yo, b[:K], mate(*me), put(7))
+        settle(yo, b, mate(*me), put(7))
+
+    most = jnp.max(jnp.abs(out[0, :DATA]), axis=0, keepdims=True)
+    for z in range(1, Z):
+        peak = jnp.max(jnp.abs(out[z, :DATA]), axis=0, keepdims=True)
+        most = jnp.maximum(most, peak)
+    most = jnp.maximum(jnp.max(most, axis=1, keepdims=True), 1e-30)
+    power = jnp.ceil(jnp.log2(jnp.broadcast_to(most, (8, 128))))
+    spread = 1.0 + lax.axis_index("z").astype(jnp.float32) / Z
+    by = jnp.exp2(TOP - power) * spread
+    scale[...] = by
+    mark = jnp.broadcast_to((power / by)[:1, :1], (MARK, W))
+    for z in range(Z):
+        out[z, DATA:] = mark
 
 
 def late_kernel(xl, vd, out):
     def put(tile):
-        out[...] = tile.reshape(N_BULK, SLAB, W)
-
-    settle(xl, vd[:K], diag(*position()), put)
-
-
-def pack_kernel(stamp, e, v, out):
+        out[...] = tile.reshape(Z, W // Z, W)
+
+    settle(xl, vd, diag(*position()), put)
+
+
+def pack_kernel(stamp, got, out):
     me = place(*position())
     k = 0
     for t in range(SLOTS):
-        tile = e[pl.ds(t * SLAB, SLAB)] if t < EARLY else v[...]
+        rows = pl.ds(t * SLAB, SLAB)
+        tile = got[0, rows] + got[1, rows] + got[2, rows] + got[3, rows]
         for _ in range(1 if t < 2 else 2):
             out[stamp[me, k]] = tile
             k += 1
@@ -206,27 +223,26 @@
             out[j] = jnp.zeros((SLAB, W), jnp.float32)
 
 
-def call(kernel, shape, n_smem, n_tiles, *ins):
+def call(kernel, shapes, n_smem, n_tiles, *ins):
     vmem = pl.BlockSpec(memory_space=pltpu.VMEM)
     smem = pl.BlockSpec(memory_space=pltpu.SMEM)
+    size = sum(int(np.prod(shape)) for shape in shapes)
     return pl.pallas_call(
         kernel,
-        out_shape=jax.ShapeDtypeStruct(shape, jnp.float32),
+        out_shape=[jax.ShapeDtypeStruct(shape, jnp.float32) for shape in shapes],
         in_specs=[smem] * n_smem + [vmem] * (len(ins) - n_smem),
-        out_specs=vmem,
+        out_specs=[vmem] * len(shapes),
         compiler_params=pltpu.CompilerParams(vmem_limit_bytes=40 * 2**20),
         cost_estimate=pl.CostEstimate(
             flops=n_tiles * 2 * W * W * K,
-            bytes_accessed=sum(v.size * v.dtype.itemsize for v in ins)
-            + 4 * int(np.prod(shape)),
+            bytes_accessed=4 * size + sum(v.size * v.dtype.itemsize for v in ins),
             transcendentals=0,
         ),
     )(*ins)
 
 
-def exchange(parts):
-    got = lax.all_to_all(parts, BULK, 0, 0, tiled=True)
-    return got.sum(0)
+def everywhere(value, axes):
+    return lax.all_to_all(value, axes, 0, 0, tiled=True)
 
 
 def local(aux_factors, tile_cols):
@@ -240,25 +256,30 @@
     xr = fetch(a, right)
     xl = fetch(a, left)
     b = fetch(a, sib)
+    yo, xr, xl = lax.optimization_barrier((yo, xr, xl))
     vd = fetch(yo, diag_via)
 
-    early = call(early_kernel, (N_BULK, EARLY * SLAB, W), 0, EARLY, a, b, xr, xl, yo)
-    late = call(late_kernel, (N_BULK, SLAB, W), 0, 1, xl, vd)
-    early, late = exchange(early), exchange(late)
-
-    mail = call(
-        pack_kernel, (N_BLK * DEPTH, SLAB, W), 1, 0, jnp.asarray(stamps()), early, late
-    )
-    mail = lax.all_to_all(mail, BLK, 0, 0, tiled=True)
-    return call(
-        pick_kernel,
-        (SLOTS, SLAB, W),
-        2,
-        0,
-        jnp.asarray(addresses()),
-        tile_cols,
-        mail,
-    )
+    early, scale = call(
+        early_kernel, [(Z, DATA + MARK, W), (8, 128)], 0, EARLY, a, b, xr, xl, yo
+    )
+    early = everywhere((early * scale[0, 0]).astype(jnp.float16), "z")
+    (late,) = call(late_kernel, [(Z, W // Z, W)], 0, 1, xl, vd)
+    early, late = lax.optimization_barrier((early, late))
+    late = everywhere(late, "z").sum(0)
+
+    power = early[:, DATA:DATA + 1, :1].astype(jnp.float32)
+    spread = 1.0 + lax.broadcasted_iota(jnp.float32, (Z, 1, 1), 0) / Z
+    early = early[:, :DATA].astype(jnp.float32) * (jnp.exp2(power - TOP) / spread)
+    early = early.sum(0).reshape(H, EARLY * SLAB, W)
+    late = late.reshape(H, SLAB, W)
+
+    parts = everywhere(jnp.concatenate([early, late], 1), "h")
+    (mail,) = call(
+        pack_kernel, [(N_BLK * DEPTH, SLAB, W)], 1, 0, jnp.asarray(stamps()), parts
+    )
+    mail = everywhere(mail, BLK)
+    table = jnp.asarray(addresses())
+    return call(pick_kernel, [(SLOTS, SLAB, W)], 2, 0, table, tile_cols, mail)[0]
 
 
 def solution(mesh):

time: 190 us -> 137 us (0.72)
  the two profiles are of different devices: /device:TPU:80 before, /device:TPU:1 now
where the time goes in v4:
time: 137 us; the launch traced here: 136 us
  waiting for transfers between devices  55.3 us (40%)
  starting transfers between devices  35.1 us (26%)
  blocking collectives  32.7 us (24%)
  Pallas kernels  7.98 us (6%)
  other arithmetic  4.37 us (3%)
    ppermute x5, waiting for transfers between devices, fetch(): lax.ppermute(value, BLK, [(place(*role(*d)), place(*d)) for d in ALL])  43.8 us
    all_to_all x2, blocking collectives, everywhere(): return lax.all_to_all(value, axes, 0, 0, tiled=True)  32.7 us
    ppermute x5, starting transfers between devices, fetch(): lax.ppermute(value, BLK, [(place(*role(*d)), place(*d)) for d in ALL])  18.7 us
    all_to_all x2, starting transfers between devices, everywhere(): return lax.all_to_all(value, axes, 0, 0, tiled=True)  16.3 us
    all_to_all x2, waiting for transfers between devices, everywhere(): return lax.all_to_all(value, axes, 0, 0, tiled=True)  11.5 us
    pallas_call x4, Pallas kernels, call(): pl.pallas_call(kernel, out_shape=[jax.ShapeDtypeStruct(shape, jnp.float32...  7.98 us
  transfers between devices with their start and end apart: 7, of which 6 were waited for; matrix products, arithmetic and copies ran while one was open for 0% of the time, Pallas kernels for 1%

profile of v4, /device:TPU:1, one launch (start us, length us, event | category | flops | bytes accessed | tf_op | source)
XLA Modules:
  0.0 136.1 jit_solution(16263851068110335822)
XLA Ops:
  0.0 0.7 convert_element_type.14
  0.7 1.3 fusion.1.a
  2.0 4.0 %collective-permute-start.1 = (bf16[2064,256]{1,0:T(8,128)(2,1)S(1)}, bf16[2064,256]{1,0:T(8,128)(2,1)S(1)}, u32[]{:S(2)}, u32[]{:S(2)}) collective-permute-start(bf16[2064,256]{1,0:T(8,128)(2,1)S(1)} %fusion.1.a), channel_id=1, source_target_pairs={{8,0},{9,1},{11,2},{10,3},{13,4},{12,5},{15,6},{14,7},{0,8},{1,9},... | collective-permute-start | bytes 3170312 | tf_op jit(solution)/shard_map/ppermute | solution.py:121
  6.0 4.9 %collective-permute-start.2 = (bf16[2064,256]{1,0:T(8,128)(2,1)S(1)}, bf16[2064,256]{1,0:T(8,128)(2,1)S(1)}, u32[]{:S(2)}, u32[]{:S(2)}) collective-permute-start(bf16[2064,256]{1,0:T(8,128)(2,1)S(1)} %fusion.1.a), channel_id=1, source_target_pairs={{2,0},{3,1},{4,2},{5,3},{6,4},{7,5},{0,6},{1,7},{10,8},{11,9},{12,... | collective-permute-start | bytes 3170312 | tf_op jit(solution)/shard_map/ppermute | solution.py:121
  11.0 1.9 %collective-permute-start.3 = (bf16[2064,256]{1,0:T(8,128)(2,1)S(1)}, bf16[2064,256]{1,0:T(8,128)(2,1)S(1)}, u32[]{:S(2)}, u32[]{:S(2)}) collective-permute-start(bf16[2064,256]{1,0:T(8,128)(2,1)S(1)} %fusion.1.a), channel_id=1, source_target_pairs={{6,0},{7,1},{0,2},{1,3},{3,4},{2,5},{5,6},{4,7},{14,8},{15,9},{8,1... | collective-permute-start | bytes 3170312 | tf_op jit(solution)/shard_map/ppermute | solution.py:121
  12.9 5.6 %collective-permute-start = (bf16[2064,256]{1,0:T(8,128)(2,1)S(1)}, bf16[2064,256]{1,0:T(8,128)(2,1)S(1)}, u32[]{:S(2)}, u32[]{:S(2)}) collective-permute-start(bf16[2064,256]{1,0:T(8,128)(2,1)S(1)} %fusion.1.a), channel_id=1, source_target_pairs={{1,0},{0,1},{3,2},{2,3},{5,4},{4,5},{7,6},{6,7},{9,8},{8,9},{11,10... | collective-permute-start | bytes 3170312 | tf_op jit(solution)/shard_map/ppermute | solution.py:121
  18.5 5.6 %collective-permute-done.1.yo = bf16[2064,256]{1,0:T(8,128)(2,1)S(1)} collective-permute-done((bf16[2064,256]{1,0:T(8,128)(2,1)S(1)}, bf16[2064,256]{1,0:T(8,128)(2,1)S(1)}, u32[]{:S(2)}, u32[]{:S(2)}) %collective-permute-start.1) | collective-permute-done | bytes 1056800 | tf_op jit(solution)/shard_map/ppermute | solution.py:121
  24.1 8.0 %collective-permute-done.2.xr = bf16[2064,256]{1,0:T(8,128)(2,1)S(1)} collective-permute-done((bf16[2064,256]{1,0:T(8,128)(2,1)S(1)}, bf16[2064,256]{1,0:T(8,128)(2,1)S(1)}, u32[]{:S(2)}, u32[]{:S(2)}) %collective-permute-start.2) | collective-permute-done | bytes 1056800 | tf_op jit(solution)/shard_map/ppermute | solution.py:121
  32.1 5.0 %collective-permute-done.3.xl = bf16[2064,256]{1,0:T(8,128)(2,1)S(1)} collective-permute-done((bf16[2064,256]{1,0:T(8,128)(2,1)S(1)}, bf16[2064,256]{1,0:T(8,128)(2,1)S(1)}, u32[]{:S(2)}, u32[]{:S(2)}) %collective-permute-start.3) | collective-permute-done | bytes 1056800 | tf_op jit(solution)/shard_map/ppermute | solution.py:121
  37.1 4.5 %shard_map.46 = (f32[8,272,256]{2,1,0:T(8,128)S(1)}, f32[8,128]{1,0:T(8,128)S(1)}) custom-call(bf16[2064,256]{1,0:T(8,128)(2,1)S(1)} %fusion.1.a, bf16[2064,256]{1,0:T(8,128)(2,1)S(1)} %collective-permute-done.b, bf16[2064,256]{1,0:T(8,128)(2,1)S(1)} %collective-permute-done.2.xr, bf16[2064,256]{1,0:T(8,128)(2,1)S(1)} %collective-permute-done.3.xl, ...), custom_call_target="tpu_custom_call" | custom-call | flops 2147483648 | bytes 7516160 | tf_op jit(solution)/shard_map/pallas_call | solution.py:230
  41.7 0.5 slice.9
  42.2 1.9 %multiply_convert_fusion = f16[8,272,256]{2,1,0:T(8,128)(2,1)} fusion(f32[8,272,256]{2,1,0:T(8,128)S(1)} %get-tuple-element.15, f32[]{:T(128)} %bitcast.1), kind=kLoop, calls=%fused_computation | loop fusion | flops 1114112 | bytes 3342340 | tf_op jit(solution)/shard_map/convert_element_type | solution.py:265
  44.1 11.9 %all-to-all-start = ((f16[8,272,256]{2,1,0:T(8,128)(2,1)}), f16[8,272,256]{2,1,0:T(8,128)(2,1)S(1)}, u32[]{:S(2)}, u32[]{:S(2)}) async-start(f16[8,272,256]{2,1,0:T(8,128)(2,1)} %multiply_convert_fusion), calls=%async_computation | async-start | bytes 2228224 | tf_op jit(solution)/shard_map/all_to_all | solution.py:245
  56.0 2.2 %collective-permute-start.4 = (bf16[2064,256]{1,0:T(8,128)(2,1)S(1)}, bf16[2064,256]{1,0:T(8,128)(2,1)S(1)}, u32[]{:S(2)}, u32[]{:S(2)}) collective-permute-start(bf16[2064,256]{1,0:T(8,128)(2,1)S(1)} %collective-permute-done.1.yo), channel_id=1, source_target_pairs={{3,0},{2,1},{5,2},{4,3},{6,4},{7,5},{1,6},{0,7},{10,8},{11,9},{12,... | collective-permute-start | bytes 3170312 | tf_op jit(solution)/shard_map/ppermute | solution.py:121
  58.2 25.2 %collective-permute-done.4.vd = bf16[2064,256]{1,0:T(8,128)(2,1)S(1)} collective-permute-done((bf16[2064,256]{1,0:T(8,128)(2,1)S(1)}, bf16[2064,256]{1,0:T(8,128)(2,1)S(1)}, u32[]{:S(2)}, u32[]{:S(2)}) %collective-permute-start.4) | collective-permute-done | bytes 1056800 | tf_op jit(solution)/shard_map/ppermute | solution.py:121
  83.4 1.3 shard_map.47
  84.7 1.9 %all-to-all-done = f16[8,272,256]{2,1,0:T(8,128)(2,1)S(1)} async-done(((f16[8,272,256]{2,1,0:T(8,128)(2,1)}), f16[8,272,256]{2,1,0:T(8,128)(2,1)S(1)}, u32[]{:S(2)}, u32[]{:S(2)}) %all-to-all-start) | async-done | bytes 1114144 | tf_op jit(solution)/shard_map/all_to_all | solution.py:245
  86.6 4.5 %all-to-all-start.1 = ((f32[8,32,256]{2,1,0:T(8,128)}), f32[8,32,256]{2,1,0:T(8,128)S(1)}, u32[]{:S(2)}, u32[]{:S(2)}) async-start(f32[8,32,256]{2,1,0:T(8,128)} %shard_map.47), calls=%async_computation.1 | async-start | bytes 524288 | tf_op jit(solution)/shard_map/all_to_all | solution.py:245
  91.2 0.3 multiply_reduce_fusion
  91.5 9.6 %all-to-all-done.1 = f32[8,32,256]{2,1,0:T(8,128)S(1)} async-done(((f32[8,32,256]{2,1,0:T(8,128)}), f32[8,32,256]{2,1,0:T(8,128)S(1)}, u32[]{:S(2)}, u32[]{:S(2)}) %all-to-all-start.1) | async-done | bytes 262176 | tf_op jit(solution)/shard_map/all_to_all | solution.py:245
  101.2 14.4 %all_to_all.20.got = f32[4,72,256]{2,1,0:T(8,128)S(1)} all-to-all(f32[4,72,256]{2,1,0:T(8,128)S(1)} %pad_maximum_fusion), channel_id=1, replica_groups=mesh['z'=8,'h'=4,'l'=2,'x'=4,'c'=2] {'h'}, dimensions={0} | all-to-all | bytes 589824 | tf_op jit(solution)/shard_map/all_to_all | solution.py:245
  115.6 0.7 shard_map.48
  116.3 18.3 %all_to_all.21.got = f32[64,8,256]{2,1,0:T(8,128)S(1)} all-to-all(f32[64,8,256]{2,1,0:T(8,128)S(1)} %shard_map.48), channel_id=1, replica_groups=mesh['z'=8,'h'=4,'l'=2,'x'=4,'c'=2] {'l','x','c'}, dimensions={0} | all-to-all | bytes 1048576 | tf_op jit(solution)/shard_map/all_to_all | solution.py:245
  134.6 1.5 %shard_map.49 = f32[9,8,256]{2,1,0:T(8,128)} custom-call(s32[16,16]{1,0:T(8,128)S(1)} %copy-done, s32[1,9]{1,0:T(1,128)S(1)} %copy-done.2, f32[64,8,256]{2,1,0:T(8,128)S(1)} %all_to_all.21.got), custom_call_target="tpu_custom_call" | custom-call | bytes 599076 | tf_op jit(solution)/shard_map/pallas_call | solution.py:230
  (10 shorter events, 0.2 us)
Async XLA Ops:
  2.0 22.2 %collective-permute-start.1 = (bf16[2064,256]{1,0:T(8,128)(2,1)S(1)}, bf16[2064,256]{1,0:T(8,128)(2,1)S(1)}, u32[]{:S(2)}, u32[]{:S(2)}) collective-permute-start(bf16[2064,256]{1,0:T(8,128)(2,1)S(1)} %fusion.1.a), channel_id=1, source_target_pairs={{8,0},{9,1},{11,2},{10,3},{13,4},{12,5},{15,6},{14,7},{0,8},{1,9},... | collective-permute-start | bytes 3170312 | tf_op jit(solution)/shard_map/ppermute | solution.py:121
  6.0 26.1 %collective-permute-start.2 = (bf16[2064,256]{1,0:T(8,128)(2,1)S(1)}, bf16[2064,256]{1,0:T(8,128)(2,1)S(1)}, u32[]{:S(2)}, u32[]{:S(2)}) collective-permute-start(bf16[2064,256]{1,0:T(8,128)(2,1)S(1)} %fusion.1.a), channel_id=1, source_target_pairs={{2,0},{3,1},{4,2},{5,3},{6,4},{7,5},{0,6},{1,7},{10,8},{11,9},{12,... | collective-permute-start | bytes 3170312 | tf_op jit(solution)/shard_map/ppermute | solution.py:121
  11.0 26.2 %collective-permute-start.3 = (bf16[2064,256]{1,0:T(8,128)(2,1)S(1)}, bf16[2064,256]{1,0:T(8,128)(2,1)S(1)}, u32[]{:S(2)}, u32[]{:S(2)}) collective-permute-start(bf16[2064,256]{1,0:T(8,128)(2,1)S(1)} %fusion.1.a), channel_id=1, source_target_pairs={{6,0},{7,1},{0,2},{1,3},{3,4},{2,5},{5,6},{4,7},{14,8},{15,9},{8,1... | collective-permute-start | bytes 3170312 | tf_op jit(solution)/shard_map/ppermute | solution.py:121
  12.9 24.3 %collective-permute-start = (bf16[2064,256]{1,0:T(8,128)(2,1)S(1)}, bf16[2064,256]{1,0:T(8,128)(2,1)S(1)}, u32[]{:S(2)}, u32[]{:S(2)}) collective-permute-start(bf16[2064,256]{1,0:T(8,128)(2,1)S(1)} %fusion.1.a), channel_id=1, source_target_pairs={{1,0},{0,1},{3,2},{2,3},{5,4},{4,5},{7,6},{6,7},{9,8},{8,9},{11,10... | collective-permute-start | bytes 3170312 | tf_op jit(solution)/shard_map/ppermute | solution.py:121
  44.1 42.5 %all-to-all-start = ((f16[8,272,256]{2,1,0:T(8,128)(2,1)}), f16[8,272,256]{2,1,0:T(8,128)(2,1)S(1)}, u32[]{:S(2)}, u32[]{:S(2)}) async-start(f16[8,272,256]{2,1,0:T(8,128)(2,1)} %multiply_convert_fusion), calls=%async_computation | async-start | bytes 2228224 | tf_op jit(solution)/shard_map/all_to_all | solution.py:245
  56.0 27.4 %collective-permute-start.4 = (bf16[2064,256]{1,0:T(8,128)(2,1)S(1)}, bf16[2064,256]{1,0:T(8,128)(2,1)S(1)}, u32[]{:S(2)}, u32[]{:S(2)}) collective-permute-start(bf16[2064,256]{1,0:T(8,128)(2,1)S(1)} %collective-permute-done.1.yo), channel_id=1, source_target_pairs={{3,0},{2,1},{5,2},{4,3},{6,4},{7,5},{1,6},{0,7},{10,8},{11,9},{12,... | collective-permute-start | bytes 3170312 | tf_op jit(solution)/shard_map/ppermute | solution.py:121
  86.6 14.6 %all-to-all-start.1 = ((f32[8,32,256]{2,1,0:T(8,128)}), f32[8,32,256]{2,1,0:T(8,128)S(1)}, u32[]{:S(2)}, u32[]{:S(2)}) async-start(f32[8,32,256]{2,1,0:T(8,128)} %shard_map.47), calls=%async_computation.1 | async-start | bytes 524288 | tf_op jit(solution)/shard_map/all_to_all | solution.py:245
  91.2 24.4 %copy-start.1 = (s32[16,16]{1,0:T(8,128)S(1)}, s32[16,16]{1,0:T(8,128)}, u32[]{:S(2)}) copy-start(s32[16,16]{1,0:T(8,128)} %constant.19.clone.stamp) | copy-start | bytes 3076
  101.2 33.4 %copy-start = (s32[16,16]{1,0:T(8,128)S(1)}, s32[16,16]{1,0:T(8,128)}, u32[]{:S(2)}) copy-start(s32[16,16]{1,0:T(8,128)} %constant.20.clone.table) | copy-start | bytes 3076
  101.2 33.4 %copy-start.2 = (s32[1,9]{1,0:T(1,128)S(1)}, s32[1,9]{1,0:T(1,128)}, u32[]{:S(2)}) copy-start(s32[1,9]{1,0:T(1,128)} %cols.1) | copy-start | bytes 112

commit v5 on v3

--- a/solution.py
+++ b/solution.py
@@ -9,14 +9,15 @@
 
 Z, H, L, X, C = 8, 4, 2, 4, 2
 BLK = ("l", "x", "c")
+N_BLK, N_BULK = L * X * C, Z * H
 BULK = ("z", "h")
-N_BLK, N_BULK = L * X * C, Z * H
 SLOTS = 9
 W = 256
 K = 2048
+HALF = K // 2
 SLAB = W // N_BULK
-EARLY = 8
 DEPTH = 4
+MARK, TOP = 16, 14.0
 
 
 def place(l, x, c):
@@ -36,31 +37,15 @@
 
 
 def left(l, x, c):
-    return (l, (x + 3) & 3, c ^ (x >> 1))
-
-
-def flip(x):
-    return (x + 3) >> 2
-
-
-def over(l, x, c):
-    return (1 - l, x, c ^ flip(x))
+    return (l, (x + 3) & 3, c ^ l ^ (x >> 1))
 
 
 def diag(l, x, c):
-    return (1 - l, (x + 1) & 3, c ^ (x >> 1) ^ l)
+    return (1 - l, (x + 1) & 3, c ^ l)
 
 
 def diag_via(l, x, c):
-    return (l, (x + 1) & 3, c ^ (x >> 1) ^ l ^ flip((x + 1) & 3))
-
-
-def mate_bit(l, x):
-    return flip(x) ^ l
-
-
-def mate(l, x, c):
-    return (l, x, c ^ mate_bit(l, x))
+    return (1 - l, x, c ^ l)
 
 
 ALL = [(l, x, c) for l in range(L) for x in range(X) for c in range(C)]
@@ -69,12 +54,13 @@
     (own, sib),
     (right, own),
     (right, sib),
-    (right, over),
     (right, left),
-    (over, left),
-    (over, mate),
-    (left, diag),
+    (diag, right),
+    (diag, own),
+    (diag, sib),
+    (diag, left),
 ]
+GROUPS = (5, 4)
 
 
 def mailing(l, x, c):
@@ -130,63 +116,80 @@
     )
 
 
+def product(p, q):
+    return dot(p[0][:HALF], q[0][:HALF]) + dot(p[1][...], q[1][...])
+
+
 def owns(carrier, block):
-    row = carrier[K:].astype(jnp.float32)
+    row = carrier[0][HALF:].astype(jnp.float32)
     return jnp.max(jnp.where(row == block.astype(jnp.float32), 1.0, 0.0)) > 0.5
 
 
+def writer(out, slot, count):
+    def put(tile):
+        tile = tile.reshape(Z, H, SLAB, W)
+        for h in range(H):
+            out[:, pl.ds((h * count + slot) * SLAB, SLAB)] = tile[:, h]
+
+    return put
+
+
 def settle(carrier, rhs, block, put):
-    tile = dot(carrier[:K], rhs)
     kept = owns(carrier, place(*block))
 
     @pl.when(kept)
     def _():
-        put(tile)
+        put(product(carrier, rhs))
 
     @pl.when(jnp.logical_not(kept))
     def _():
-        put(tile.T)
-
-
-def early_kernel(a, b, xr, xl, yo, out):
+        put(product(rhs, carrier))
+
+
+def squeeze(out):
+    data = out.shape[1] - MARK
+    most = jnp.zeros((1, W), jnp.float32)
+    for z in range(Z):
+        peak = jnp.max(jnp.abs(out[z, :data]), axis=0, keepdims=True)
+        most = jnp.maximum(most, peak)
+    most = jnp.maximum(jnp.max(most, axis=1, keepdims=True), 1e-30)
+    power = jnp.ceil(jnp.log2(jnp.broadcast_to(most, (SLAB, W))))
+    spread = 1.0 + lax.axis_index("z").astype(jnp.float32) / Z
+    by = (jnp.exp2(TOP - power) * spread)[:1]
+    for z in range(Z):
+        out[z, :data] = out[z, :data] * by
+        out[z, data:] = jnp.broadcast_to(power[:1], (MARK, W))
+
+
+def early_kernel(a, b, w, x1, x2, out):
+    a, b, w = ((r.at[0], r.at[1]) for r in (a, b, w))
     me = position()
-
-    def put(slot):
-        def write(tile):
-            out[:, pl.ds(slot * SLAB, SLAB)] = tile.reshape(N_BULK, SLAB, W)
-
-        return write
-
-    put(0)(dot(a[:K], a[:K]))
-    put(1)(dot(a[:K], b[:K]))
-    settle(xr, a[:K], own(*me), put(2))
-    settle(xr, b[:K], sib(*me), put(3))
-    settle(xr, yo[:K], over(*me), put(4))
-    settle(xr, xl[:K], left(*me), put(5))
-    settle(yo, xl[:K], left(*me), put(6))
-    mine = mate_bit(*me[:2]) == 0
-
-    @pl.when(mine)
-    def _():
-        settle(yo, a[:K], mate(*me), put(7))
-
-    @pl.when(jnp.logical_not(mine))
-    def _():
-        settle(yo, b[:K], mate(*me), put(7))
-
-
-def late_kernel(xl, vd, out):
-    def put(tile):
-        out[...] = tile.reshape(N_BULK, SLAB, W)
-
-    settle(xl, vd[:K], diag(*position()), put)
-
-
-def pack_kernel(stamp, e, v, out):
+    x = (x1, x2)
+    writer(out, 0, 5)(product(a, a))
+    writer(out, 1, 5)(product(a, b))
+    settle(x, a, own(*me), writer(out, 2, 5))
+    settle(x, b, sib(*me), writer(out, 3, 5))
+    settle(x, w, left(*me), writer(out, 4, 5))
+    squeeze(out)
+
+
+def late_kernel(a, b, w, x1, x2, v1, v2, out):
+    a, b, w = ((r.at[0], r.at[1]) for r in (a, b, w))
+    me = position()
+    x, v = (x1, x2), (v1, v2)
+    settle(v, x, right(*me), writer(out, 0, 4))
+    settle(v, a, own(*me), writer(out, 1, 4))
+    settle(v, b, sib(*me), writer(out, 2, 4))
+    settle(v, w, left(*me), writer(out, 3, 4))
+    squeeze(out)
+
+
+def pack_kernel(stamp, got, out):
     me = place(*position())
     k = 0
     for t in range(SLOTS):
-        tile = e[pl.ds(t * SLAB, SLAB)] if t < EARLY else v[...]
+        rows = pl.ds(t * SLAB, SLAB)
+        tile = got[0, rows] + got[1, rows] + got[2, rows] + got[3, rows]
         for _ in range(1 if t < 2 else 2):
             out[stamp[me, k]] = tile
             k += 1
@@ -217,16 +220,28 @@
         compiler_params=pltpu.CompilerParams(vmem_limit_bytes=40 * 2**20),
         cost_estimate=pl.CostEstimate(
             flops=n_tiles * 2 * W * W * K,
-            bytes_accessed=sum(v.size * v.dtype.itemsize for v in ins)
-            + 4 * int(np.prod(shape)),
+            bytes_accessed=4 * int(np.prod(shape))
+            + sum(v.size * v.dtype.itemsize for v in ins),
             transcendentals=0,
         ),
     )(*ins)
 
 
-def exchange(parts):
-    got = lax.all_to_all(parts, BULK, 0, 0, tiled=True)
-    return got.sum(0)
+def everywhere(value, axes):
+    return lax.all_to_all(value, axes, 0, 0, tiled=True)
+
+
+def tiles(kernel, count, *ins):
+    shape = (Z, count * W // Z + MARK, W)
+    return call(kernel, shape, 0, count, *ins).astype(jnp.float16)
+
+
+def total(got):
+    data = got.shape[1] - MARK
+    power = got[:, data : data + 1, :1].astype(jnp.float32)
+    spread = 1.0 + lax.broadcasted_iota(jnp.float32, (Z, 1, 1), 0) / Z
+    got = got[:, :data].astype(jnp.float32) * (jnp.exp2(power - TOP) / spread)
+    return got.sum(0).reshape(H, data // H, W)
 
 
 def local(aux_factors, tile_cols):
@@ -235,30 +250,29 @@
         ((0, 15), (0, W - SLOTS)),
         constant_values=-2,
     )
-    a = jnp.concatenate([aux_factors.reshape(K, W), row])
-    yo = fetch(a, over)
-    xr = fetch(a, right)
-    xl = fetch(a, left)
+    a1, a2, a = lax.optimization_barrier(
+        (jnp.concatenate([aux_factors[0], row]), aux_factors[1], aux_factors)
+    )
+    x1 = fetch(a1, right)
+    w = fetch(a, left)
+    x2 = fetch(a2, right)
     b = fetch(a, sib)
-    vd = fetch(yo, diag_via)
-
-    early = call(early_kernel, (N_BULK, EARLY * SLAB, W), 0, EARLY, a, b, xr, xl, yo)
-    late = call(late_kernel, (N_BULK, SLAB, W), 0, 1, xl, vd)
-    early, late = exchange(early), exchange(late)
-
-    mail = call(
-        pack_kernel, (N_BLK * DEPTH, SLAB, W), 1, 0, jnp.asarray(stamps()), early, late
-    )
-    mail = lax.all_to_all(mail, BLK, 0, 0, tiled=True)
-    return call(
-        pick_kernel,
-        (SLOTS, SLAB, W),
-        2,
-        0,
-        jnp.asarray(addresses()),
-        tile_cols,
-        mail,
-    )
+    v1 = fetch(x1, diag_via)
+    v2 = fetch(x2, diag_via)
+
+    x1, v1 = lax.optimization_barrier((x1, v1))
+    early = tiles(early_kernel, GROUPS[0], a, b, w, x1, x2)
+    early = everywhere(early, "z")
+    late = tiles(late_kernel, GROUPS[1], a, b, w, x1, x2, v1, v2)
+    early, late = lax.optimization_barrier((early, late))
+    late = everywhere(late, "z")
+
+    parts = jnp.concatenate([total(early), total(late)], 1)
+    parts = everywhere(parts, "h")
+    mail = call(pack_kernel, (N_BLK * DEPTH, SLAB, W), 1, 0, jnp.asarray(stamps()), parts)
+    mail = everywhere(mail, BLK)
+    table = jnp.asarray(addresses())
+    return call(pick_kernel, (SLOTS, SLAB, W), 2, 0, table, tile_cols, mail)
 
 
 def solution(mesh):

time: 190 us -> 137 us (0.72)
  the two profiles are of different devices: /device:TPU:80 before, /device:TPU:1 now
where the time goes in v5:
time: 137 us
  starting transfers between devices  43 us (31%)
  waiting for transfers between devices  41.1 us (30%)
  blocking collectives  34.9 us (25%)
  Pallas kernels  7.55 us (6%)
  local copies, waits for them, and re-layouts  5.32 us (4%)
  other arithmetic  4.5 us (3%)
    all_to_all x2, blocking collectives, everywhere(): return lax.all_to_all(value, axes, 0, 0, tiled=True)  34.9 us
    ppermute x6, starting transfers between devices, fetch(): lax.ppermute(value, BLK, [(place(*role(*d)), place(*d)) for d in ALL])  28.2 us
    ppermute x6, waiting for transfers between devices, fetch(): lax.ppermute(value, BLK, [(place(*role(*d)), place(*d)) for d in ALL])  25.1 us
    all_to_all x2, waiting for transfers between devices, everywhere(): return lax.all_to_all(value, axes, 0, 0, tiled=True)  16 us
    all_to_all x2, starting transfers between devices, everywhere(): return lax.all_to_all(value, axes, 0, 0, tiled=True)  14.8 us
    pallas_call x4, Pallas kernels, call(): pl.pallas_call(kernel, out_shape=jax.ShapeDtypeStruct(shape, jnp.float32)...  7.55 us
    unnamed x20, local copies, waits for them, and re-layouts  3.96 us
  transfers between devices with their start and end apart: 8, of which 5 were waited for; matrix products, arithmetic and copies ran while one was open for 2% of the time, Pallas kernels for 2%

profile of v5, /device:TPU:1, one launch (start us, length us, event | category | flops | bytes accessed | tf_op | source)
XLA Modules:
  0.0 136.6 jit_solution(7934902055981235360)
XLA Ops:
  0.0 1.4 %slice_bitcast_fusion = (bf16[1024,256]{1,0:T(8,128)(2,1)S(1)}, bf16[1024,256]{1,0:T(8,128)(2,1)S(1)}) fusion(bf16[2,1024,256]{2,1,0:T(8,128)(2,1)} %a.1), kind=kLoop, calls=%fused_computation.5 | loop fusion | bytes 2097152 | tf_op jit(solution)/shard_map/squeeze | solution.py:254
  1.4 5.2 %collective-permute-start.2 = (bf16[1040,256]{1,0:T(8,128)(2,1)S(1)}, bf16[1040,256]{1,0:T(8,128)(2,1)S(1)}, u32[]{:S(2)}, u32[]{:S(2)}) collective-permute-start(bf16[1040,256]{1,0:T(8,128)(2,1)S(1)} %fusion.1), channel_id=1, source_target_pairs={{2,0},{3,1},{4,2},{5,3},{6,4},{7,5},{0,6},{1,7},{10,8},{11,9},{12,... | collective-permute-start | bytes 1597448 | tf_op jit(solution)/shard_map/ppermute | solution.py:106
  6.7 5.5 %collective-permute-start = (bf16[2,1024,256]{2,1,0:T(8,128)(2,1)S(1)}, bf16[2,1024,256]{2,1,0:T(8,128)(2,1)S(1)}, u32[]{:S(2)}, u32[]{:S(2)}) collective-permute-start(bf16[2,1024,256]{2,1,0:T(8,128)(2,1)S(1)} %copy-done), channel_id=1, source_target_pairs={{1,0},{0,1},{3,2},{2,3},{5,4},{4,5},{7,6},{6,7},{9,8},{8,9},{11,10... | collective-permute-start | bytes 3145736 | tf_op jit(solution)/shard_map/ppermute | solution.py:106
  12.2 3.6 %collective-permute-start.1 = (bf16[2,1024,256]{2,1,0:T(8,128)(2,1)S(1)}, bf16[2,1024,256]{2,1,0:T(8,128)(2,1)S(1)}, u32[]{:S(2)}, u32[]{:S(2)}) collective-permute-start(bf16[2,1024,256]{2,1,0:T(8,128)(2,1)S(1)} %copy-done), channel_id=1, source_target_pairs={{6,0},{7,1},{0,2},{1,3},{3,4},{2,5},{5,6},{4,7},{15,8},{14,9},{9,1... | collective-permute-start | bytes 3145736 | tf_op jit(solution)/shard_map/ppermute | solution.py:106
  15.8 6.2 %collective-permute-start.3 = (bf16[1040,256]{1,0:T(8,128)(2,1)S(1)}, bf16[1040,256]{1,0:T(8,128)(2,1)S(1)}, u32[]{:S(2)}, u32[]{:S(2)}) collective-permute-start(bf16[1040,256]{1,0:T(8,128)(2,1)S(1)} %collective-permute-done.2.x1), channel_id=1, source_target_pairs={{8,0},{9,1},{10,2},{11,3},{12,4},{13,5},{14,6},{15,7},{1,8},{0,9},... | collective-permute-start | bytes 1597448 | tf_op jit(solution)/shard_map/ppermute | solution.py:106
  22.0 5.3 %collective-permute-start.4 = (bf16[1024,256]{1,0:T(8,128)(2,1)S(1)}, bf16[1024,256]{1,0:T(8,128)(2,1)S(1)}, u32[]{:S(2)}, u32[]{:S(2)}) collective-permute-start(bf16[1024,256]{1,0:T(8,128)(2,1)S(1)} %get-tuple-element.15), channel_id=1, source_target_pairs={{2,0},{3,1},{4,2},{5,3},{6,4},{7,5},{0,6},{1,7},{10,8},{11,9},{12,... | collective-permute-start | bytes 1572872 | tf_op jit(solution)/shard_map/ppermute | solution.py:106
  27.4 6.1 %collective-permute-done.3.v1 = bf16[1040,256]{1,0:T(8,128)(2,1)S(1)} collective-permute-done((bf16[1040,256]{1,0:T(8,128)(2,1)S(1)}, bf16[1040,256]{1,0:T(8,128)(2,1)S(1)}, u32[]{:S(2)}, u32[]{:S(2)}) %collective-permute-start.3) | collective-permute-done | bytes 532512 | tf_op jit(solution)/shard_map/ppermute | solution.py:106
  34.3 4.2 %collective-permute-done.4.x2 = bf16[1024,256]{1,0:T(8,128)(2,1)S(1)} collective-permute-done((bf16[1024,256]{1,0:T(8,128)(2,1)S(1)}, bf16[1024,256]{1,0:T(8,128)(2,1)S(1)}, u32[]{:S(2)}, u32[]{:S(2)}) %collective-permute-start.4) | collective-permute-done | bytes 524320 | tf_op jit(solution)/shard_map/ppermute | solution.py:106
  38.5 1.5 %collective-permute-done.1.w = bf16[2,1024,256]{2,1,0:T(8,128)(2,1)S(1)} collective-permute-done((bf16[2,1024,256]{2,1,0:T(8,128)(2,1)S(1)}, bf16[2,1024,256]{2,1,0:T(8,128)(2,1)S(1)}, u32[]{:S(2)}, u32[]{:S(2)}) %collective-permute-start.1) | collective-permute-done | bytes 1048608 | tf_op jit(solution)/shard_map/ppermute | solution.py:106
  40.1 2.7 %shard_map.46 = f32[8,176,256]{2,1,0:T(8,128)S(1)} custom-call(bf16[2,1024,256]{2,1,0:T(8,128)(2,1)S(1)} %copy-done, bf16[2,1024,256]{2,1,0:T(8,128)(2,1)S(1)} %collective-permute-done.b, bf16[2,1024,256]{2,1,0:T(8,128)(2,1)S(1)} %collective-permute-done.1.w, bf16[1040,256]{1,0:T(8,128)(2,1)S(1)} %collective-permute-done.2.x1, ...), custom_call_target="tpu_custom_call" | custom-call | flops 1342177280 | bytes 5644288 | tf_op jit(solution)/shard_map/pallas_call | solution.py:215
  42.8 1.0 convert_element_type.24
  43.8 8.5 %all-to-all-start = ((f16[8,176,256]{2,1,0:T(8,128)(2,1)}), f16[8,176,256]{2,1,0:T(8,128)(2,1)}, u32[]{:S(2)}, u32[]{:S(2)}) async-start(f16[8,176,256]{2,1,0:T(8,128)(2,1)} %convert_element_type.24), calls=%async_computation | async-start | bytes 1441792 | tf_op jit(solution)/shard_map/all_to_all | solution.py:231
  52.3 2.3 %collective-permute-start.5 = (bf16[1024,256]{1,0:T(8,128)(2,1)}, bf16[1024,256]{1,0:T(8,128)(2,1)S(1)}, u32[]{:S(2)}, u32[]{:S(2)}) collective-permute-start(bf16[1024,256]{1,0:T(8,128)(2,1)} %copy-done.3), channel_id=1, source_target_pairs={{8,0},{9,1},{10,2},{11,3},{12,4},{13,5},{14,6},{15,7},{1,8},{0,9},... | collective-permute-start | bytes 1572872 | tf_op jit(solution)/shard_map/ppermute | solution.py:106
  54.7 13.2 %collective-permute-done.5.v2 = bf16[1024,256]{1,0:T(8,128)(2,1)S(1)} collective-permute-done((bf16[1024,256]{1,0:T(8,128)(2,1)}, bf16[1024,256]{1,0:T(8,128)(2,1)S(1)}, u32[]{:S(2)}, u32[]{:S(2)}) %collective-permute-start.5) | collective-permute-done | bytes 524320 | tf_op jit(solution)/shard_map/ppermute | solution.py:106
  67.9 1.0 copy-done.2
  68.9 1.0 copy-done.4
  70.0 1.0 copy-done.6
  71.0 2.7 %shard_map.47 = f32[8,144,256]{2,1,0:T(8,128)S(1)} custom-call(bf16[2,1024,256]{2,1,0:T(8,128)(2,1)S(1)} %copy-done, bf16[2,1024,256]{2,1,0:T(8,128)(2,1)S(1)} %collective-permute-done.b, bf16[2,1024,256]{2,1,0:T(8,128)(2,1)S(1)} %collective-permute-done.1.w, bf16[1040,256]{1,0:T(8,128)(2,1)S(1)} %copy-done.2, bf16[1024,256]{1,0:T(8,128)(2,1)S(1)} %copy-done.4, ...), custom_call_target="tpu_custom_call" | custom-call | flops 1073741824 | bytes 6438912 | tf_op jit(solution)/shard_map/pallas_call | solution.py:215
  74.6 6.3 %all-to-all-start.1 = ((f16[8,144,256]{2,1,0:T(8,128)(2,1)}), f16[8,144,256]{2,1,0:T(8,128)(2,1)S(1)}, u32[]{:S(2)}, u32[]{:S(2)}) async-start(f16[8,144,256]{2,1,0:T(8,128)(2,1)} %convert_element_type.25), calls=%async_computation.1 | async-start | bytes 1179648 | tf_op jit(solution)/shard_map/all_to_all | solution.py:231
  81.8 1.3 multiply_reduce_fusion
  83.1 16.0 %all-to-all-done.1 = f16[8,144,256]{2,1,0:T(8,128)(2,1)S(1)} async-done(((f16[8,144,256]{2,1,0:T(8,128)(2,1)}), f16[8,144,256]{2,1,0:T(8,128)(2,1)S(1)}, u32[]{:S(2)}, u32[]{:S(2)}) %all-to-all-start.1) | async-done | bytes 589856 | tf_op jit(solution)/shard_map/all_to_all | solution.py:231
  99.5 13.1 %all_to_all.20.got = f32[4,72,256]{2,1,0:T(8,128)S(1)} all-to-all(f32[4,72,256]{2,1,0:T(8,128)S(1)} %pad_maximum_fusion), channel_id=1, replica_groups=mesh['z'=8,'h'=4,'l'=2,'x'=4,'c'=2] {'h'}, dimensions={0} | all-to-all | bytes 589824 | tf_op jit(solution)/shard_map/all_to_all | solution.py:231
  113.3 21.8 %all_to_all.21.got = f32[64,8,256]{2,1,0:T(8,128)S(1)} all-to-all(f32[64,8,256]{2,1,0:T(8,128)S(1)} %shard_map.48), channel_id=1, replica_groups=mesh['z'=8,'h'=4,'l'=2,'x'=4,'c'=2] {'l','x','c'}, dimensions={0} | all-to-all | bytes 1048576 | tf_op jit(solution)/shard_map/all_to_all | solution.py:231
  135.1 1.5 %shard_map.49 = f32[9,8,256]{2,1,0:T(8,128)} custom-call(s32[16,16]{1,0:T(8,128)S(1)} %copy-done.7, s32[1,9]{1,0:T(1,128)S(1)} %copy-done.9, f32[64,8,256]{2,1,0:T(8,128)S(1)} %all_to_all.21.got), custom_call_target="tpu_custom_call" | custom-call | bytes 599076 | tf_op jit(solution)/shard_map/pallas_call | solution.py:215
  (28 shorter events, 3.7 us)
Async XLA Ops:
  0.0 6.7 %copy-start = (bf16[2,1024,256]{2,1,0:T(8,128)(2,1)S(1)}, bf16[2,1024,256]{2,1,0:T(8,128)(2,1)}, u32[]{:S(2)}) copy-start(bf16[2,1024,256]{2,1,0:T(8,128)(2,1)} %a.1) | copy-start | bytes 3145732
  0.0 1.4 %copy-start.9 = (s32[1,9]{1,0:T(1,128)S(1)}, s32[1,9]{1,0:T(1,128)}, u32[]{:S(2)}) copy-start(s32[1,9]{1,0:T(1,128)} %cols.1) | copy-start | bytes 112
  1.4 14.4 %collective-permute-start.2 = (bf16[1040,256]{1,0:T(8,128)(2,1)S(1)}, bf16[1040,256]{1,0:T(8,128)(2,1)S(1)}, u32[]{:S(2)}, u32[]{:S(2)}) collective-permute-start(bf16[1040,256]{1,0:T(8,128)(2,1)S(1)} %fusion.1), channel_id=1, source_target_pairs={{2,0},{3,1},{4,2},{5,3},{6,4},{7,5},{0,6},{1,7},{10,8},{11,9},{12,... | collective-permute-start | bytes 1597448 | tf_op jit(solution)/shard_map/ppermute | solution.py:106
  6.7 31.8 %collective-permute-start = (bf16[2,1024,256]{2,1,0:T(8,128)(2,1)S(1)}, bf16[2,1024,256]{2,1,0:T(8,128)(2,1)S(1)}, u32[]{:S(2)}, u32[]{:S(2)}) collective-permute-start(bf16[2,1024,256]{2,1,0:T(8,128)(2,1)S(1)} %copy-done), channel_id=1, source_target_pairs={{1,0},{0,1},{3,2},{2,3},{5,4},{4,5},{7,6},{6,7},{9,8},{8,9},{11,10... | collective-permute-start | bytes 3145736 | tf_op jit(solution)/shard_map/ppermute | solution.py:106
  12.2 27.9 %collective-permute-start.1 = (bf16[2,1024,256]{2,1,0:T(8,128)(2,1)S(1)}, bf16[2,1024,256]{2,1,0:T(8,128)(2,1)S(1)}, u32[]{:S(2)}, u32[]{:S(2)}) collective-permute-start(bf16[2,1024,256]{2,1,0:T(8,128)(2,1)S(1)} %copy-done), channel_id=1, source_target_pairs={{6,0},{7,1},{0,2},{1,3},{3,4},{2,5},{5,6},{4,7},{15,8},{14,9},{9,1... | collective-permute-start | bytes 3145736 | tf_op jit(solution)/shard_map/ppermute | solution.py:106
  15.8 26.9 %copy-start.1 = (bf16[1040,256]{1,0:T(8,128)(2,1)}, bf16[1040,256]{1,0:T(8,128)(2,1)S(1)}, u32[]{:S(2)}) copy-start(bf16[1040,256]{1,0:T(8,128)(2,1)S(1)} %collective-permute-done.2.x1) | copy-start | bytes 1597444
  15.8 17.6 %collective-permute-start.3 = (bf16[1040,256]{1,0:T(8,128)(2,1)S(1)}, bf16[1040,256]{1,0:T(8,128)(2,1)S(1)}, u32[]{:S(2)}, u32[]{:S(2)}) collective-permute-start(bf16[1040,256]{1,0:T(8,128)(2,1)S(1)} %collective-permute-done.2.x1), channel_id=1, source_target_pairs={{8,0},{9,1},{10,2},{11,3},{12,4},{13,5},{14,6},{15,7},{1,8},{0,9},... | collective-permute-start | bytes 1597448 | tf_op jit(solution)/shard_map/ppermute | solution.py:106
  22.0 16.5 %collective-permute-start.4 = (bf16[1024,256]{1,0:T(8,128)(2,1)S(1)}, bf16[1024,256]{1,0:T(8,128)(2,1)S(1)}, u32[]{:S(2)}, u32[]{:S(2)}) collective-permute-start(bf16[1024,256]{1,0:T(8,128)(2,1)S(1)} %get-tuple-element.15), channel_id=1, source_target_pairs={{2,0},{3,1},{4,2},{5,3},{6,4},{7,5},{0,6},{1,7},{10,8},{11,9},{12,... | collective-permute-start | bytes 1572872 | tf_op jit(solution)/shard_map/ppermute | solution.py:106
  33.5 0.8 copy-start.5
  38.5 4.3 %copy-start.3 = (bf16[1024,256]{1,0:T(8,128)(2,1)}, bf16[1024,256]{1,0:T(8,128)(2,1)S(1)}, u32[]{:S(2)}) copy-start(bf16[1024,256]{1,0:T(8,128)(2,1)S(1)} %collective-permute-done.4.x2) | copy-start | bytes 1572868
  43.8 30.8 %all-to-all-start = ((f16[8,176,256]{2,1,0:T(8,128)(2,1)}), f16[8,176,256]{2,1,0:T(8,128)(2,1)}, u32[]{:S(2)}, u32[]{:S(2)}) async-start(f16[8,176,256]{2,1,0:T(8,128)(2,1)} %convert_element_type.24), calls=%async_computation | async-start | bytes 1441792 | tf_op jit(solution)/shard_map/all_to_all | solution.py:231
  52.3 15.6 %collective-permute-start.5 = (bf16[1024,256]{1,0:T(8,128)(2,1)}, bf16[1024,256]{1,0:T(8,128)(2,1)S(1)}, u32[]{:S(2)}, u32[]{:S(2)}) collective-permute-start(bf16[1024,256]{1,0:T(8,128)(2,1)} %copy-done.3), channel_id=1, source_target_pairs={{8,0},{9,1},{10,2},{11,3},{12,4},{13,5},{14,6},{15,7},{1,8},{0,9},... | collective-permute-start | bytes 1572872 | tf_op jit(solution)/shard_map/ppermute | solution.py:106
  67.9 1.0 copy-start.2
  68.9 1.0 copy-start.4
  70.0 1.0 copy-start.6
  74.6 24.5 %all-to-all-start.1 = ((f16[8,144,256]{2,1,0:T(8,128)(2,1)}), f16[8,144,256]{2,1,0:T(8,128)(2,1)S(1)}, u32[]{:S(2)}, u32[]{:S(2)}) async-start(f16[8,144,256]{2,1,0:T(8,128)(2,1)} %convert_element_type.25), calls=%async_computation.1 | async-start | bytes 1179648 | tf_op jit(solution)/shard_map/all_to_all | solution.py:231
  81.8 30.8 %copy-start.8 = (s32[16,16]{1,0:T(8,128)S(1)}, s32[16,16]{1,0:T(8,128)}, u32[]{:S(2)}) copy-start(s32[16,16]{1,0:T(8,128)} %constant.20.clone.stamp) | copy-start | bytes 3076
  99.5 35.6 %copy-start.7 = (s32[16,16]{1,0:T(8,128)S(1)}, s32[16,16]{1,0:T(8,128)}, u32[]{:S(2)}) copy-start(s32[16,16]{1,0:T(8,128)} %constant.21.clone.table) | copy-start | bytes 3076

commit v6 on v5

v6 whole, which is shorter than its diff:
```python
import jax
import jax.numpy as jnp
import numpy as np
from jax import lax
from jax.experimental import pallas as pl
from jax.experimental.pallas import tpu as pltpu
from jax.sharding import Mesh
from jax.sharding import PartitionSpec as P

Z, H, L, X, C = 8, 4, 2, 4, 2
BLK = ("l", "x", "c")
N_BLK, N_BULK = L * X * C, Z * H
BULK = ("z", "h")
SLOTS = 9
W = 256
K = 2048
PARTS = (768, 768, 512)
STARTS = (0, 768, 1536)
SLAB = W // N_BULK
DEPTH = 4
TOP = 14.0


def place(l, x, c):
    return (l * X + x) * C + c


def own(l, x, c):
    return (l, x, c)


def sib(l, x, c):
    return (l, x, 1 - c)


def right(l, x, c):
    return (l, (x + 1) & 3, c)


def left(l, x, c):
    return (l, (x + 3) & 3, c ^ l ^ (x >> 1))


def diag(l, x, c):
    return (1 - l, (x + 1) & 3, c ^ l)


def diag_via(l, x, c):
    return (1 - l, x, c ^ l)


ALL = [(l, x, c) for l in range(L) for x in range(X) for c in range(C)]
TILES = [
    (own, own),
    (own, sib),
    (right, own),
    (right, sib),
    (right, left),
    (diag, right),
    (diag, own),
    (diag, sib),
    (diag, left),
]
EARLY, LATE = 5, 4


def mailing(l, x, c):
    me = (l, x, c)
    out = {}
    for t, (p, q) in enumerate(TILES):
        p, q = p(*me), q(*me)
        ends = [(p, q)] if t < 2 else [(p, q), (q, p)]
        for owner, other in ends:
            out.setdefault(place(*owner), []).append((t, place(*other)))
    return out


def addresses():
    table = np.full((N_BLK, N_BLK), -1, np.int32)
    for d in ALL:
        for owner, items in mailing(*d).items():
            assert len(items) <= DEPTH
            for slot, (_, other) in enumerate(items):
                assert table[owner, other] < 0
                table[owner, other] = place(*d) * DEPTH + slot
    assert (table >= 0).all()
    return table


def stamps():
    rows = []
    for d in ALL:
        where = {}
        for owner, items in mailing(*d).items():
            for slot, (t, _) in enumerate(items):
                where[(t, owner)] = owner * DEPTH + slot
        row = []
        for t, (p, q) in enumerate(TILES):
            row.append(where[(t, place(*p(*d)))])
            if t >= 2:
                row.append(where[(t, place(*q(*d)))])
        rows.append(row)
    return np.array(rows, np.int32)


def fetch(value, role):
    return lax.ppermute(value, BLK, [(place(*role(*d)), place(*d)) for d in ALL])


def position():
    return tuple(lax.axis_index(name) for name in BLK)


def dot(a, b):
    return lax.dot_general(
        a, b, (((0,), (0,)), ((), ())), preferred_element_type=jnp.float32
    )


def product(p, q):
    tile = dot(p[0][: PARTS[0]], q[0][: PARTS[0]])
    for u, v in zip(p[1:], q[1:]):
        tile += dot(u[...], v[...])
    return tile


def parted(block):
    return tuple(block.at[pl.ds(at, n)] for at, n in zip(STARTS, PARTS))


def owns(carrier, block):
    row = carrier[0][PARTS[0] :].astype(jnp.float32)
    return jnp.max(jnp.where(row == block.astype(jnp.float32), 1.0, 0.0)) > 0.5


def writer(out, slot):
    def put(tile):
        out[:, pl.ds(slot * SLAB, SLAB)] = tile.reshape(N_BULK, SLAB, W)

    return put


def settle(carrier, rhs, block, put):
    kept = owns(carrier, place(*block))

    @pl.when(kept)
    def _():
        put(product(carrier, rhs))

    @pl.when(jnp.logical_not(kept))
    def _():
        put(product(rhs, carrier))


def squeeze(out, rows):
    most = jnp.max(jnp.abs(out[:, :rows]), axis=0)
    most = jnp.max(jnp.max(most, axis=0, keepdims=True), axis=1, keepdims=True)
    most = jnp.maximum(most, 1e-30)
    power = jnp.ceil(jnp.log2(jnp.broadcast_to(most, (SLAB, W))))
    rank = lax.axis_index("z") * H + lax.axis_index("h")
    spread = 1.0 + rank.astype(jnp.float32) / N_BULK
    by = (jnp.exp2(TOP - power) * spread)[:1]
    for k in range(N_BULK):
        out[k, :rows] = out[k, :rows] * by
    return power


def early_kernel(a, b, w, x1, x2, x3, out, mark):
    a, b, w = parted(a), parted(b), parted(w)
    me = position()
    x = (x1, x2, x3)
    writer(out, 0)(product(a, a))
    writer(out, 1)(product(a, b))
    settle(x, a, own(*me), writer(out, 2))
    settle(x, b, sib(*me), writer(out, 3))
    settle(x, w, left(*me), writer(out, 4))
    mark[...] = squeeze(out, EARLY * SLAB)


def late_kernel(a, b, w, x1, x2, x3, v1, v2, v3, mark, out):
    a, b, w = parted(a), parted(b), parted(w)
    me = position()
    x, v = (x1, x2, x3), (v1, v2, v3)
    settle(v, x, right(*me), writer(out, 0))
    settle(v, a, own(*me), writer(out, 1))
    settle(v, b, sib(*me), writer(out, 2))
    settle(v, w, left(*me), writer(out, 3))
    power = squeeze(out, LATE * SLAB)
    first = lax.broadcasted_iota(jnp.int32, (SLAB, W), 0) < SLAB // 2
    power = jnp.where(first, mark[...], power)
    for k in range(N_BULK):
        out[k, LATE * SLAB :] = power


def pack_kernel(stamp, early, late, out):
    me = place(*position())
    k = 0
    for t in range(SLOTS):
        if t < EARLY:
            tile = early[pl.ds(t * SLAB, SLAB)]
        else:
            tile = late[pl.ds((t - EARLY) * SLAB, SLAB)]
        for _ in range(1 if t < 2 else 2):
            out[stamp[me, k]] = tile
            k += 1


def pick_kernel(table, cols, got, out):
    me = place(*position())
    for j in range(SLOTS):
        b = cols[0, j]
        slab = got[table[me, jnp.maximum(b, 0)]]
        out[j] = jnp.where(b >= 0, slab, 0.0)


def call(kernel, shapes, n_smem, n_tiles, *ins):
    vmem = pl.BlockSpec(memory_space=pltpu.VMEM)
    smem = pl.BlockSpec(memory_space=pltpu.SMEM)
    size = sum(int(np.prod(shape)) for shape in shapes)
    return pl.pallas_call(
        kernel,
        out_shape=[jax.ShapeDtypeStruct(shape, jnp.float32) for shape in shapes],
        in_specs=[smem] * n_smem + [vmem] * (len(ins) - n_smem),
        out_specs=[vmem] * len(shapes),
        compiler_params=pltpu.CompilerParams(vmem_limit_bytes=24 * 2**20),
        cost_estimate=pl.CostEstimate(
            flops=n_tiles * 2 * W * W * K,
            bytes_accessed=4 * size + sum(v.size * v.dtype.itemsize for v in ins),
            transcendentals=0,
        ),
    )(*ins)


def everywhere(value, axes):
    return lax.all_to_all(value, axes, 0, 0, tiled=True)


def total(got, power):
    spread = 1.0 + lax.broadcasted_iota(jnp.float32, (N_BULK, 1, 1), 0) / N_BULK
    by = jnp.exp2(power.astype(jnp.float32) - TOP) / spread
    return (got.astype(jnp.float32) * by).sum(0)


def local(aux_factors, tile_cols):
    row = jnp.pad(
        tile_cols.astype(jnp.bfloat16),
        ((0, 15), (0, W - SLOTS)),
        constant_values=-2,
    )
    a = aux_factors.reshape(K, W)
    send = [a[at : at + n] for at, n in zip(STARTS, PARTS)]
    send[0] = jnp.concatenate([send[0], row])
    x = [fetch(part, right) for part in send]
    w = fetch(a, left)
    b = fetch(a, sib)
    v = [fetch(part, diag_via) for part in x]

    shape = (N_BULK, EARLY * SLAB, W)
    early, mark = call(early_kernel, [shape, (SLAB, W)], 0, EARLY, a, b, w, *x)
    shape = (N_BULK, (LATE + 1) * SLAB, W)
    (late,) = call(late_kernel, [shape], 0, LATE, a, b, w, *x, *v, mark)
    parts = jnp.concatenate([early, late], 1).astype(jnp.float16)
    got = everywhere(parts, BULK)
    at, end = EARLY * SLAB, SLOTS * SLAB
    early = total(got[:, :at], got[:, end : end + 1, :1])
    late = total(got[:, at:end], got[:, -1:, :1])

    shape = (N_BLK * DEPTH, SLAB, W)
    (mail,) = call(pack_kernel, [shape], 1, 0, jnp.asarray(stamps()), early, late)
    mail = everywhere(mail, BLK)
    table = jnp.asarray(addresses())
    return call(pick_kernel, [(SLOTS, SLAB, W)], 2, 0, table, tile_cols, mail)[0]


def solution(mesh):
    fine = Mesh(mesh.devices.reshape(Z, H, L, X, C), (*BULK, *BLK))
    in_specs = (P(BULK, None, BLK), P(BLK, None))
    out_specs = P(BLK, BULK, None)
    return jax.shard_map(
        local, mesh=fine, in_specs=in_specs, out_specs=out_specs, check_vma=False
    )
```

time: 137 us -> 132 us (0.964)
  the two profiles are of different devices: /device:TPU:1 before, /device:TPU:16 now
where the time goes in v6:
time: 132 us; the launch traced here: 131 us
  blocking collectives  77.4 us (59%)
  waiting for transfers between devices  21.7 us (16%)
  starting transfers between devices  21.4 us (16%)
  Pallas kernels  7.44 us (6%)
  other arithmetic  1.97 us (1%)
    all_to_all x2, blocking collectives, everywhere(): return lax.all_to_all(value, axes, 0, 0, tiled=True)  77.4 us
    ppermute x8, waiting for transfers between devices, fetch(): lax.ppermute(value, BLK, [(place(*role(*d)), place(*d)) for d in ALL])  21.7 us
    ppermute x8, starting transfers between devices, fetch(): lax.ppermute(value, BLK, [(place(*role(*d)), place(*d)) for d in ALL])  21.4 us
    pallas_call x4, Pallas kernels, call(): pl.pallas_call(kernel, out_shape=[jax.ShapeDtypeStruct(shape, jnp.float32...  7.44 us
  transfers between devices with their start and end apart: 8, of which 4 were waited for; matrix products, arithmetic and copies ran while one was open for 1% of the time, Pallas kernels for 2%

profile of v6, /device:TPU:16, one launch (start us, length us, event | category | flops | bytes accessed | tf_op | source)
XLA Modules:
  0.0 131.3 jit_solution(10779788524294058658)
XLA Ops:
  0.0 3.5 %collective-permute-start.1 = (bf16[2048,256]{1,0:T(8,128)(2,1)}, bf16[2048,256]{1,0:T(8,128)(2,1)S(1)}, u32[]{:S(2)}, u32[]{:S(2)}) collective-permute-start(bf16[2048,256]{1,0:T(8,128)(2,1)} %bitcast.1), channel_id=1, source_target_pairs={{6,0},{7,1},{0,2},{1,3},{3,4},{2,5},{5,6},{4,7},{15,8},{14,9},{9,1... | collective-permute-start | bytes 3145736 | tf_op jit(solution)/shard_map/ppermute | solution.py:107
  3.5 1.9 %collective-permute-start = (bf16[2048,256]{1,0:T(8,128)(2,1)}, bf16[2048,256]{1,0:T(8,128)(2,1)S(1)}, u32[]{:S(2)}, u32[]{:S(2)}) collective-permute-start(bf16[2048,256]{1,0:T(8,128)(2,1)} %bitcast.2), channel_id=1, source_target_pairs={{1,0},{0,1},{3,2},{2,3},{5,4},{4,5},{7,6},{6,7},{9,8},{8,9},{11,10... | collective-permute-start | bytes 3145736 | tf_op jit(solution)/shard_map/ppermute | solution.py:107
  5.5 0.7 convert_element_type.18
  6.1 1.2 fusion.12
  7.3 3.7 %collective-permute-start.2 = (bf16[784,256]{1,0:T(8,128)(2,1)S(1)}, bf16[784,256]{1,0:T(8,128)(2,1)S(1)}, u32[]{:S(2)}, u32[]{:S(2)}) collective-permute-start(bf16[784,256]{1,0:T(8,128)(2,1)S(1)} %fusion.1), channel_id=1, source_target_pairs={{2,0},{3,1},{4,2},{5,3},{6,4},{7,5},{0,6},{1,7},{10,8},{11,9},{12,... | collective-permute-start | bytes 1204232 | tf_op jit(solution)/shard_map/ppermute | solution.py:107
  11.0 3.6 %collective-permute-start.3 = (bf16[768,256]{1,0:T(8,128)(2,1)S(1)}, bf16[768,256]{1,0:T(8,128)(2,1)S(1)}, u32[]{:S(2)}, u32[]{:S(2)}) collective-permute-start(bf16[768,256]{1,0:T(8,128)(2,1)S(1)} %get-tuple-element.11), channel_id=1, source_target_pairs={{2,0},{3,1},{4,2},{5,3},{6,4},{7,5},{0,6},{1,7},{10,8},{11,9},{12,... | collective-permute-start | bytes 1179656 | tf_op jit(solution)/shard_map/ppermute | solution.py:107
  14.6 2.7 %collective-permute-start.4 = (bf16[512,256]{1,0:T(8,128)(2,1)S(1)}, bf16[512,256]{1,0:T(8,128)(2,1)S(1)}, u32[]{:S(2)}, u32[]{:S(2)}) collective-permute-start(bf16[512,256]{1,0:T(8,128)(2,1)S(1)} %slice.30), channel_id=1, source_target_pairs={{2,0},{3,1},{4,2},{5,3},{6,4},{7,5},{0,6},{1,7},{10,8},{11,9},{12,... | collective-permute-start | bytes 786440 | tf_op jit(solution)/shard_map/ppermute | solution.py:107
  17.3 4.0 %collective-permute-done.2.x1 = bf16[784,256]{1,0:T(8,128)(2,1)S(1)} collective-permute-done((bf16[784,256]{1,0:T(8,128)(2,1)S(1)}, bf16[784,256]{1,0:T(8,128)(2,1)S(1)}, u32[]{:S(2)}, u32[]{:S(2)}) %collective-permute-start.2) | collective-permute-done | bytes 401440 | tf_op jit(solution)/shard_map/ppermute | solution.py:107
  21.3 1.9 %collective-permute-start.5 = (bf16[784,256]{1,0:T(8,128)(2,1)S(1)}, bf16[784,256]{1,0:T(8,128)(2,1)S(1)}, u32[]{:S(2)}, u32[]{:S(2)}) collective-permute-start(bf16[784,256]{1,0:T(8,128)(2,1)S(1)} %collective-permute-done.2.x1), channel_id=1, source_target_pairs={{8,0},{9,1},{10,2},{11,3},{12,4},{13,5},{14,6},{15,7},{1,8},{0,9},... | collective-permute-start | bytes 1204232 | tf_op jit(solution)/shard_map/ppermute | solution.py:107
  23.2 6.5 %collective-permute-done.3.x2 = bf16[768,256]{1,0:T(8,128)(2,1)S(1)} collective-permute-done((bf16[768,256]{1,0:T(8,128)(2,1)S(1)}, bf16[768,256]{1,0:T(8,128)(2,1)S(1)}, u32[]{:S(2)}, u32[]{:S(2)}) %collective-permute-start.3) | collective-permute-done | bytes 393248 | tf_op jit(solution)/shard_map/ppermute | solution.py:107
  29.7 1.9 %collective-permute-start.6 = (bf16[768,256]{1,0:T(8,128)(2,1)S(1)}, bf16[768,256]{1,0:T(8,128)(2,1)S(1)}, u32[]{:S(2)}, u32[]{:S(2)}) collective-permute-start(bf16[768,256]{1,0:T(8,128)(2,1)S(1)} %collective-permute-done.3.x2), channel_id=1, source_target_pairs={{8,0},{9,1},{10,2},{11,3},{12,4},{13,5},{14,6},{15,7},{1,8},{0,9},... | collective-permute-start | bytes 1179656 | tf_op jit(solution)/shard_map/ppermute | solution.py:107
  31.7 3.3 %collective-permute-done.4.x3 = bf16[512,256]{1,0:T(8,128)(2,1)S(1)} collective-permute-done((bf16[512,256]{1,0:T(8,128)(2,1)S(1)}, bf16[512,256]{1,0:T(8,128)(2,1)S(1)}, u32[]{:S(2)}, u32[]{:S(2)}) %collective-permute-start.4) | collective-permute-done | bytes 262176 | tf_op jit(solution)/shard_map/ppermute | solution.py:107
  35.0 2.2 %collective-permute-start.7 = (bf16[512,256]{1,0:T(8,128)(2,1)S(1)}, bf16[512,256]{1,0:T(8,128)(2,1)S(1)}, u32[]{:S(2)}, u32[]{:S(2)}) collective-permute-start(bf16[512,256]{1,0:T(8,128)(2,1)S(1)} %collective-permute-done.4.x3), channel_id=1, source_target_pairs={{8,0},{9,1},{10,2},{11,3},{12,4},{13,5},{14,6},{15,7},{1,8},{0,9},... | collective-permute-start | bytes 786440 | tf_op jit(solution)/shard_map/ppermute | solution.py:107
  37.1 2.7 %shard_map.46 = (f32[32,40,256]{2,1,0:T(8,128)S(1)}, f32[8,256]{1,0:T(8,128)S(1)}) custom-call(bf16[2048,256]{1,0:T(8,128)(2,1)S(1)} %bitcast.5, bf16[2048,256]{1,0:T(8,128)(2,1)S(1)} %collective-permute-done.b, bf16[2048,256]{1,0:T(8,128)(2,1)S(1)} %collective-permute-done.1.w, bf16[784,256]{1,0:T(8,128)(2,1)S(1)} %collective-permute-done.2.x1, ...), custom_call_target="tpu_custom_call" | custom-call | flops 1342177280 | bytes 5521408 | tf_op jit(solution)/shard_map/pallas_call | solution.py:220
  39.8 7.9 %collective-permute-done.7.v3 = bf16[512,256]{1,0:T(8,128)(2,1)S(1)} collective-permute-done((bf16[512,256]{1,0:T(8,128)(2,1)S(1)}, bf16[512,256]{1,0:T(8,128)(2,1)S(1)}, u32[]{:S(2)}, u32[]{:S(2)}) %collective-permute-start.7) | collective-permute-done | bytes 262176 | tf_op jit(solution)/shard_map/ppermute | solution.py:107
  47.8 2.7 %shard_map.47 = f32[32,40,256]{2,1,0:T(8,128)S(1)} custom-call(bf16[2048,256]{1,0:T(8,128)(2,1)S(1)} %bitcast.6, bf16[2048,256]{1,0:T(8,128)(2,1)S(1)} %collective-permute-done.b, bf16[2048,256]{1,0:T(8,128)(2,1)S(1)} %collective-permute-done.1.w, bf16[784,256]{1,0:T(8,128)(2,1)S(1)} %collective-permute-done.2.x1, ...), custom_call_target="tpu_custom_call" | custom-call | flops 1073741824 | bytes 6578176 | tf_op jit(solution)/shard_map/pallas_call | solution.py:220
  50.7 0.3 pad_maximum_fusion
  51.1 52.5 %all_to_all.10 = f16[32,80,256]{2,1,0:T(8,128)(2,1)S(1)} all-to-all(f16[32,80,256]{2,1,0:T(8,128)(2,1)S(1)} %pad_maximum_fusion), channel_id=1, replica_groups=mesh['z'=8,'h'=4,'l'=2,'x'=4,'c'=2] {'z','h'}, dimensions={0} | all-to-all | bytes 2621440 | tf_op jit(solution)/shard_map/all_to_all | solution.py:235
  103.5 0.3 fusion.11
  103.9 0.2 multiply_reduce_fusion.1.late
  104.1 0.2 multiply_reduce_fusion.early
  104.3 0.7 shard_map.48
  105.0 24.9 %all_to_all.11.got = f32[64,8,256]{2,1,0:T(8,128)S(1)} all-to-all(f32[64,8,256]{2,1,0:T(8,128)S(1)} %shard_map.48), channel_id=1, replica_groups=mesh['z'=8,'h'=4,'l'=2,'x'=4,'c'=2] {'l','x','c'}, dimensions={0} | all-to-all | bytes 1048576 | tf_op jit(solution)/shard_map/all_to_all | solution.py:235
  129.9 1.4 %shard_map.49 = f32[9,8,256]{2,1,0:T(8,128)} custom-call(s32[16,16]{1,0:T(8,128)S(1)} %copy-done.1, s32[1,9]{1,0:T(1,128)S(1)} %copy-done.3, f32[64,8,256]{2,1,0:T(8,128)S(1)} %all_to_all.11.got), custom_call_target="tpu_custom_call" | custom-call | bytes 599076 | tf_op jit(solution)/shard_map/pallas_call | solution.py:220
  (16 shorter events, 0.3 us)
Async XLA Ops:
  0.0 14.6 %copy-start = (bf16[2,1024,256]{2,1,0:T(8,128)(2,1)S(1)}, bf16[2,1024,256]{2,1,0:T(8,128)(2,1)}, u32[]{:S(2)}) copy-start(bf16[2,1024,256]{2,1,0:T(8,128)(2,1)} %param.4) | copy-start | bytes 3145732
  0.0 37.1 %collective-permute-start.1 = (bf16[2048,256]{1,0:T(8,128)(2,1)}, bf16[2048,256]{1,0:T(8,128)(2,1)S(1)}, u32[]{:S(2)}, u32[]{:S(2)}) collective-permute-start(bf16[2048,256]{1,0:T(8,128)(2,1)} %bitcast.1), channel_id=1, source_target_pairs={{6,0},{7,1},{0,2},{1,3},{3,4},{2,5},{5,6},{4,7},{15,8},{14,9},{9,1... | collective-permute-start | bytes 3145736 | tf_op jit(solution)/shard_map/ppermute | solution.py:107
  3.5 33.6 %collective-permute-start = (bf16[2048,256]{1,0:T(8,128)(2,1)}, bf16[2048,256]{1,0:T(8,128)(2,1)S(1)}, u32[]{:S(2)}, u32[]{:S(2)}) collective-permute-start(bf16[2048,256]{1,0:T(8,128)(2,1)} %bitcast.2), channel_id=1, source_target_pairs={{1,0},{0,1},{3,2},{2,3},{5,4},{4,5},{7,6},{6,7},{9,8},{8,9},{11,10... | collective-permute-start | bytes 3145736 | tf_op jit(solution)/shard_map/ppermute | solution.py:107
  7.3 14.0 %collective-permute-start.2 = (bf16[784,256]{1,0:T(8,128)(2,1)S(1)}, bf16[784,256]{1,0:T(8,128)(2,1)S(1)}, u32[]{:S(2)}, u32[]{:S(2)}) collective-permute-start(bf16[784,256]{1,0:T(8,128)(2,1)S(1)} %fusion.1), channel_id=1, source_target_pairs={{2,0},{3,1},{4,2},{5,3},{6,4},{7,5},{0,6},{1,7},{10,8},{11,9},{12,... | collective-permute-start | bytes 1204232 | tf_op jit(solution)/shard_map/ppermute | solution.py:107
  11.0 18.7 %collective-permute-start.3 = (bf16[768,256]{1,0:T(8,128)(2,1)S(1)}, bf16[768,256]{1,0:T(8,128)(2,1)S(1)}, u32[]{:S(2)}, u32[]{:S(2)}) collective-permute-start(bf16[768,256]{1,0:T(8,128)(2,1)S(1)} %get-tuple-element.11), channel_id=1, source_target_pairs={{2,0},{3,1},{4,2},{5,3},{6,4},{7,5},{0,6},{1,7},{10,8},{11,9},{12,... | collective-permute-start | bytes 1179656 | tf_op jit(solution)/shard_map/ppermute | solution.py:107
  14.6 20.4 %collective-permute-start.4 = (bf16[512,256]{1,0:T(8,128)(2,1)S(1)}, bf16[512,256]{1,0:T(8,128)(2,1)S(1)}, u32[]{:S(2)}, u32[]{:S(2)}) collective-permute-start(bf16[512,256]{1,0:T(8,128)(2,1)S(1)} %slice.30), channel_id=1, source_target_pairs={{2,0},{3,1},{4,2},{5,3},{6,4},{7,5},{0,6},{1,7},{10,8},{11,9},{12,... | collective-permute-start | bytes 786440 | tf_op jit(solution)/shard_map/ppermute | solution.py:107
  21.3 26.4 %collective-permute-start.5 = (bf16[784,256]{1,0:T(8,128)(2,1)S(1)}, bf16[784,256]{1,0:T(8,128)(2,1)S(1)}, u32[]{:S(2)}, u32[]{:S(2)}) collective-permute-start(bf16[784,256]{1,0:T(8,128)(2,1)S(1)} %collective-permute-done.2.x1), channel_id=1, source_target_pairs={{8,0},{9,1},{10,2},{11,3},{12,4},{13,5},{14,6},{15,7},{1,8},{0,9},... | collective-permute-start | bytes 1204232 | tf_op jit(solution)/shard_map/ppermute | solution.py:107
  29.7 18.0 %collective-permute-start.6 = (bf16[768,256]{1,0:T(8,128)(2,1)S(1)}, bf16[768,256]{1,0:T(8,128)(2,1)S(1)}, u32[]{:S(2)}, u32[]{:S(2)}) collective-permute-start(bf16[768,256]{1,0:T(8,128)(2,1)S(1)} %collective-permute-done.3.x2), channel_id=1, source_target_pairs={{8,0},{9,1},{10,2},{11,3},{12,4},{13,5},{14,6},{15,7},{1,8},{0,9},... | collective-permute-start | bytes 1179656 | tf_op jit(solution)/shard_map/ppermute | solution.py:107
  35.0 12.8 %collective-permute-start.7 = (bf16[512,256]{1,0:T(8,128)(2,1)S(1)}, bf16[512,256]{1,0:T(8,128)(2,1)S(1)}, u32[]{:S(2)}, u32[]{:S(2)}) collective-permute-start(bf16[512,256]{1,0:T(8,128)(2,1)S(1)} %collective-permute-done.4.x3), channel_id=1, source_target_pairs={{8,0},{9,1},{10,2},{11,3},{12,4},{13,5},{14,6},{15,7},{1,8},{0,9},... | collective-permute-start | bytes 786440 | tf_op jit(solution)/shard_map/ppermute | solution.py:107
  51.1 53.2 %copy-start.2 = (s32[16,16]{1,0:T(8,128)S(1)}, s32[16,16]{1,0:T(8,128)}, u32[]{:S(2)}) copy-start(s32[16,16]{1,0:T(8,128)} %constant.20.clone.stamp) | copy-start | bytes 3076
  104.0 25.9 %copy-start.1 = (s32[16,16]{1,0:T(8,128)S(1)}, s32[16,16]{1,0:T(8,128)}, u32[]{:S(2)}) copy-start(s32[16,16]{1,0:T(8,128)} %constant.21.clone.table) | copy-start | bytes 3076
  104.0 25.9 %copy-start.3 = (s32[1,9]{1,0:T(1,128)S(1)}, s32[1,9]{1,0:T(1,128)}, u32[]{:S(2)}) copy-start(s32[1,9]{1,0:T(1,128)} %cols.1) | copy-start | bytes 112

commit v7 on v6

v7 whole, which is shorter than its diff:
```python
import jax
import jax.numpy as jnp
import numpy as np
from jax import lax
from jax.experimental import pallas as pl
from jax.experimental.pallas import tpu as pltpu
from jax.sharding import Mesh
from jax.sharding import PartitionSpec as P

Z, H, L, X, C = 8, 4, 2, 4, 2
BLK = ("l", "x", "c")
N_BLK, N_BULK = L * X * C, Z * H
BULK = ("z", "h")
SLOTS = 9
W = 256
K = 2048
PARTS = (1040, 1008)
STARTS = (0, 1040)
HALF = W // 2
SLAB = W // N_BULK
DEPTH = 4
TOP = 14.0


def place(l, x, c):
    return (l * X + x) * C + c


def own(l, x, c):
    return (l, x, c)


def sib(l, x, c):
    return (l, x, 1 - c)


def right(l, x, c):
    return (l, (x + 1) & 3, c)


def left(l, x, c):
    return (l, (x + 3) & 3, c ^ l ^ (x >> 1))


def diag(l, x, c):
    return (1 - l, (x + 1) & 3, c ^ l)


def diag_via(l, x, c):
    return (1 - l, x, c ^ l)


ALL = [(l, x, c) for l in range(L) for x in range(X) for c in range(C)]
TILES = [
    (own, own),
    (own, sib),
    (right, own),
    (right, sib),
    (right, left),
    (diag, right),
    (diag, own),
    (diag, sib),
    (diag, left),
]
EARLY, LATE = 5, 4


def ends(t, device):
    p, q = (place(*role(*device)) for role in TILES[t])
    return [(p, q)] if p == q else [(p, q), (q, p)]


def mailing(device):
    out = {}
    for t in range(SLOTS):
        for owner, other in ends(t, device):
            out.setdefault(owner, []).append((t, other))
    return out


def addresses():
    table = np.full((N_BLK, N_BLK + 1), -1, np.int32)
    for d in ALL:
        for owner, items in mailing(d).items():
            assert len(items) <= DEPTH
            for slot, (t, other) in enumerate(items):
                column = N_BLK if t == 1 and d[2] == 1 else other
                assert table[owner, column] < 0
                table[owner, column] = place(*d) * DEPTH + slot
    assert (table >= 0).all()
    return table


def stamps():
    rows = []
    for d in ALL:
        sent = mailing(d)
        row = []
        for t in range(SLOTS):
            for owner, other in ends(t, d):
                row.append(owner * DEPTH + sent[owner].index((t, other)))
        rows.append(row)
    return np.array(rows, np.int32)


def fetch(value, role):
    return lax.ppermute(value, BLK, [(place(*role(*d)), place(*d)) for d in ALL])


def position():
    return tuple(lax.axis_index(name) for name in BLK)


def dot(a, b):
    return lax.dot_general(
        a, b, (((0,), (0,)), ((), ())), preferred_element_type=jnp.float32
    )


def product(p, q):
    tile = dot(p[0][...], q[0][...])
    for u, v, n in zip(p[1:], q[1:], PARTS[1:]):
        tile += dot(u[:n], v[:n])
    return tile


def parted(block):
    return tuple(block.at[pl.ds(at, n)] for at, n in zip(STARTS, PARTS))


def owns(carrier, block):
    row = carrier[-1][PARTS[-1] :].astype(jnp.float32)
    return jnp.max(jnp.where(row == block.astype(jnp.float32), 1.0, 0.0)) > 0.5


def writer(out, slot):
    def put(tile):
        out[:, pl.ds(slot * SLAB, SLAB)] = tile.reshape(N_BULK, SLAB, W)

    return put


def settle(carrier, rhs, block, put):
    kept = owns(carrier, place(*block))

    @pl.when(kept)
    def _():
        put(product(carrier, rhs))

    @pl.when(jnp.logical_not(kept))
    def _():
        put(product(rhs, carrier))


def peak(out, rows):
    return jnp.max(jnp.max(jnp.abs(out[:, rows]), axis=0), axis=0, keepdims=True)


def early_kernel(cols, a, b, w, x1, x2, v1, out, most):
    del v1
    a, b, w = parted(a), parted(b), parted(w)
    me = position()
    x = (x1, x2)
    writer(out, 0)(product(a, a))
    other = place(*sib(*me))
    mine = cols[0, 0] == other
    for j in range(1, SLOTS):
        mine = jnp.logical_or(mine, cols[0, j] == other)
    for core in range(C):
        lanes = pl.ds(core * HALF, HALF)
        for kept, lhs, rhs in ((True, a, b), (False, b, a)):

            @pl.when(jnp.logical_and(me[2] == core, mine == kept))
            def _():
                tile = product(lhs, [part.at[:, lanes] for part in rhs])
                out[:, SLAB : 2 * SLAB, :HALF] = tile.reshape(N_BULK, SLAB, HALF)

    out[:, SLAB : 2 * SLAB, HALF:] = jnp.zeros((N_BULK, SLAB, HALF), jnp.float32)
    settle(x, a, own(*me), writer(out, 2))
    settle(x, b, sib(*me), writer(out, 3))
    settle(x, w, left(*me), writer(out, 4))
    most[...] = jnp.broadcast_to(peak(out, slice(0, EARLY * SLAB)), (SLAB, W))


def late_kernel(a, b, w, x1, x2, v1, v2, early, most, out):
    a, b, w = parted(a), parted(b), parted(w)
    me = position()
    x, v = (x1, x2), (v1, v2)
    settle(v, x, right(*me), writer(out, 5))
    settle(v, a, own(*me), writer(out, 6))
    settle(v, b, sib(*me), writer(out, 7))
    settle(v, w, left(*me), writer(out, 8))

    n = EARLY * SLAB
    most = jnp.maximum(peak(out, slice(n, SLOTS * SLAB)), most[:1])
    most = jnp.maximum(jnp.max(most, axis=1, keepdims=True), 1e-30)
    power = jnp.ceil(jnp.log2(jnp.broadcast_to(most, (SLAB, W))))
    rank = lax.axis_index("z") * H + lax.axis_index("h")
    spread = 1.0 + rank.astype(jnp.float32) / N_BULK
    by = (jnp.exp2(TOP - power) * spread)[:1]
    for k in range(N_BULK):
        out[k, :n] = early[k] * by
        out[k, n:] = out[k, n:] * by
        out[k, SLAB : 2 * SLAB, HALF:] = power[:, HALF:]


def pack_kernel(stamp, done, out):
    me = place(*position())
    k = 0
    for t in range(SLOTS):
        tile = done[pl.ds(t * SLAB, SLAB)]
        for _ in range(1 if t == 0 else 2):
            out[stamp[me, k]] = tile
            k += 1


def pick_kernel(table, cols, got, out):
    me = position()
    other = place(*sib(*me))
    me = place(*me)
    halves = (got[table[me, other]], got[table[me, N_BLK]])
    halves = jnp.concatenate([half[:, :HALF] for half in halves], axis=1)
    for j in range(SLOTS):
        b = cols[0, j]
        slab = got[table[me, jnp.maximum(b, 0)]]
        slab = jnp.where(b == other, halves, slab)
        out[j] = jnp.where(b >= 0, slab, 0.0)


def call(kernel, shapes, n_smem, n_tiles, *ins):
    vmem = pl.BlockSpec(memory_space=pltpu.VMEM)
    smem = pl.BlockSpec(memory_space=pltpu.SMEM)
    size = sum(int(np.prod(shape)) for shape in shapes)
    return pl.pallas_call(
        kernel,
        out_shape=[jax.ShapeDtypeStruct(shape, jnp.float32) for shape in shapes],
        in_specs=[smem] * n_smem + [vmem] * (len(ins) - n_smem),
        out_specs=[vmem] * len(shapes),
        compiler_params=pltpu.CompilerParams(vmem_limit_bytes=24 * 2**20),
        cost_estimate=pl.CostEstimate(
            flops=n_tiles * 2 * W * W * K,
            bytes_accessed=4 * size + sum(v.size * v.dtype.itemsize for v in ins),
            transcendentals=0,
        ),
    )(*ins)


def everywhere(value, axes):
    return lax.all_to_all(value, axes, 0, 0, tiled=True)


def total(got):
    spread = 1.0 + lax.broadcasted_iota(jnp.float32, (N_BULK, 1, 1), 0) / N_BULK
    power = got[:, SLAB : SLAB + 1, HALF : HALF + 1].astype(jnp.float32)
    return (got.astype(jnp.float32) * (jnp.exp2(power - TOP) / spread)).sum(0)


def local(aux_factors, tile_cols):
    row = jnp.pad(
        tile_cols.astype(jnp.bfloat16),
        ((0, 15), (0, W - SLOTS)),
        constant_values=-2,
    )
    a = aux_factors.reshape(K, W)
    send = [a[at : at + n] for at, n in zip(STARTS, PARTS)]
    send[-1] = jnp.concatenate([send[-1], row])
    x = [fetch(part, right) for part in send]
    w = fetch(a, left)
    b = fetch(a, sib)
    v = [fetch(part, diag_via) for part in x]

    shapes = [(N_BULK, EARLY * SLAB, W), (SLAB, W)]
    early = call(early_kernel, shapes, 1, EARLY, tile_cols, a, b, w, *x, v[0])
    shapes = [(N_BULK, SLOTS * SLAB, W)]
    (parts,) = call(late_kernel, shapes, 0, LATE, a, b, w, *x, *v, *early)
    done = total(everywhere(parts.astype(jnp.float16), BULK))

    shapes = [(N_BLK * DEPTH, SLAB, W)]
    (mail,) = call(pack_kernel, shapes, 1, 0, jnp.asarray(stamps()), done)
    mail = everywhere(mail, BLK)
    table = jnp.asarray(addresses())
    return call(pick_kernel, [(SLOTS, SLAB, W)], 2, 0, table, tile_cols, mail)[0]


def solution(mesh):
    fine = Mesh(mesh.devices.reshape(Z, H, L, X, C), (*BULK, *BLK))
    in_specs = (P(BULK, None, BLK), P(BLK, None))
    out_specs = P(BLK, BULK, None)
    return jax.shard_map(
        local, mesh=fine, in_specs=in_specs, out_specs=out_specs, check_vma=False
    )
```

time: 132 us -> 124 us (0.939)
  the two profiles are of different devices: /device:TPU:16 before, /device:TPU:1 now
where the time goes in v7:
time: 124 us
  blocking collectives  71.7 us (58%)
  starting transfers between devices  23.5 us (19%)
  waiting for transfers between devices  17.5 us (14%)
  Pallas kernels  8.59 us (7%)
    all_to_all x2, blocking collectives, everywhere(): return lax.all_to_all(value, axes, 0, 0, tiled=True)  71.7 us
    ppermute x6, starting transfers between devices, fetch(): lax.ppermute(value, BLK, [(place(*role(*d)), place(*d)) for d in ALL])  23.5 us
    ppermute x6, waiting for transfers between devices, fetch(): lax.ppermute(value, BLK, [(place(*role(*d)), place(*d)) for d in ALL])  17.5 us
    pallas_call x4, Pallas kernels, call(): pl.pallas_call(kernel, out_shape=[jax.ShapeDtypeStruct(shape, jnp.float32...  8.59 us
  transfers between devices with their start and end apart: 6, of which 3 were waited for; matrix products, arithmetic and copies ran while one was open for 0% of the time, Pallas kernels for 3%

profile of v7, /device:TPU:1, one launch (start us, length us, event | category | flops | bytes accessed | tf_op | source)
XLA Modules:
  0.0 123.5 jit_solution(5043910265630950976)
XLA Ops:
  0.0 1.2 slice.12
  1.2 5.2 %collective-permute-start.2 = (bf16[1040,256]{1,0:T(8,128)(2,1)S(1)}, bf16[1040,256]{1,0:T(8,128)(2,1)S(1)}, u32[]{:S(2)}, u32[]{:S(2)}) collective-permute-start(bf16[1040,256]{1,0:T(8,128)(2,1)S(1)} %slice.12), channel_id=1, source_target_pairs={{2,0},{3,1},{4,2},{5,3},{6,4},{7,5},{0,6},{1,7},{10,8},{11,9},{12,... | collective-permute-start | bytes 1597448 | tf_op jit(solution)/shard_map/ppermute | solution.py:107
  6.4 1.9 %collective-permute-start.1 = (bf16[2048,256]{1,0:T(8,128)(2,1)}, bf16[2048,256]{1,0:T(8,128)(2,1)S(1)}, u32[]{:S(2)}, u32[]{:S(2)}) collective-permute-start(bf16[2048,256]{1,0:T(8,128)(2,1)} %bitcast.2), channel_id=1, source_target_pairs={{6,0},{7,1},{0,2},{1,3},{3,4},{2,5},{5,6},{4,7},{15,8},{14,9},{9,1... | collective-permute-start | bytes 3145736 | tf_op jit(solution)/shard_map/ppermute | solution.py:107
  8.3 7.5 %collective-permute-start = (bf16[2048,256]{1,0:T(8,128)(2,1)}, bf16[2048,256]{1,0:T(8,128)(2,1)S(1)}, u32[]{:S(2)}, u32[]{:S(2)}) collective-permute-start(bf16[2048,256]{1,0:T(8,128)(2,1)} %bitcast.3), channel_id=1, source_target_pairs={{1,0},{0,1},{3,2},{2,3},{5,4},{4,5},{7,6},{6,7},{9,8},{8,9},{11,10... | collective-permute-start | bytes 3145736 | tf_op jit(solution)/shard_map/ppermute | solution.py:107
  15.8 0.0 copy-done
  16.0 2.9 %collective-permute-start.3 = (bf16[1024,256]{1,0:T(8,128)(2,1)S(1)}, bf16[1024,256]{1,0:T(8,128)(2,1)S(1)}, u32[]{:S(2)}, u32[]{:S(2)}) collective-permute-start(bf16[1024,256]{1,0:T(8,128)(2,1)S(1)} %fusion.1), channel_id=1, source_target_pairs={{2,0},{3,1},{4,2},{5,3},{6,4},{7,5},{0,6},{1,7},{10,8},{11,9},{12,... | collective-permute-start | bytes 1572872 | tf_op jit(solution)/shard_map/ppermute | solution.py:107
  18.8 0.0 collective-permute-done.2.x1
  18.8 4.1 %collective-permute-start.4 = (bf16[1040,256]{1,0:T(8,128)(2,1)S(1)}, bf16[1040,256]{1,0:T(8,128)(2,1)S(1)}, u32[]{:S(2)}, u32[]{:S(2)}) collective-permute-start(bf16[1040,256]{1,0:T(8,128)(2,1)S(1)} %collective-permute-done.2.x1), channel_id=1, source_target_pairs={{8,0},{9,1},{10,2},{11,3},{12,4},{13,5},{14,6},{15,7},{1,8},{0,9},... | collective-permute-start | bytes 1597448 | tf_op jit(solution)/shard_map/ppermute | solution.py:107
  22.9 8.5 %collective-permute-done.3.x2 = bf16[1024,256]{1,0:T(8,128)(2,1)S(1)} collective-permute-done((bf16[1024,256]{1,0:T(8,128)(2,1)S(1)}, bf16[1024,256]{1,0:T(8,128)(2,1)S(1)}, u32[]{:S(2)}, u32[]{:S(2)}) %collective-permute-start.3) | collective-permute-done | bytes 524320 | tf_op jit(solution)/shard_map/ppermute | solution.py:107
  31.4 1.9 %collective-permute-start.5 = (bf16[1024,256]{1,0:T(8,128)(2,1)S(1)}, bf16[1024,256]{1,0:T(8,128)(2,1)S(1)}, u32[]{:S(2)}, u32[]{:S(2)}) collective-permute-start(bf16[1024,256]{1,0:T(8,128)(2,1)S(1)} %collective-permute-done.3.x2), channel_id=1, source_target_pairs={{8,0},{9,1},{10,2},{11,3},{12,4},{13,5},{14,6},{15,7},{1,8},{0,9},... | collective-permute-start | bytes 1572872 | tf_op jit(solution)/shard_map/ppermute | solution.py:107
  33.3 0.0 collective-permute-done.1.w
  33.3 0.0 collective-permute-done.b
  33.3 0.5 collective-permute-done.4.v1
  33.8 3.6 %shard_map.46 = (f32[32,40,256]{2,1,0:T(8,128)S(1)}, f32[8,256]{1,0:T(8,128)S(1)}) custom-call(s32[1,9]{1,0:T(1,128)S(1)} %copy-done.3, bf16[2048,256]{1,0:T(8,128)(2,1)S(1)} %bitcast.5, bf16[2048,256]{1,0:T(8,128)(2,1)S(1)} %collective-permute-done.b, bf16[2048,256]{1,0:T(8,128)(2,1)S(1)} %collective-permute-done.1.w, ...), custom_call_target="tpu_custom_call" | custom-call | flops 1342177280 | bytes 6053924 | tf_op jit(solution)/shard_map/pallas_call | solution.py:234
  37.4 8.5 %collective-permute-done.5.v2 = bf16[1024,256]{1,0:T(8,128)(2,1)S(1)} collective-permute-done((bf16[1024,256]{1,0:T(8,128)(2,1)S(1)}, bf16[1024,256]{1,0:T(8,128)(2,1)S(1)}, u32[]{:S(2)}, u32[]{:S(2)}) %collective-permute-start.5) | collective-permute-done | bytes 524320 | tf_op jit(solution)/shard_map/ppermute | solution.py:107
  45.9 2.9 %shard_map.47 = f32[32,72,256]{2,1,0:T(8,128)S(1)} custom-call(bf16[2048,256]{1,0:T(8,128)(2,1)S(1)} %bitcast.6, bf16[2048,256]{1,0:T(8,128)(2,1)S(1)} %collective-permute-done.b, bf16[2048,256]{1,0:T(8,128)(2,1)S(1)} %collective-permute-done.1.w, bf16[1040,256]{1,0:T(8,128)(2,1)S(1)} %collective-permute-done.2.x1, ...), custom_call_target="tpu_custom_call" | custom-call | flops 1073741824 | bytes 8937472 | tf_op jit(solution)/shard_map/pallas_call | solution.py:234
  48.9 0.2 convert_element_type.15
  49.1 0.0 copy-start.2
  49.1 49.9 %all_to_all.10 = f16[32,72,256]{2,1,0:T(8,128)(2,1)S(1)} all-to-all(f16[32,72,256]{2,1,0:T(8,128)(2,1)S(1)} %convert_element_type.15), channel_id=1, replica_groups=mesh['z'=8,'h'=4,'l'=2,'x'=4,'c'=2] {'z','h'}, dimensions={0} | all-to-all | bytes 2359296 | tf_op jit(solution)/shard_map/all_to_all | solution.py:249
  99.0 0.3 fusion.6
  99.3 0.3 multiply_reduce_fusion.done
  99.6 0.7 shard_map.48
  100.4 21.8 %all_to_all.11.got = f32[64,8,256]{2,1,0:T(8,128)S(1)} all-to-all(f32[64,8,256]{2,1,0:T(8,128)S(1)} %shard_map.48), channel_id=1, replica_groups=mesh['z'=8,'h'=4,'l'=2,'x'=4,'c'=2] {'l','x','c'}, dimensions={0} | all-to-all | bytes 1048576 | tf_op jit(solution)/shard_map/all_to_all | solution.py:249
  122.2 1.4 %shard_map.49 = f32[9,8,256]{2,1,0:T(8,128)} custom-call(s32[16,17]{1,0:T(8,128)S(1)} %copy-done.1, s32[1,9]{1,0:T(1,128)S(1)} %copy-done.3, f32[64,8,256]{2,1,0:T(8,128)S(1)} %all_to_all.11.got), custom_call_target="tpu_custom_call" | custom-call | bytes 599140 | tf_op jit(solution)/shard_map/pallas_call | solution.py:234
  (9 shorter events, 0.1 us)
Async XLA Ops:
  0.0 15.8 %copy-start = (bf16[2,1024,256]{2,1,0:T(8,128)(2,1)S(1)}, bf16[2,1024,256]{2,1,0:T(8,128)(2,1)}, u32[]{:S(2)}) copy-start(bf16[2,1024,256]{2,1,0:T(8,128)(2,1)} %param.4) | copy-start | bytes 3145732
  0.0 15.9 %copy-start.3 = (s32[1,9]{1,0:T(1,128)S(1)}, s32[1,9]{1,0:T(1,128)}, u32[]{:S(2)}) copy-start(s32[1,9]{1,0:T(1,128)} %cols.3) | copy-start | bytes 112
  1.2 17.6 %collective-permute-start.2 = (bf16[1040,256]{1,0:T(8,128)(2,1)S(1)}, bf16[1040,256]{1,0:T(8,128)(2,1)S(1)}, u32[]{:S(2)}, u32[]{:S(2)}) collective-permute-start(bf16[1040,256]{1,0:T(8,128)(2,1)S(1)} %slice.12), channel_id=1, source_target_pairs={{2,0},{3,1},{4,2},{5,3},{6,4},{7,5},{0,6},{1,7},{10,8},{11,9},{12,... | collective-permute-start | bytes 1597448 | tf_op jit(solution)/shard_map/ppermute | solution.py:107
  6.4 26.9 %collective-permute-start.1 = (bf16[2048,256]{1,0:T(8,128)(2,1)}, bf16[2048,256]{1,0:T(8,128)(2,1)S(1)}, u32[]{:S(2)}, u32[]{:S(2)}) collective-permute-start(bf16[2048,256]{1,0:T(8,128)(2,1)} %bitcast.2), channel_id=1, source_target_pairs={{6,0},{7,1},{0,2},{1,3},{3,4},{2,5},{5,6},{4,7},{15,8},{14,9},{9,1... | collective-permute-start | bytes 3145736 | tf_op jit(solution)/shard_map/ppermute | solution.py:107
  8.3 25.0 %collective-permute-start = (bf16[2048,256]{1,0:T(8,128)(2,1)}, bf16[2048,256]{1,0:T(8,128)(2,1)S(1)}, u32[]{:S(2)}, u32[]{:S(2)}) collective-permute-start(bf16[2048,256]{1,0:T(8,128)(2,1)} %bitcast.3), channel_id=1, source_target_pairs={{1,0},{0,1},{3,2},{2,3},{5,4},{4,5},{7,6},{6,7},{9,8},{8,9},{11,10... | collective-permute-start | bytes 3145736 | tf_op jit(solution)/shard_map/ppermute | solution.py:107
  16.0 15.4 %collective-permute-start.3 = (bf16[1024,256]{1,0:T(8,128)(2,1)S(1)}, bf16[1024,256]{1,0:T(8,128)(2,1)S(1)}, u32[]{:S(2)}, u32[]{:S(2)}) collective-permute-start(bf16[1024,256]{1,0:T(8,128)(2,1)S(1)} %fusion.1), channel_id=1, source_target_pairs={{2,0},{3,1},{4,2},{5,3},{6,4},{7,5},{0,6},{1,7},{10,8},{11,9},{12,... | collective-permute-start | bytes 1572872 | tf_op jit(solution)/shard_map/ppermute | solution.py:107
  18.8 15.0 %collective-permute-start.4 = (bf16[1040,256]{1,0:T(8,128)(2,1)S(1)}, bf16[1040,256]{1,0:T(8,128)(2,1)S(1)}, u32[]{:S(2)}, u32[]{:S(2)}) collective-permute-start(bf16[1040,256]{1,0:T(8,128)(2,1)S(1)} %collective-permute-done.2.x1), channel_id=1, source_target_pairs={{8,0},{9,1},{10,2},{11,3},{12,4},{13,5},{14,6},{15,7},{1,8},{0,9},... | collective-permute-start | bytes 1597448 | tf_op jit(solution)/shard_map/ppermute | solution.py:107
  31.4 14.5 %collective-permute-start.5 = (bf16[1024,256]{1,0:T(8,128)(2,1)S(1)}, bf16[1024,256]{1,0:T(8,128)(2,1)S(1)}, u32[]{:S(2)}, u32[]{:S(2)}) collective-permute-start(bf16[1024,256]{1,0:T(8,128)(2,1)S(1)} %collective-permute-done.3.x2), channel_id=1, source_target_pairs={{8,0},{9,1},{10,2},{11,3},{12,4},{13,5},{14,6},{15,7},{1,8},{0,9},... | collective-permute-start | bytes 1572872 | tf_op jit(solution)/shard_map/ppermute | solution.py:107
  49.1 50.6 %copy-start.2 = (s32[16,17]{1,0:T(8,128)S(1)}, s32[16,17]{1,0:T(8,128)}, u32[]{:S(2)}) copy-start(s32[16,17]{1,0:T(8,128)} %constant.19.clone.stamp) | copy-start | bytes 3268
  99.3 22.8 %copy-start.1 = (s32[16,17]{1,0:T(8,128)S(1)}, s32[16,17]{1,0:T(8,128)}, u32[]{:S(2)}) copy-start(s32[16,17]{1,0:T(8,128)} %constant.20.clone.table) | copy-start | bytes 3268

commit v8 on v7

--- a/solution.py
+++ b/solution.py
@@ -18,7 +18,6 @@
 STARTS = (0, 1040)
 HALF = W // 2
 SLAB = W // N_BULK
-DEPTH = 4
 TOP = 14.0
 
 
@@ -70,41 +69,39 @@
     return [(p, q)] if p == q else [(p, q), (q, p)]
 
 
-def mailing(device):
-    out = {}
-    for t in range(SLOTS):
-        for owner, other in ends(t, device):
-            out.setdefault(owner, []).append((t, other))
-    return out
+MAIL = ((sib, (1, 3, 7)), (right, (2, 3, 4, 5)), (diag, (5, 6, 7, 8)), (left, (4, 8)))
 
 
 def addresses():
     table = np.full((N_BLK, N_BLK + 1), -1, np.int32)
+
+    def enter(owner, t, device, index):
+        pair = [place(*role(*device)) for role in TILES[t]]
+        if owner not in pair:
+            return
+        pair.remove(owner)
+        column = N_BLK if t == 1 and device[2] == 1 else pair[0]
+        assert table[owner, column] < 0
+        table[owner, column] = index
+
     for d in ALL:
-        for owner, items in mailing(d).items():
-            assert len(items) <= DEPTH
-            for slot, (t, other) in enumerate(items):
-                column = N_BLK if t == 1 and d[2] == 1 else other
-                assert table[owner, column] < 0
-                table[owner, column] = place(*d) * DEPTH + slot
+        for t in range(SLOTS):
+            enter(place(*d), t, d, t)
+        index = SLOTS
+        for role, sent in MAIL:
+            for t in sent:
+                enter(place(*role(*d)), t, d, index)
+                index += 1
     assert (table >= 0).all()
     return table
 
 
-def stamps():
-    rows = []
-    for d in ALL:
-        sent = mailing(d)
-        row = []
-        for t in range(SLOTS):
-            for owner, other in ends(t, d):
-                row.append(owner * DEPTH + sent[owner].index((t, other)))
-        rows.append(row)
-    return np.array(rows, np.int32)
-
-
 def fetch(value, role):
     return lax.ppermute(value, BLK, [(place(*role(*d)), place(*d)) for d in ALL])
+
+
+def hand(value, role):
+    return lax.ppermute(value, BLK, [(place(*d), place(*role(*d))) for d in ALL])
 
 
 def position():
@@ -204,17 +201,13 @@
         out[k, SLAB : 2 * SLAB, HALF:] = power[:, HALF:]
 
 
-def pack_kernel(stamp, done, out):
-    me = place(*position())
-    k = 0
-    for t in range(SLOTS):
-        tile = done[pl.ds(t * SLAB, SLAB)]
-        for _ in range(1 if t == 0 else 2):
-            out[stamp[me, k]] = tile
-            k += 1
-
-
-def pick_kernel(table, cols, got, out):
+def pick_kernel(table, cols, *refs):
+    *parts, out, got = refs
+    at = 0
+    for part in parts:
+        n = part.shape[0] // SLAB
+        got[pl.ds(at, n)] = part[...].reshape(n, SLAB, W)
+        at += n
     me = position()
     other = place(*sib(*me))
     me = place(*me)
@@ -227,7 +220,7 @@
         out[j] = jnp.where(b >= 0, slab, 0.0)
 
 
-def call(kernel, shapes, n_smem, n_tiles, *ins):
+def call(kernel, shapes, n_smem, n_tiles, *ins, scratch=()):
     vmem = pl.BlockSpec(memory_space=pltpu.VMEM)
     smem = pl.BlockSpec(memory_space=pltpu.SMEM)
     size = sum(int(np.prod(shape)) for shape in shapes)
@@ -236,6 +229,7 @@
         out_shape=[jax.ShapeDtypeStruct(shape, jnp.float32) for shape in shapes],
         in_specs=[smem] * n_smem + [vmem] * (len(ins) - n_smem),
         out_specs=[vmem] * len(shapes),
+        scratch_shapes=[pltpu.VMEM(shape, jnp.float32) for shape in scratch],
         compiler_params=pltpu.CompilerParams(vmem_limit_bytes=24 * 2**20),
         cost_estimate=pl.CostEstimate(
             flops=n_tiles * 2 * W * W * K,
@@ -275,11 +269,21 @@
     (parts,) = call(late_kernel, shapes, 0, LATE, a, b, w, *x, *v, *early)
     done = total(everywhere(parts.astype(jnp.float16), BULK))
 
-    shapes = [(N_BLK * DEPTH, SLAB, W)]
-    (mail,) = call(pack_kernel, shapes, 1, 0, jnp.asarray(stamps()), done)
-    mail = everywhere(mail, BLK)
-    table = jnp.asarray(addresses())
-    return call(pick_kernel, [(SLOTS, SLAB, W)], 2, 0, table, tile_cols, mail)[0]
+    parts = [done]
+    for role, sent in MAIL:
+        slabs = [done[t * SLAB : (t + 1) * SLAB] for t in sent]
+        parts.append(hand(jnp.concatenate(slabs), role))
+    count = sum(part.shape[0] for part in parts) // SLAB
+    return call(
+        pick_kernel,
+        [(SLOTS, SLAB, W)],
+        2,
+        0,
+        jnp.asarray(addresses()),
+        tile_cols,
+        *parts,
+        scratch=[(count, SLAB, W)],
+    )[0]
 
 
 def solution(mesh):

time: 124 us -> 122 us (0.984)
  blocking collectives: 71.7 us -> 49.9 us
  starting transfers between devices: 23.5 us -> 41.7 us
  waiting for transfers between devices: 17.5 us -> 19.3 us
    all_to_all x2 -> x1, blocking collectives: 71.7 us -> 49.9 us  [everywhere(): return lax.all_to_all(value, axes, 0, 0, tiled=True)]
    ppermute x0 -> x4, starting transfers between devices: none -> 18.2 us  [hand(): lax.ppermute(value, BLK, [(place(*d), place(*role(*d))) for d in ALL])]
    ppermute x0 -> x4, waiting for transfers between devices: none -> 1.82 us  [hand(): lax.ppermute(value, BLK, [(place(*d), place(*role(*d))) for d in ALL])]
    pallas_call x4 -> x3, Pallas kernels: 8.59 us -> 7.89 us  [call(): pl.pallas_call(kernel, out_shape=[jax.ShapeDtypeStruct(shape, jnp.float32...]
  transfers between devices with their start and end apart: 6 -> 10, of which waited for: 3 -> 4; matrix products, arithmetic and copies ran while one was open for 0% -> 0% of each run, Pallas kernels for 3% -> 3%
where the time goes in v8:
time: 122 us; the launch traced here: 121 us
  blocking collectives  49.9 us (41%)
  starting transfers between devices  41.7 us (34%)
  waiting for transfers between devices  19.3 us (16%)
  Pallas kernels  7.89 us (6%)
  local copies, waits for them, and re-layouts  1.23 us (1%)
    all_to_all x1, blocking collectives, everywhere(): return lax.all_to_all(value, axes, 0, 0, tiled=True)  49.9 us
    ppermute x6, starting transfers between devices, fetch(): lax.ppermute(value, BLK, [(place(*role(*d)), place(*d)) for d in ALL])  23.5 us
    ppermute x4, starting transfers between devices, hand(): lax.ppermute(value, BLK, [(place(*d), place(*role(*d))) for d in ALL])  18.2 us
    ppermute x6, waiting for transfers between devices, fetch(): lax.ppermute(value, BLK, [(place(*role(*d)), place(*d)) for d in ALL])  17.5 us
    pallas_call x3, Pallas kernels, call(): pl.pallas_call(kernel, out_shape=[jax.ShapeDtypeStruct(shape, jnp.float32...  7.89 us
  transfers between devices with their start and end apart: 10, of which 4 were waited for; matrix products, arithmetic and copies ran while one was open for 0% of the time, Pallas kernels for 3%

profile of v8, /device:TPU:1, one launch (start us, length us, event | category | flops | bytes accessed | tf_op | source)
XLA Modules:
  0.0 121.1 jit_solution(16160485631163783737)
XLA Ops:
  0.0 1.2 slice.48
  1.2 5.2 %collective-permute-start.2 = (bf16[1040,256]{1,0:T(8,128)(2,1)S(1)}, bf16[1040,256]{1,0:T(8,128)(2,1)S(1)}, u32[]{:S(2)}, u32[]{:S(2)}) collective-permute-start(bf16[1040,256]{1,0:T(8,128)(2,1)S(1)} %slice.48), channel_id=1, source_target_pairs={{2,0},{3,1},{4,2},{5,3},{6,4},{7,5},{0,6},{1,7},{10,8},{11,9},{12,... | collective-permute-start | bytes 1597448 | tf_op jit(solution)/shard_map/ppermute | solution.py:100
  6.4 1.9 %collective-permute-start.1 = (bf16[2048,256]{1,0:T(8,128)(2,1)}, bf16[2048,256]{1,0:T(8,128)(2,1)S(1)}, u32[]{:S(2)}, u32[]{:S(2)}) collective-permute-start(bf16[2048,256]{1,0:T(8,128)(2,1)} %bitcast.2), channel_id=1, source_target_pairs={{6,0},{7,1},{0,2},{1,3},{3,4},{2,5},{5,6},{4,7},{15,8},{14,9},{9,1... | collective-permute-start | bytes 3145736 | tf_op jit(solution)/shard_map/ppermute | solution.py:100
  8.3 7.5 %collective-permute-start = (bf16[2048,256]{1,0:T(8,128)(2,1)}, bf16[2048,256]{1,0:T(8,128)(2,1)S(1)}, u32[]{:S(2)}, u32[]{:S(2)}) collective-permute-start(bf16[2048,256]{1,0:T(8,128)(2,1)} %bitcast.3), channel_id=1, source_target_pairs={{1,0},{0,1},{3,2},{2,3},{5,4},{4,5},{7,6},{6,7},{9,8},{8,9},{11,10... | collective-permute-start | bytes 3145736 | tf_op jit(solution)/shard_map/ppermute | solution.py:100
  16.0 2.9 %collective-permute-start.3 = (bf16[1024,256]{1,0:T(8,128)(2,1)S(1)}, bf16[1024,256]{1,0:T(8,128)(2,1)S(1)}, u32[]{:S(2)}, u32[]{:S(2)}) collective-permute-start(bf16[1024,256]{1,0:T(8,128)(2,1)S(1)} %fusion.1), channel_id=1, source_target_pairs={{2,0},{3,1},{4,2},{5,3},{6,4},{7,5},{0,6},{1,7},{10,8},{11,9},{12,... | collective-permute-start | bytes 1572872 | tf_op jit(solution)/shard_map/ppermute | solution.py:100
  18.8 0.0 collective-permute-done.2.x1
  18.8 4.1 %collective-permute-start.4 = (bf16[1040,256]{1,0:T(8,128)(2,1)S(1)}, bf16[1040,256]{1,0:T(8,128)(2,1)S(1)}, u32[]{:S(2)}, u32[]{:S(2)}) collective-permute-start(bf16[1040,256]{1,0:T(8,128)(2,1)S(1)} %collective-permute-done.2.x1), channel_id=1, source_target_pairs={{8,0},{9,1},{10,2},{11,3},{12,4},{13,5},{14,6},{15,7},{1,8},{0,9},... | collective-permute-start | bytes 1597448 | tf_op jit(solution)/shard_map/ppermute | solution.py:100
  22.9 8.5 %collective-permute-done.3.x2 = bf16[1024,256]{1,0:T(8,128)(2,1)S(1)} collective-permute-done((bf16[1024,256]{1,0:T(8,128)(2,1)S(1)}, bf16[1024,256]{1,0:T(8,128)(2,1)S(1)}, u32[]{:S(2)}, u32[]{:S(2)}) %collective-permute-start.3) | collective-permute-done | bytes 524320 | tf_op jit(solution)/shard_map/ppermute | solution.py:100
  31.4 1.9 %collective-permute-start.5 = (bf16[1024,256]{1,0:T(8,128)(2,1)S(1)}, bf16[1024,256]{1,0:T(8,128)(2,1)S(1)}, u32[]{:S(2)}, u32[]{:S(2)}) collective-permute-start(bf16[1024,256]{1,0:T(8,128)(2,1)S(1)} %collective-permute-done.3.x2), channel_id=1, source_target_pairs={{8,0},{9,1},{10,2},{11,3},{12,4},{13,5},{14,6},{15,7},{1,8},{0,9},... | collective-permute-start | bytes 1572872 | tf_op jit(solution)/shard_map/ppermute | solution.py:100
  33.3 0.0 collective-permute-done.b
  33.3 0.5 collective-permute-done.4.v1
  33.8 3.6 %shard_map.37 = (f32[32,40,256]{2,1,0:T(8,128)S(1)}, f32[8,256]{1,0:T(8,128)S(1)}) custom-call(s32[1,9]{1,0:T(1,128)S(1)} %copy-done.2, bf16[2048,256]{1,0:T(8,128)(2,1)S(1)} %bitcast.5, bf16[2048,256]{1,0:T(8,128)(2,1)S(1)} %collective-permute-done.b, bf16[2048,256]{1,0:T(8,128)(2,1)S(1)} %collective-permute-done.1.w, ...), custom_call_target="tpu_custom_call" | custom-call | flops 1342177280 | bytes 6053924 | tf_op jit(solution)/shard_map/pallas_call | solution.py:227
  37.4 8.5 %collective-permute-done.5.v2 = bf16[1024,256]{1,0:T(8,128)(2,1)S(1)} collective-permute-done((bf16[1024,256]{1,0:T(8,128)(2,1)S(1)}, bf16[1024,256]{1,0:T(8,128)(2,1)S(1)}, u32[]{:S(2)}, u32[]{:S(2)}) %collective-permute-start.5) | collective-permute-done | bytes 524320 | tf_op jit(solution)/shard_map/ppermute | solution.py:100
  45.9 2.9 %shard_map.38 = f32[32,72,256]{2,1,0:T(8,128)S(1)} custom-call(bf16[2048,256]{1,0:T(8,128)(2,1)S(1)} %bitcast.6, bf16[2048,256]{1,0:T(8,128)(2,1)S(1)} %collective-permute-done.b, bf16[2048,256]{1,0:T(8,128)(2,1)S(1)} %collective-permute-done.1.w, bf16[1040,256]{1,0:T(8,128)(2,1)S(1)} %collective-permute-done.2.x1, ...), custom_call_target="tpu_custom_call" | custom-call | flops 1073741824 | bytes 8937472 | tf_op jit(solution)/shard_map/pallas_call | solution.py:227
  48.9 0.2 convert_element_type.15
  49.1 49.9 %all_to_all.5 = f16[32,72,256]{2,1,0:T(8,128)(2,1)S(1)} all-to-all(f16[32,72,256]{2,1,0:T(8,128)(2,1)S(1)} %convert_element_type.15), channel_id=1, replica_groups=mesh['z'=8,'h'=4,'l'=2,'x'=4,'c'=2] {'z','h'}, dimensions={0} | all-to-all | bytes 2359296 | tf_op jit(solution)/shard_map/all_to_all | solution.py:243
  99.0 0.3 fusion.6
  99.3 0.3 multiply_reduce_fusion.refs_0_
  99.7 3.8 %collective-permute-start.6 = (f32[24,256]{1,0:T(8,128)S(1)}, f32[24,256]{1,0:T(8,128)S(1)}, u32[]{:S(2)}, u32[]{:S(2)}) collective-permute-start(f32[24,256]{1,0:T(8,128)S(1)} %pad_maximum_fusion), channel_id=1, source_target_pairs={{0,1},{1,0},{2,3},{3,2},{4,5},{5,4},{6,7},{7,6},{8,9},{9,8},{10,11... | collective-permute-start | bytes 73736 | tf_op jit(solution)/shard_map/ppermute | solution.py:104
  103.4 8.0 %collective-permute-start.8 = (f32[32,256]{1,0:T(8,128)S(1)}, f32[32,256]{1,0:T(8,128)S(1)}, u32[]{:S(2)}, u32[]{:S(2)}) collective-permute-start(f32[32,256]{1,0:T(8,128)S(1)} %get-tuple-element.14), channel_id=1, source_target_pairs={{0,10},{1,11},{2,12},{3,13},{4,14},{5,15},{6,8},{7,9},{8,3},{9,2},... | collective-permute-start | bytes 98312 | tf_op jit(solution)/shard_map/ppermute | solution.py:104
  111.4 3.2 %collective-permute-start.7 = (f32[32,256]{1,0:T(8,128)S(1)}, f32[32,256]{1,0:T(8,128)S(1)}, u32[]{:S(2)}, u32[]{:S(2)}) collective-permute-start(f32[32,256]{1,0:T(8,128)S(1)} %get-tuple-element.15), channel_id=1, source_target_pairs={{0,2},{1,3},{2,4},{3,5},{4,6},{5,7},{6,0},{7,1},{8,10},{9,11},{10,... | collective-permute-start | bytes 98312 | tf_op jit(solution)/shard_map/ppermute | solution.py:104
  114.6 3.3 %collective-permute-start.9 = (f32[16,256]{1,0:T(8,128)S(1)}, f32[16,256]{1,0:T(8,128)S(1)}, u32[]{:S(2)}, u32[]{:S(2)}) collective-permute-start(f32[16,256]{1,0:T(8,128)S(1)} %pad_maximum_fusion.1), channel_id=1, source_target_pairs={{0,6},{1,7},{2,0},{3,1},{4,3},{5,2},{6,5},{7,4},{8,15},{9,14},{10,... | collective-permute-start | bytes 49160 | tf_op jit(solution)/shard_map/ppermute | solution.py:104
  117.9 1.8 %collective-permute-done.9.refs_4_ = f32[16,256]{1,0:T(8,128)S(1)} collective-permute-done((f32[16,256]{1,0:T(8,128)S(1)}, f32[16,256]{1,0:T(8,128)S(1)}, u32[]{:S(2)}, u32[]{:S(2)}) %collective-permute-start.9) | collective-permute-done | bytes 16416 | tf_op jit(solution)/shard_map/ppermute | solution.py:104
  119.8 1.4 %shard_map.39 = f32[9,8,256]{2,1,0:T(8,128)} custom-call(s32[16,17]{1,0:T(8,128)S(1)} %copy-done.1, s32[1,9]{1,0:T(1,128)S(1)} %copy-done.2, f32[72,256]{1,0:T(8,128)S(1)} %multiply_reduce_fusion.refs_0_, f32[24,256]{1,0:T(8,128)S(1)} %collective-permute-done.6.refs_1_, f32[32,256]{1,0:T(8,128)S(1)} %collective-permute-done.7.refs_2_, ...), custom_call_target="tpu_custom_call" | custom-call | bytes 255076 | tf_op jit(solution)/shard_map/pallas_call | solution.py:227
  (17 shorter events, 0.1 us)
Async XLA Ops:
  0.0 15.8 %copy-start = (bf16[2,1024,256]{2,1,0:T(8,128)(2,1)S(1)}, bf16[2,1024,256]{2,1,0:T(8,128)(2,1)}, u32[]{:S(2)}) copy-start(bf16[2,1024,256]{2,1,0:T(8,128)(2,1)} %param.3) | copy-start | bytes 3145732
  0.0 15.9 %copy-start.2 = (s32[1,9]{1,0:T(1,128)S(1)}, s32[1,9]{1,0:T(1,128)}, u32[]{:S(2)}) copy-start(s32[1,9]{1,0:T(1,128)} %cols.3) | copy-start | bytes 112
  1.2 17.6 %collective-permute-start.2 = (bf16[1040,256]{1,0:T(8,128)(2,1)S(1)}, bf16[1040,256]{1,0:T(8,128)(2,1)S(1)}, u32[]{:S(2)}, u32[]{:S(2)}) collective-permute-start(bf16[1040,256]{1,0:T(8,128)(2,1)S(1)} %slice.48), channel_id=1, source_target_pairs={{2,0},{3,1},{4,2},{5,3},{6,4},{7,5},{0,6},{1,7},{10,8},{11,9},{12,... | collective-permute-start | bytes 1597448 | tf_op jit(solution)/shard_map/ppermute | solution.py:100
  6.4 26.9 %collective-permute-start.1 = (bf16[2048,256]{1,0:T(8,128)(2,1)}, bf16[2048,256]{1,0:T(8,128)(2,1)S(1)}, u32[]{:S(2)}, u32[]{:S(2)}) collective-permute-start(bf16[2048,256]{1,0:T(8,128)(2,1)} %bitcast.2), channel_id=1, source_target_pairs={{6,0},{7,1},{0,2},{1,3},{3,4},{2,5},{5,6},{4,7},{15,8},{14,9},{9,1... | collective-permute-start | bytes 3145736 | tf_op jit(solution)/shard_map/ppermute | solution.py:100
  8.3 25.0 %collective-permute-start = (bf16[2048,256]{1,0:T(8,128)(2,1)}, bf16[2048,256]{1,0:T(8,128)(2,1)S(1)}, u32[]{:S(2)}, u32[]{:S(2)}) collective-permute-start(bf16[2048,256]{1,0:T(8,128)(2,1)} %bitcast.3), channel_id=1, source_target_pairs={{1,0},{0,1},{3,2},{2,3},{5,4},{4,5},{7,6},{6,7},{9,8},{8,9},{11,10... | collective-permute-start | bytes 3145736 | tf_op jit(solution)/shard_map/ppermute | solution.py:100
  16.0 15.4 %collective-permute-start.3 = (bf16[1024,256]{1,0:T(8,128)(2,1)S(1)}, bf16[1024,256]{1,0:T(8,128)(2,1)S(1)}, u32[]{:S(2)}, u32[]{:S(2)}) collective-permute-start(bf16[1024,256]{1,0:T(8,128)(2,1)S(1)} %fusion.1), channel_id=1, source_target_pairs={{2,0},{3,1},{4,2},{5,3},{6,4},{7,5},{0,6},{1,7},{10,8},{11,9},{12,... | collective-permute-start | bytes 1572872 | tf_op jit(solution)/shard_map/ppermute | solution.py:100
  18.8 15.0 %collective-permute-start.4 = (bf16[1040,256]{1,0:T(8,128)(2,1)S(1)}, bf16[1040,256]{1,0:T(8,128)(2,1)S(1)}, u32[]{:S(2)}, u32[]{:S(2)}) collective-permute-start(bf16[1040,256]{1,0:T(8,128)(2,1)S(1)} %collective-permute-done.2.x1), channel_id=1, source_target_pairs={{8,0},{9,1},{10,2},{11,3},{12,4},{13,5},{14,6},{15,7},{1,8},{0,9},... | collective-permute-start | bytes 1597448 | tf_op jit(solution)/shard_map/ppermute | solution.py:100
  31.4 14.5 %collective-permute-start.5 = (bf16[1024,256]{1,0:T(8,128)(2,1)S(1)}, bf16[1024,256]{1,0:T(8,128)(2,1)S(1)}, u32[]{:S(2)}, u32[]{:S(2)}) collective-permute-start(bf16[1024,256]{1,0:T(8,128)(2,1)S(1)} %collective-permute-done.3.x2), channel_id=1, source_target_pairs={{8,0},{9,1},{10,2},{11,3},{12,4},{13,5},{14,6},{15,7},{1,8},{0,9},... | collective-permute-start | bytes 1572872 | tf_op jit(solution)/shard_map/ppermute | solution.py:100
  99.0 20.8 %copy-start.1 = (s32[16,17]{1,0:T(8,128)S(1)}, s32[16,17]{1,0:T(8,128)}, u32[]{:S(2)}) copy-start(s32[16,17]{1,0:T(8,128)} %constant.17.clone.table) | copy-start | bytes 3268
  99.7 20.1 %collective-permute-start.6 = (f32[24,256]{1,0:T(8,128)S(1)}, f32[24,256]{1,0:T(8,128)S(1)}, u32[]{:S(2)}, u32[]{:S(2)}) collective-permute-start(f32[24,256]{1,0:T(8,128)S(1)} %pad_maximum_fusion), channel_id=1, source_target_pairs={{0,1},{1,0},{2,3},{3,2},{4,5},{5,4},{6,7},{7,6},{8,9},{9,8},{10,11... | collective-permute-start | bytes 73736 | tf_op jit(solution)/shard_map/ppermute | solution.py:104
  103.4 16.3 %collective-permute-start.8 = (f32[32,256]{1,0:T(8,128)S(1)}, f32[32,256]{1,0:T(8,128)S(1)}, u32[]{:S(2)}, u32[]{:S(2)}) collective-permute-start(f32[32,256]{1,0:T(8,128)S(1)} %get-tuple-element.14), channel_id=1, source_target_pairs={{0,10},{1,11},{2,12},{3,13},{4,14},{5,15},{6,8},{7,9},{8,3},{9,2},... | collective-permute-start | bytes 98312 | tf_op jit(solution)/shard_map/ppermute | solution.py:104
  111.4 8.3 %collective-permute-start.7 = (f32[32,256]{1,0:T(8,128)S(1)}, f32[32,256]{1,0:T(8,128)S(1)}, u32[]{:S(2)}, u32[]{:S(2)}) collective-permute-start(f32[32,256]{1,0:T(8,128)S(1)} %get-tuple-element.15), channel_id=1, source_target_pairs={{0,2},{1,3},{2,4},{3,5},{4,6},{5,7},{6,0},{7,1},{8,10},{9,11},{10,... | collective-permute-start | bytes 98312 | tf_op jit(solution)/shard_map/ppermute | solution.py:104
  114.6 5.2 %collective-permute-start.9 = (f32[16,256]{1,0:T(8,128)S(1)}, f32[16,256]{1,0:T(8,128)S(1)}, u32[]{:S(2)}, u32[]{:S(2)}) collective-permute-start(f32[16,256]{1,0:T(8,128)S(1)} %pad_maximum_fusion.1), channel_id=1, source_target_pairs={{0,6},{1,7},{2,0},{3,1},{4,3},{5,2},{6,5},{7,4},{8,15},{9,14},{10,... | collective-permute-start | bytes 49160 | tf_op jit(solution)/shard_map/ppermute | solution.py:104

commit v9 on v8

--- a/solution.py
+++ b/solution.py
@@ -18,6 +18,7 @@
 STARTS = (0, 1040)
 HALF = W // 2
 SLAB = W // N_BULK
+FIRST, SECOND = 8, 4
 TOP = 14.0
 
 
@@ -179,26 +180,31 @@
     most[...] = jnp.broadcast_to(peak(out, slice(0, EARLY * SLAB)), (SLAB, W))
 
 
-def late_kernel(a, b, w, x1, x2, v1, v2, early, most, out):
+def late_kernel(a, b, w, x1, x2, v1, v2, early, most, out, late):
     a, b, w = parted(a), parted(b), parted(w)
     me = position()
     x, v = (x1, x2), (v1, v2)
-    settle(v, x, right(*me), writer(out, 5))
-    settle(v, a, own(*me), writer(out, 6))
-    settle(v, b, sib(*me), writer(out, 7))
-    settle(v, w, left(*me), writer(out, 8))
-
-    n = EARLY * SLAB
-    most = jnp.maximum(peak(out, slice(n, SLOTS * SLAB)), most[:1])
+    settle(v, x, right(*me), writer(late, 0))
+    settle(v, a, own(*me), writer(late, 1))
+    settle(v, b, sib(*me), writer(late, 2))
+    settle(v, w, left(*me), writer(late, 3))
+
+    most = jnp.maximum(peak(late, slice(0, LATE * SLAB)), most[:1])
     most = jnp.maximum(jnp.max(most, axis=1, keepdims=True), 1e-30)
     power = jnp.ceil(jnp.log2(jnp.broadcast_to(most, (SLAB, W))))
-    rank = lax.axis_index("z") * H + lax.axis_index("h")
-    spread = 1.0 + rank.astype(jnp.float32) / N_BULK
+    z, h = lax.axis_index("z"), lax.axis_index("h")
+    first = me[2] == 0
+    rank = jnp.where(first, z, h * 2 + (z & 1))
+    spread = 1.0 + rank.astype(jnp.float32) / FIRST
     by = (jnp.exp2(TOP - power) * spread)[:1]
-    for k in range(N_BULK):
-        out[k, :n] = early[k] * by
-        out[k, n:] = out[k, n:] * by
-        out[k, SLAB : 2 * SLAB, HALF:] = power[:, HALF:]
+    for z in range(Z):
+        for h in range(H):
+            k = z * H + h
+            to = jnp.where(first, z, h * 2 + z % 2)
+            at = pl.multiple_of(jnp.where(first, h, z // 2) * SLOTS * SLAB, SLAB)
+            out[to, pl.ds(at, EARLY * SLAB)] = early[k] * by
+            out[to, pl.ds(at + EARLY * SLAB, LATE * SLAB)] = late[k] * by
+            out[to, pl.ds(at + SLAB, SLAB), HALF:] = power[:, HALF:]
 
 
 def pick_kernel(table, cols, *refs):
@@ -239,14 +245,37 @@
     )(*ins)
 
 
-def everywhere(value, axes):
-    return lax.all_to_all(value, axes, 0, 0, tiled=True)
-
-
-def total(got):
-    spread = 1.0 + lax.broadcasted_iota(jnp.float32, (N_BULK, 1, 1), 0) / N_BULK
+def rounds():
+    first, second = [], []
+
+    def device(z, h, core, chip):
+        return ((z * H + h) * N_BLK) + chip * C + core
+
+    for chip in range(N_BLK // C):
+        for h in range(H):
+            first.append([device(z, h, 0, chip) for z in range(Z)])
+            for q in range(2):
+                second.append([device(z, h, 1, chip) for z in range(q, Z, 2)])
+        for z in range(Z):
+            second.append([device(z, h, 0, chip) for h in range(H)])
+        for z in range(0, Z, 2):
+            first.append([device(z + q, h, 1, chip) for h in range(H) for q in range(2)])
+    return first, second
+
+
+def exchange(value, groups):
+    return lax.all_to_all(
+        value, (*BULK, *BLK), 0, 0, axis_index_groups=groups, tiled=True
+    )
+
+
+def total(parts):
+    first, second = rounds()
+    got = exchange(parts.astype(jnp.float16), first)
+    spread = 1.0 + lax.broadcasted_iota(jnp.float32, (FIRST, 1, 1), 0) / FIRST
     power = got[:, SLAB : SLAB + 1, HALF : HALF + 1].astype(jnp.float32)
-    return (got.astype(jnp.float32) * (jnp.exp2(power - TOP) / spread)).sum(0)
+    got = (got.astype(jnp.float32) * (jnp.exp2(power - TOP) / spread)).sum(0)
+    return exchange(got.reshape(SECOND, SLOTS * SLAB, W), second).sum(0)
 
 
 def local(aux_factors, tile_cols):
@@ -265,9 +294,11 @@
 
     shapes = [(N_BULK, EARLY * SLAB, W), (SLAB, W)]
     early = call(early_kernel, shapes, 1, EARLY, tile_cols, a, b, w, *x, v[0])
-    shapes = [(N_BULK, SLOTS * SLAB, W)]
-    (parts,) = call(late_kernel, shapes, 0, LATE, a, b, w, *x, *v, *early)
-    done = total(everywhere(parts.astype(jnp.float16), BULK))
+    shapes = [(FIRST, SECOND * SLOTS * SLAB, W)]
+    scratch = [(N_BULK, LATE * SLAB, W)]
+    ins = (a, b, w, *x, *v, *early)
+    (parts,) = call(late_kernel, shapes, 0, LATE, *ins, scratch=scratch)
+    done = total(parts)
 
     parts = [done]
     for role, sent in MAIL:

time: 122 us -> 120 us (0.984)
  blocking collectives: 49.9 us -> 44 us
  starting transfers between devices: 41.7 us -> 45.5 us
    all_to_all x1 -> x2, blocking collectives: 49.9 us -> 44 us  [exchange(): lax.all_to_all(value, (*BULK, *BLK), 0, 0, axis_index_groups=groups, tile...]
    ppermute x4, starting transfers between devices: 18.2 us -> 22 us  [hand(): lax.ppermute(value, BLK, [(place(*d), place(*role(*d))) for d in ALL])]
where the time goes in v9:
time: 120 us; the launch traced here: 119 us
  starting transfers between devices  45.5 us (38%)
  blocking collectives  44 us (37%)
  waiting for transfers between devices  19.2 us (16%)
  Pallas kernels  7.94 us (7%)
  local copies, waits for them, and re-layouts  1.23 us (1%)
    all_to_all x2, blocking collectives, exchange(): lax.all_to_all(value, (*BULK, *BLK), 0, 0, axis_index_groups=groups, tile...  44 us
    ppermute x6, starting transfers between devices, fetch(): lax.ppermute(value, BLK, [(place(*role(*d)), place(*d)) for d in ALL])  23.5 us
    ppermute x4, starting transfers between devices, hand(): lax.ppermute(value, BLK, [(place(*d), place(*role(*d))) for d in ALL])  22 us
    ppermute x6, waiting for transfers between devices, fetch(): lax.ppermute(value, BLK, [(place(*role(*d)), place(*d)) for d in ALL])  17.5 us
    pallas_call x3, Pallas kernels, call(): pl.pallas_call(kernel, out_shape=[jax.ShapeDtypeStruct(shape, jnp.float32...  7.94 us
  transfers between devices with their start and end apart: 10, of which 4 were waited for; matrix products, arithmetic and copies ran while one was open for 0% of the time, Pallas kernels for 3%

profile of v9, /device:TPU:1, one launch (start us, length us, event | category | flops | bytes accessed | tf_op | source)
XLA Modules:
  0.0 118.9 jit_solution(12483681145985633412)
XLA Ops:
  0.0 1.2 slice.48
  1.2 5.2 %collective-permute-start.2 = (bf16[1040,256]{1,0:T(8,128)(2,1)S(1)}, bf16[1040,256]{1,0:T(8,128)(2,1)S(1)}, u32[]{:S(2)}, u32[]{:S(2)}) collective-permute-start(bf16[1040,256]{1,0:T(8,128)(2,1)S(1)} %slice.48), channel_id=1, source_target_pairs={{2,0},{3,1},{4,2},{5,3},{6,4},{7,5},{0,6},{1,7},{10,8},{11,9},{12,... | collective-permute-start | bytes 1597448 | tf_op jit(solution)/shard_map/ppermute | solution.py:101
  6.4 1.9 %collective-permute-start.1 = (bf16[2048,256]{1,0:T(8,128)(2,1)}, bf16[2048,256]{1,0:T(8,128)(2,1)S(1)}, u32[]{:S(2)}, u32[]{:S(2)}) collective-permute-start(bf16[2048,256]{1,0:T(8,128)(2,1)} %bitcast.3), channel_id=1, source_target_pairs={{6,0},{7,1},{0,2},{1,3},{3,4},{2,5},{5,6},{4,7},{15,8},{14,9},{9,1... | collective-permute-start | bytes 3145736 | tf_op jit(solution)/shard_map/ppermute | solution.py:101
  8.3 7.5 %collective-permute-start = (bf16[2048,256]{1,0:T(8,128)(2,1)}, bf16[2048,256]{1,0:T(8,128)(2,1)S(1)}, u32[]{:S(2)}, u32[]{:S(2)}) collective-permute-start(bf16[2048,256]{1,0:T(8,128)(2,1)} %bitcast.4), channel_id=1, source_target_pairs={{1,0},{0,1},{3,2},{2,3},{5,4},{4,5},{7,6},{6,7},{9,8},{8,9},{11,10... | collective-permute-start | bytes 3145736 | tf_op jit(solution)/shard_map/ppermute | solution.py:101
  16.0 2.9 %collective-permute-start.3 = (bf16[1024,256]{1,0:T(8,128)(2,1)S(1)}, bf16[1024,256]{1,0:T(8,128)(2,1)S(1)}, u32[]{:S(2)}, u32[]{:S(2)}) collective-permute-start(bf16[1024,256]{1,0:T(8,128)(2,1)S(1)} %fusion.1), channel_id=1, source_target_pairs={{2,0},{3,1},{4,2},{5,3},{6,4},{7,5},{0,6},{1,7},{10,8},{11,9},{12,... | collective-permute-start | bytes 1572872 | tf_op jit(solution)/shard_map/ppermute | solution.py:101
  18.8 0.0 collective-permute-done.2.x1
  18.8 4.1 %collective-permute-start.4 = (bf16[1040,256]{1,0:T(8,128)(2,1)S(1)}, bf16[1040,256]{1,0:T(8,128)(2,1)S(1)}, u32[]{:S(2)}, u32[]{:S(2)}) collective-permute-start(bf16[1040,256]{1,0:T(8,128)(2,1)S(1)} %collective-permute-done.2.x1), channel_id=1, source_target_pairs={{8,0},{9,1},{10,2},{11,3},{12,4},{13,5},{14,6},{15,7},{1,8},{0,9},... | collective-permute-start | bytes 1597448 | tf_op jit(solution)/shard_map/ppermute | solution.py:101
  22.9 8.5 %collective-permute-done.3.x2 = bf16[1024,256]{1,0:T(8,128)(2,1)S(1)} collective-permute-done((bf16[1024,256]{1,0:T(8,128)(2,1)S(1)}, bf16[1024,256]{1,0:T(8,128)(2,1)S(1)}, u32[]{:S(2)}, u32[]{:S(2)}) %collective-permute-start.3) | collective-permute-done | bytes 524320 | tf_op jit(solution)/shard_map/ppermute | solution.py:101
  31.4 1.9 %collective-permute-start.5 = (bf16[1024,256]{1,0:T(8,128)(2,1)S(1)}, bf16[1024,256]{1,0:T(8,128)(2,1)S(1)}, u32[]{:S(2)}, u32[]{:S(2)}) collective-permute-start(bf16[1024,256]{1,0:T(8,128)(2,1)S(1)} %collective-permute-done.3.x2), channel_id=1, source_target_pairs={{8,0},{9,1},{10,2},{11,3},{12,4},{13,5},{14,6},{15,7},{1,8},{0,9},... | collective-permute-start | bytes 1572872 | tf_op jit(solution)/shard_map/ppermute | solution.py:101
  33.3 0.5 collective-permute-done.4.v1
  33.8 3.6 %shard_map.37 = (f32[32,40,256]{2,1,0:T(8,128)S(1)}, f32[8,256]{1,0:T(8,128)S(1)}) custom-call(s32[1,9]{1,0:T(1,128)S(1)} %copy-done.2, bf16[2048,256]{1,0:T(8,128)(2,1)S(1)} %bitcast.6, bf16[2048,256]{1,0:T(8,128)(2,1)S(1)} %collective-permute-done.b, bf16[2048,256]{1,0:T(8,128)(2,1)S(1)} %collective-permute-done.1.w, ...), custom_call_target="tpu_custom_call" | custom-call | flops 1342177280 | bytes 6053924 | tf_op jit(solution)/shard_map/pallas_call | solution.py:233
  37.4 8.5 %collective-permute-done.5.v2 = bf16[1024,256]{1,0:T(8,128)(2,1)S(1)} collective-permute-done((bf16[1024,256]{1,0:T(8,128)(2,1)S(1)}, bf16[1024,256]{1,0:T(8,128)(2,1)S(1)}, u32[]{:S(2)}, u32[]{:S(2)}) %collective-permute-start.5) | collective-permute-done | bytes 524320 | tf_op jit(solution)/shard_map/ppermute | solution.py:101
  45.9 3.0 %shard_map.38 = f32[8,288,256]{2,1,0:T(8,128)S(1)} custom-call(bf16[2048,256]{1,0:T(8,128)(2,1)S(1)} %bitcast.7, bf16[2048,256]{1,0:T(8,128)(2,1)S(1)} %collective-permute-done.b, bf16[2048,256]{1,0:T(8,128)(2,1)S(1)} %collective-permute-done.1.w, bf16[1040,256]{1,0:T(8,128)(2,1)S(1)} %collective-permute-done.2.x1, ...), custom_call_target="tpu_custom_call" | custom-call | flops 1073741824 | bytes 8937472 | tf_op jit(solution)/shard_map/pallas_call | solution.py:233
  48.9 0.2 convert_element_type.15
  49.1 25.7 %all_to_all.10 = f16[8,288,256]{2,1,0:T(8,128)(2,1)S(1)} all-to-all(f16[8,288,256]{2,1,0:T(8,128)(2,1)S(1)} %convert_element_type.15), channel_id=1, replica_groups={{0,64,128,192,256,320,384,448},{16,80,144,208,272,336,400,464},{32,96,1..., dimensions={0} | all-to-all | bytes 2359296 | tf_op jit(solution)/shard_map/all_to_all | solution.py:267
  74.9 0.2 fusion.6
  75.0 0.3 multiply_reduce_fusion
  75.3 18.3 %all_to_all.11 = f32[4,72,256]{2,1,0:T(8,128)S(1)} all-to-all(f32[4,72,256]{2,1,0:T(8,128)S(1)} %bitcast.8), channel_id=1, replica_groups={{1,129,257,385},{65,193,321,449},{17,145,273,401},{81,209,337,465},{33,..., dimensions={0} | all-to-all | bytes 589824 | tf_op jit(solution)/shard_map/all_to_all | solution.py:267
  93.7 11.8 %collective-permute-start.6 = (f32[24,256]{1,0:T(8,128)S(1)}, f32[24,256]{1,0:T(8,128)S(1)}, u32[]{:S(2)}, u32[]{:S(2)}) collective-permute-start(f32[24,256]{1,0:T(8,128)S(1)} %pad_maximum_fusion), channel_id=1, source_target_pairs={{0,1},{1,0},{2,3},{3,2},{4,5},{5,4},{6,7},{7,6},{8,9},{9,8},{10,11... | collective-permute-start | bytes 73736 | tf_op jit(solution)/shard_map/ppermute | solution.py:105
  105.5 3.7 %collective-permute-start.8 = (f32[32,256]{1,0:T(8,128)S(1)}, f32[32,256]{1,0:T(8,128)S(1)}, u32[]{:S(2)}, u32[]{:S(2)}) collective-permute-start(f32[32,256]{1,0:T(8,128)S(1)} %get-tuple-element.14), channel_id=1, source_target_pairs={{0,10},{1,11},{2,12},{3,13},{4,14},{5,15},{6,8},{7,9},{8,3},{9,2},... | collective-permute-start | bytes 98312 | tf_op jit(solution)/shard_map/ppermute | solution.py:105
  109.2 3.1 %collective-permute-start.7 = (f32[32,256]{1,0:T(8,128)S(1)}, f32[32,256]{1,0:T(8,128)S(1)}, u32[]{:S(2)}, u32[]{:S(2)}) collective-permute-start(f32[32,256]{1,0:T(8,128)S(1)} %get-tuple-element.15), channel_id=1, source_target_pairs={{0,2},{1,3},{2,4},{3,5},{4,6},{5,7},{6,0},{7,1},{8,10},{9,11},{10,... | collective-permute-start | bytes 98312 | tf_op jit(solution)/shard_map/ppermute | solution.py:105
  112.4 3.4 %collective-permute-start.9 = (f32[16,256]{1,0:T(8,128)S(1)}, f32[16,256]{1,0:T(8,128)S(1)}, u32[]{:S(2)}, u32[]{:S(2)}) collective-permute-start(f32[16,256]{1,0:T(8,128)S(1)} %pad_maximum_fusion.1), channel_id=1, source_target_pairs={{0,6},{1,7},{2,0},{3,1},{4,3},{5,2},{6,5},{7,4},{8,15},{9,14},{10,... | collective-permute-start | bytes 49160 | tf_op jit(solution)/shard_map/ppermute | solution.py:105
  115.7 1.8 %collective-permute-done.9.refs_4_ = f32[16,256]{1,0:T(8,128)S(1)} collective-permute-done((f32[16,256]{1,0:T(8,128)S(1)}, f32[16,256]{1,0:T(8,128)S(1)}, u32[]{:S(2)}, u32[]{:S(2)}) %collective-permute-start.9) | collective-permute-done | bytes 16416 | tf_op jit(solution)/shard_map/ppermute | solution.py:105
  117.5 1.4 %shard_map.39 = f32[9,8,256]{2,1,0:T(8,128)} custom-call(s32[16,17]{1,0:T(8,128)S(1)} %copy-done.1, s32[1,9]{1,0:T(1,128)S(1)} %copy-done.2, f32[72,256]{1,0:T(8,128)S(1)} %reduce_sum.19.refs_0_, f32[24,256]{1,0:T(8,128)S(1)} %collective-permute-done.6.refs_1_, f32[32,256]{1,0:T(8,128)S(1)} %collective-permute-done.7.refs_2_, ...), custom_call_target="tpu_custom_call" | custom-call | bytes 255076 | tf_op jit(solution)/shard_map/pallas_call | solution.py:233
  (19 shorter events, 0.1 us)
Async XLA Ops:
  0.0 15.8 %copy-start = (bf16[2,1024,256]{2,1,0:T(8,128)(2,1)S(1)}, bf16[2,1024,256]{2,1,0:T(8,128)(2,1)}, u32[]{:S(2)}) copy-start(bf16[2,1024,256]{2,1,0:T(8,128)(2,1)} %param.3) | copy-start | bytes 3145732
  0.0 15.9 %copy-start.2 = (s32[1,9]{1,0:T(1,128)S(1)}, s32[1,9]{1,0:T(1,128)}, u32[]{:S(2)}) copy-start(s32[1,9]{1,0:T(1,128)} %cols.3) | copy-start | bytes 112
  1.2 17.6 %collective-permute-start.2 = (bf16[1040,256]{1,0:T(8,128)(2,1)S(1)}, bf16[1040,256]{1,0:T(8,128)(2,1)S(1)}, u32[]{:S(2)}, u32[]{:S(2)}) collective-permute-start(bf16[1040,256]{1,0:T(8,128)(2,1)S(1)} %slice.48), channel_id=1, source_target_pairs={{2,0},{3,1},{4,2},{5,3},{6,4},{7,5},{0,6},{1,7},{10,8},{11,9},{12,... | collective-permute-start | bytes 1597448 | tf_op jit(solution)/shard_map/ppermute | solution.py:101
  6.4 26.9 %collective-permute-start.1 = (bf16[2048,256]{1,0:T(8,128)(2,1)}, bf16[2048,256]{1,0:T(8,128)(2,1)S(1)}, u32[]{:S(2)}, u32[]{:S(2)}) collective-permute-start(bf16[2048,256]{1,0:T(8,128)(2,1)} %bitcast.3), channel_id=1, source_target_pairs={{6,0},{7,1},{0,2},{1,3},{3,4},{2,5},{5,6},{4,7},{15,8},{14,9},{9,1... | collective-permute-start | bytes 3145736 | tf_op jit(solution)/shard_map/ppermute | solution.py:101
  8.3 25.0 %collective-permute-start = (bf16[2048,256]{1,0:T(8,128)(2,1)}, bf16[2048,256]{1,0:T(8,128)(2,1)S(1)}, u32[]{:S(2)}, u32[]{:S(2)}) collective-permute-start(bf16[2048,256]{1,0:T(8,128)(2,1)} %bitcast.4), channel_id=1, source_target_pairs={{1,0},{0,1},{3,2},{2,3},{5,4},{4,5},{7,6},{6,7},{9,8},{8,9},{11,10... | collective-permute-start | bytes 3145736 | tf_op jit(solution)/shard_map/ppermute | solution.py:101
  16.0 15.4 %collective-permute-start.3 = (bf16[1024,256]{1,0:T(8,128)(2,1)S(1)}, bf16[1024,256]{1,0:T(8,128)(2,1)S(1)}, u32[]{:S(2)}, u32[]{:S(2)}) collective-permute-start(bf16[1024,256]{1,0:T(8,128)(2,1)S(1)} %fusion.1), channel_id=1, source_target_pairs={{2,0},{3,1},{4,2},{5,3},{6,4},{7,5},{0,6},{1,7},{10,8},{11,9},{12,... | collective-permute-start | bytes 1572872 | tf_op jit(solution)/shard_map/ppermute | solution.py:101
  18.8 15.0 %collective-permute-start.4 = (bf16[1040,256]{1,0:T(8,128)(2,1)S(1)}, bf16[1040,256]{1,0:T(8,128)(2,1)S(1)}, u32[]{:S(2)}, u32[]{:S(2)}) collective-permute-start(bf16[1040,256]{1,0:T(8,128)(2,1)S(1)} %collective-permute-done.2.x1), channel_id=1, source_target_pairs={{8,0},{9,1},{10,2},{11,3},{12,4},{13,5},{14,6},{15,7},{1,8},{0,9},... | collective-permute-start | bytes 1597448 | tf_op jit(solution)/shard_map/ppermute | solution.py:101
  31.4 14.5 %collective-permute-start.5 = (bf16[1024,256]{1,0:T(8,128)(2,1)S(1)}, bf16[1024,256]{1,0:T(8,128)(2,1)S(1)}, u32[]{:S(2)}, u32[]{:S(2)}) collective-permute-start(bf16[1024,256]{1,0:T(8,128)(2,1)S(1)} %collective-permute-done.3.x2), channel_id=1, source_target_pairs={{8,0},{9,1},{10,2},{11,3},{12,4},{13,5},{14,6},{15,7},{1,8},{0,9},... | collective-permute-start | bytes 1572872 | tf_op jit(solution)/shard_map/ppermute | solution.py:101
  75.0 42.5 %copy-start.1 = (s32[16,17]{1,0:T(8,128)S(1)}, s32[16,17]{1,0:T(8,128)}, u32[]{:S(2)}) copy-start(s32[16,17]{1,0:T(8,128)} %constant.17.clone.table) | copy-start | bytes 3268
  93.7 23.9 %collective-permute-start.6 = (f32[24,256]{1,0:T(8,128)S(1)}, f32[24,256]{1,0:T(8,128)S(1)}, u32[]{:S(2)}, u32[]{:S(2)}) collective-permute-start(f32[24,256]{1,0:T(8,128)S(1)} %pad_maximum_fusion), channel_id=1, source_target_pairs={{0,1},{1,0},{2,3},{3,2},{4,5},{5,4},{6,7},{7,6},{8,9},{9,8},{10,11... | collective-permute-start | bytes 73736 | tf_op jit(solution)/shard_map/ppermute | solution.py:105
  105.5 12.0 %collective-permute-start.8 = (f32[32,256]{1,0:T(8,128)S(1)}, f32[32,256]{1,0:T(8,128)S(1)}, u32[]{:S(2)}, u32[]{:S(2)}) collective-permute-start(f32[32,256]{1,0:T(8,128)S(1)} %get-tuple-element.14), channel_id=1, source_target_pairs={{0,10},{1,11},{2,12},{3,13},{4,14},{5,15},{6,8},{7,9},{8,3},{9,2},... | collective-permute-start | bytes 98312 | tf_op jit(solution)/shard_map/ppermute | solution.py:105
  109.2 8.3 %collective-permute-start.7 = (f32[32,256]{1,0:T(8,128)S(1)}, f32[32,256]{1,0:T(8,128)S(1)}, u32[]{:S(2)}, u32[]{:S(2)}) collective-permute-start(f32[32,256]{1,0:T(8,128)S(1)} %get-tuple-element.15), channel_id=1, source_target_pairs={{0,2},{1,3},{2,4},{3,5},{4,6},{5,7},{6,0},{7,1},{8,10},{9,11},{10,... | collective-permute-start | bytes 98312 | tf_op jit(solution)/shard_map/ppermute | solution.py:105
  112.4 5.2 %collective-permute-start.9 = (f32[16,256]{1,0:T(8,128)S(1)}, f32[16,256]{1,0:T(8,128)S(1)}, u32[]{:S(2)}, u32[]{:S(2)}) collective-permute-start(f32[16,256]{1,0:T(8,128)S(1)} %pad_maximum_fusion.1), channel_id=1, source_target_pairs={{0,6},{1,7},{2,0},{3,1},{4,3},{5,2},{6,5},{7,4},{8,15},{9,14},{10,... | collective-permute-start | bytes 49160 | tf_op jit(solution)/shard_map/ppermute | solution.py:105

commit v10 on v9

--- a/solution.py
+++ b/solution.py
@@ -126,9 +126,14 @@
     return tuple(block.at[pl.ds(at, n)] for at, n in zip(STARTS, PARTS))
 
 
-def owns(carrier, block):
+def owned(carrier, *blocks):
     row = carrier[-1][PARTS[-1] :].astype(jnp.float32)
-    return jnp.max(jnp.where(row == block.astype(jnp.float32), 1.0, 0.0)) > 0.5
+    bits = jnp.zeros_like(row)
+    for k, block in enumerate(blocks):
+        here = row == place(*block).astype(jnp.float32)
+        bits = jnp.where(here, float(1 << k), bits)
+    bits = jnp.sum(bits).astype(jnp.int32)
+    return [(bits >> k) & 1 == 1 for k in range(len(blocks))]
 
 
 def writer(out, slot):
@@ -138,9 +143,7 @@
     return put
 
 
-def settle(carrier, rhs, block, put):
-    kept = owns(carrier, place(*block))
-
+def settle(carrier, rhs, kept, put):
     @pl.when(kept)
     def _():
         put(product(carrier, rhs))
@@ -174,9 +177,9 @@
                 out[:, SLAB : 2 * SLAB, :HALF] = tile.reshape(N_BULK, SLAB, HALF)
 
     out[:, SLAB : 2 * SLAB, HALF:] = jnp.zeros((N_BULK, SLAB, HALF), jnp.float32)
-    settle(x, a, own(*me), writer(out, 2))
-    settle(x, b, sib(*me), writer(out, 3))
-    settle(x, w, left(*me), writer(out, 4))
+    kept = owned(x, own(*me), sib(*me), left(*me))
+    for slot, rhs in enumerate((a, b, w)):
+        settle(x, rhs, kept[slot], writer(out, 2 + slot))
     most[...] = jnp.broadcast_to(peak(out, slice(0, EARLY * SLAB)), (SLAB, W))
 
 
@@ -184,10 +187,9 @@
     a, b, w = parted(a), parted(b), parted(w)
     me = position()
     x, v = (x1, x2), (v1, v2)
-    settle(v, x, right(*me), writer(late, 0))
-    settle(v, a, own(*me), writer(late, 1))
-    settle(v, b, sib(*me), writer(late, 2))
-    settle(v, w, left(*me), writer(late, 3))
+    kept = owned(v, right(*me), own(*me), sib(*me), left(*me))
+    for slot, rhs in enumerate((x, a, b, w)):
+        settle(v, rhs, kept[slot], writer(late, slot))
 
     most = jnp.maximum(peak(late, slice(0, LATE * SLAB)), most[:1])
     most = jnp.maximum(jnp.max(most, axis=1, keepdims=True), 1e-30)

time: 120 us -> 119 us (level)
  no operation moved by 1% of the time
where the time goes in v10:
time: 119 us
  starting transfers between devices  45.5 us (38%)
  blocking collectives  44 us (37%)
  waiting for transfers between devices  19.5 us (16%)
  Pallas kernels  7.34 us (6%)
  local copies, waits for them, and re-layouts  1.23 us (1%)
    all_to_all x2, blocking collectives, exchange(): lax.all_to_all(value, (*BULK, *BLK), 0, 0, axis_index_groups=groups, tile...  44 us
    ppermute x6, starting transfers between devices, fetch(): lax.ppermute(value, BLK, [(place(*role(*d)), place(*d)) for d in ALL])  23.5 us
    ppermute x4, starting transfers between devices, hand(): lax.ppermute(value, BLK, [(place(*d), place(*role(*d))) for d in ALL])  22 us
    ppermute x6, waiting for transfers between devices, fetch(): lax.ppermute(value, BLK, [(place(*role(*d)), place(*d)) for d in ALL])  17.7 us
    pallas_call x3, Pallas kernels, call(): pl.pallas_call(kernel, out_shape=[jax.ShapeDtypeStruct(shape, jnp.float32...  7.34 us
  transfers between devices with their start and end apart: 10, of which 4 were waited for; matrix products, arithmetic and copies ran while one was open for 0% of the time, Pallas kernels for 3%

profile of v10, /device:TPU:1, one launch (start us, length us, event | category | flops | bytes accessed | tf_op | source)
XLA Modules:
  0.0 118.5 jit_solution(2118344448305017628)
XLA Ops:
  0.0 1.2 slice.48
  1.2 5.2 %collective-permute-start.2 = (bf16[1040,256]{1,0:T(8,128)(2,1)S(1)}, bf16[1040,256]{1,0:T(8,128)(2,1)S(1)}, u32[]{:S(2)}, u32[]{:S(2)}) collective-permute-start(bf16[1040,256]{1,0:T(8,128)(2,1)S(1)} %slice.48), channel_id=1, source_target_pairs={{2,0},{3,1},{4,2},{5,3},{6,4},{7,5},{0,6},{1,7},{10,8},{11,9},{12,... | collective-permute-start | bytes 1597448 | tf_op jit(solution)/shard_map/ppermute | solution.py:101
  6.4 1.9 %collective-permute-start.1 = (bf16[2048,256]{1,0:T(8,128)(2,1)}, bf16[2048,256]{1,0:T(8,128)(2,1)S(1)}, u32[]{:S(2)}, u32[]{:S(2)}) collective-permute-start(bf16[2048,256]{1,0:T(8,128)(2,1)} %bitcast.3), channel_id=1, source_target_pairs={{6,0},{7,1},{0,2},{1,3},{3,4},{2,5},{5,6},{4,7},{15,8},{14,9},{9,1... | collective-permute-start | bytes 3145736 | tf_op jit(solution)/shard_map/ppermute | solution.py:101
  8.3 7.5 %collective-permute-start = (bf16[2048,256]{1,0:T(8,128)(2,1)}, bf16[2048,256]{1,0:T(8,128)(2,1)S(1)}, u32[]{:S(2)}, u32[]{:S(2)}) collective-permute-start(bf16[2048,256]{1,0:T(8,128)(2,1)} %bitcast.4), channel_id=1, source_target_pairs={{1,0},{0,1},{3,2},{2,3},{5,4},{4,5},{7,6},{6,7},{9,8},{8,9},{11,10... | collective-permute-start | bytes 3145736 | tf_op jit(solution)/shard_map/ppermute | solution.py:101
  16.0 2.9 %collective-permute-start.3 = (bf16[1024,256]{1,0:T(8,128)(2,1)S(1)}, bf16[1024,256]{1,0:T(8,128)(2,1)S(1)}, u32[]{:S(2)}, u32[]{:S(2)}) collective-permute-start(bf16[1024,256]{1,0:T(8,128)(2,1)S(1)} %fusion.1), channel_id=1, source_target_pairs={{2,0},{3,1},{4,2},{5,3},{6,4},{7,5},{0,6},{1,7},{10,8},{11,9},{12,... | collective-permute-start | bytes 1572872 | tf_op jit(solution)/shard_map/ppermute | solution.py:101
  18.8 0.0 collective-permute-done.2.x1
  18.8 4.1 %collective-permute-start.4 = (bf16[1040,256]{1,0:T(8,128)(2,1)S(1)}, bf16[1040,256]{1,0:T(8,128)(2,1)S(1)}, u32[]{:S(2)}, u32[]{:S(2)}) collective-permute-start(bf16[1040,256]{1,0:T(8,128)(2,1)S(1)} %collective-permute-done.2.x1), channel_id=1, source_target_pairs={{8,0},{9,1},{10,2},{11,3},{12,4},{13,5},{14,6},{15,7},{1,8},{0,9},... | collective-permute-start | bytes 1597448 | tf_op jit(solution)/shard_map/ppermute | solution.py:101
  22.9 8.5 %collective-permute-done.3.x2 = bf16[1024,256]{1,0:T(8,128)(2,1)S(1)} collective-permute-done((bf16[1024,256]{1,0:T(8,128)(2,1)S(1)}, bf16[1024,256]{1,0:T(8,128)(2,1)S(1)}, u32[]{:S(2)}, u32[]{:S(2)}) %collective-permute-start.3) | collective-permute-done | bytes 524320 | tf_op jit(solution)/shard_map/ppermute | solution.py:101
  31.4 1.9 %collective-permute-start.5 = (bf16[1024,256]{1,0:T(8,128)(2,1)S(1)}, bf16[1024,256]{1,0:T(8,128)(2,1)S(1)}, u32[]{:S(2)}, u32[]{:S(2)}) collective-permute-start(bf16[1024,256]{1,0:T(8,128)(2,1)S(1)} %collective-permute-done.3.x2), channel_id=1, source_target_pairs={{8,0},{9,1},{10,2},{11,3},{12,4},{13,5},{14,6},{15,7},{1,8},{0,9},... | collective-permute-start | bytes 1572872 | tf_op jit(solution)/shard_map/ppermute | solution.py:101
  33.3 0.5 collective-permute-done.4.v1
  33.8 3.4 %shard_map.37 = (f32[32,40,256]{2,1,0:T(8,128)S(1)}, f32[8,256]{1,0:T(8,128)S(1)}) custom-call(s32[1,9]{1,0:T(1,128)S(1)} %copy-done.2, bf16[2048,256]{1,0:T(8,128)(2,1)S(1)} %bitcast.6, bf16[2048,256]{1,0:T(8,128)(2,1)S(1)} %collective-permute-done.b, bf16[2048,256]{1,0:T(8,128)(2,1)S(1)} %collective-permute-done.1.w, ...), custom_call_target="tpu_custom_call" | custom-call | flops 1342177280 | bytes 6053924 | tf_op jit(solution)/shard_map/pallas_call | solution.py:235
  37.2 8.7 %collective-permute-done.5.v2 = bf16[1024,256]{1,0:T(8,128)(2,1)S(1)} collective-permute-done((bf16[1024,256]{1,0:T(8,128)(2,1)S(1)}, bf16[1024,256]{1,0:T(8,128)(2,1)S(1)}, u32[]{:S(2)}, u32[]{:S(2)}) %collective-permute-start.5) | collective-permute-done | bytes 524320 | tf_op jit(solution)/shard_map/ppermute | solution.py:101
  45.9 2.6 %shard_map.38 = f32[8,288,256]{2,1,0:T(8,128)S(1)} custom-call(bf16[2048,256]{1,0:T(8,128)(2,1)S(1)} %bitcast.7, bf16[2048,256]{1,0:T(8,128)(2,1)S(1)} %collective-permute-done.b, bf16[2048,256]{1,0:T(8,128)(2,1)S(1)} %collective-permute-done.1.w, bf16[1040,256]{1,0:T(8,128)(2,1)S(1)} %collective-permute-done.2.x1, ...), custom_call_target="tpu_custom_call" | custom-call | flops 1073741824 | bytes 8937472 | tf_op jit(solution)/shard_map/pallas_call | solution.py:235
  48.5 0.2 convert_element_type.15
  48.8 25.7 %all_to_all.10 = f16[8,288,256]{2,1,0:T(8,128)(2,1)S(1)} all-to-all(f16[8,288,256]{2,1,0:T(8,128)(2,1)S(1)} %convert_element_type.15), channel_id=1, replica_groups={{0,64,128,192,256,320,384,448},{16,80,144,208,272,336,400,464},{32,96,1..., dimensions={0} | all-to-all | bytes 2359296 | tf_op jit(solution)/shard_map/all_to_all | solution.py:269
  74.5 0.2 fusion.6
  74.7 0.3 multiply_reduce_fusion
  75.0 18.3 %all_to_all.11 = f32[4,72,256]{2,1,0:T(8,128)S(1)} all-to-all(f32[4,72,256]{2,1,0:T(8,128)S(1)} %bitcast.8), channel_id=1, replica_groups={{1,129,257,385},{65,193,321,449},{17,145,273,401},{81,209,337,465},{33,..., dimensions={0} | all-to-all | bytes 589824 | tf_op jit(solution)/shard_map/all_to_all | solution.py:269
  93.3 11.8 %collective-permute-start.6 = (f32[24,256]{1,0:T(8,128)S(1)}, f32[24,256]{1,0:T(8,128)S(1)}, u32[]{:S(2)}, u32[]{:S(2)}) collective-permute-start(f32[24,256]{1,0:T(8,128)S(1)} %pad_maximum_fusion), channel_id=1, source_target_pairs={{0,1},{1,0},{2,3},{3,2},{4,5},{5,4},{6,7},{7,6},{8,9},{9,8},{10,11... | collective-permute-start | bytes 73736 | tf_op jit(solution)/shard_map/ppermute | solution.py:105
  105.1 3.7 %collective-permute-start.8 = (f32[32,256]{1,0:T(8,128)S(1)}, f32[32,256]{1,0:T(8,128)S(1)}, u32[]{:S(2)}, u32[]{:S(2)}) collective-permute-start(f32[32,256]{1,0:T(8,128)S(1)} %get-tuple-element.14), channel_id=1, source_target_pairs={{0,10},{1,11},{2,12},{3,13},{4,14},{5,15},{6,8},{7,9},{8,3},{9,2},... | collective-permute-start | bytes 98312 | tf_op jit(solution)/shard_map/ppermute | solution.py:105
  108.9 3.1 %collective-permute-start.7 = (f32[32,256]{1,0:T(8,128)S(1)}, f32[32,256]{1,0:T(8,128)S(1)}, u32[]{:S(2)}, u32[]{:S(2)}) collective-permute-start(f32[32,256]{1,0:T(8,128)S(1)} %get-tuple-element.15), channel_id=1, source_target_pairs={{0,2},{1,3},{2,4},{3,5},{4,6},{5,7},{6,0},{7,1},{8,10},{9,11},{10,... | collective-permute-start | bytes 98312 | tf_op jit(solution)/shard_map/ppermute | solution.py:105
  112.0 3.4 %collective-permute-start.9 = (f32[16,256]{1,0:T(8,128)S(1)}, f32[16,256]{1,0:T(8,128)S(1)}, u32[]{:S(2)}, u32[]{:S(2)}) collective-permute-start(f32[16,256]{1,0:T(8,128)S(1)} %pad_maximum_fusion.1), channel_id=1, source_target_pairs={{0,6},{1,7},{2,0},{3,1},{4,3},{5,2},{6,5},{7,4},{8,15},{9,14},{10,... | collective-permute-start | bytes 49160 | tf_op jit(solution)/shard_map/ppermute | solution.py:105
  115.4 1.8 %collective-permute-done.9.refs_4_ = f32[16,256]{1,0:T(8,128)S(1)} collective-permute-done((f32[16,256]{1,0:T(8,128)S(1)}, f32[16,256]{1,0:T(8,128)S(1)}, u32[]{:S(2)}, u32[]{:S(2)}) %collective-permute-start.9) | collective-permute-done | bytes 16416 | tf_op jit(solution)/shard_map/ppermute | solution.py:105
  117.2 1.4 %shard_map.39 = f32[9,8,256]{2,1,0:T(8,128)} custom-call(s32[16,17]{1,0:T(8,128)S(1)} %copy-done.1, s32[1,9]{1,0:T(1,128)S(1)} %copy-done.2, f32[72,256]{1,0:T(8,128)S(1)} %reduce_sum.19.refs_0_, f32[24,256]{1,0:T(8,128)S(1)} %collective-permute-done.6.refs_1_, f32[32,256]{1,0:T(8,128)S(1)} %collective-permute-done.7.refs_2_, ...), custom_call_target="tpu_custom_call" | custom-call | bytes 255076 | tf_op jit(solution)/shard_map/pallas_call | solution.py:235
  (19 shorter events, 0.1 us)
Async XLA Ops:
  0.0 15.8 %copy-start = (bf16[2,1024,256]{2,1,0:T(8,128)(2,1)S(1)}, bf16[2,1024,256]{2,1,0:T(8,128)(2,1)}, u32[]{:S(2)}) copy-start(bf16[2,1024,256]{2,1,0:T(8,128)(2,1)} %param.3) | copy-start | bytes 3145732
  0.0 15.9 %copy-start.2 = (s32[1,9]{1,0:T(1,128)S(1)}, s32[1,9]{1,0:T(1,128)}, u32[]{:S(2)}) copy-start(s32[1,9]{1,0:T(1,128)} %cols.3) | copy-start | bytes 112
  1.2 17.6 %collective-permute-start.2 = (bf16[1040,256]{1,0:T(8,128)(2,1)S(1)}, bf16[1040,256]{1,0:T(8,128)(2,1)S(1)}, u32[]{:S(2)}, u32[]{:S(2)}) collective-permute-start(bf16[1040,256]{1,0:T(8,128)(2,1)S(1)} %slice.48), channel_id=1, source_target_pairs={{2,0},{3,1},{4,2},{5,3},{6,4},{7,5},{0,6},{1,7},{10,8},{11,9},{12,... | collective-permute-start | bytes 1597448 | tf_op jit(solution)/shard_map/ppermute | solution.py:101
  6.4 26.9 %collective-permute-start.1 = (bf16[2048,256]{1,0:T(8,128)(2,1)}, bf16[2048,256]{1,0:T(8,128)(2,1)S(1)}, u32[]{:S(2)}, u32[]{:S(2)}) collective-permute-start(bf16[2048,256]{1,0:T(8,128)(2,1)} %bitcast.3), channel_id=1, source_target_pairs={{6,0},{7,1},{0,2},{1,3},{3,4},{2,5},{5,6},{4,7},{15,8},{14,9},{9,1... | collective-permute-start | bytes 3145736 | tf_op jit(solution)/shard_map/ppermute | solution.py:101
  8.3 25.0 %collective-permute-start = (bf16[2048,256]{1,0:T(8,128)(2,1)}, bf16[2048,256]{1,0:T(8,128)(2,1)S(1)}, u32[]{:S(2)}, u32[]{:S(2)}) collective-permute-start(bf16[2048,256]{1,0:T(8,128)(2,1)} %bitcast.4), channel_id=1, source_target_pairs={{1,0},{0,1},{3,2},{2,3},{5,4},{4,5},{7,6},{6,7},{9,8},{8,9},{11,10... | collective-permute-start | bytes 3145736 | tf_op jit(solution)/shard_map/ppermute | solution.py:101
  16.0 15.4 %collective-permute-start.3 = (bf16[1024,256]{1,0:T(8,128)(2,1)S(1)}, bf16[1024,256]{1,0:T(8,128)(2,1)S(1)}, u32[]{:S(2)}, u32[]{:S(2)}) collective-permute-start(bf16[1024,256]{1,0:T(8,128)(2,1)S(1)} %fusion.1), channel_id=1, source_target_pairs={{2,0},{3,1},{4,2},{5,3},{6,4},{7,5},{0,6},{1,7},{10,8},{11,9},{12,... | collective-permute-start | bytes 1572872 | tf_op jit(solution)/shard_map/ppermute | solution.py:101
  18.8 15.0 %collective-permute-start.4 = (bf16[1040,256]{1,0:T(8,128)(2,1)S(1)}, bf16[1040,256]{1,0:T(8,128)(2,1)S(1)}, u32[]{:S(2)}, u32[]{:S(2)}) collective-permute-start(bf16[1040,256]{1,0:T(8,128)(2,1)S(1)} %collective-permute-done.2.x1), channel_id=1, source_target_pairs={{8,0},{9,1},{10,2},{11,3},{12,4},{13,5},{14,6},{15,7},{1,8},{0,9},... | collective-permute-start | bytes 1597448 | tf_op jit(solution)/shard_map/ppermute | solution.py:101
  31.4 14.5 %collective-permute-start.5 = (bf16[1024,256]{1,0:T(8,128)(2,1)S(1)}, bf16[1024,256]{1,0:T(8,128)(2,1)S(1)}, u32[]{:S(2)}, u32[]{:S(2)}) collective-permute-start(bf16[1024,256]{1,0:T(8,128)(2,1)S(1)} %collective-permute-done.3.x2), channel_id=1, source_target_pairs={{8,0},{9,1},{10,2},{11,3},{12,4},{13,5},{14,6},{15,7},{1,8},{0,9},... | collective-permute-start | bytes 1572872 | tf_op jit(solution)/shard_map/ppermute | solution.py:101
  74.7 42.5 %copy-start.1 = (s32[16,17]{1,0:T(8,128)S(1)}, s32[16,17]{1,0:T(8,128)}, u32[]{:S(2)}) copy-start(s32[16,17]{1,0:T(8,128)} %constant.17.clone.table) | copy-start | bytes 3268
  93.3 23.9 %collective-permute-start.6 = (f32[24,256]{1,0:T(8,128)S(1)}, f32[24,256]{1,0:T(8,128)S(1)}, u32[]{:S(2)}, u32[]{:S(2)}) collective-permute-start(f32[24,256]{1,0:T(8,128)S(1)} %pad_maximum_fusion), channel_id=1, source_target_pairs={{0,1},{1,0},{2,3},{3,2},{4,5},{5,4},{6,7},{7,6},{8,9},{9,8},{10,11... | collective-permute-start | bytes 73736 | tf_op jit(solution)/shard_map/ppermute | solution.py:105
  105.1 12.0 %collective-permute-start.8 = (f32[32,256]{1,0:T(8,128)S(1)}, f32[32,256]{1,0:T(8,128)S(1)}, u32[]{:S(2)}, u32[]{:S(2)}) collective-permute-start(f32[32,256]{1,0:T(8,128)S(1)} %get-tuple-element.14), channel_id=1, source_target_pairs={{0,10},{1,11},{2,12},{3,13},{4,14},{5,15},{6,8},{7,9},{8,3},{9,2},... | collective-permute-start | bytes 98312 | tf_op jit(solution)/shard_map/ppermute | solution.py:105
  108.9 8.3 %collective-permute-start.7 = (f32[32,256]{1,0:T(8,128)S(1)}, f32[32,256]{1,0:T(8,128)S(1)}, u32[]{:S(2)}, u32[]{:S(2)}) collective-permute-start(f32[32,256]{1,0:T(8,128)S(1)} %get-tuple-element.15), channel_id=1, source_target_pairs={{0,2},{1,3},{2,4},{3,5},{4,6},{5,7},{6,0},{7,1},{8,10},{9,11},{10,... | collective-permute-start | bytes 98312 | tf_op jit(solution)/shard_map/ppermute | solution.py:105
  112.0 5.2 %collective-permute-start.9 = (f32[16,256]{1,0:T(8,128)S(1)}, f32[16,256]{1,0:T(8,128)S(1)}, u32[]{:S(2)}, u32[]{:S(2)}) collective-permute-start(f32[16,256]{1,0:T(8,128)S(1)} %pad_maximum_fusion.1), channel_id=1, source_target_pairs={{0,6},{1,7},{2,0},{3,1},{4,3},{5,2},{6,5},{7,4},{8,15},{9,14},{10,... | collective-permute-start | bytes 49160 | tf_op jit(solution)/shard_map/ppermute | solution.py:105

commit v11 on v10

--- a/solution.py
+++ b/solution.py
@@ -115,19 +115,21 @@
     )
 
 
+def partial(p, q, k):
+    n = PARTS[k]
+    return dot(p[k][:n], q[k][:n])
+
+
 def product(p, q):
-    tile = dot(p[0][...], q[0][...])
-    for u, v, n in zip(p[1:], q[1:], PARTS[1:]):
-        tile += dot(u[:n], v[:n])
-    return tile
+    return partial(p, q, 0) + partial(p, q, 1)
 
 
 def parted(block):
     return tuple(block.at[pl.ds(at, n)] for at, n in zip(STARTS, PARTS))
 
 
-def owned(carrier, *blocks):
-    row = carrier[-1][PARTS[-1] :].astype(jnp.float32)
+def owned(row, *blocks):
+    row = row.astype(jnp.float32)
     bits = jnp.zeros_like(row)
     for k, block in enumerate(blocks):
         here = row == place(*block).astype(jnp.float32)
@@ -136,6 +138,13 @@
     return [(bits >> k) & 1 == 1 for k in range(len(blocks))]
 
 
+def listed(cols, block):
+    here = cols[0, 0] == place(*block)
+    for j in range(1, SLOTS):
+        here = jnp.logical_or(here, cols[0, j] == place(*block))
+    return here
+
+
 def writer(out, slot):
     def put(tile):
         out[:, pl.ds(slot * SLAB, SLAB)] = tile.reshape(N_BULK, SLAB, W)
@@ -143,30 +152,27 @@
     return put
 
 
-def settle(carrier, rhs, kept, put):
+def settle(lhs, rhs, kept, put, of=product):
     @pl.when(kept)
     def _():
-        put(product(carrier, rhs))
+        put(of(lhs, rhs))
 
     @pl.when(jnp.logical_not(kept))
     def _():
-        put(product(rhs, carrier))
+        put(of(rhs, lhs))
 
 
 def peak(out, rows):
     return jnp.max(jnp.max(jnp.abs(out[:, rows]), axis=0), axis=0, keepdims=True)
 
 
-def early_kernel(cols, a, b, w, x1, x2, v1, out, most):
-    del v1
+def early_kernel(cols, a, b, w, x1, x2, v1, out, most, begun, flags):
+    rows = [r[end:] for r, end in ((b, K), (w, K), (x2, PARTS[1]))]
     a, b, w = parted(a), parted(b), parted(w)
     me = position()
-    x = (x1, x2)
+    x, v = (x1, x2), (v1,)
     writer(out, 0)(product(a, a))
-    other = place(*sib(*me))
-    mine = cols[0, 0] == other
-    for j in range(1, SLOTS):
-        mine = jnp.logical_or(mine, cols[0, j] == other)
+    mine = listed(cols, sib(*me))
     for core in range(C):
         lanes = pl.ds(core * HALF, HALF)
         for kept, lhs, rhs in ((True, a, b), (False, b, a)):
@@ -177,19 +183,28 @@
                 out[:, SLAB : 2 * SLAB, :HALF] = tile.reshape(N_BULK, SLAB, HALF)
 
     out[:, SLAB : 2 * SLAB, HALF:] = jnp.zeros((N_BULK, SLAB, HALF), jnp.float32)
-    kept = owned(x, own(*me), sib(*me), left(*me))
+    by_b, by_w = (owned(row, diag(*me))[0] for row in rows[:2])
+    *kept, by_x = owned(rows[2], own(*me), sib(*me), left(*me), diag(*me))
     for slot, rhs in enumerate((a, b, w)):
         settle(x, rhs, kept[slot], writer(out, 2 + slot))
+    others = (by_x, listed(cols, diag(*me)), by_b, by_w)
+    for slot, (rhs, theirs) in enumerate(zip((x, a, b, w), others)):
+        flags[0, slot] = theirs.astype(jnp.int32)
+        settle(rhs, v, theirs, writer(begun, slot), lambda p, q: partial(p, q, 0))
     most[...] = jnp.broadcast_to(peak(out, slice(0, EARLY * SLAB)), (SLAB, W))
 
 
-def late_kernel(a, b, w, x1, x2, v1, v2, early, most, out, late):
+def late_kernel(flags, a, b, w, x2, v2, early, most, begun, out, late):
     a, b, w = parted(a), parted(b), parted(w)
     me = position()
-    x, v = (x1, x2), (v1, v2)
-    kept = owned(v, right(*me), own(*me), sib(*me), left(*me))
+    x, v = (None, x2), (None, v2)
     for slot, rhs in enumerate((x, a, b, w)):
-        settle(v, rhs, kept[slot], writer(late, slot))
+        rows = pl.ds(slot * SLAB, SLAB)
+
+        def put(tile):
+            late[:, rows] = begun[:, rows] + tile.reshape(N_BULK, SLAB, W)
+
+        settle(rhs, v, flags[0, slot] == 1, put, lambda p, q: partial(p, q, 1))
 
     most = jnp.maximum(peak(late, slice(0, LATE * SLAB)), most[:1])
     most = jnp.maximum(jnp.max(most, axis=1, keepdims=True), 1e-30)
@@ -228,15 +243,20 @@
         out[j] = jnp.where(b >= 0, slab, 0.0)
 
 
-def call(kernel, shapes, n_smem, n_tiles, *ins, scratch=()):
+def call(kernel, shapes, n_smem, n_tiles, *ins, scratch=(), n_flags=0):
     vmem = pl.BlockSpec(memory_space=pltpu.VMEM)
     smem = pl.BlockSpec(memory_space=pltpu.SMEM)
     size = sum(int(np.prod(shape)) for shape in shapes)
+    out_shape = [jax.ShapeDtypeStruct(shape, jnp.float32) for shape in shapes]
+    out_specs = [vmem] * len(shapes)
+    if n_flags:
+        out_shape.append(jax.ShapeDtypeStruct((1, n_flags), jnp.int32))
+        out_specs.append(smem)
     return pl.pallas_call(
         kernel,
-        out_shape=[jax.ShapeDtypeStruct(shape, jnp.float32) for shape in shapes],
+        out_shape=out_shape,
         in_specs=[smem] * n_smem + [vmem] * (len(ins) - n_smem),
-        out_specs=[vmem] * len(shapes),
+        out_specs=out_specs,
         scratch_shapes=[pltpu.VMEM(shape, jnp.float32) for shape in scratch],
         compiler_params=pltpu.CompilerParams(vmem_limit_bytes=24 * 2**20),
         cost_estimate=pl.CostEstimate(
@@ -287,19 +307,19 @@
         constant_values=-2,
     )
     a = aux_factors.reshape(K, W)
-    send = [a[at : at + n] for at, n in zip(STARTS, PARTS)]
-    send[-1] = jnp.concatenate([send[-1], row])
-    x = [fetch(part, right) for part in send]
-    w = fetch(a, left)
-    b = fetch(a, sib)
+    rowed = jnp.concatenate([a, row])
+    x = [fetch(part, right) for part in (a[: PARTS[0]], rowed[PARTS[0] :])]
+    w = fetch(rowed, left)
+    b = fetch(rowed, sib)
     v = [fetch(part, diag_via) for part in x]
 
-    shapes = [(N_BULK, EARLY * SLAB, W), (SLAB, W)]
-    early = call(early_kernel, shapes, 1, EARLY, tile_cols, a, b, w, *x, v[0])
+    late_shape = (N_BULK, LATE * SLAB, W)
+    shapes = [(N_BULK, EARLY * SLAB, W), (SLAB, W), late_shape]
+    ins = (tile_cols, a, b, w, *x, v[0])
+    *early, flags = call(early_kernel, shapes, 1, EARLY, *ins, n_flags=LATE)
     shapes = [(FIRST, SECOND * SLOTS * SLAB, W)]
-    scratch = [(N_BULK, LATE * SLAB, W)]
-    ins = (a, b, w, *x, *v, *early)
-    (parts,) = call(late_kernel, shapes, 0, LATE, *ins, scratch=scratch)
+    ins = (flags, a, b, w, x[1], v[1], *early)
+    (parts,) = call(late_kernel, shapes, 1, LATE, *ins, scratch=[late_shape])
     done = total(parts)
 
     parts = [done]

time: 119 us -> 118 us (level)
  waiting for transfers between devices: 19.5 us -> 17.5 us
  Pallas kernels: 7.34 us -> 9.13 us
    pallas_call x3, Pallas kernels: 7.34 us -> 9.13 us  [call(): pl.pallas_call(kernel, out_shape=out_shape, in_specs=[smem] * n_smem + [v...]
    ppermute x6, waiting for transfers between devices: 17.7 us -> 16.3 us  [fetch(): lax.ppermute(value, BLK, [(place(*role(*d)), place(*d)) for d in ALL])]
  transfers between devices with their start and end apart: 10 -> 10, of which waited for: 4 -> 4; matrix products, arithmetic and copies ran while one was open for 0% -> 1% of each run, Pallas kernels for 3% -> 5%
where the time goes in v11:
time: 118 us
  starting transfers between devices  45.1 us (38%)
  blocking collectives  43.1 us (37%)
  waiting for transfers between devices  17.5 us (15%)
  Pallas kernels  9.13 us (8%)
  other arithmetic  1.44 us (1%)
  local copies, waits for them, and re-layouts  1.23 us (1%)
    all_to_all x2, blocking collectives, exchange(): lax.all_to_all(value, (*BULK, *BLK), 0, 0, axis_index_groups=groups, tile...  43.1 us
    ppermute x6, starting transfers between devices, fetch(): lax.ppermute(value, BLK, [(place(*role(*d)), place(*d)) for d in ALL])  22.8 us
    ppermute x4, starting transfers between devices, hand(): lax.ppermute(value, BLK, [(place(*d), place(*role(*d))) for d in ALL])  22.3 us
    ppermute x6, waiting for transfers between devices, fetch(): lax.ppermute(value, BLK, [(place(*role(*d)), place(*d)) for d in ALL])  16.3 us
    pallas_call x3, Pallas kernels, call(): pl.pallas_call(kernel, out_shape=out_shape, in_specs=[smem] * n_smem + [v...  9.13 us
  transfers between devices with their start and end apart: 10, of which 4 were waited for; matrix products, arithmetic and copies ran while one was open for 1% of the time, Pallas kernels for 5%

profile of v11, /device:TPU:1, one launch (start us, length us, event | category | flops | bytes accessed | tf_op | source)
XLA Modules:
  0.0 117.7 jit_solution(17658392029436267951)
XLA Ops:
  0.0 1.2 slice.48
  1.2 5.2 %collective-permute-start.2 = (bf16[1040,256]{1,0:T(8,128)(2,1)S(1)}, bf16[1040,256]{1,0:T(8,128)(2,1)S(1)}, u32[]{:S(2)}, u32[]{:S(2)}) collective-permute-start(bf16[1040,256]{1,0:T(8,128)(2,1)S(1)} %slice.48), channel_id=1, source_target_pairs={{2,0},{3,1},{4,2},{5,3},{6,4},{7,5},{0,6},{1,7},{10,8},{11,9},{12,... | collective-permute-start | bytes 1597448 | tf_op jit(solution)/shard_map/ppermute | solution.py:101
  6.4 0.7 convert_element_type.14
  7.1 1.9 %collective-permute-start.1 = (bf16[2064,256]{1,0:T(8,128)(2,1)S(1)}, bf16[2064,256]{1,0:T(8,128)(2,1)S(1)}, u32[]{:S(2)}, u32[]{:S(2)}) collective-permute-start(bf16[2064,256]{1,0:T(8,128)(2,1)S(1)} %fusion.1), channel_id=1, source_target_pairs={{6,0},{7,1},{0,2},{1,3},{3,4},{2,5},{5,6},{4,7},{15,8},{14,9},{9,1... | collective-permute-start | bytes 3170312 | tf_op jit(solution)/shard_map/ppermute | solution.py:101
  9.1 7.5 %collective-permute-start = (bf16[2064,256]{1,0:T(8,128)(2,1)S(1)}, bf16[2064,256]{1,0:T(8,128)(2,1)S(1)}, u32[]{:S(2)}, u32[]{:S(2)}) collective-permute-start(bf16[2064,256]{1,0:T(8,128)(2,1)S(1)} %fusion.1), channel_id=1, source_target_pairs={{1,0},{0,1},{3,2},{2,3},{5,4},{4,5},{7,6},{6,7},{9,8},{8,9},{11,10... | collective-permute-start | bytes 3170312 | tf_op jit(solution)/shard_map/ppermute | solution.py:101
  16.6 2.9 %collective-permute-start.3 = (bf16[1024,256]{1,0:T(8,128)(2,1)S(1)}, bf16[1024,256]{1,0:T(8,128)(2,1)S(1)}, u32[]{:S(2)}, u32[]{:S(2)}) collective-permute-start(bf16[1024,256]{1,0:T(8,128)(2,1)S(1)} %slice.49), channel_id=1, source_target_pairs={{2,0},{3,1},{4,2},{5,3},{6,4},{7,5},{0,6},{1,7},{10,8},{11,9},{12,... | collective-permute-start | bytes 1572872 | tf_op jit(solution)/shard_map/ppermute | solution.py:101
  19.5 3.4 %collective-permute-start.4 = (bf16[1040,256]{1,0:T(8,128)(2,1)S(1)}, bf16[1040,256]{1,0:T(8,128)(2,1)S(1)}, u32[]{:S(2)}, u32[]{:S(2)}) collective-permute-start(bf16[1040,256]{1,0:T(8,128)(2,1)S(1)} %collective-permute-done.2.x1), channel_id=1, source_target_pairs={{8,0},{9,1},{10,2},{11,3},{12,4},{13,5},{14,6},{15,7},{1,8},{0,9},... | collective-permute-start | bytes 1597448 | tf_op jit(solution)/shard_map/ppermute | solution.py:101
  22.9 9.1 %collective-permute-done.3.x2 = bf16[1024,256]{1,0:T(8,128)(2,1)S(1)} collective-permute-done((bf16[1024,256]{1,0:T(8,128)(2,1)S(1)}, bf16[1024,256]{1,0:T(8,128)(2,1)S(1)}, u32[]{:S(2)}, u32[]{:S(2)}) %collective-permute-start.3) | collective-permute-done | bytes 524320 | tf_op jit(solution)/shard_map/ppermute | solution.py:101
  32.0 1.9 %collective-permute-start.5 = (bf16[1024,256]{1,0:T(8,128)(2,1)S(1)}, bf16[1024,256]{1,0:T(8,128)(2,1)S(1)}, u32[]{:S(2)}, u32[]{:S(2)}) collective-permute-start(bf16[1024,256]{1,0:T(8,128)(2,1)S(1)} %collective-permute-done.3.x2), channel_id=1, source_target_pairs={{8,0},{9,1},{10,2},{11,3},{12,4},{13,5},{14,6},{15,7},{1,8},{0,9},... | collective-permute-start | bytes 1572872 | tf_op jit(solution)/shard_map/ppermute | solution.py:101
  34.0 0.8 collective-permute-done.4.v1
  34.8 5.5 %shard_map.37 = (f32[32,40,256]{2,1,0:T(8,128)S(1)}, f32[8,256]{1,0:T(8,128)S(1)}, f32[32,32,256]{2,1,0:T(8,128)S(1)}, s32[1,4]{1,0:T(1,128)S(1)}) custom-call(s32[1,9]{1,0:T(1,128)S(1)} %copy-done.2, bf16[2048,256]{1,0:T(8,128)(2,1)S(1)} %bitcast.4, bf16[2064,256]{1,0:T(8,128)(2,1)S(1)} %collective-permute-done.b, ...), custom_call_target="tpu_custom_call" | custom-call | flops 1342177280 | bytes 7118884 | tf_op jit(solution)/shard_map/pallas_call | solution.py:255
  40.2 6.3 %collective-permute-done.5.v2 = bf16[1024,256]{1,0:T(8,128)(2,1)S(1)} collective-permute-done((bf16[1024,256]{1,0:T(8,128)(2,1)S(1)}, bf16[1024,256]{1,0:T(8,128)(2,1)S(1)}, u32[]{:S(2)}, u32[]{:S(2)}) %collective-permute-start.5) | collective-permute-done | bytes 524320 | tf_op jit(solution)/shard_map/ppermute | solution.py:101
  46.6 2.3 %shard_map.38 = f32[8,288,256]{2,1,0:T(8,128)S(1)} custom-call(s32[1,4]{1,0:T(1,128)S(1)} %get-tuple-element.9.flags, bf16[2048,256]{1,0:T(8,128)(2,1)S(1)} %bitcast.5, bf16[2064,256]{1,0:T(8,128)(2,1)S(1)} %collective-permute-done.b, bf16[2064,256]{1,0:T(8,128)(2,1)S(1)} %collective-permute-done.1.w, bf16[1024,256]{1,0:T(8,128)(2,1)S(1)} %collective-permute-done.3.x2, ...), custom_call_target="tpu_custom_call" | custom-call | flops 1073741824 | bytes 8937488 | tf_op jit(solution)/shard_map/pallas_call | solution.py:255
  48.9 0.2 convert_element_type.15
  49.1 25.0 %all_to_all.10 = f16[8,288,256]{2,1,0:T(8,128)(2,1)S(1)} all-to-all(f16[8,288,256]{2,1,0:T(8,128)(2,1)S(1)} %convert_element_type.15), channel_id=1, replica_groups={{0,64,128,192,256,320,384,448},{16,80,144,208,272,336,400,464},{32,96,1..., dimensions={0} | all-to-all | bytes 2359296 | tf_op jit(solution)/shard_map/all_to_all | solution.py:289
  74.2 0.2 fusion.6
  74.3 0.3 multiply_reduce_fusion
  74.6 18.1 %all_to_all.11 = f32[4,72,256]{2,1,0:T(8,128)S(1)} all-to-all(f32[4,72,256]{2,1,0:T(8,128)S(1)} %bitcast.6), channel_id=1, replica_groups={{1,129,257,385},{65,193,321,449},{17,145,273,401},{81,209,337,465},{33,..., dimensions={0} | all-to-all | bytes 589824 | tf_op jit(solution)/shard_map/all_to_all | solution.py:289
  92.8 11.6 %collective-permute-start.6 = (f32[24,256]{1,0:T(8,128)S(1)}, f32[24,256]{1,0:T(8,128)S(1)}, u32[]{:S(2)}, u32[]{:S(2)}) collective-permute-start(f32[24,256]{1,0:T(8,128)S(1)} %pad_maximum_fusion), channel_id=1, source_target_pairs={{0,1},{1,0},{2,3},{3,2},{4,5},{5,4},{6,7},{7,6},{8,9},{9,8},{10,11... | collective-permute-start | bytes 73736 | tf_op jit(solution)/shard_map/ppermute | solution.py:105
  104.4 4.1 %collective-permute-start.8 = (f32[32,256]{1,0:T(8,128)S(1)}, f32[32,256]{1,0:T(8,128)S(1)}, u32[]{:S(2)}, u32[]{:S(2)}) collective-permute-start(f32[32,256]{1,0:T(8,128)S(1)} %get-tuple-element.18), channel_id=1, source_target_pairs={{0,10},{1,11},{2,12},{3,13},{4,14},{5,15},{6,8},{7,9},{8,3},{9,2},... | collective-permute-start | bytes 98312 | tf_op jit(solution)/shard_map/ppermute | solution.py:105
  108.6 3.1 %collective-permute-start.7 = (f32[32,256]{1,0:T(8,128)S(1)}, f32[32,256]{1,0:T(8,128)S(1)}, u32[]{:S(2)}, u32[]{:S(2)}) collective-permute-start(f32[32,256]{1,0:T(8,128)S(1)} %get-tuple-element.19), channel_id=1, source_target_pairs={{0,2},{1,3},{2,4},{3,5},{4,6},{5,7},{6,0},{7,1},{8,10},{9,11},{10,... | collective-permute-start | bytes 98312 | tf_op jit(solution)/shard_map/ppermute | solution.py:105
  111.7 3.4 %collective-permute-start.9 = (f32[16,256]{1,0:T(8,128)S(1)}, f32[16,256]{1,0:T(8,128)S(1)}, u32[]{:S(2)}, u32[]{:S(2)}) collective-permute-start(f32[16,256]{1,0:T(8,128)S(1)} %pad_maximum_fusion.1), channel_id=1, source_target_pairs={{0,6},{1,7},{2,0},{3,1},{4,3},{5,2},{6,5},{7,4},{8,15},{9,14},{10,... | collective-permute-start | bytes 49160 | tf_op jit(solution)/shard_map/ppermute | solution.py:105
  115.1 1.3 %collective-permute-done.9.refs_4_ = f32[16,256]{1,0:T(8,128)S(1)} collective-permute-done((f32[16,256]{1,0:T(8,128)S(1)}, f32[16,256]{1,0:T(8,128)S(1)}, u32[]{:S(2)}, u32[]{:S(2)}) %collective-permute-start.9) | collective-permute-done | bytes 16416 | tf_op jit(solution)/shard_map/ppermute | solution.py:105
  116.4 1.4 %shard_map.39 = f32[9,8,256]{2,1,0:T(8,128)} custom-call(s32[16,17]{1,0:T(8,128)S(1)} %copy-done.1, s32[1,9]{1,0:T(1,128)S(1)} %copy-done.2, f32[72,256]{1,0:T(8,128)S(1)} %reduce_sum.19.refs_0_, f32[24,256]{1,0:T(8,128)S(1)} %collective-permute-done.6.refs_1_, f32[32,256]{1,0:T(8,128)S(1)} %collective-permute-done.7.refs_2_, ...), custom_call_target="tpu_custom_call" | custom-call | bytes 255076 | tf_op jit(solution)/shard_map/pallas_call | solution.py:255
  (19 shorter events, 0.2 us)
Async XLA Ops:
  0.0 7.1 %copy-start = (bf16[2,1024,256]{2,1,0:T(8,128)(2,1)S(1)}, bf16[2,1024,256]{2,1,0:T(8,128)(2,1)}, u32[]{:S(2)}) copy-start(bf16[2,1024,256]{2,1,0:T(8,128)(2,1)} %param.3) | copy-start | bytes 3145732
  1.2 18.3 %collective-permute-start.2 = (bf16[1040,256]{1,0:T(8,128)(2,1)S(1)}, bf16[1040,256]{1,0:T(8,128)(2,1)S(1)}, u32[]{:S(2)}, u32[]{:S(2)}) collective-permute-start(bf16[1040,256]{1,0:T(8,128)(2,1)S(1)} %slice.48), channel_id=1, source_target_pairs={{2,0},{3,1},{4,2},{5,3},{6,4},{7,5},{0,6},{1,7},{10,8},{11,9},{12,... | collective-permute-start | bytes 1597448 | tf_op jit(solution)/shard_map/ppermute | solution.py:101
  7.1 27.7 %copy-start.2 = (s32[1,9]{1,0:T(1,128)S(1)}, s32[1,9]{1,0:T(1,128)}, u32[]{:S(2)}) copy-start(s32[1,9]{1,0:T(1,128)} %cols.3) | copy-start | bytes 112
  7.1 26.8 %collective-permute-start.1 = (bf16[2064,256]{1,0:T(8,128)(2,1)S(1)}, bf16[2064,256]{1,0:T(8,128)(2,1)S(1)}, u32[]{:S(2)}, u32[]{:S(2)}) collective-permute-start(bf16[2064,256]{1,0:T(8,128)(2,1)S(1)} %fusion.1), channel_id=1, source_target_pairs={{6,0},{7,1},{0,2},{1,3},{3,4},{2,5},{5,6},{4,7},{15,8},{14,9},{9,1... | collective-permute-start | bytes 3170312 | tf_op jit(solution)/shard_map/ppermute | solution.py:101
  9.1 24.9 %collective-permute-start = (bf16[2064,256]{1,0:T(8,128)(2,1)S(1)}, bf16[2064,256]{1,0:T(8,128)(2,1)S(1)}, u32[]{:S(2)}, u32[]{:S(2)}) collective-permute-start(bf16[2064,256]{1,0:T(8,128)(2,1)S(1)} %fusion.1), channel_id=1, source_target_pairs={{1,0},{0,1},{3,2},{2,3},{5,4},{4,5},{7,6},{6,7},{9,8},{8,9},{11,10... | collective-permute-start | bytes 3170312 | tf_op jit(solution)/shard_map/ppermute | solution.py:101
  16.6 15.4 %collective-permute-start.3 = (bf16[1024,256]{1,0:T(8,128)(2,1)S(1)}, bf16[1024,256]{1,0:T(8,128)(2,1)S(1)}, u32[]{:S(2)}, u32[]{:S(2)}) collective-permute-start(bf16[1024,256]{1,0:T(8,128)(2,1)S(1)} %slice.49), channel_id=1, source_target_pairs={{2,0},{3,1},{4,2},{5,3},{6,4},{7,5},{0,6},{1,7},{10,8},{11,9},{12,... | collective-permute-start | bytes 1572872 | tf_op jit(solution)/shard_map/ppermute | solution.py:101
  19.5 15.3 %collective-permute-start.4 = (bf16[1040,256]{1,0:T(8,128)(2,1)S(1)}, bf16[1040,256]{1,0:T(8,128)(2,1)S(1)}, u32[]{:S(2)}, u32[]{:S(2)}) collective-permute-start(bf16[1040,256]{1,0:T(8,128)(2,1)S(1)} %collective-permute-done.2.x1), channel_id=1, source_target_pairs={{8,0},{9,1},{10,2},{11,3},{12,4},{13,5},{14,6},{15,7},{1,8},{0,9},... | collective-permute-start | bytes 1597448 | tf_op jit(solution)/shard_map/ppermute | solution.py:101
  32.0 14.5 %collective-permute-start.5 = (bf16[1024,256]{1,0:T(8,128)(2,1)S(1)}, bf16[1024,256]{1,0:T(8,128)(2,1)S(1)}, u32[]{:S(2)}, u32[]{:S(2)}) collective-permute-start(bf16[1024,256]{1,0:T(8,128)(2,1)S(1)} %collective-permute-done.3.x2), channel_id=1, source_target_pairs={{8,0},{9,1},{10,2},{11,3},{12,4},{13,5},{14,6},{15,7},{1,8},{0,9},... | collective-permute-start | bytes 1572872 | tf_op jit(solution)/shard_map/ppermute | solution.py:101
  74.3 42.0 %copy-start.1 = (s32[16,17]{1,0:T(8,128)S(1)}, s32[16,17]{1,0:T(8,128)}, u32[]{:S(2)}) copy-start(s32[16,17]{1,0:T(8,128)} %constant.17.clone.table) | copy-start | bytes 3268
  92.8 23.6 %collective-permute-start.6 = (f32[24,256]{1,0:T(8,128)S(1)}, f32[24,256]{1,0:T(8,128)S(1)}, u32[]{:S(2)}, u32[]{:S(2)}) collective-permute-start(f32[24,256]{1,0:T(8,128)S(1)} %pad_maximum_fusion), channel_id=1, source_target_pairs={{0,1},{1,0},{2,3},{3,2},{4,5},{5,4},{6,7},{7,6},{8,9},{9,8},{10,11... | collective-permute-start | bytes 73736 | tf_op jit(solution)/shard_map/ppermute | solution.py:105
  104.4 11.9 %collective-permute-start.8 = (f32[32,256]{1,0:T(8,128)S(1)}, f32[32,256]{1,0:T(8,128)S(1)}, u32[]{:S(2)}, u32[]{:S(2)}) collective-permute-start(f32[32,256]{1,0:T(8,128)S(1)} %get-tuple-element.18), channel_id=1, source_target_pairs={{0,10},{1,11},{2,12},{3,13},{4,14},{5,15},{6,8},{7,9},{8,3},{9,2},... | collective-permute-start | bytes 98312 | tf_op jit(solution)/shard_map/ppermute | solution.py:105
  108.6 7.8 %collective-permute-start.7 = (f32[32,256]{1,0:T(8,128)S(1)}, f32[32,256]{1,0:T(8,128)S(1)}, u32[]{:S(2)}, u32[]{:S(2)}) collective-permute-start(f32[32,256]{1,0:T(8,128)S(1)} %get-tuple-element.19), channel_id=1, source_target_pairs={{0,2},{1,3},{2,4},{3,5},{4,6},{5,7},{6,0},{7,1},{8,10},{9,11},{10,... | collective-permute-start | bytes 98312 | tf_op jit(solution)/shard_map/ppermute | solution.py:105
  111.7 4.6 %collective-permute-start.9 = (f32[16,256]{1,0:T(8,128)S(1)}, f32[16,256]{1,0:T(8,128)S(1)}, u32[]{:S(2)}, u32[]{:S(2)}) collective-permute-start(f32[16,256]{1,0:T(8,128)S(1)} %pad_maximum_fusion.1), channel_id=1, source_target_pairs={{0,6},{1,7},{2,0},{3,1},{4,3},{5,2},{6,5},{7,4},{8,15},{9,14},{10,... | collective-permute-start | bytes 49160 | tf_op jit(solution)/shard_map/ppermute | solution.py:105

commit v12 on v11

--- a/solution.py
+++ b/solution.py
@@ -210,7 +210,7 @@
     most = jnp.maximum(jnp.max(most, axis=1, keepdims=True), 1e-30)
     power = jnp.ceil(jnp.log2(jnp.broadcast_to(most, (SLAB, W))))
     z, h = lax.axis_index("z"), lax.axis_index("h")
-    first = me[2] == 0
+    first = me[2] == 1
     rank = jnp.where(first, z, h * 2 + (z & 1))
     spread = 1.0 + rank.astype(jnp.float32) / FIRST
     by = (jnp.exp2(TOP - power) * spread)[:1]
@@ -275,13 +275,13 @@
 
     for chip in range(N_BLK // C):
         for h in range(H):
-            first.append([device(z, h, 0, chip) for z in range(Z)])
+            first.append([device(z, h, 1, chip) for z in range(Z)])
             for q in range(2):
-                second.append([device(z, h, 1, chip) for z in range(q, Z, 2)])
+                second.append([device(z, h, 0, chip) for z in range(q, Z, 2)])
         for z in range(Z):
-            second.append([device(z, h, 0, chip) for h in range(H)])
+            second.append([device(z, h, 1, chip) for h in range(H)])
         for z in range(0, Z, 2):
-            first.append([device(z + q, h, 1, chip) for h in range(H) for q in range(2)])
+            first.append([device(z + q, h, 0, chip) for h in range(H) for q in range(2)])
     return first, second
 
 

time: 118 us -> 116 us (0.983)
  starting transfers between devices: 45.1 us -> 35.4 us
  blocking collectives: 43.1 us -> 49.8 us
    ppermute x4, starting transfers between devices: 22.3 us -> 12.5 us  [hand(): lax.ppermute(value, BLK, [(place(*d), place(*role(*d))) for d in ALL])]
    all_to_all x2, blocking collectives: 43.1 us -> 49.8 us  [exchange(): lax.all_to_all(value, (*BULK, *BLK), 0, 0, axis_index_groups=groups, tile...]
where the time goes in v12:
time: 116 us; the launch traced here: 115 us
  blocking collectives  49.8 us (43%)
  starting transfers between devices  35.4 us (31%)
  waiting for transfers between devices  17.6 us (15%)
  Pallas kernels  9.12 us (8%)
  other arithmetic  1.44 us (1%)
  local copies, waits for them, and re-layouts  1.23 us (1%)
    all_to_all x2, blocking collectives, exchange(): lax.all_to_all(value, (*BULK, *BLK), 0, 0, axis_index_groups=groups, tile...  49.8 us
    ppermute x6, starting transfers between devices, fetch(): lax.ppermute(value, BLK, [(place(*role(*d)), place(*d)) for d in ALL])  22.8 us
    ppermute x6, waiting for transfers between devices, fetch(): lax.ppermute(value, BLK, [(place(*role(*d)), place(*d)) for d in ALL])  16.3 us
    ppermute x4, starting transfers between devices, hand(): lax.ppermute(value, BLK, [(place(*d), place(*role(*d))) for d in ALL])  12.5 us
    pallas_call x3, Pallas kernels, call(): pl.pallas_call(kernel, out_shape=out_shape, in_specs=[smem] * n_smem + [v...  9.12 us
  transfers between devices with their start and end apart: 10, of which 4 were waited for; matrix products, arithmetic and copies ran while one was open for 1% of the time, Pallas kernels for 5%

profile of v12, /device:TPU:1, one launch (start us, length us, event | category | flops | bytes accessed | tf_op | source)
XLA Modules:
  0.0 114.7 jit_solution(8793629588359685973)
XLA Ops:
  0.0 1.2 %slice.48 = bf16[1040,256]{1,0:T(8,128)(2,1)S(1)} slice(bf16[2048,256]{1,0:T(8,128)(2,1)} %bitcast.2), slice={[0:1040], [0:256]} | slice | bytes 1064960 | tf_op jit(solution)/shard_map/slice | solution.py:311
  1.2 5.2 %collective-permute-start.2 = (bf16[1040,256]{1,0:T(8,128)(2,1)S(1)}, bf16[1040,256]{1,0:T(8,128)(2,1)S(1)}, u32[]{:S(2)}, u32[]{:S(2)}) collective-permute-start(bf16[1040,256]{1,0:T(8,128)(2,1)S(1)} %slice.48), channel_id=1, source_target_pairs={{2,0},{3,1},{4,2},{5,3},{6,4},{7,5},{0,6},{1,7},{10,8},{11,9},{12,... | collective-permute-start | bytes 1597448 | tf_op jit(solution)/shard_map/ppermute | solution.py:101
  6.4 0.7 convert_element_type.14
  7.1 1.9 %collective-permute-start.1 = (bf16[2064,256]{1,0:T(8,128)(2,1)S(1)}, bf16[2064,256]{1,0:T(8,128)(2,1)S(1)}, u32[]{:S(2)}, u32[]{:S(2)}) collective-permute-start(bf16[2064,256]{1,0:T(8,128)(2,1)S(1)} %fusion.1), channel_id=1, source_target_pairs={{6,0},{7,1},{0,2},{1,3},{3,4},{2,5},{5,6},{4,7},{15,8},{14,9},{9,1... | collective-permute-start | bytes 3170312 | tf_op jit(solution)/shard_map/ppermute | solution.py:101
  9.1 7.5 %collective-permute-start = (bf16[2064,256]{1,0:T(8,128)(2,1)S(1)}, bf16[2064,256]{1,0:T(8,128)(2,1)S(1)}, u32[]{:S(2)}, u32[]{:S(2)}) collective-permute-start(bf16[2064,256]{1,0:T(8,128)(2,1)S(1)} %fusion.1), channel_id=1, source_target_pairs={{1,0},{0,1},{3,2},{2,3},{5,4},{4,5},{7,6},{6,7},{9,8},{8,9},{11,10... | collective-permute-start | bytes 3170312 | tf_op jit(solution)/shard_map/ppermute | solution.py:101
  16.6 2.9 %collective-permute-start.3 = (bf16[1024,256]{1,0:T(8,128)(2,1)S(1)}, bf16[1024,256]{1,0:T(8,128)(2,1)S(1)}, u32[]{:S(2)}, u32[]{:S(2)}) collective-permute-start(bf16[1024,256]{1,0:T(8,128)(2,1)S(1)} %slice.49), channel_id=1, source_target_pairs={{2,0},{3,1},{4,2},{5,3},{6,4},{7,5},{0,6},{1,7},{10,8},{11,9},{12,... | collective-permute-start | bytes 1572872 | tf_op jit(solution)/shard_map/ppermute | solution.py:101
  19.5 3.4 %collective-permute-start.4 = (bf16[1040,256]{1,0:T(8,128)(2,1)S(1)}, bf16[1040,256]{1,0:T(8,128)(2,1)S(1)}, u32[]{:S(2)}, u32[]{:S(2)}) collective-permute-start(bf16[1040,256]{1,0:T(8,128)(2,1)S(1)} %collective-permute-done.2.x1), channel_id=1, source_target_pairs={{8,0},{9,1},{10,2},{11,3},{12,4},{13,5},{14,6},{15,7},{1,8},{0,9},... | collective-permute-start | bytes 1597448 | tf_op jit(solution)/shard_map/ppermute | solution.py:101
  22.9 9.1 %collective-permute-done.3.x2 = bf16[1024,256]{1,0:T(8,128)(2,1)S(1)} collective-permute-done((bf16[1024,256]{1,0:T(8,128)(2,1)S(1)}, bf16[1024,256]{1,0:T(8,128)(2,1)S(1)}, u32[]{:S(2)}, u32[]{:S(2)}) %collective-permute-start.3) | collective-permute-done | bytes 524320 | tf_op jit(solution)/shard_map/ppermute | solution.py:101
  32.0 1.9 %collective-permute-start.5 = (bf16[1024,256]{1,0:T(8,128)(2,1)S(1)}, bf16[1024,256]{1,0:T(8,128)(2,1)S(1)}, u32[]{:S(2)}, u32[]{:S(2)}) collective-permute-start(bf16[1024,256]{1,0:T(8,128)(2,1)S(1)} %collective-permute-done.3.x2), channel_id=1, source_target_pairs={{8,0},{9,1},{10,2},{11,3},{12,4},{13,5},{14,6},{15,7},{1,8},{0,9},... | collective-permute-start | bytes 1572872 | tf_op jit(solution)/shard_map/ppermute | solution.py:101
  34.0 0.8 collective-permute-done.4.v1
  34.8 5.4 %shard_map.37 = (f32[32,40,256]{2,1,0:T(8,128)S(1)}, f32[8,256]{1,0:T(8,128)S(1)}, f32[32,32,256]{2,1,0:T(8,128)S(1)}, s32[1,4]{1,0:T(1,128)S(1)}) custom-call(s32[1,9]{1,0:T(1,128)S(1)} %copy-done.2, bf16[2048,256]{1,0:T(8,128)(2,1)S(1)} %bitcast.4, bf16[2064,256]{1,0:T(8,128)(2,1)S(1)} %collective-permute-done.b, ...), custom_call_target="tpu_custom_call" | custom-call | flops 1342177280 | bytes 7118884 | tf_op jit(solution)/shard_map/pallas_call | solution.py:255
  40.2 6.4 %collective-permute-done.5.v2 = bf16[1024,256]{1,0:T(8,128)(2,1)S(1)} collective-permute-done((bf16[1024,256]{1,0:T(8,128)(2,1)S(1)}, bf16[1024,256]{1,0:T(8,128)(2,1)S(1)}, u32[]{:S(2)}, u32[]{:S(2)}) %collective-permute-start.5) | collective-permute-done | bytes 524320 | tf_op jit(solution)/shard_map/ppermute | solution.py:101
  46.6 2.3 %shard_map.38 = f32[8,288,256]{2,1,0:T(8,128)S(1)} custom-call(s32[1,4]{1,0:T(1,128)S(1)} %get-tuple-element.9.flags, bf16[2048,256]{1,0:T(8,128)(2,1)S(1)} %bitcast.5, bf16[2064,256]{1,0:T(8,128)(2,1)S(1)} %collective-permute-done.b, bf16[2064,256]{1,0:T(8,128)(2,1)S(1)} %collective-permute-done.1.w, bf16[1024,256]{1,0:T(8,128)(2,1)S(1)} %collective-permute-done.3.x2, ...), custom_call_target="tpu_custom_call" | custom-call | flops 1073741824 | bytes 8937488 | tf_op jit(solution)/shard_map/pallas_call | solution.py:255
  48.9 0.2 convert_element_type.15
  49.1 33.5 %all_to_all.10 = f16[8,288,256]{2,1,0:T(8,128)(2,1)S(1)} all-to-all(f16[8,288,256]{2,1,0:T(8,128)(2,1)S(1)} %convert_element_type.15), channel_id=1, replica_groups={{1,65,129,193,257,321,385,449},{17,81,145,209,273,337,401,465},{33,97,1..., dimensions={0} | all-to-all | bytes 2359296 | tf_op jit(solution)/shard_map/all_to_all | solution.py:289
  82.7 0.2 fusion.6
  82.8 0.3 multiply_reduce_fusion
  83.1 16.2 %all_to_all.11 = f32[4,72,256]{2,1,0:T(8,128)S(1)} all-to-all(f32[4,72,256]{2,1,0:T(8,128)S(1)} %bitcast.6), channel_id=1, replica_groups={{0,128,256,384},{64,192,320,448},{16,144,272,400},{80,208,336,464},{32,..., dimensions={0} | all-to-all | bytes 589824 | tf_op jit(solution)/shard_map/all_to_all | solution.py:289
  99.4 1.9 %collective-permute-start.6 = (f32[24,256]{1,0:T(8,128)S(1)}, f32[24,256]{1,0:T(8,128)S(1)}, u32[]{:S(2)}, u32[]{:S(2)}) collective-permute-start(f32[24,256]{1,0:T(8,128)S(1)} %pad_maximum_fusion), channel_id=1, source_target_pairs={{0,1},{1,0},{2,3},{3,2},{4,5},{5,4},{6,7},{7,6},{8,9},{9,8},{10,11... | collective-permute-start | bytes 73736 | tf_op jit(solution)/shard_map/ppermute | solution.py:105
  101.4 4.1 %collective-permute-start.8 = (f32[32,256]{1,0:T(8,128)S(1)}, f32[32,256]{1,0:T(8,128)S(1)}, u32[]{:S(2)}, u32[]{:S(2)}) collective-permute-start(f32[32,256]{1,0:T(8,128)S(1)} %get-tuple-element.18), channel_id=1, source_target_pairs={{0,10},{1,11},{2,12},{3,13},{4,14},{5,15},{6,8},{7,9},{8,3},{9,2},... | collective-permute-start | bytes 98312 | tf_op jit(solution)/shard_map/ppermute | solution.py:105
  105.5 3.1 %collective-permute-start.7 = (f32[32,256]{1,0:T(8,128)S(1)}, f32[32,256]{1,0:T(8,128)S(1)}, u32[]{:S(2)}, u32[]{:S(2)}) collective-permute-start(f32[32,256]{1,0:T(8,128)S(1)} %get-tuple-element.19), channel_id=1, source_target_pairs={{0,2},{1,3},{2,4},{3,5},{4,6},{5,7},{6,0},{7,1},{8,10},{9,11},{10,... | collective-permute-start | bytes 98312 | tf_op jit(solution)/shard_map/ppermute | solution.py:105
  108.6 3.4 %collective-permute-start.9 = (f32[16,256]{1,0:T(8,128)S(1)}, f32[16,256]{1,0:T(8,128)S(1)}, u32[]{:S(2)}, u32[]{:S(2)}) collective-permute-start(f32[16,256]{1,0:T(8,128)S(1)} %pad_maximum_fusion.1), channel_id=1, source_target_pairs={{0,6},{1,7},{2,0},{3,1},{4,3},{5,2},{6,5},{7,4},{8,15},{9,14},{10,... | collective-permute-start | bytes 49160 | tf_op jit(solution)/shard_map/ppermute | solution.py:105
  112.0 1.3 %collective-permute-done.9.refs_4_ = f32[16,256]{1,0:T(8,128)S(1)} collective-permute-done((f32[16,256]{1,0:T(8,128)S(1)}, f32[16,256]{1,0:T(8,128)S(1)}, u32[]{:S(2)}, u32[]{:S(2)}) %collective-permute-start.9) | collective-permute-done | bytes 16416 | tf_op jit(solution)/shard_map/ppermute | solution.py:105
  113.3 1.4 %shard_map.39 = f32[9,8,256]{2,1,0:T(8,128)} custom-call(s32[16,17]{1,0:T(8,128)S(1)} %copy-done.1, s32[1,9]{1,0:T(1,128)S(1)} %copy-done.2, f32[72,256]{1,0:T(8,128)S(1)} %reduce_sum.19.refs_0_, f32[24,256]{1,0:T(8,128)S(1)} %collective-permute-done.6.refs_1_, f32[32,256]{1,0:T(8,128)S(1)} %collective-permute-done.7.refs_2_, ...), custom_call_target="tpu_custom_call" | custom-call | bytes 255076 | tf_op jit(solution)/shard_map/pallas_call | solution.py:255
  (19 shorter events, 0.2 us)
Async XLA Ops:
  0.0 7.1 %copy-start = (bf16[2,1024,256]{2,1,0:T(8,128)(2,1)S(1)}, bf16[2,1024,256]{2,1,0:T(8,128)(2,1)}, u32[]{:S(2)}) copy-start(bf16[2,1024,256]{2,1,0:T(8,128)(2,1)} %param.3) | copy-start | bytes 3145732
  1.2 18.3 %collective-permute-start.2 = (bf16[1040,256]{1,0:T(8,128)(2,1)S(1)}, bf16[1040,256]{1,0:T(8,128)(2,1)S(1)}, u32[]{:S(2)}, u32[]{:S(2)}) collective-permute-start(bf16[1040,256]{1,0:T(8,128)(2,1)S(1)} %slice.48), channel_id=1, source_target_pairs={{2,0},{3,1},{4,2},{5,3},{6,4},{7,5},{0,6},{1,7},{10,8},{11,9},{12,... | collective-permute-start | bytes 1597448 | tf_op jit(solution)/shard_map/ppermute | solution.py:101
  7.1 27.7 %copy-start.2 = (s32[1,9]{1,0:T(1,128)S(1)}, s32[1,9]{1,0:T(1,128)}, u32[]{:S(2)}) copy-start(s32[1,9]{1,0:T(1,128)} %cols.3) | copy-start | bytes 112
  7.1 26.8 %collective-permute-start.1 = (bf16[2064,256]{1,0:T(8,128)(2,1)S(1)}, bf16[2064,256]{1,0:T(8,128)(2,1)S(1)}, u32[]{:S(2)}, u32[]{:S(2)}) collective-permute-start(bf16[2064,256]{1,0:T(8,128)(2,1)S(1)} %fusion.1), channel_id=1, source_target_pairs={{6,0},{7,1},{0,2},{1,3},{3,4},{2,5},{5,6},{4,7},{15,8},{14,9},{9,1... | collective-permute-start | bytes 3170312 | tf_op jit(solution)/shard_map/ppermute | solution.py:101
  9.1 24.9 %collective-permute-start = (bf16[2064,256]{1,0:T(8,128)(2,1)S(1)}, bf16[2064,256]{1,0:T(8,128)(2,1)S(1)}, u32[]{:S(2)}, u32[]{:S(2)}) collective-permute-start(bf16[2064,256]{1,0:T(8,128)(2,1)S(1)} %fusion.1), channel_id=1, source_target_pairs={{1,0},{0,1},{3,2},{2,3},{5,4},{4,5},{7,6},{6,7},{9,8},{8,9},{11,10... | collective-permute-start | bytes 3170312 | tf_op jit(solution)/shard_map/ppermute | solution.py:101
  16.6 15.4 %collective-permute-start.3 = (bf16[1024,256]{1,0:T(8,128)(2,1)S(1)}, bf16[1024,256]{1,0:T(8,128)(2,1)S(1)}, u32[]{:S(2)}, u32[]{:S(2)}) collective-permute-start(bf16[1024,256]{1,0:T(8,128)(2,1)S(1)} %slice.49), channel_id=1, source_target_pairs={{2,0},{3,1},{4,2},{5,3},{6,4},{7,5},{0,6},{1,7},{10,8},{11,9},{12,... | collective-permute-start | bytes 1572872 | tf_op jit(solution)/shard_map/ppermute | solution.py:101
  19.5 15.3 %collective-permute-start.4 = (bf16[1040,256]{1,0:T(8,128)(2,1)S(1)}, bf16[1040,256]{1,0:T(8,128)(2,1)S(1)}, u32[]{:S(2)}, u32[]{:S(2)}) collective-permute-start(bf16[1040,256]{1,0:T(8,128)(2,1)S(1)} %collective-permute-done.2.x1), channel_id=1, source_target_pairs={{8,0},{9,1},{10,2},{11,3},{12,4},{13,5},{14,6},{15,7},{1,8},{0,9},... | collective-permute-start | bytes 1597448 | tf_op jit(solution)/shard_map/ppermute | solution.py:101
  32.0 14.5 %collective-permute-start.5 = (bf16[1024,256]{1,0:T(8,128)(2,1)S(1)}, bf16[1024,256]{1,0:T(8,128)(2,1)S(1)}, u32[]{:S(2)}, u32[]{:S(2)}) collective-permute-start(bf16[1024,256]{1,0:T(8,128)(2,1)S(1)} %collective-permute-done.3.x2), channel_id=1, source_target_pairs={{8,0},{9,1},{10,2},{11,3},{12,4},{13,5},{14,6},{15,7},{1,8},{0,9},... | collective-permute-start | bytes 1572872 | tf_op jit(solution)/shard_map/ppermute | solution.py:101
  82.8 30.5 %copy-start.1 = (s32[16,17]{1,0:T(8,128)S(1)}, s32[16,17]{1,0:T(8,128)}, u32[]{:S(2)}) copy-start(s32[16,17]{1,0:T(8,128)} %constant.17.clone.table) | copy-start | bytes 3268
  99.4 13.9 %collective-permute-start.6 = (f32[24,256]{1,0:T(8,128)S(1)}, f32[24,256]{1,0:T(8,128)S(1)}, u32[]{:S(2)}, u32[]{:S(2)}) collective-permute-start(f32[24,256]{1,0:T(8,128)S(1)} %pad_maximum_fusion), channel_id=1, source_target_pairs={{0,1},{1,0},{2,3},{3,2},{4,5},{5,4},{6,7},{7,6},{8,9},{9,8},{10,11... | collective-permute-start | bytes 73736 | tf_op jit(solution)/shard_map/ppermute | solution.py:105
  101.4 11.9 %collective-permute-start.8 = (f32[32,256]{1,0:T(8,128)S(1)}, f32[32,256]{1,0:T(8,128)S(1)}, u32[]{:S(2)}, u32[]{:S(2)}) collective-permute-start(f32[32,256]{1,0:T(8,128)S(1)} %get-tuple-element.18), channel_id=1, source_target_pairs={{0,10},{1,11},{2,12},{3,13},{4,14},{5,15},{6,8},{7,9},{8,3},{9,2},... | collective-permute-start | bytes 98312 | tf_op jit(solution)/shard_map/ppermute | solution.py:105
  105.5 7.8 %collective-permute-start.7 = (f32[32,256]{1,0:T(8,128)S(1)}, f32[32,256]{1,0:T(8,128)S(1)}, u32[]{:S(2)}, u32[]{:S(2)}) collective-permute-start(f32[32,256]{1,0:T(8,128)S(1)} %get-tuple-element.19), channel_id=1, source_target_pairs={{0,2},{1,3},{2,4},{3,5},{4,6},{5,7},{6,0},{7,1},{8,10},{9,11},{10,... | collective-permute-start | bytes 98312 | tf_op jit(solution)/shard_map/ppermute | solution.py:105
  108.6 4.7 %collective-permute-start.9 = (f32[16,256]{1,0:T(8,128)S(1)}, f32[16,256]{1,0:T(8,128)S(1)}, u32[]{:S(2)}, u32[]{:S(2)}) collective-permute-start(f32[16,256]{1,0:T(8,128)S(1)} %pad_maximum_fusion.1), channel_id=1, source_target_pairs={{0,6},{1,7},{2,0},{3,1},{4,3},{5,2},{6,5},{7,4},{8,15},{9,14},{10,... | collective-permute-start | bytes 49160 | tf_op jit(solution)/shard_map/ppermute | solution.py:105

commit v13 on v12

--- a/solution.py
+++ b/solution.py
@@ -70,13 +70,15 @@
     return [(p, q)] if p == q else [(p, q), (q, p)]
 
 
-MAIL = ((sib, (1, 3, 7)), (right, (2, 3, 4, 5)), (diag, (5, 6, 7, 8)), (left, (4, 8)))
+MAIL = ((sib, (1, 3, 7)), (right, (2, 3, 4, 5)), (diag, (5, 6, 7, 8)), (left, (4, 8, None, None)))
 
 
 def addresses():
     table = np.full((N_BLK, N_BLK + 1), -1, np.int32)
 
     def enter(owner, t, device, index):
+        if t is None:
+            return
         pair = [place(*role(*device)) for role in TILES[t]]
         if owner not in pair:
             return
@@ -324,6 +326,7 @@
 
     parts = [done]
     for role, sent in MAIL:
+        sent = [t or 0 for t in sent]
         slabs = [done[t * SLAB : (t + 1) * SLAB] for t in sent]
         parts.append(hand(jnp.concatenate(slabs), role))
     count = sum(part.shape[0] for part in parts) // SLAB

time: 116 us -> 115 us (level)
  starting transfers between devices: 35.4 us -> 34.2 us
    ppermute x4, starting transfers between devices: 12.5 us -> 11.3 us  [hand(): lax.ppermute(value, BLK, [(place(*d), place(*role(*d))) for d in ALL])]
  transfers between devices with their start and end apart: 10 -> 10, of which waited for: 4 -> 6; matrix products, arithmetic and copies ran while one was open for 1% -> 1% of each run, Pallas kernels for 5% -> 5%
where the time goes in v13:
time: 115 us; the launch traced here: 114 us
  blocking collectives  49.8 us (43%)
  starting transfers between devices  34.2 us (30%)
  waiting for transfers between devices  18 us (16%)
  Pallas kernels  9.11 us (8%)
  other arithmetic  1.44 us (1%)
  local copies, waits for them, and re-layouts  1.23 us (1%)
    all_to_all x2, blocking collectives, exchange(): lax.all_to_all(value, (*BULK, *BLK), 0, 0, axis_index_groups=groups, tile...  49.8 us
    ppermute x6, starting transfers between devices, fetch(): lax.ppermute(value, BLK, [(place(*role(*d)), place(*d)) for d in ALL])  22.8 us
    ppermute x6, waiting for transfers between devices, fetch(): lax.ppermute(value, BLK, [(place(*role(*d)), place(*d)) for d in ALL])  16.3 us
    ppermute x4, starting transfers between devices, hand(): lax.ppermute(value, BLK, [(place(*d), place(*role(*d))) for d in ALL])  11.3 us
    pallas_call x3, Pallas kernels, call(): pl.pallas_call(kernel, out_shape=out_shape, in_specs=[smem] * n_smem + [v...  9.11 us
  transfers between devices with their start and end apart: 10, of which 6 were waited for; matrix products, arithmetic and copies ran while one was open for 1% of the time, Pallas kernels for 5%

profile of v13, /device:TPU:1, one launch (start us, length us, event | category | flops | bytes accessed | tf_op | source)
XLA Modules:
  0.0 113.9 jit_solution(15455389216737515632)
XLA Ops:
  0.0 1.2 %slice.53 = bf16[1040,256]{1,0:T(8,128)(2,1)S(1)} slice(bf16[2048,256]{1,0:T(8,128)(2,1)} %bitcast.2), slice={[0:1040], [0:256]} | slice | bytes 1064960 | tf_op jit(solution)/shard_map/slice | solution.py:313
  1.2 5.2 %collective-permute-start.2 = (bf16[1040,256]{1,0:T(8,128)(2,1)S(1)}, bf16[1040,256]{1,0:T(8,128)(2,1)S(1)}, u32[]{:S(2)}, u32[]{:S(2)}) collective-permute-start(bf16[1040,256]{1,0:T(8,128)(2,1)S(1)} %slice.53), channel_id=1, source_target_pairs={{2,0},{3,1},{4,2},{5,3},{6,4},{7,5},{0,6},{1,7},{10,8},{11,9},{12,... | collective-permute-start | bytes 1597448 | tf_op jit(solution)/shard_map/ppermute | solution.py:103
  6.4 0.7 convert_element_type.14
  7.1 1.9 %collective-permute-start.1 = (bf16[2064,256]{1,0:T(8,128)(2,1)S(1)}, bf16[2064,256]{1,0:T(8,128)(2,1)S(1)}, u32[]{:S(2)}, u32[]{:S(2)}) collective-permute-start(bf16[2064,256]{1,0:T(8,128)(2,1)S(1)} %fusion.1), channel_id=1, source_target_pairs={{6,0},{7,1},{0,2},{1,3},{3,4},{2,5},{5,6},{4,7},{15,8},{14,9},{9,1... | collective-permute-start | bytes 3170312 | tf_op jit(solution)/shard_map/ppermute | solution.py:103
  9.1 7.5 %collective-permute-start = (bf16[2064,256]{1,0:T(8,128)(2,1)S(1)}, bf16[2064,256]{1,0:T(8,128)(2,1)S(1)}, u32[]{:S(2)}, u32[]{:S(2)}) collective-permute-start(bf16[2064,256]{1,0:T(8,128)(2,1)S(1)} %fusion.1), channel_id=1, source_target_pairs={{1,0},{0,1},{3,2},{2,3},{5,4},{4,5},{7,6},{6,7},{9,8},{8,9},{11,10... | collective-permute-start | bytes 3170312 | tf_op jit(solution)/shard_map/ppermute | solution.py:103
  16.6 2.9 %collective-permute-start.3 = (bf16[1024,256]{1,0:T(8,128)(2,1)S(1)}, bf16[1024,256]{1,0:T(8,128)(2,1)S(1)}, u32[]{:S(2)}, u32[]{:S(2)}) collective-permute-start(bf16[1024,256]{1,0:T(8,128)(2,1)S(1)} %slice.54), channel_id=1, source_target_pairs={{2,0},{3,1},{4,2},{5,3},{6,4},{7,5},{0,6},{1,7},{10,8},{11,9},{12,... | collective-permute-start | bytes 1572872 | tf_op jit(solution)/shard_map/ppermute | solution.py:103
  19.5 3.4 %collective-permute-start.4 = (bf16[1040,256]{1,0:T(8,128)(2,1)S(1)}, bf16[1040,256]{1,0:T(8,128)(2,1)S(1)}, u32[]{:S(2)}, u32[]{:S(2)}) collective-permute-start(bf16[1040,256]{1,0:T(8,128)(2,1)S(1)} %collective-permute-done.2.x1), channel_id=1, source_target_pairs={{8,0},{9,1},{10,2},{11,3},{12,4},{13,5},{14,6},{15,7},{1,8},{0,9},... | collective-permute-start | bytes 1597448 | tf_op jit(solution)/shard_map/ppermute | solution.py:103
  22.9 9.1 %collective-permute-done.3.x2 = bf16[1024,256]{1,0:T(8,128)(2,1)S(1)} collective-permute-done((bf16[1024,256]{1,0:T(8,128)(2,1)S(1)}, bf16[1024,256]{1,0:T(8,128)(2,1)S(1)}, u32[]{:S(2)}, u32[]{:S(2)}) %collective-permute-start.3) | collective-permute-done | bytes 524320 | tf_op jit(solution)/shard_map/ppermute | solution.py:103
  32.0 1.9 %collective-permute-start.5 = (bf16[1024,256]{1,0:T(8,128)(2,1)S(1)}, bf16[1024,256]{1,0:T(8,128)(2,1)S(1)}, u32[]{:S(2)}, u32[]{:S(2)}) collective-permute-start(bf16[1024,256]{1,0:T(8,128)(2,1)S(1)} %collective-permute-done.3.x2), channel_id=1, source_target_pairs={{8,0},{9,1},{10,2},{11,3},{12,4},{13,5},{14,6},{15,7},{1,8},{0,9},... | collective-permute-start | bytes 1572872 | tf_op jit(solution)/shard_map/ppermute | solution.py:103
  34.0 0.8 collective-permute-done.4.v1
  34.8 5.5 %shard_map.37 = (f32[32,40,256]{2,1,0:T(8,128)S(1)}, f32[8,256]{1,0:T(8,128)S(1)}, f32[32,32,256]{2,1,0:T(8,128)S(1)}, s32[1,4]{1,0:T(1,128)S(1)}) custom-call(s32[1,9]{1,0:T(1,128)S(1)} %copy-done.2, bf16[2048,256]{1,0:T(8,128)(2,1)S(1)} %bitcast.4, bf16[2064,256]{1,0:T(8,128)(2,1)S(1)} %collective-permute-done.b, ...), custom_call_target="tpu_custom_call" | custom-call | flops 1342177280 | bytes 7118884 | tf_op jit(solution)/shard_map/pallas_call | solution.py:257
  40.2 6.3 %collective-permute-done.5.v2 = bf16[1024,256]{1,0:T(8,128)(2,1)S(1)} collective-permute-done((bf16[1024,256]{1,0:T(8,128)(2,1)S(1)}, bf16[1024,256]{1,0:T(8,128)(2,1)S(1)}, u32[]{:S(2)}, u32[]{:S(2)}) %collective-permute-start.5) | collective-permute-done | bytes 524320 | tf_op jit(solution)/shard_map/ppermute | solution.py:103
  46.6 2.3 %shard_map.38 = f32[8,288,256]{2,1,0:T(8,128)S(1)} custom-call(s32[1,4]{1,0:T(1,128)S(1)} %get-tuple-element.9.flags, bf16[2048,256]{1,0:T(8,128)(2,1)S(1)} %bitcast.5, bf16[2064,256]{1,0:T(8,128)(2,1)S(1)} %collective-permute-done.b, bf16[2064,256]{1,0:T(8,128)(2,1)S(1)} %collective-permute-done.1.w, bf16[1024,256]{1,0:T(8,128)(2,1)S(1)} %collective-permute-done.3.x2, ...), custom_call_target="tpu_custom_call" | custom-call | flops 1073741824 | bytes 8937488 | tf_op jit(solution)/shard_map/pallas_call | solution.py:257
  48.9 0.2 convert_element_type.15
  49.1 33.6 %all_to_all.10 = f16[8,288,256]{2,1,0:T(8,128)(2,1)S(1)} all-to-all(f16[8,288,256]{2,1,0:T(8,128)(2,1)S(1)} %convert_element_type.15), channel_id=1, replica_groups={{1,65,129,193,257,321,385,449},{17,81,145,209,273,337,401,465},{33,97,1..., dimensions={0} | all-to-all | bytes 2359296 | tf_op jit(solution)/shard_map/all_to_all | solution.py:291
  82.8 0.3 multiply_reduce_fusion
  83.1 16.2 %all_to_all.11 = f32[4,72,256]{2,1,0:T(8,128)S(1)} all-to-all(f32[4,72,256]{2,1,0:T(8,128)S(1)} %bitcast.6), channel_id=1, replica_groups={{0,128,256,384},{64,192,320,448},{16,144,272,400},{80,208,336,464},{32,..., dimensions={0} | all-to-all | bytes 589824 | tf_op jit(solution)/shard_map/all_to_all | solution.py:291
  99.4 5.3 %collective-permute-start.9 = (f32[32,256]{1,0:T(8,128)S(1)}, f32[32,256]{1,0:T(8,128)S(1)}, u32[]{:S(2)}, u32[]{:S(2)}) collective-permute-start(f32[32,256]{1,0:T(8,128)S(1)} %pad_maximum_fusion), channel_id=1, source_target_pairs={{0,6},{1,7},{2,0},{3,1},{4,3},{5,2},{6,5},{7,4},{8,15},{9,14},{10,... | collective-permute-start | bytes 98312 | tf_op jit(solution)/shard_map/ppermute | solution.py:107
  104.8 1.9 %collective-permute-start.8 = (f32[32,256]{1,0:T(8,128)S(1)}, f32[32,256]{1,0:T(8,128)S(1)}, u32[]{:S(2)}, u32[]{:S(2)}) collective-permute-start(f32[32,256]{1,0:T(8,128)S(1)} %get-tuple-element.19), channel_id=1, source_target_pairs={{0,10},{1,11},{2,12},{3,13},{4,14},{5,15},{6,8},{7,9},{8,3},{9,2},... | collective-permute-start | bytes 98312 | tf_op jit(solution)/shard_map/ppermute | solution.py:107
  106.7 2.2 %collective-permute-start.7 = (f32[32,256]{1,0:T(8,128)S(1)}, f32[32,256]{1,0:T(8,128)S(1)}, u32[]{:S(2)}, u32[]{:S(2)}) collective-permute-start(f32[32,256]{1,0:T(8,128)S(1)} %get-tuple-element.20), channel_id=1, source_target_pairs={{0,2},{1,3},{2,4},{3,5},{4,6},{5,7},{6,0},{7,1},{8,10},{9,11},{10,... | collective-permute-start | bytes 98312 | tf_op jit(solution)/shard_map/ppermute | solution.py:107
  108.9 1.9 %collective-permute-start.6 = (f32[24,256]{1,0:T(8,128)S(1)}, f32[24,256]{1,0:T(8,128)S(1)}, u32[]{:S(2)}, u32[]{:S(2)}) collective-permute-start(f32[24,256]{1,0:T(8,128)S(1)} %pad_maximum_fusion.1), channel_id=1, source_target_pairs={{0,1},{1,0},{2,3},{3,2},{4,5},{5,4},{6,7},{7,6},{8,9},{9,8},{10,11... | collective-permute-start | bytes 73736 | tf_op jit(solution)/shard_map/ppermute | solution.py:107
  110.8 1.2 %collective-permute-done.6.refs_1_ = f32[24,256]{1,0:T(8,128)S(1)} collective-permute-done((f32[24,256]{1,0:T(8,128)S(1)}, f32[24,256]{1,0:T(8,128)S(1)}, u32[]{:S(2)}, u32[]{:S(2)}) %collective-permute-start.6) | collective-permute-done | bytes 24608 | tf_op jit(solution)/shard_map/ppermute | solution.py:107
  112.1 0.5 collective-permute-done.7.refs_2_
  112.6 1.4 %shard_map.39 = f32[9,8,256]{2,1,0:T(8,128)} custom-call(s32[16,17]{1,0:T(8,128)S(1)} %copy-done.1, s32[1,9]{1,0:T(1,128)S(1)} %copy-done.2, f32[72,256]{1,0:T(8,128)S(1)} %reduce_sum.19.refs_0_, f32[24,256]{1,0:T(8,128)S(1)} %collective-permute-done.6.refs_1_, f32[32,256]{1,0:T(8,128)S(1)} %collective-permute-done.7.refs_2_, ...), custom_call_target="tpu_custom_call" | custom-call | bytes 271460 | tf_op jit(solution)/shard_map/pallas_call | solution.py:257
  (19 shorter events, 0.5 us)
Async XLA Ops:
  0.0 7.1 %copy-start = (bf16[2,1024,256]{2,1,0:T(8,128)(2,1)S(1)}, bf16[2,1024,256]{2,1,0:T(8,128)(2,1)}, u32[]{:S(2)}) copy-start(bf16[2,1024,256]{2,1,0:T(8,128)(2,1)} %param.3) | copy-start | bytes 3145732
  1.2 18.3 %collective-permute-start.2 = (bf16[1040,256]{1,0:T(8,128)(2,1)S(1)}, bf16[1040,256]{1,0:T(8,128)(2,1)S(1)}, u32[]{:S(2)}, u32[]{:S(2)}) collective-permute-start(bf16[1040,256]{1,0:T(8,128)(2,1)S(1)} %slice.53), channel_id=1, source_target_pairs={{2,0},{3,1},{4,2},{5,3},{6,4},{7,5},{0,6},{1,7},{10,8},{11,9},{12,... | collective-permute-start | bytes 1597448 | tf_op jit(solution)/shard_map/ppermute | solution.py:103
  7.1 27.7 %copy-start.2 = (s32[1,9]{1,0:T(1,128)S(1)}, s32[1,9]{1,0:T(1,128)}, u32[]{:S(2)}) copy-start(s32[1,9]{1,0:T(1,128)} %cols.3) | copy-start | bytes 112
  7.1 26.8 %collective-permute-start.1 = (bf16[2064,256]{1,0:T(8,128)(2,1)S(1)}, bf16[2064,256]{1,0:T(8,128)(2,1)S(1)}, u32[]{:S(2)}, u32[]{:S(2)}) collective-permute-start(bf16[2064,256]{1,0:T(8,128)(2,1)S(1)} %fusion.1), channel_id=1, source_target_pairs={{6,0},{7,1},{0,2},{1,3},{3,4},{2,5},{5,6},{4,7},{15,8},{14,9},{9,1... | collective-permute-start | bytes 3170312 | tf_op jit(solution)/shard_map/ppermute | solution.py:103
  9.1 24.9 %collective-permute-start = (bf16[2064,256]{1,0:T(8,128)(2,1)S(1)}, bf16[2064,256]{1,0:T(8,128)(2,1)S(1)}, u32[]{:S(2)}, u32[]{:S(2)}) collective-permute-start(bf16[2064,256]{1,0:T(8,128)(2,1)S(1)} %fusion.1), channel_id=1, source_target_pairs={{1,0},{0,1},{3,2},{2,3},{5,4},{4,5},{7,6},{6,7},{9,8},{8,9},{11,10... | collective-permute-start | bytes 3170312 | tf_op jit(solution)/shard_map/ppermute | solution.py:103
  16.6 15.4 %collective-permute-start.3 = (bf16[1024,256]{1,0:T(8,128)(2,1)S(1)}, bf16[1024,256]{1,0:T(8,128)(2,1)S(1)}, u32[]{:S(2)}, u32[]{:S(2)}) collective-permute-start(bf16[1024,256]{1,0:T(8,128)(2,1)S(1)} %slice.54), channel_id=1, source_target_pairs={{2,0},{3,1},{4,2},{5,3},{6,4},{7,5},{0,6},{1,7},{10,8},{11,9},{12,... | collective-permute-start | bytes 1572872 | tf_op jit(solution)/shard_map/ppermute | solution.py:103
  19.5 15.3 %collective-permute-start.4 = (bf16[1040,256]{1,0:T(8,128)(2,1)S(1)}, bf16[1040,256]{1,0:T(8,128)(2,1)S(1)}, u32[]{:S(2)}, u32[]{:S(2)}) collective-permute-start(bf16[1040,256]{1,0:T(8,128)(2,1)S(1)} %collective-permute-done.2.x1), channel_id=1, source_target_pairs={{8,0},{9,1},{10,2},{11,3},{12,4},{13,5},{14,6},{15,7},{1,8},{0,9},... | collective-permute-start | bytes 1597448 | tf_op jit(solution)/shard_map/ppermute | solution.py:103
  32.0 14.5 %collective-permute-start.5 = (bf16[1024,256]{1,0:T(8,128)(2,1)S(1)}, bf16[1024,256]{1,0:T(8,128)(2,1)S(1)}, u32[]{:S(2)}, u32[]{:S(2)}) collective-permute-start(bf16[1024,256]{1,0:T(8,128)(2,1)S(1)} %collective-permute-done.3.x2), channel_id=1, source_target_pairs={{8,0},{9,1},{10,2},{11,3},{12,4},{13,5},{14,6},{15,7},{1,8},{0,9},... | collective-permute-start | bytes 1572872 | tf_op jit(solution)/shard_map/ppermute | solution.py:103
  82.8 29.7 %copy-start.1 = (s32[16,17]{1,0:T(8,128)S(1)}, s32[16,17]{1,0:T(8,128)}, u32[]{:S(2)}) copy-start(s32[16,17]{1,0:T(8,128)} %constant.17.clone.table) | copy-start | bytes 3268
  99.4 12.5 %collective-permute-start.9 = (f32[32,256]{1,0:T(8,128)S(1)}, f32[32,256]{1,0:T(8,128)S(1)}, u32[]{:S(2)}, u32[]{:S(2)}) collective-permute-start(f32[32,256]{1,0:T(8,128)S(1)} %pad_maximum_fusion), channel_id=1, source_target_pairs={{0,6},{1,7},{2,0},{3,1},{4,3},{5,2},{6,5},{7,4},{8,15},{9,14},{10,... | collective-permute-start | bytes 98312 | tf_op jit(solution)/shard_map/ppermute | solution.py:107
  104.8 7.3 %collective-permute-start.8 = (f32[32,256]{1,0:T(8,128)S(1)}, f32[32,256]{1,0:T(8,128)S(1)}, u32[]{:S(2)}, u32[]{:S(2)}) collective-permute-start(f32[32,256]{1,0:T(8,128)S(1)} %get-tuple-element.19), channel_id=1, source_target_pairs={{0,10},{1,11},{2,12},{3,13},{4,14},{5,15},{6,8},{7,9},{8,3},{9,2},... | collective-permute-start | bytes 98312 | tf_op jit(solution)/shard_map/ppermute | solution.py:107
  106.7 5.9 %collective-permute-start.7 = (f32[32,256]{1,0:T(8,128)S(1)}, f32[32,256]{1,0:T(8,128)S(1)}, u32[]{:S(2)}, u32[]{:S(2)}) collective-permute-start(f32[32,256]{1,0:T(8,128)S(1)} %get-tuple-element.20), channel_id=1, source_target_pairs={{0,2},{1,3},{2,4},{3,5},{4,6},{5,7},{6,0},{7,1},{8,10},{9,11},{10,... | collective-permute-start | bytes 98312 | tf_op jit(solution)/shard_map/ppermute | solution.py:107
  108.9 3.1 %collective-permute-start.6 = (f32[24,256]{1,0:T(8,128)S(1)}, f32[24,256]{1,0:T(8,128)S(1)}, u32[]{:S(2)}, u32[]{:S(2)}) collective-permute-start(f32[24,256]{1,0:T(8,128)S(1)} %pad_maximum_fusion.1), channel_id=1, source_target_pairs={{0,1},{1,0},{2,3},{3,2},{4,5},{5,4},{6,7},{7,6},{8,9},{9,8},{10,11... | collective-permute-start | bytes 73736 | tf_op jit(solution)/shard_map/ppermute | solution.py:107

commit v14 on v13

--- a/solution.py
+++ b/solution.py
@@ -70,7 +70,7 @@
     return [(p, q)] if p == q else [(p, q), (q, p)]
 
 
-MAIL = ((sib, (1, 3, 7)), (right, (2, 3, 4, 5)), (diag, (5, 6, 7, 8)), (left, (4, 8, None, None)))
+MAIL = ((sib, (1, 3, 7)), (right, (2, 3, 4, 5, None)), (diag, (5, 6, 7, 8, None)), (left, (4, 8, None, None)))
 
 
 def addresses():

time: 115 us -> 115 us (level)
  no operation moved by 1% of the time
where the time goes in v14:
time: 115 us; the launch traced here: 114 us
  blocking collectives  49.8 us (43%)
  starting transfers between devices  34.2 us (30%)
  waiting for transfers between devices  18.1 us (16%)
  Pallas kernels  9.12 us (8%)
  other arithmetic  1.45 us (1%)
  local copies, waits for them, and re-layouts  1.23 us (1%)
    all_to_all x2, blocking collectives, exchange(): lax.all_to_all(value, (*BULK, *BLK), 0, 0, axis_index_groups=groups, tile...  49.8 us
    ppermute x6, starting transfers between devices, fetch(): lax.ppermute(value, BLK, [(place(*role(*d)), place(*d)) for d in ALL])  22.8 us
    ppermute x6, waiting for transfers between devices, fetch(): lax.ppermute(value, BLK, [(place(*role(*d)), place(*d)) for d in ALL])  16.3 us
    ppermute x4, starting transfers between devices, hand(): lax.ppermute(value, BLK, [(place(*d), place(*role(*d))) for d in ALL])  11.3 us
    pallas_call x3, Pallas kernels, call(): pl.pallas_call(kernel, out_shape=out_shape, in_specs=[smem] * n_smem + [v...  9.12 us
  transfers between devices with their start and end apart: 10, of which 6 were waited for; matrix products, arithmetic and copies ran while one was open for 1% of the time, Pallas kernels for 5%

profile of v14, /device:TPU:1, one launch (start us, length us, event | category | flops | bytes accessed | tf_op | source)
XLA Modules:
  0.0 114.0 jit_solution(13293019028086124766)
XLA Ops:
  0.0 1.2 %slice.55 = bf16[1040,256]{1,0:T(8,128)(2,1)S(1)} slice(bf16[2048,256]{1,0:T(8,128)(2,1)} %bitcast.2), slice={[0:1040], [0:256]} | slice | bytes 1064960 | tf_op jit(solution)/shard_map/slice | solution.py:313
  1.2 5.2 %collective-permute-start.2 = (bf16[1040,256]{1,0:T(8,128)(2,1)S(1)}, bf16[1040,256]{1,0:T(8,128)(2,1)S(1)}, u32[]{:S(2)}, u32[]{:S(2)}) collective-permute-start(bf16[1040,256]{1,0:T(8,128)(2,1)S(1)} %slice.55), channel_id=1, source_target_pairs={{2,0},{3,1},{4,2},{5,3},{6,4},{7,5},{0,6},{1,7},{10,8},{11,9},{12,... | collective-permute-start | bytes 1597448 | tf_op jit(solution)/shard_map/ppermute | solution.py:103
  6.4 0.7 convert_element_type.14
  7.1 1.9 %collective-permute-start.1 = (bf16[2064,256]{1,0:T(8,128)(2,1)S(1)}, bf16[2064,256]{1,0:T(8,128)(2,1)S(1)}, u32[]{:S(2)}, u32[]{:S(2)}) collective-permute-start(bf16[2064,256]{1,0:T(8,128)(2,1)S(1)} %fusion.1), channel_id=1, source_target_pairs={{6,0},{7,1},{0,2},{1,3},{3,4},{2,5},{5,6},{4,7},{15,8},{14,9},{9,1... | collective-permute-start | bytes 3170312 | tf_op jit(solution)/shard_map/ppermute | solution.py:103
  9.1 7.5 %collective-permute-start = (bf16[2064,256]{1,0:T(8,128)(2,1)S(1)}, bf16[2064,256]{1,0:T(8,128)(2,1)S(1)}, u32[]{:S(2)}, u32[]{:S(2)}) collective-permute-start(bf16[2064,256]{1,0:T(8,128)(2,1)S(1)} %fusion.1), channel_id=1, source_target_pairs={{1,0},{0,1},{3,2},{2,3},{5,4},{4,5},{7,6},{6,7},{9,8},{8,9},{11,10... | collective-permute-start | bytes 3170312 | tf_op jit(solution)/shard_map/ppermute | solution.py:103
  16.6 2.9 %collective-permute-start.3 = (bf16[1024,256]{1,0:T(8,128)(2,1)S(1)}, bf16[1024,256]{1,0:T(8,128)(2,1)S(1)}, u32[]{:S(2)}, u32[]{:S(2)}) collective-permute-start(bf16[1024,256]{1,0:T(8,128)(2,1)S(1)} %slice.56), channel_id=1, source_target_pairs={{2,0},{3,1},{4,2},{5,3},{6,4},{7,5},{0,6},{1,7},{10,8},{11,9},{12,... | collective-permute-start | bytes 1572872 | tf_op jit(solution)/shard_map/ppermute | solution.py:103
  19.5 3.4 %collective-permute-start.4 = (bf16[1040,256]{1,0:T(8,128)(2,1)S(1)}, bf16[1040,256]{1,0:T(8,128)(2,1)S(1)}, u32[]{:S(2)}, u32[]{:S(2)}) collective-permute-start(bf16[1040,256]{1,0:T(8,128)(2,1)S(1)} %collective-permute-done.2.x1), channel_id=1, source_target_pairs={{8,0},{9,1},{10,2},{11,3},{12,4},{13,5},{14,6},{15,7},{1,8},{0,9},... | collective-permute-start | bytes 1597448 | tf_op jit(solution)/shard_map/ppermute | solution.py:103
  22.9 9.1 %collective-permute-done.3.x2 = bf16[1024,256]{1,0:T(8,128)(2,1)S(1)} collective-permute-done((bf16[1024,256]{1,0:T(8,128)(2,1)S(1)}, bf16[1024,256]{1,0:T(8,128)(2,1)S(1)}, u32[]{:S(2)}, u32[]{:S(2)}) %collective-permute-start.3) | collective-permute-done | bytes 524320 | tf_op jit(solution)/shard_map/ppermute | solution.py:103
  32.0 1.9 %collective-permute-start.5 = (bf16[1024,256]{1,0:T(8,128)(2,1)S(1)}, bf16[1024,256]{1,0:T(8,128)(2,1)S(1)}, u32[]{:S(2)}, u32[]{:S(2)}) collective-permute-start(bf16[1024,256]{1,0:T(8,128)(2,1)S(1)} %collective-permute-done.3.x2), channel_id=1, source_target_pairs={{8,0},{9,1},{10,2},{11,3},{12,4},{13,5},{14,6},{15,7},{1,8},{0,9},... | collective-permute-start | bytes 1572872 | tf_op jit(solution)/shard_map/ppermute | solution.py:103
  34.0 0.8 collective-permute-done.4.v1
  34.8 5.5 %shard_map.37 = (f32[32,40,256]{2,1,0:T(8,128)S(1)}, f32[8,256]{1,0:T(8,128)S(1)}, f32[32,32,256]{2,1,0:T(8,128)S(1)}, s32[1,4]{1,0:T(1,128)S(1)}) custom-call(s32[1,9]{1,0:T(1,128)S(1)} %copy-done.2, bf16[2048,256]{1,0:T(8,128)(2,1)S(1)} %bitcast.4, bf16[2064,256]{1,0:T(8,128)(2,1)S(1)} %collective-permute-done.b, ...), custom_call_target="tpu_custom_call" | custom-call | flops 1342177280 | bytes 7118884 | tf_op jit(solution)/shard_map/pallas_call | solution.py:257
  40.2 6.3 %collective-permute-done.5.v2 = bf16[1024,256]{1,0:T(8,128)(2,1)S(1)} collective-permute-done((bf16[1024,256]{1,0:T(8,128)(2,1)S(1)}, bf16[1024,256]{1,0:T(8,128)(2,1)S(1)}, u32[]{:S(2)}, u32[]{:S(2)}) %collective-permute-start.5) | collective-permute-done | bytes 524320 | tf_op jit(solution)/shard_map/ppermute | solution.py:103
  46.6 2.3 %shard_map.38 = f32[8,288,256]{2,1,0:T(8,128)S(1)} custom-call(s32[1,4]{1,0:T(1,128)S(1)} %get-tuple-element.9.flags, bf16[2048,256]{1,0:T(8,128)(2,1)S(1)} %bitcast.5, bf16[2064,256]{1,0:T(8,128)(2,1)S(1)} %collective-permute-done.b, bf16[2064,256]{1,0:T(8,128)(2,1)S(1)} %collective-permute-done.1.w, bf16[1024,256]{1,0:T(8,128)(2,1)S(1)} %collective-permute-done.3.x2, ...), custom_call_target="tpu_custom_call" | custom-call | flops 1073741824 | bytes 8937488 | tf_op jit(solution)/shard_map/pallas_call | solution.py:257
  48.9 0.2 convert_element_type.15
  49.1 33.6 %all_to_all.10 = f16[8,288,256]{2,1,0:T(8,128)(2,1)S(1)} all-to-all(f16[8,288,256]{2,1,0:T(8,128)(2,1)S(1)} %convert_element_type.15), channel_id=1, replica_groups={{1,65,129,193,257,321,385,449},{17,81,145,209,273,337,401,465},{33,97,1..., dimensions={0} | all-to-all | bytes 2359296 | tf_op jit(solution)/shard_map/all_to_all | solution.py:291
  82.8 0.3 multiply_reduce_fusion
  83.1 16.2 %all_to_all.11 = f32[4,72,256]{2,1,0:T(8,128)S(1)} all-to-all(f32[4,72,256]{2,1,0:T(8,128)S(1)} %bitcast.6), channel_id=1, replica_groups={{0,128,256,384},{64,192,320,448},{16,144,272,400},{80,208,336,464},{32,..., dimensions={0} | all-to-all | bytes 589824 | tf_op jit(solution)/shard_map/all_to_all | solution.py:291
  99.4 5.3 %collective-permute-start.9 = (f32[32,256]{1,0:T(8,128)S(1)}, f32[32,256]{1,0:T(8,128)S(1)}, u32[]{:S(2)}, u32[]{:S(2)}) collective-permute-start(f32[32,256]{1,0:T(8,128)S(1)} %pad_maximum_fusion.2), channel_id=1, source_target_pairs={{0,6},{1,7},{2,0},{3,1},{4,3},{5,2},{6,5},{7,4},{8,15},{9,14},{10,... | collective-permute-start | bytes 98312 | tf_op jit(solution)/shard_map/ppermute | solution.py:107
  104.8 1.9 %collective-permute-start.8 = (f32[40,256]{1,0:T(8,128)S(1)}, f32[40,256]{1,0:T(8,128)S(1)}, u32[]{:S(2)}, u32[]{:S(2)}) collective-permute-start(f32[40,256]{1,0:T(8,128)S(1)} %get-tuple-element.21), channel_id=1, source_target_pairs={{0,10},{1,11},{2,12},{3,13},{4,14},{5,15},{6,8},{7,9},{8,3},{9,2},... | collective-permute-start | bytes 122888 | tf_op jit(solution)/shard_map/ppermute | solution.py:107
  106.7 2.2 %collective-permute-start.7 = (f32[40,256]{1,0:T(8,128)S(1)}, f32[40,256]{1,0:T(8,128)S(1)}, u32[]{:S(2)}, u32[]{:S(2)}) collective-permute-start(f32[40,256]{1,0:T(8,128)S(1)} %get-tuple-element.22), channel_id=1, source_target_pairs={{0,2},{1,3},{2,4},{3,5},{4,6},{5,7},{6,0},{7,1},{8,10},{9,11},{10,... | collective-permute-start | bytes 122888 | tf_op jit(solution)/shard_map/ppermute | solution.py:107
  108.9 1.9 %collective-permute-start.6 = (f32[24,256]{1,0:T(8,128)S(1)}, f32[24,256]{1,0:T(8,128)S(1)}, u32[]{:S(2)}, u32[]{:S(2)}) collective-permute-start(f32[24,256]{1,0:T(8,128)S(1)} %pad_maximum_fusion.3), channel_id=1, source_target_pairs={{0,1},{1,0},{2,3},{3,2},{4,5},{5,4},{6,7},{7,6},{8,9},{9,8},{10,11... | collective-permute-start | bytes 73736 | tf_op jit(solution)/shard_map/ppermute | solution.py:107
  110.8 1.2 %collective-permute-done.6.refs_1_ = f32[24,256]{1,0:T(8,128)S(1)} collective-permute-done((f32[24,256]{1,0:T(8,128)S(1)}, f32[24,256]{1,0:T(8,128)S(1)}, u32[]{:S(2)}, u32[]{:S(2)}) %collective-permute-start.6) | collective-permute-done | bytes 24608 | tf_op jit(solution)/shard_map/ppermute | solution.py:107
  112.2 0.5 collective-permute-done.7.refs_2_
  112.7 1.4 %shard_map.39 = f32[9,8,256]{2,1,0:T(8,128)} custom-call(s32[16,17]{1,0:T(8,128)S(1)} %copy-done.1, s32[1,9]{1,0:T(1,128)S(1)} %copy-done.2, f32[72,256]{1,0:T(8,128)S(1)} %reduce_sum.19.refs_0_, f32[24,256]{1,0:T(8,128)S(1)} %collective-permute-done.6.refs_1_, f32[40,256]{1,0:T(8,128)S(1)} %collective-permute-done.7.refs_2_, ...), custom_call_target="tpu_custom_call" | custom-call | bytes 287844 | tf_op jit(solution)/shard_map/pallas_call | solution.py:257
  (20 shorter events, 0.6 us)
Async XLA Ops:
  0.0 7.1 %copy-start = (bf16[2,1024,256]{2,1,0:T(8,128)(2,1)S(1)}, bf16[2,1024,256]{2,1,0:T(8,128)(2,1)}, u32[]{:S(2)}) copy-start(bf16[2,1024,256]{2,1,0:T(8,128)(2,1)} %param.3) | copy-start | bytes 3145732
  1.2 18.3 %collective-permute-start.2 = (bf16[1040,256]{1,0:T(8,128)(2,1)S(1)}, bf16[1040,256]{1,0:T(8,128)(2,1)S(1)}, u32[]{:S(2)}, u32[]{:S(2)}) collective-permute-start(bf16[1040,256]{1,0:T(8,128)(2,1)S(1)} %slice.55), channel_id=1, source_target_pairs={{2,0},{3,1},{4,2},{5,3},{6,4},{7,5},{0,6},{1,7},{10,8},{11,9},{12,... | collective-permute-start | bytes 1597448 | tf_op jit(solution)/shard_map/ppermute | solution.py:103
  7.1 27.7 %copy-start.2 = (s32[1,9]{1,0:T(1,128)S(1)}, s32[1,9]{1,0:T(1,128)}, u32[]{:S(2)}) copy-start(s32[1,9]{1,0:T(1,128)} %cols.3) | copy-start | bytes 112
  7.1 26.8 %collective-permute-start.1 = (bf16[2064,256]{1,0:T(8,128)(2,1)S(1)}, bf16[2064,256]{1,0:T(8,128)(2,1)S(1)}, u32[]{:S(2)}, u32[]{:S(2)}) collective-permute-start(bf16[2064,256]{1,0:T(8,128)(2,1)S(1)} %fusion.1), channel_id=1, source_target_pairs={{6,0},{7,1},{0,2},{1,3},{3,4},{2,5},{5,6},{4,7},{15,8},{14,9},{9,1... | collective-permute-start | bytes 3170312 | tf_op jit(solution)/shard_map/ppermute | solution.py:103
  9.1 24.9 %collective-permute-start = (bf16[2064,256]{1,0:T(8,128)(2,1)S(1)}, bf16[2064,256]{1,0:T(8,128)(2,1)S(1)}, u32[]{:S(2)}, u32[]{:S(2)}) collective-permute-start(bf16[2064,256]{1,0:T(8,128)(2,1)S(1)} %fusion.1), channel_id=1, source_target_pairs={{1,0},{0,1},{3,2},{2,3},{5,4},{4,5},{7,6},{6,7},{9,8},{8,9},{11,10... | collective-permute-start | bytes 3170312 | tf_op jit(solution)/shard_map/ppermute | solution.py:103
  16.6 15.4 %collective-permute-start.3 = (bf16[1024,256]{1,0:T(8,128)(2,1)S(1)}, bf16[1024,256]{1,0:T(8,128)(2,1)S(1)}, u32[]{:S(2)}, u32[]{:S(2)}) collective-permute-start(bf16[1024,256]{1,0:T(8,128)(2,1)S(1)} %slice.56), channel_id=1, source_target_pairs={{2,0},{3,1},{4,2},{5,3},{6,4},{7,5},{0,6},{1,7},{10,8},{11,9},{12,... | collective-permute-start | bytes 1572872 | tf_op jit(solution)/shard_map/ppermute | solution.py:103
  19.5 15.3 %collective-permute-start.4 = (bf16[1040,256]{1,0:T(8,128)(2,1)S(1)}, bf16[1040,256]{1,0:T(8,128)(2,1)S(1)}, u32[]{:S(2)}, u32[]{:S(2)}) collective-permute-start(bf16[1040,256]{1,0:T(8,128)(2,1)S(1)} %collective-permute-done.2.x1), channel_id=1, source_target_pairs={{8,0},{9,1},{10,2},{11,3},{12,4},{13,5},{14,6},{15,7},{1,8},{0,9},... | collective-permute-start | bytes 1597448 | tf_op jit(solution)/shard_map/ppermute | solution.py:103
  32.0 14.5 %collective-permute-start.5 = (bf16[1024,256]{1,0:T(8,128)(2,1)S(1)}, bf16[1024,256]{1,0:T(8,128)(2,1)S(1)}, u32[]{:S(2)}, u32[]{:S(2)}) collective-permute-start(bf16[1024,256]{1,0:T(8,128)(2,1)S(1)} %collective-permute-done.3.x2), channel_id=1, source_target_pairs={{8,0},{9,1},{10,2},{11,3},{12,4},{13,5},{14,6},{15,7},{1,8},{0,9},... | collective-permute-start | bytes 1572872 | tf_op jit(solution)/shard_map/ppermute | solution.py:103
  82.8 29.8 %copy-start.1 = (s32[16,17]{1,0:T(8,128)S(1)}, s32[16,17]{1,0:T(8,128)}, u32[]{:S(2)}) copy-start(s32[16,17]{1,0:T(8,128)} %constant.17.clone.table) | copy-start | bytes 3268
  99.4 12.6 %collective-permute-start.9 = (f32[32,256]{1,0:T(8,128)S(1)}, f32[32,256]{1,0:T(8,128)S(1)}, u32[]{:S(2)}, u32[]{:S(2)}) collective-permute-start(f32[32,256]{1,0:T(8,128)S(1)} %pad_maximum_fusion.2), channel_id=1, source_target_pairs={{0,6},{1,7},{2,0},{3,1},{4,3},{5,2},{6,5},{7,4},{8,15},{9,14},{10,... | collective-permute-start | bytes 98312 | tf_op jit(solution)/shard_map/ppermute | solution.py:107
  104.8 7.4 %collective-permute-start.8 = (f32[40,256]{1,0:T(8,128)S(1)}, f32[40,256]{1,0:T(8,128)S(1)}, u32[]{:S(2)}, u32[]{:S(2)}) collective-permute-start(f32[40,256]{1,0:T(8,128)S(1)} %get-tuple-element.21), channel_id=1, source_target_pairs={{0,10},{1,11},{2,12},{3,13},{4,14},{5,15},{6,8},{7,9},{8,3},{9,2},... | collective-permute-start | bytes 122888 | tf_op jit(solution)/shard_map/ppermute | solution.py:107
  106.7 6.0 %collective-permute-start.7 = (f32[40,256]{1,0:T(8,128)S(1)}, f32[40,256]{1,0:T(8,128)S(1)}, u32[]{:S(2)}, u32[]{:S(2)}) collective-permute-start(f32[40,256]{1,0:T(8,128)S(1)} %get-tuple-element.22), channel_id=1, source_target_pairs={{0,2},{1,3},{2,4},{3,5},{4,6},{5,7},{6,0},{7,1},{8,10},{9,11},{10,... | collective-permute-start | bytes 122888 | tf_op jit(solution)/shard_map/ppermute | solution.py:107
  108.9 3.1 %collective-permute-start.6 = (f32[24,256]{1,0:T(8,128)S(1)}, f32[24,256]{1,0:T(8,128)S(1)}, u32[]{:S(2)}, u32[]{:S(2)}) collective-permute-start(f32[24,256]{1,0:T(8,128)S(1)} %pad_maximum_fusion.3), channel_id=1, source_target_pairs={{0,1},{1,0},{2,3},{3,2},{4,5},{5,4},{6,7},{7,6},{8,9},{9,8},{10,11... | collective-permute-start | bytes 73736 | tf_op jit(solution)/shard_map/ppermute | solution.py:107

commit v15 on v13

--- a/solution.py
+++ b/solution.py
@@ -14,8 +14,8 @@
 SLOTS = 9
 W = 256
 K = 2048
-PARTS = (1040, 1008)
-STARTS = (0, 1040)
+PARTS = (1056, 992)
+STARTS = (0, 1056)
 HALF = W // 2
 SLAB = W // N_BULK
 FIRST, SECOND = 8, 4

time: 115 us -> 116 us (level)
  no operation moved by 1% of the time
where the time goes in v15:
time: 116 us; the launch traced here: 114 us
  blocking collectives  50.5 us (44%)
  starting transfers between devices  34.1 us (29%)
  waiting for transfers between devices  17.7 us (15%)
  Pallas kernels  9.11 us (8%)
  other arithmetic  1.44 us (1%)
  local copies, waits for them, and re-layouts  1.23 us (1%)
    all_to_all x2, blocking collectives, exchange(): lax.all_to_all(value, (*BULK, *BLK), 0, 0, axis_index_groups=groups, tile...  50.5 us
    ppermute x6, starting transfers between devices, fetch(): lax.ppermute(value, BLK, [(place(*role(*d)), place(*d)) for d in ALL])  23 us
    ppermute x6, waiting for transfers between devices, fetch(): lax.ppermute(value, BLK, [(place(*role(*d)), place(*d)) for d in ALL])  15.7 us
    ppermute x4, starting transfers between devices, hand(): lax.ppermute(value, BLK, [(place(*d), place(*role(*d))) for d in ALL])  11.1 us
    pallas_call x3, Pallas kernels, call(): pl.pallas_call(kernel, out_shape=out_shape, in_specs=[smem] * n_smem + [v...  9.11 us
  transfers between devices with their start and end apart: 10, of which 6 were waited for; matrix products, arithmetic and copies ran while one was open for 1% of the time, Pallas kernels for 5%

profile of v15, /device:TPU:1, one launch (start us, length us, event | category | flops | bytes accessed | tf_op | source)
XLA Modules:
  0.0 114.3 jit_solution(2178053427754994481)
XLA Ops:
  0.0 1.2 %slice.53 = bf16[1056,256]{1,0:T(8,128)(2,1)S(1)} slice(bf16[2048,256]{1,0:T(8,128)(2,1)} %bitcast.2), slice={[0:1056], [0:256]} | slice | bytes 1081344 | tf_op jit(solution)/shard_map/slice | solution.py:313
  1.2 5.2 %collective-permute-start.2 = (bf16[1056,256]{1,0:T(8,128)(2,1)S(1)}, bf16[1056,256]{1,0:T(8,128)(2,1)S(1)}, u32[]{:S(2)}, u32[]{:S(2)}) collective-permute-start(bf16[1056,256]{1,0:T(8,128)(2,1)S(1)} %slice.53), channel_id=1, source_target_pairs={{2,0},{3,1},{4,2},{5,3},{6,4},{7,5},{0,6},{1,7},{10,8},{11,9},{12,... | collective-permute-start | bytes 1622024 | tf_op jit(solution)/shard_map/ppermute | solution.py:103
  6.4 0.7 convert_element_type.14
  7.1 1.9 %collective-permute-start.1 = (bf16[2064,256]{1,0:T(8,128)(2,1)S(1)}, bf16[2064,256]{1,0:T(8,128)(2,1)S(1)}, u32[]{:S(2)}, u32[]{:S(2)}) collective-permute-start(bf16[2064,256]{1,0:T(8,128)(2,1)S(1)} %fusion.1), channel_id=1, source_target_pairs={{6,0},{7,1},{0,2},{1,3},{3,4},{2,5},{5,6},{4,7},{15,8},{14,9},{9,1... | collective-permute-start | bytes 3170312 | tf_op jit(solution)/shard_map/ppermute | solution.py:103
  9.1 7.5 %collective-permute-start = (bf16[2064,256]{1,0:T(8,128)(2,1)S(1)}, bf16[2064,256]{1,0:T(8,128)(2,1)S(1)}, u32[]{:S(2)}, u32[]{:S(2)}) collective-permute-start(bf16[2064,256]{1,0:T(8,128)(2,1)S(1)} %fusion.1), channel_id=1, source_target_pairs={{1,0},{0,1},{3,2},{2,3},{5,4},{4,5},{7,6},{6,7},{9,8},{8,9},{11,10... | collective-permute-start | bytes 3170312 | tf_op jit(solution)/shard_map/ppermute | solution.py:103
  16.6 2.9 %collective-permute-start.3 = (bf16[1008,256]{1,0:T(8,128)(2,1)S(1)}, bf16[1008,256]{1,0:T(8,128)(2,1)S(1)}, u32[]{:S(2)}, u32[]{:S(2)}) collective-permute-start(bf16[1008,256]{1,0:T(8,128)(2,1)S(1)} %slice.54), channel_id=1, source_target_pairs={{2,0},{3,1},{4,2},{5,3},{6,4},{7,5},{0,6},{1,7},{10,8},{11,9},{12,... | collective-permute-start | bytes 1548296 | tf_op jit(solution)/shard_map/ppermute | solution.py:103
  19.5 3.6 %collective-permute-start.4 = (bf16[1056,256]{1,0:T(8,128)(2,1)S(1)}, bf16[1056,256]{1,0:T(8,128)(2,1)S(1)}, u32[]{:S(2)}, u32[]{:S(2)}) collective-permute-start(bf16[1056,256]{1,0:T(8,128)(2,1)S(1)} %collective-permute-done.2.x1), channel_id=1, source_target_pairs={{8,0},{9,1},{10,2},{11,3},{12,4},{13,5},{14,6},{15,7},{1,8},{0,9},... | collective-permute-start | bytes 1622024 | tf_op jit(solution)/shard_map/ppermute | solution.py:103
  23.1 8.8 %collective-permute-done.3.x2 = bf16[1008,256]{1,0:T(8,128)(2,1)S(1)} collective-permute-done((bf16[1008,256]{1,0:T(8,128)(2,1)S(1)}, bf16[1008,256]{1,0:T(8,128)(2,1)S(1)}, u32[]{:S(2)}, u32[]{:S(2)}) %collective-permute-start.3) | collective-permute-done | bytes 516128 | tf_op jit(solution)/shard_map/ppermute | solution.py:103
  31.9 1.9 %collective-permute-start.5 = (bf16[1008,256]{1,0:T(8,128)(2,1)S(1)}, bf16[1008,256]{1,0:T(8,128)(2,1)S(1)}, u32[]{:S(2)}, u32[]{:S(2)}) collective-permute-start(bf16[1008,256]{1,0:T(8,128)(2,1)S(1)} %collective-permute-done.3.x2), channel_id=1, source_target_pairs={{8,0},{9,1},{10,2},{11,3},{12,4},{13,5},{14,6},{15,7},{1,8},{0,9},... | collective-permute-start | bytes 1548296 | tf_op jit(solution)/shard_map/ppermute | solution.py:103
  33.8 1.1 collective-permute-done.4.v1
  35.0 5.4 %shard_map.37 = (f32[32,40,256]{2,1,0:T(8,128)S(1)}, f32[8,256]{1,0:T(8,128)S(1)}, f32[32,32,256]{2,1,0:T(8,128)S(1)}, s32[1,4]{1,0:T(1,128)S(1)}) custom-call(s32[1,9]{1,0:T(1,128)S(1)} %copy-done.2, bf16[2048,256]{1,0:T(8,128)(2,1)S(1)} %bitcast.4, bf16[2064,256]{1,0:T(8,128)(2,1)S(1)} %collective-permute-done.b, ...), custom_call_target="tpu_custom_call" | custom-call | flops 1342177280 | bytes 7127076 | tf_op jit(solution)/shard_map/pallas_call | solution.py:257
  40.4 5.8 %collective-permute-done.5.v2 = bf16[1008,256]{1,0:T(8,128)(2,1)S(1)} collective-permute-done((bf16[1008,256]{1,0:T(8,128)(2,1)S(1)}, bf16[1008,256]{1,0:T(8,128)(2,1)S(1)}, u32[]{:S(2)}, u32[]{:S(2)}) %collective-permute-start.5) | collective-permute-done | bytes 516128 | tf_op jit(solution)/shard_map/ppermute | solution.py:103
  46.2 2.3 %shard_map.38 = f32[8,288,256]{2,1,0:T(8,128)S(1)} custom-call(s32[1,4]{1,0:T(1,128)S(1)} %get-tuple-element.9.flags, bf16[2048,256]{1,0:T(8,128)(2,1)S(1)} %bitcast.5, bf16[2064,256]{1,0:T(8,128)(2,1)S(1)} %collective-permute-done.b, bf16[2064,256]{1,0:T(8,128)(2,1)S(1)} %collective-permute-done.1.w, bf16[1008,256]{1,0:T(8,128)(2,1)S(1)} %collective-permute-done.3.x2, ...), custom_call_target="tpu_custom_call" | custom-call | flops 1073741824 | bytes 8921104 | tf_op jit(solution)/shard_map/pallas_call | solution.py:257
  48.8 34.3 %all_to_all.10 = f16[8,288,256]{2,1,0:T(8,128)(2,1)S(1)} all-to-all(f16[8,288,256]{2,1,0:T(8,128)(2,1)S(1)} %convert_element_type.15), channel_id=1, replica_groups={{1,65,129,193,257,321,385,449},{17,81,145,209,273,337,401,465},{33,97,1..., dimensions={0} | all-to-all | bytes 2359296 | tf_op jit(solution)/shard_map/all_to_all | solution.py:291
  83.2 0.3 multiply_reduce_fusion
  83.5 16.2 %all_to_all.11 = f32[4,72,256]{2,1,0:T(8,128)S(1)} all-to-all(f32[4,72,256]{2,1,0:T(8,128)S(1)} %bitcast.6), channel_id=1, replica_groups={{0,128,256,384},{64,192,320,448},{16,144,272,400},{80,208,336,464},{32,..., dimensions={0} | all-to-all | bytes 589824 | tf_op jit(solution)/shard_map/all_to_all | solution.py:291
  99.8 5.3 %collective-permute-start.9 = (f32[32,256]{1,0:T(8,128)S(1)}, f32[32,256]{1,0:T(8,128)S(1)}, u32[]{:S(2)}, u32[]{:S(2)}) collective-permute-start(f32[32,256]{1,0:T(8,128)S(1)} %pad_maximum_fusion), channel_id=1, source_target_pairs={{0,6},{1,7},{2,0},{3,1},{4,3},{5,2},{6,5},{7,4},{8,15},{9,14},{10,... | collective-permute-start | bytes 98312 | tf_op jit(solution)/shard_map/ppermute | solution.py:107
  105.1 1.9 %collective-permute-start.8 = (f32[32,256]{1,0:T(8,128)S(1)}, f32[32,256]{1,0:T(8,128)S(1)}, u32[]{:S(2)}, u32[]{:S(2)}) collective-permute-start(f32[32,256]{1,0:T(8,128)S(1)} %get-tuple-element.19), channel_id=1, source_target_pairs={{0,10},{1,11},{2,12},{3,13},{4,14},{5,15},{6,8},{7,9},{8,3},{9,2},... | collective-permute-start | bytes 98312 | tf_op jit(solution)/shard_map/ppermute | solution.py:107
  107.1 2.0 %collective-permute-start.7 = (f32[32,256]{1,0:T(8,128)S(1)}, f32[32,256]{1,0:T(8,128)S(1)}, u32[]{:S(2)}, u32[]{:S(2)}) collective-permute-start(f32[32,256]{1,0:T(8,128)S(1)} %get-tuple-element.20), channel_id=1, source_target_pairs={{0,2},{1,3},{2,4},{3,5},{4,6},{5,7},{6,0},{7,1},{8,10},{9,11},{10,... | collective-permute-start | bytes 98312 | tf_op jit(solution)/shard_map/ppermute | solution.py:107
  109.0 1.9 %collective-permute-start.6 = (f32[24,256]{1,0:T(8,128)S(1)}, f32[24,256]{1,0:T(8,128)S(1)}, u32[]{:S(2)}, u32[]{:S(2)}) collective-permute-start(f32[24,256]{1,0:T(8,128)S(1)} %pad_maximum_fusion.1), channel_id=1, source_target_pairs={{0,1},{1,0},{2,3},{3,2},{4,5},{5,4},{6,7},{7,6},{8,9},{9,8},{10,11... | collective-permute-start | bytes 73736 | tf_op jit(solution)/shard_map/ppermute | solution.py:107
  111.0 1.2 %collective-permute-done.6.refs_1_ = f32[24,256]{1,0:T(8,128)S(1)} collective-permute-done((f32[24,256]{1,0:T(8,128)S(1)}, f32[24,256]{1,0:T(8,128)S(1)}, u32[]{:S(2)}, u32[]{:S(2)}) %collective-permute-start.6) | collective-permute-done | bytes 24608 | tf_op jit(solution)/shard_map/ppermute | solution.py:107
  112.1 0.3 collective-permute-done.8.refs_3_
  112.5 0.5 collective-permute-done.7.refs_2_
  112.9 1.4 %shard_map.39 = f32[9,8,256]{2,1,0:T(8,128)} custom-call(s32[16,17]{1,0:T(8,128)S(1)} %copy-done.1, s32[1,9]{1,0:T(1,128)S(1)} %copy-done.2, f32[72,256]{1,0:T(8,128)S(1)} %reduce_sum.19.refs_0_, f32[24,256]{1,0:T(8,128)S(1)} %collective-permute-done.6.refs_1_, f32[32,256]{1,0:T(8,128)S(1)} %collective-permute-done.7.refs_2_, ...), custom_call_target="tpu_custom_call" | custom-call | bytes 271460 | tf_op jit(solution)/shard_map/pallas_call | solution.py:257
  (19 shorter events, 0.5 us)
Async XLA Ops:
  0.0 7.1 %copy-start = (bf16[2,1024,256]{2,1,0:T(8,128)(2,1)S(1)}, bf16[2,1024,256]{2,1,0:T(8,128)(2,1)}, u32[]{:S(2)}) copy-start(bf16[2,1024,256]{2,1,0:T(8,128)(2,1)} %param.3) | copy-start | bytes 3145732
  1.2 18.3 %collective-permute-start.2 = (bf16[1056,256]{1,0:T(8,128)(2,1)S(1)}, bf16[1056,256]{1,0:T(8,128)(2,1)S(1)}, u32[]{:S(2)}, u32[]{:S(2)}) collective-permute-start(bf16[1056,256]{1,0:T(8,128)(2,1)S(1)} %slice.53), channel_id=1, source_target_pairs={{2,0},{3,1},{4,2},{5,3},{6,4},{7,5},{0,6},{1,7},{10,8},{11,9},{12,... | collective-permute-start | bytes 1622024 | tf_op jit(solution)/shard_map/ppermute | solution.py:103
  7.1 27.9 %copy-start.2 = (s32[1,9]{1,0:T(1,128)S(1)}, s32[1,9]{1,0:T(1,128)}, u32[]{:S(2)}) copy-start(s32[1,9]{1,0:T(1,128)} %cols.3) | copy-start | bytes 112
  7.1 26.7 %collective-permute-start.1 = (bf16[2064,256]{1,0:T(8,128)(2,1)S(1)}, bf16[2064,256]{1,0:T(8,128)(2,1)S(1)}, u32[]{:S(2)}, u32[]{:S(2)}) collective-permute-start(bf16[2064,256]{1,0:T(8,128)(2,1)S(1)} %fusion.1), channel_id=1, source_target_pairs={{6,0},{7,1},{0,2},{1,3},{3,4},{2,5},{5,6},{4,7},{15,8},{14,9},{9,1... | collective-permute-start | bytes 3170312 | tf_op jit(solution)/shard_map/ppermute | solution.py:103
  9.1 24.7 %collective-permute-start = (bf16[2064,256]{1,0:T(8,128)(2,1)S(1)}, bf16[2064,256]{1,0:T(8,128)(2,1)S(1)}, u32[]{:S(2)}, u32[]{:S(2)}) collective-permute-start(bf16[2064,256]{1,0:T(8,128)(2,1)S(1)} %fusion.1), channel_id=1, source_target_pairs={{1,0},{0,1},{3,2},{2,3},{5,4},{4,5},{7,6},{6,7},{9,8},{8,9},{11,10... | collective-permute-start | bytes 3170312 | tf_op jit(solution)/shard_map/ppermute | solution.py:103
  16.6 15.3 %collective-permute-start.3 = (bf16[1008,256]{1,0:T(8,128)(2,1)S(1)}, bf16[1008,256]{1,0:T(8,128)(2,1)S(1)}, u32[]{:S(2)}, u32[]{:S(2)}) collective-permute-start(bf16[1008,256]{1,0:T(8,128)(2,1)S(1)} %slice.54), channel_id=1, source_target_pairs={{2,0},{3,1},{4,2},{5,3},{6,4},{7,5},{0,6},{1,7},{10,8},{11,9},{12,... | collective-permute-start | bytes 1548296 | tf_op jit(solution)/shard_map/ppermute | solution.py:103
  19.5 15.5 %collective-permute-start.4 = (bf16[1056,256]{1,0:T(8,128)(2,1)S(1)}, bf16[1056,256]{1,0:T(8,128)(2,1)S(1)}, u32[]{:S(2)}, u32[]{:S(2)}) collective-permute-start(bf16[1056,256]{1,0:T(8,128)(2,1)S(1)} %collective-permute-done.2.x1), channel_id=1, source_target_pairs={{8,0},{9,1},{10,2},{11,3},{12,4},{13,5},{14,6},{15,7},{1,8},{0,9},... | collective-permute-start | bytes 1622024 | tf_op jit(solution)/shard_map/ppermute | solution.py:103
  31.9 14.4 %collective-permute-start.5 = (bf16[1008,256]{1,0:T(8,128)(2,1)S(1)}, bf16[1008,256]{1,0:T(8,128)(2,1)S(1)}, u32[]{:S(2)}, u32[]{:S(2)}) collective-permute-start(bf16[1008,256]{1,0:T(8,128)(2,1)S(1)} %collective-permute-done.3.x2), channel_id=1, source_target_pairs={{8,0},{9,1},{10,2},{11,3},{12,4},{13,5},{14,6},{15,7},{1,8},{0,9},... | collective-permute-start | bytes 1548296 | tf_op jit(solution)/shard_map/ppermute | solution.py:103
  83.2 29.8 %copy-start.1 = (s32[16,17]{1,0:T(8,128)S(1)}, s32[16,17]{1,0:T(8,128)}, u32[]{:S(2)}) copy-start(s32[16,17]{1,0:T(8,128)} %constant.17.clone.table) | copy-start | bytes 3268
  99.8 12.3 %collective-permute-start.9 = (f32[32,256]{1,0:T(8,128)S(1)}, f32[32,256]{1,0:T(8,128)S(1)}, u32[]{:S(2)}, u32[]{:S(2)}) collective-permute-start(f32[32,256]{1,0:T(8,128)S(1)} %pad_maximum_fusion), channel_id=1, source_target_pairs={{0,6},{1,7},{2,0},{3,1},{4,3},{5,2},{6,5},{7,4},{8,15},{9,14},{10,... | collective-permute-start | bytes 98312 | tf_op jit(solution)/shard_map/ppermute | solution.py:107
  105.1 7.3 %collective-permute-start.8 = (f32[32,256]{1,0:T(8,128)S(1)}, f32[32,256]{1,0:T(8,128)S(1)}, u32[]{:S(2)}, u32[]{:S(2)}) collective-permute-start(f32[32,256]{1,0:T(8,128)S(1)} %get-tuple-element.19), channel_id=1, source_target_pairs={{0,10},{1,11},{2,12},{3,13},{4,14},{5,15},{6,8},{7,9},{8,3},{9,2},... | collective-permute-start | bytes 98312 | tf_op jit(solution)/shard_map/ppermute | solution.py:107
  107.1 5.9 %collective-permute-start.7 = (f32[32,256]{1,0:T(8,128)S(1)}, f32[32,256]{1,0:T(8,128)S(1)}, u32[]{:S(2)}, u32[]{:S(2)}) collective-permute-start(f32[32,256]{1,0:T(8,128)S(1)} %get-tuple-element.20), channel_id=1, source_target_pairs={{0,2},{1,3},{2,4},{3,5},{4,6},{5,7},{6,0},{7,1},{8,10},{9,11},{10,... | collective-permute-start | bytes 98312 | tf_op jit(solution)/shard_map/ppermute | solution.py:107
  109.0 3.1 %collective-permute-start.6 = (f32[24,256]{1,0:T(8,128)S(1)}, f32[24,256]{1,0:T(8,128)S(1)}, u32[]{:S(2)}, u32[]{:S(2)}) collective-permute-start(f32[24,256]{1,0:T(8,128)S(1)} %pad_maximum_fusion.1), channel_id=1, source_target_pairs={{0,1},{1,0},{2,3},{3,2},{4,5},{5,4},{6,7},{7,6},{8,9},{9,8},{10,11... | collective-permute-start | bytes 73736 | tf_op jit(solution)/shard_map/ppermute | solution.py:107
